TPU v7x, 32 devices: a whole 2x2x4 slice. The times are simulated.
32 devices in a mesh: dp: 8 (over z, x), tp: 4 (over y, core).
Axes of the slice: x: 2, y: 2, z: 4, core: 2. Of those that a mesh axis runs over, the one named last changes fastest.
Arguments:
- events: float32 [16384, 512], P('dp'), may hold values from -6 to 6
- valid_counts: int32 [8], replicated, may hold values from 1 to 2048, 8192 in all
- mix_cotangent: float32 [16384, 768], P('dp'), may hold values from -6 to 6
- expert_in: float32 [6, 512, 256], P(None, None, 'tp'), may hold values from -0.25 to 0.25
- expert_in_bias: float32 [6, 256], P(None, 'tp'), may hold values from -3 to 3
- expert_out: float32 [6, 256, 256], P(None, None, 'tp'), may hold values from -0.375 to 0.375
- expert_out_bias: float32 [6, 256], P(None, 'tp'), may hold values from -3 to 3
- norm_gain: float32 [6, 256], P(None, 'tp'), may hold values from 0.1 to 1.9
- norm_shift: float32 [6, 256], P(None, 'tp'), may hold values from -2 to 2
- gate_weight: float32 [512, 14], replicated, may hold values from -0.125 to 0.125
Outputs:
- mixtures: float32 [16384, 768], P('dp')
- events_grad: float32 [16384, 512], P('dp')
- expert_in_grad: float32 [6, 512, 256], P(None, None, 'tp')
- expert_in_bias_grad: float32 [6, 256], P(None, 'tp')
- expert_out_grad: float32 [6, 256, 256], P(None, None, 'tp')
- expert_out_bias_grad: float32 [6, 256], P(None, 'tp')
- norm_gain_grad: float32 [6, 256], P(None, 'tp')
- norm_shift_grad: float32 [6, 256], P(None, 'tp')
- gate_weight_grad: float32 [512, 14], replicated
Inputs may be any that keep to these rules, and one draw needn't show every extreme that they name: valid_counts[i] is the number of valid rows of index i of dp, which are its first rows; the entries sum to 1024 times the number of indices of dp, and some entry equals 2048.
All inputs are finite; a program needn't handle non-finite values.
Results may differ from a plain program's by a relative error of at most 0.0003.
Values sent between devices are 32-bit elements; how exact they have to be, the bound alone decides.
No kernel may reach another device: no remote copies, remote signals or barrier semaphores. Data moves between devices by JAX's collectives and lax.ppermute only.
A program may use at most 128 MiB of HBM per device.

v0:
```python
import jax
import jax.numpy as jnp
from jax import lax
from jax.sharding import PartitionSpec as P

D = 512
O = 256
BAL = 1024


highest = lax.Precision.HIGHEST
epsilon = 1e-05


def mixing(logits):
    task_a = jax.nn.softmax(logits[:, 0:4], axis=-1)
    task_b = jax.nn.softmax(logits[:, 4:8], axis=-1)
    shared = jax.nn.softmax(logits[:, 8:14], axis=-1)
    blank = jnp.zeros((logits.shape[0], 2), logits.dtype)
    row_a = jnp.concatenate([task_a[:, 0:2], blank, task_a[:, 2:4]], axis=1)
    row_b = jnp.concatenate([blank, task_b], axis=1)
    return jnp.stack([row_a, row_b, shared], axis=1)


def expert_pass(rows_x, rows_cot, weights):
    w_in, b_in, w_out, b_out, gain, shift, gate_w = weights
    count = rows_x.shape[0]
    pre = jnp.einsum("rd,edh->reh", rows_x, w_in, precision=highest) + b_in[None]
    sigma = jax.nn.sigmoid(pre)
    hidden = pre * sigma
    hidden_all = lax.all_gather(hidden, "tp", axis=2, tiled=True)
    normed_in = jnp.einsum("reh,eho->reo", hidden_all, w_out, precision=highest) + b_out[None]
    first = jnp.sum(normed_in, axis=-1)
    second = jnp.sum(normed_in * normed_in, axis=-1)
    first, second = lax.psum((first, second), "tp")
    mean_z = first / O
    rstd = lax.rsqrt(second / O - mean_z * mean_z + epsilon)
    unit = (normed_in - mean_z[..., None]) * rstd[..., None]
    expert_y = unit * gain[None] + shift[None]
    logits = jnp.dot(rows_x, gate_w, precision=highest)
    coef, coef_pull = jax.vjp(mixing, logits)
    mixed_local = jnp.einsum("rte,reo->rto", coef, expert_y, precision=highest)
    cot_all = rows_cot.reshape(count, 3, O)
    mixed = lax.all_gather(mixed_local, "tp", axis=2, tiled=True)
    cot_local = lax.dynamic_slice_in_dim(
        cot_all, lax.axis_index("tp") * expert_y.shape[2], expert_y.shape[2], 2
    )
    dy = jnp.einsum("rte,rto->reo", coef, cot_local, precision=highest)
    dcoef = jnp.einsum("rto,reo->rte", cot_local, expert_y, precision=highest)
    gain_grad = jnp.sum(dy * unit, axis=0)
    shift_grad = jnp.sum(dy, axis=0)
    dunit = dy * gain[None]
    back_first = jnp.sum(dunit, axis=-1)
    back_second = jnp.sum(dunit * unit, axis=-1)
    dcoef, back_first, back_second = lax.psum((dcoef, back_first, back_second), "tp")
    dnormed = rstd[..., None] * (
        dunit - back_first[..., None] / O - unit * back_second[..., None] / O
    )
    out_bias_grad = jnp.sum(dnormed, axis=0)
    out_grad = jnp.einsum("reh,reo->eho", hidden_all, dnormed, precision=highest)
    dhidden = jnp.einsum("reo,eho->reh", dnormed, w_out, precision=highest)
    dhidden = lax.psum_scatter(dhidden, "tp", scatter_dimension=2, tiled=True)
    dpre = dhidden * sigma * (1.0 + pre * (1.0 - sigma))
    in_bias_grad = jnp.sum(dpre, axis=0)
    in_grad = jnp.einsum("rd,reh->edh", rows_x, dpre, precision=highest)
    x_grad = jnp.einsum("reh,edh->rd", dpre, w_in, precision=highest)
    x_grad = lax.psum(x_grad, "tp")
    (dlogits,) = coef_pull(dcoef)
    gate_grad = jnp.dot(rows_x.T, dlogits, precision=highest)
    x_grad = x_grad + jnp.dot(dlogits, gate_w.T, precision=highest)
    grads = (in_grad, in_bias_grad, out_grad, out_bias_grad, gain_grad, shift_grad, gate_grad)
    return (mixed.reshape(count, 3 * O), x_grad, grads)


def per_device(
    events,
    valid_counts,
    mix_cotangent,
    expert_in,
    expert_in_bias,
    expert_out,
    expert_out_bias,
    norm_gain,
    norm_shift,
    gate_weight,
):
    devices_dp = lax.axis_size("dp")
    rank = lax.axis_index("dp")
    slots = events.shape[0]
    live = (jnp.arange(slots, dtype=jnp.int32) < valid_counts[rank]).astype(jnp.float32)[:, None]
    per_peer = slots // devices_dp
    starts = jnp.cumsum(valid_counts) - valid_counts
    offset = starts[rank] % devices_dp

    def to_slots(values):
        return jnp.roll(
            (values * live).reshape(per_peer, devices_dp, values.shape[1]), offset, axis=1
        )

    sent_x = to_slots(events)
    sent_cot = to_slots(mix_cotangent)
    got_x, got_cot = (
        lax.all_to_all(sent_x, "dp", split_axis=1, concat_axis=1, tiled=True),
        lax.all_to_all(sent_cot, "dp", split_axis=1, concat_axis=1, tiled=True),
    )
    global_rank = jnp.arange(BAL, dtype=jnp.int32) * devices_dp + rank
    ends = jnp.cumsum(valid_counts)
    source = jnp.sum((ends[None, :] <= global_rank[:, None]).astype(jnp.int32), axis=1)
    one_hot = (source[:, None] == jnp.arange(devices_dp, dtype=jnp.int32)[None, :]).astype(
        jnp.int32
    )
    within = global_rank - jnp.sum(one_hot * starts[None, :], axis=1)
    flat_slot = within // devices_dp * devices_dp + source
    rows_x = got_x.reshape(per_peer * devices_dp, D)[flat_slot]
    rows_cot = got_cot.reshape(per_peer * devices_dp, 3 * O)[flat_slot]
    weights = (
        expert_in,
        expert_in_bias,
        expert_out,
        expert_out_bias,
        norm_gain,
        norm_shift,
        gate_weight,
    )
    mixed, x_grad, grads = expert_pass(rows_x, rows_cot, weights)
    in_grad, in_bias_grad, out_grad, out_bias_grad, gain_grad, shift_grad, gate_grad = grads

    def home_slots(values):
        placed = (
            jnp.zeros((per_peer * devices_dp, values.shape[1]), jnp.float32)
            .at[flat_slot]
            .set(values)
        )
        return placed.reshape(per_peer, devices_dp, values.shape[1])

    home_mix = home_slots(mixed)
    home_grad = home_slots(x_grad)
    back_mix, back_grad = (
        lax.all_to_all(home_mix, "dp", split_axis=1, concat_axis=1, tiled=True),
        lax.all_to_all(home_grad, "dp", split_axis=1, concat_axis=1, tiled=True),
    )
    mixed = jnp.roll(back_mix, -offset, axis=1).reshape(slots, 3 * O)
    x_grad = jnp.roll(back_grad, -offset, axis=1).reshape(slots, D)
    summed = lax.psum(
        (in_grad, in_bias_grad, out_grad, out_bias_grad, gain_grad, shift_grad, gate_grad), "dp"
    )
    return (
        mixed,
        x_grad,
        summed[0],
        summed[1],
        summed[2],
        summed[3],
        summed[4],
        summed[5],
        summed[6],
    )


def solution(mesh):
    return jax.shard_map(
        per_device,
        mesh=mesh,
        in_specs=(
            P("dp", None),
            P(),
            P("dp", None),
            P(None, None, "tp"),
            P(None, "tp"),
            P(None, None, "tp"),
            P(None, "tp"),
            P(None, "tp"),
            P(None, "tp"),
            P(),
        ),
        out_specs=(
            P("dp", None),
            P("dp", None),
            P(None, None, "tp"),
            P(None, "tp"),
            P(None, None, "tp"),
            P(None, "tp"),
            P(None, "tp"),
            P(None, "tp"),
            P(),
        ),
        check_vma=False,
    )
```

profile of v0, /device:TPU:0, one launch (start us, length us, event | category | flops | bytes accessed | tf_op | source)
XLA Modules:
  0.0 720.4 jit_solution(4291756926835952626)
XLA Ops:
  16.9 4.4 copy.87
  21.3 7.3 %all-to-all-start = ((f32[256,8,512]{2,0,1:T(8,128)}), f32[256,8,512]{2,0,1:T(8,128)}, u32[]{:S(2)}, u32[]{:S(2)}) async-start(f32[256,8,512]{2,0,1:T(8,128)} %copy.87), calls=%async_computation | async-start | bytes 8388608 | tf_op jit(solution)/shard_map/all_to_all | solution.py:103
  33.4 4.6 copy.96
  38.1 83.8 %all-to-all-done = f32[256,8,512]{2,0,1:T(8,128)} async-done(((f32[256,8,512]{2,0,1:T(8,128)}), f32[256,8,512]{2,0,1:T(8,128)}, u32[]{:S(2)}, u32[]{:S(2)}) %all-to-all-start) | async-done | bytes 4194336 | tf_op jit(solution)/shard_map/all_to_all | solution.py:103
  121.8 4.8 all-to-all-start.2
  127.1 6.6 copy.114
  133.7 6.2 gather_fusion
  150.1 113.8 %all-to-all-done.2 = f32[256,8,768]{2,0,1:T(8,128)} async-done(((f32[256,8,768]{2,0,1:T(8,128)}), f32[256,8,768]{2,0,1:T(8,128)}, u32[]{:S(2)}, u32[]{:S(2)}) %all-to-all-start.2) | async-done | bytes 6291488 | tf_op jit(solution)/shard_map/all_to_all | solution.py:104
  263.9 9.1 %copy.113 = f32[256,8,768]{2,1,0:T(8,128)} copy(f32[256,8,768]{2,0,1:T(8,128)} %all-to-all-done.2) | data formatting | bytes 12582912 | tf_op jit(solution)/shard_map/all_to_all | solution.py:104
  273.0 8.6 %gather_fusion.1 = f32[1024,768]{1,0:T(8,128)} fusion(f32[2048,768]{1,0:T(8,128)} %bitcast.96, s32[1024]{0:T(1024)S(1)} %broadcast_clamp_fusion), kind=kCustom, calls=%fused_computation.1 | custom fusion | bytes 6295552 | tf_op jit(solution)/shard_map/gather | solution.py:115
  290.0 11.4 %fusion.31 = (f32[6,64]{1,0:T(8,128)S(1)}, f32[1024,6,64]{2,1,0:T(8,128)}) fusion(f32[1024,3,6]{2,1,0:T(4,128)} %copy.89, f32[1024,3,64]{2,1,0:T(4,128)} %copy.110), kind=kOutput, calls=%fused_computation.100 | convolution fusion | flops 14548608 | bytes 2434560 | tf_op jit(solution)/shard_map/rte,rto->reo/dot_general | solution.py:48
  305.2 8.0 %bitcast_reduce_fusion = (f32[1024,6]{0,1:T(8,128)S(1)}, f32[1024,6]{0,1:T(8,128)S(1)}, f32[6,1024,64]{1,2,0:T(8,128)}) fusion(f32[6,64]{1,0:T(8,128)S(1)} %copy-done.8, f32[1024,6,256]{0,2,1:T(8,128)} %all-gather.3.cloned.1.call-done, f32[6,256,64]{1,2,0:T(8,128)S(1)} %copy-done.4), kind=kOutput, calls=%fused_computation.33 | convolution fusion | flops 1209520128 | bytes 8308224 | tf_op jit(solution)/shard_map/reh,eho->reo/dot_general | solution.py:32
  313.2 10.8 %all-reduce.8 = (f32[1024,6]{0,1:T(8,128)S(1)}, f32[1024,6]{0,1:T(8,128)S(1)}) all-reduce(f32[1024,6]{0,1:T(8,128)S(1)} %get-tuple-element.15, f32[1024,6]{0,1:T(8,128)S(1)} %get-tuple-element.14), channel_id=1, replica_groups=mesh['dp'=8,'tp'=4] {'tp'}, use_global_device_ids=true, to_apply=%region_12.14 | all-reduce | flops 12288 | bytes 98304 | tf_op jit(solution)/shard_map/psum | solution.py:35
  326.7 12.0 %all-reduce.7 = (f32[1024,6]{0,1:T(8,128)}, f32[1024,6]{0,1:T(8,128)}) all-reduce(f32[1024,6]{0,1:T(8,128)S(1)} %get-tuple-element.12, f32[1024,6]{0,1:T(8,128)S(1)} %get-tuple-element.13), channel_id=1, replica_groups=mesh['dp'=8,'tp'=4] {'tp'}, use_global_device_ids=true, to_apply=%region_17.20 | all-reduce | flops 12288 | bytes 98304 | tf_op jit(solution)/shard_map/psum | solution.py:55
  347.4 11.0 %fusion.34 = f32[1024,3,64]{2,1,0:T(4,128)} fusion(f32[1024,3,6]{2,1,0:T(4,128)} %copy.89, f32[1024,6,64]{2,1,0:T(8,128)} %copy.90), kind=kOutput, calls=%fused_computation.103 | convolution fusion | flops 14155776 | bytes 2433024 | tf_op jit(solution)/shard_map/rte,reo->rto/dot_general | solution.py:42
  361.0 8.6 %convolution_bitcast_fusion = f32[1024,6,256]{0,2,1:T(8,128)} fusion(f32[1024,6,64]{0,2,1:T(8,128)} %get-tuple-element.36, f32[6,256,64]{1,2,0:T(8,128)S(1)} %copy-done.4), kind=kOutput, calls=%fused_computation.24 | convolution fusion | flops 1207959552 | bytes 8257536 | tf_op jit(solution)/shard_map/reo,eho->reh/dot_general | solution.py:61
  369.7 18.7 %all-gather.5.cloned.1.call-done = f32[1024,3,256]{0,2,1:T(8,128)} async-done(((f32[1024,3,64]{0,2,1:T(8,128)}), f32[1024,3,256]{0,2,1:T(8,128)}) %all-gather.5.cloned.1.call-update) | async-done | bytes 3145744 | tf_op jit(solution)/shard_map/all_gather | solution.py:44
  391.9 9.7 %scatter_custom_fusion = f32[2048,768]{1,0:T(8,128)} fusion(s32[1024]{0:T(1024)S(1)} %bitcast.106, f32[1024,768]{1,0:T(8,128)} %copy.92, f32[]{:T(128)} %constant.86.clone.1), kind=kCustom, calls=%fused_computation.22 | custom fusion | bytes 6291968 | tf_op jit(solution)/shard_map/scatter | solution.py:132
  401.6 7.8 %copy.93 = f32[256,8,768]{2,0,1:T(8,128)} copy(f32[256,8,768]{2,1,0:T(8,128)} %bitcast.98) | data formatting | bytes 12582912 | tf_op jit(solution)/shard_map/reshape | solution.py:134
  409.3 5.5 all-to-all-start.1
  415.2 11.1 %fusion.35 = f32[1024,3,6]{2,1,0:T(4,128)} fusion(f32[1024,3,64]{2,1,0:T(4,128)} %copy.110, f32[1024,6,64]{2,1,0:T(8,128)} %copy.90), kind=kOutput, calls=%fused_computation.104 | convolution fusion | flops 14155776 | bytes 2433024 | tf_op jit(solution)/shard_map/rto,reo->rte/dot_general | solution.py:49
  429.0 20.3 %reduce-scatter.2.cloned.1.call-done = f32[1024,6,64]{0,2,1:T(8,128)} async-done(((f32[1024,6,256]{0,2,1:T(8,128)}), f32[1024,6,64]{0,2,1:T(8,128)}) %reduce-scatter.2.cloned.1.call-update) | async-done | bytes 1572880 | tf_op jit(solution)/shard_map/reduce_scatter | solution.py:62
  453.1 4.8 convolution_bitcast_fusion.1
  457.9 53.3 %all-reduce.15.cloned.1.call-done = (f32[1024,512]{1,0:T(8,128)}, f32[1024,3,6]{0,2,1:T(8,128)}) async-done(((f32[1024,512]{1,0:T(8,128)}, f32[1024,3,6]{0,2,1:T(8,128)}), (f32[1024,512]{1,0:T(8,128)}, f32[1024,3,6]{0,2,1:T(8,128)})) %all-reduce.15.cloned.1.call-update) | async-done | bytes 2170896 | tf_op jit(solution)/shard_map/psum | solution.py:67
  517.0 8.2 %scatter_custom_fusion.1 = f32[2048,512]{1,0:T(8,128)} fusion(s32[1024]{0:T(1024)S(1)} %bitcast.107, f32[1024,512]{1,0:T(8,128)} %get-tuple-element.33, f32[1024,512]{1,0:T(8,128)} %fusion.20, f32[]{:T(128)} %constant.86.clone.1), kind=kCustom, calls=%fused_computation.27 | custom fusion | flops 524288 | bytes 8388612 | tf_op jit(solution)/shard_map/scatter | solution.py:132
  525.2 6.6 copy.105
  531.8 21.6 %all-to-all-done.1 = f32[256,8,768]{2,0,1:T(8,128)} async-done(((f32[256,8,768]{2,0,1:T(8,128)}), f32[256,8,768]{2,0,1:T(8,128)}, u32[]{:S(2)}, u32[]{:S(2)}) %all-to-all-start.1) | async-done | bytes 6291488 | tf_op jit(solution)/shard_map/all_to_all | solution.py:139
  553.4 4.6 all-to-all-start.3
  558.3 10.3 %fusion.36 = f32[6,256,64]{1,2,0:T(8,128)} fusion(f32[1024,6,256]{0,2,1:T(8,128)} %all-gather.3.cloned.1.call-done, f32[1024,6,64]{0,2,1:T(8,128)} %get-tuple-element.36), kind=kOutput, calls=%fused_computation.105 | convolution fusion | flops 1207959552 | bytes 8257536 | tf_op jit(solution)/shard_map/reh,reo->eho/dot_general | solution.py:60
  573.4 117.4 %all-reduce.5 = (f32[6,64]{1,0:T(8,128)}, f32[6,64]{1,0:T(8,128)}, f32[6,64]{1,0:T(8,128)}, f32[6,64]{1,0:T(8,128)}, f32[512,14]{0,1:T(8,128)}) all-reduce(f32[6,64]{1,0:T(8,128)S(1)} %get-tuple-element.37, f32[6,64]{1,0:T(8,128)S(1)} %get-tuple-element.35, ...), channel_id=1, replica_groups=mesh['dp'=8,'tp'=4] {'dp'}, use_global_device_ids=true, to_apply=%region_27.30 | all-reduce | flops 8704 | bytes 69632 | tf_op jit(solution)/shard_map/psum | solution.py:144
  690.8 6.6 copy.94
  701.8 4.6 copy.106
  (95 shorter events, 81.6 us)
Async XLA Ops:
  7.2 132.8 %copy-start = (f32[6,512,64]{1,2,0:T(8,128)S(1)}, f32[6,512,64]{1,2,0:T(8,128)}, u32[]{:S(2)}) copy-start(f32[6,512,64]{1,2,0:T(8,128)} %param.17) | copy-start | bytes 2359300
  21.3 100.5 %all-to-all-start = ((f32[256,8,512]{2,0,1:T(8,128)}), f32[256,8,512]{2,0,1:T(8,128)}, u32[]{:S(2)}, u32[]{:S(2)}) async-start(f32[256,8,512]{2,0,1:T(8,128)} %copy.87), calls=%async_computation | async-start | bytes 8388608 | tf_op jit(solution)/shard_map/all_to_all | solution.py:103
  121.8 142.0 %all-to-all-start.2 = ((f32[256,8,768]{2,0,1:T(8,128)}), f32[256,8,768]{2,0,1:T(8,128)}, u32[]{:S(2)}, u32[]{:S(2)}) async-start(f32[256,8,768]{2,0,1:T(8,128)} %copy.96), calls=%async_computation.2 | async-start | bytes 12582912 | tf_op jit(solution)/shard_map/all_to_all | solution.py:104
  126.6 178.6 %all-gather.3.cloned.1.call-start = ((), (), s32[]{:S(2)}) async-start(), calls=%async_computation.5 | async-start | bytes 7864320 | tf_op jit(solution)/shard_map/all_gather | solution.py:31
  139.9 4.0 copy-start.6
  142.7 1.2 copy-start.1
  143.9 2.2 copy-start.5
  145.6 242.8 %all-gather.5.cloned.1.call-start = ((), (), s32[]{:S(2)}) async-start(), calls=%async_computation.6 | async-start | bytes 3932160 | tf_op jit(solution)/shard_map/all_gather | solution.py:44
  301.3 3.8 copy-start.4
  301.4 3.8 copy-start.8
  305.1 18.9 %copy-start.7 = (f32[6,64]{1,0:T(8,128)S(1)}, f32[6,64]{1,0:T(8,128)}, u32[]{:S(2)}) copy-start(f32[6,64]{1,0:T(8,128)} %param.21) | copy-start | bytes 4612
  313.2 26.2 %copy-start.9 = (f32[6,64]{1,0:T(8,128)S(1)}, f32[6,64]{1,0:T(8,128)}, u32[]{:S(2)}) copy-start(f32[6,64]{1,0:T(8,128)} %param.22) | copy-start | bytes 4612
  361.0 88.3 %reduce-scatter.2.cloned.1.call-start = ((), (), s32[]{:S(2)}) async-start(), calls=%async_computation.7 | async-start | bytes 7864320 | tf_op jit(solution)/shard_map/reduce_scatter | solution.py:62
  409.3 144.1 %all-to-all-start.1 = ((f32[256,8,768]{2,0,1:T(8,128)}), f32[256,8,768]{2,0,1:T(8,128)}, u32[]{:S(2)}, u32[]{:S(2)}) async-start(f32[256,8,768]{2,0,1:T(8,128)} %copy.93), calls=%async_computation.1 | async-start | bytes 12582912 | tf_op jit(solution)/shard_map/all_to_all | solution.py:139
  414.8 96.4 %all-reduce.15.cloned.1.call-start = ((), (), s32[]{:S(2)}) async-start(), calls=%async_computation.9 | async-start | bytes 4390912 | tf_op jit(solution)/shard_map/psum | solution.py:67
  451.9 1.1 copy-start.2
  457.9 54.9 %copy-start.10 = (pred[4]{0:T(512)(128)(4,1)S(1)}, pred[4]{0:T(512)(128)(4,1)}, u32[]{:S(2)}) copy-start(pred[4]{0:T(512)(128)(4,1)} %constant.103.clone.1) | copy-start | bytes 16
  553.4 148.4 %all-to-all-start.3 = ((f32[256,8,512]{2,0,1:T(8,128)}), f32[256,8,512]{2,0,1:T(8,128)}, u32[]{:S(2)}, u32[]{:S(2)}) async-start(f32[256,8,512]{2,0,1:T(8,128)} %copy.105), calls=%async_computation.4 | async-start | bytes 8388608 | tf_op jit(solution)/shard_map/all_to_all | solution.py:140
  558.0 151.6 %all-reduce.13.cloned.1.call-start = ((), (), s32[]{:S(2)}) async-start(), calls=%async_computation.8 | async-start | bytes 2359296 | tf_op jit(solution)/shard_map/psum | solution.py:144
  558.3 10.3 %copy-start.3 = (f32[1024,6,64]{0,2,1:T(8,128)S(1)}, f32[1024,6,64]{0,2,1:T(8,128)}, u32[]{:S(2)}) copy-start(f32[1024,6,64]{0,2,1:T(8,128)} %copy-done.2) | copy-start | bytes 4718596
Sparse Core Ops, SparseCore 0:
  145.7 47.6 all-gather.2
  361.1 27.2 all-gather.4
  390.9 58.3 reduce-scatter.1
  458.0 53.1 all-reduce.14
  572.3 136.8 all-reduce.12
where the time goes:
time: 728 us; the launch traced here: 720 us
  waiting for transfers between devices  312 us (43%)
  blocking collectives  140 us (19%)
  local copies, waits for them, and re-layouts  110 us (15%)
  matrix products  77.8 us (11%)
  other arithmetic  40.5 us (6%)
  starting transfers between devices  23.5 us (3%)
  between operations  16.6 us (2%)
    psum x1, blocking collectives, per_device(): lax.psum((in_grad, in_bias_grad, out_grad, out_bias_grad, gain_grad, shif...  117 us
    all_to_all x1, waiting for transfers between devices, per_device(): lax.all_to_all(sent_cot, 'dp', split_axis=1, concat_axis=1, tiled=True)  114 us
    all_to_all x1, waiting for transfers between devices, per_device(): lax.all_to_all(sent_x, 'dp', split_axis=1, concat_axis=1, tiled=True)  83.8 us
    psum x1, waiting for transfers between devices, expert_pass(): x_grad = lax.psum(x_grad, 'tp')  53.3 us
    all_to_all x1, waiting for transfers between devices, per_device(): lax.all_to_all(home_mix, 'dp', split_axis=1, concat_axis=1, tiled=True)  21.6 us
    reduce_scatter x1, waiting for transfers between devices, expert_pass(): dhidden = lax.psum_scatter(dhidden, 'tp', scatter_dimension=2, tiled=True)  20.3 us
    all_gather x1, waiting for transfers between devices, expert_pass(): mixed = lax.all_gather(mixed_local, 'tp', axis=2, tiled=True)  18.7 us
  transfers between devices with their start and end apart: 9, of which 6 were waited for; matrix products, arithmetic and copies ran while one was open for 25% of the time, Pallas kernels for 0%

commit v1 on v0

v1 whole, which is shorter than its diff:
```python
import functools

import jax
import jax.numpy as jnp
from jax import lax
from jax.experimental import pallas as pl
from jax.experimental.pallas import tpu as pltpu
from jax.sharding import PartitionSpec as P

D = 512
H = 256
O = 256
E = 6
GATE_COLS = 14
SLICE = 64
WIDE = D + H
LANES = 128
RB = 256
EPSILON = 1e-05
GROUPS = ((0, 1), (2, 3), (4, 5))
COLUMN = (
    {0: 0, 1: 1, 4: 2, 5: 3},
    {2: 4, 3: 5, 4: 6, 5: 7},
    {e: 8 + e for e in range(E)},
)
F32 = jnp.float32
BF16 = jnp.bfloat16
NN = (((1,), (0,)), ((), ()))
NT = (((1,), (1,)), ((), ()))
TN = (((0,), (0,)), ((), ()))


def split(v):
    high = v.astype(BF16)
    return high, (v - high.astype(F32)).astype(BF16)


def dot3(a, b, dims):
    def one(u, v):
        return lax.dot_general(u, v, dims, preferred_element_type=F32)

    return one(a[0], b[0]) + (one(a[0], b[1]) + one(a[1], b[0]))


def half_of(v, upper):
    return jnp.where(upper, v[:, LANES:], v[:, :LANES])


def params(mib, semantics=None):
    return pltpu.CompilerParams(vmem_limit_bytes=mib << 20, dimension_semantics=semantics)


def gate_kernel(pos, ev_ref, gw_ref, high_ref, low_ref, p_ref, gw):
    gw[...] = jnp.zeros_like(gw)
    gw[:GATE_COLS, :] = gw_ref[...]
    events = split(ev_ref[...])
    high_ref[...], low_ref[...] = events
    logits = dot3(events, split(gw[...]), NT)
    lane = lax.broadcasted_iota(jnp.int32, logits.shape, 1)
    sets = (lane < 4, (lane >= 4) & (lane < 8), (lane >= 8) & (lane < GATE_COLS))

    def per_set(values, empty, reduce):
        a, b, s = (reduce(jnp.where(m, values, empty), axis=1, keepdims=True) for m in sets)
        return jnp.where(sets[0], a, jnp.where(sets[1], b, s))

    top = per_set(logits, -3e38, jnp.max)
    shares = jnp.where(lane < GATE_COLS, jnp.exp(logits - top), 0.0)
    p = shares / per_set(shares, 0.0, jnp.sum)
    rows = pl.num_programs(0) * RB
    row = (pos[0] & 1) * rows + pl.program_id(0) * RB
    row = row + lax.broadcasted_iota(jnp.int32, logits.shape, 0)
    p_ref[...] = jnp.where((row < pos[1]) & (lane < GATE_COLS), p, 0.0)


def gates(pos, events, gate_w, rows):
    steps = rows // RB
    spec = lambda width: pl.BlockSpec((RB, width), lambda i, pos: (i, 0))
    return pl.pallas_call(
        gate_kernel,
        grid_spec=pltpu.PrefetchScalarGridSpec(
            num_scalar_prefetch=1,
            grid=(steps,),
            in_specs=[
                pl.BlockSpec((RB, D), lambda i, pos: ((pos[0] & 1) * steps + i, 0)),
                pl.BlockSpec((GATE_COLS, D), lambda i, pos: (0, 0)),
            ],
            out_specs=[spec(D), spec(D), spec(LANES)],
            scratch_shapes=[pltpu.VMEM((LANES, D), F32)],
        ),
        out_shape=[
            jax.ShapeDtypeStruct((rows, D), BF16),
            jax.ShapeDtypeStruct((rows, D), BF16),
            jax.ShapeDtypeStruct((rows, LANES), F32),
        ],
        compiler_params=params(24),
        cost_estimate=pl.CostEstimate(flops=6 * rows * D * LANES, bytes_accessed=rows * D * 8, transcendentals=0),
    )(pos, events, gate_w)


def expert_kernel(group, first, last, *refs):
    n = len(group)
    refs = list(refs)
    pos, evh_ref, evl_ref, cot_ref, p_ref = refs[:5]
    shards, small_ref = refs[5:9], refs[9]
    del refs[:10]
    mix_in = None if first else refs.pop(0)
    if last:
        dp_before, sums_before = refs[: len(GROUPS) - 1], refs[len(GROUPS) - 1 : 2 * len(GROUPS) - 2]
        del refs[: 2 * len(GROUPS) - 2]
    mix_ref, dp_ref, dph_ref, dpl_ref, winh, winl, own_ref, part_ref, sums_ref = refs[:9]
    del refs[:9]
    wouth, woutl, small, acc, sums = refs[:5]
    gate_acc = refs[5] if last else None
    step, steps = pl.program_id(0), pl.num_programs(0)
    me = pos[0]
    upper = (me >> 1) == 1

    @pl.when(step == 0)
    def _():
        acc[...] = jnp.zeros_like(acc)
        sums[...] = jnp.zeros_like(sums)
        if last:
            gate_acc[...] = jnp.zeros_like(gate_acc)
        for i, e in enumerate(group):
            parts = [shard[i] for shard in shards]
            centre = sum(jnp.sum(part[:, D:], axis=0, keepdims=True) for part in parts) / O
            for k, part in enumerate(parts):
                at = pl.multiple_of((me ^ k) * SLICE, SLICE)
                winh[pl.ds(i * H + at, SLICE), :], winl[pl.ds(i * H + at, SLICE), :] = split(part[:, :D])
                out = split(part[:, D:] - centre)
                wouth[i, pl.ds(at, SLICE), :], woutl[i, pl.ds(at, SLICE), :] = out
            for k in range(4):
                small[i, k : k + 1, :] = jnp.concatenate(
                    [small_ref[j, k, e : e + 1, :] for j in range(4)], axis=1
                )
            small[i, 1:2, :] = small[i, 1:2, :] - jnp.mean(small[i, 1:2, :], axis=1, keepdims=True)

    events = evh_ref[...], evl_ref[...]
    p = p_ref[...]
    lane = lax.broadcasted_iota(jnp.int32, p.shape, 1)
    dp = jnp.zeros_like(p)
    mixed = {}
    dpre_halves = []
    for i, e in enumerate(group):
        win = winh[i * H : (i + 1) * H, :], winl[i * H : (i + 1) * H, :]
        wout = wouth[i], woutl[i]
        b_in, b_out, gain, shift = (small[i, k : k + 1, :] for k in range(4))
        pre = dot3(events, win, NT) + b_in
        sigma = jax.nn.sigmoid(pre)
        hidden = pre * sigma
        hidden_parts = split(hidden)
        centred = dot3(hidden_parts, wout, NT) + b_out
        rstd = lax.rsqrt(jnp.mean(centred * centred, axis=1, keepdims=True) + EPSILON)
        unit = centred * rstd
        y = unit * gain + shift
        dy = None
        for t in range(3):
            if e not in COLUMN[t]:
                continue
            column = COLUMN[t][e]
            cot = cot_ref[:, t * O : (t + 1) * O]
            coef = p[:, column : column + 1]
            mixed[t] = coef * y + mixed[t] if t in mixed else coef * y
            dp = jnp.where(lane == column, jnp.sum(cot * y, axis=1, keepdims=True), dp)
            dy = coef * cot if dy is None else dy + coef * cot
        dunit = dy * gain
        back_first = jnp.mean(dunit, axis=1, keepdims=True)
        back_second = jnp.mean(dunit * unit, axis=1, keepdims=True)
        dnormed = rstd * (dunit - back_first - unit * back_second)
        dnormed_parts = split(dnormed)
        dhidden = dot3(dnormed_parts, wout, NN)
        dpre = dhidden * (sigma + hidden * (1.0 - sigma))
        dpre_parts = split(dpre)
        dph_ref[:, i * H : (i + 1) * H], dpl_ref[:, i * H : (i + 1) * H] = dpre_parts
        dpre_halves.append(tuple(half_of(v, upper) for v in dpre_parts))
        out_halves = tuple(half_of(v, upper) for v in dnormed_parts)
        acc[i * LANES : (i + 1) * LANES, D:] += dot3(out_halves, hidden_parts, TN)
        dy_half = half_of(dy, upper)
        for k, v in enumerate(
            (half_of(dpre, upper), half_of(dnormed, upper), dy_half * half_of(unit, upper), dy_half)
        ):
            sums[4 * i + k : 4 * i + k + 1, :] += jnp.sum(v, axis=0, keepdims=True)
    dpre_half = tuple(jnp.concatenate([h[k] for h in dpre_halves], axis=1) for k in range(2))
    acc[:, :D] += dot3(dpre_half, events, TN)
    for t in range(3):
        at = slice(t * O, (t + 1) * O)
        if t in mixed:
            mix_ref[:, at] = mixed[t] if first else mix_in[:, at] + mixed[t]
        else:
            mix_ref[:, at] = jnp.zeros_like(mix_ref[:, at]) if first else mix_in[:, at]
    if last:
        for other in dp_before:
            dp = dp + other[...]
        weighted = p * dp
        sets = (lane < 4, (lane >= 4) & (lane < 8), (lane >= 8) & (lane < GATE_COLS))
        a, b, s = (jnp.sum(jnp.where(m, weighted, 0.0), axis=1, keepdims=True) for m in sets)
        dlogits = weighted - p * jnp.where(sets[0], a, jnp.where(sets[1], b, s))
        dp_ref[...] = dlogits
        gate_acc[...] += dot3(split(dlogits), events, TN)
    else:
        dp_ref[...] = dp

    @pl.when(step == steps - 1)
    def _():
        mine = pl.multiple_of((me & 1) * SLICE, SLICE)
        other = pl.multiple_of(SLICE - mine, SLICE)
        for i in range(n):
            for t in range(WIDE // LANES):
                at = slice((t * n + i) * SLICE, (t * n + i + 1) * SLICE)
                lanes = slice(t * LANES, (t + 1) * LANES)
                own_ref[at, :] = acc[pl.ds(i * LANES + mine, SLICE), lanes]
                part_ref[at, :] = acc[pl.ds(i * LANES + other, SLICE), lanes]
        if last:
            sums_ref[...] = jnp.zeros_like(sums_ref)
            for g, before in enumerate(sums_before):
                sums_ref[8 * g : 8 * g + 8, :] = before[...]
            g = len(GROUPS) - 1
            sums_ref[8 * g : 8 * g + 8, :] = sums[...]
            for t in range(D // LANES):
                sums_ref[64 + 16 * t : 80 + 16 * t, :] = gate_acc[:16, t * LANES : (t + 1) * LANES]
        else:
            sums_ref[...] = sums[...]


def experts(pos, group, rows, high, low, cot, p, shards, small, mix, before):
    n = len(group)
    first, last = mix is None, before is not None
    steps = rows // RB
    block = lambda width: pl.BlockSpec((RB, width), lambda i, pos: (i, 0))
    whole = lambda shape: pl.BlockSpec(shape, lambda i, pos: (0,) * len(shape))
    in_specs = [
        block(D),
        block(D),
        pl.BlockSpec((RB, 3 * O), lambda i, pos: ((pos[0] & 1) * steps + i, 0)),
        block(LANES),
        *[whole((n, SLICE, WIDE))] * 4,
        whole(small.shape),
    ]
    args = [high, low, cot, p, *shards, small]
    aliases = {}
    if not first:
        aliases = {len(args) + 1: 0}
        in_specs.append(block(3 * O))
        args.append(mix)
    if last:
        in_specs += [block(LANES)] * len(before[0]) + [whole((8, LANES))] * len(before[1])
        args += [*before[0], *before[1]]
    payload = WIDE // LANES * n * SLICE
    sums_shape = (2 * LANES // 2, LANES) if last else (8, LANES)
    scratch = [
        pltpu.VMEM((n, O, H), BF16),
        pltpu.VMEM((n, O, H), BF16),
        pltpu.VMEM((n, 8, H), F32),
        pltpu.VMEM((n * LANES, WIDE), F32),
        pltpu.VMEM((8, LANES), F32),
    ]
    if last:
        scratch.append(pltpu.VMEM((LANES, D), F32))
    return pl.pallas_call(
        functools.partial(expert_kernel, group, first, last),
        grid_spec=pltpu.PrefetchScalarGridSpec(
            num_scalar_prefetch=1,
            grid=(steps,),
            in_specs=in_specs,
            out_specs=[
                block(3 * O),
                block(LANES),
                block(n * H),
                block(n * H),
                whole((n * H, D)),
                whole((n * H, D)),
                whole((payload, LANES)),
                whole((payload, LANES)),
                whole(sums_shape),
            ],
            scratch_shapes=scratch,
        ),
        out_shape=[
            jax.ShapeDtypeStruct((rows, 3 * O), F32),
            jax.ShapeDtypeStruct((rows, LANES), F32),
            jax.ShapeDtypeStruct((rows, n * H), BF16),
            jax.ShapeDtypeStruct((rows, n * H), BF16),
            jax.ShapeDtypeStruct((n * H, D), BF16),
            jax.ShapeDtypeStruct((n * H, D), BF16),
            jax.ShapeDtypeStruct((payload, LANES), F32),
            jax.ShapeDtypeStruct((payload, LANES), F32),
            jax.ShapeDtypeStruct(sums_shape, F32),
        ],
        input_output_aliases=aliases,
        compiler_params=params(48),
        cost_estimate=pl.CostEstimate(flops=n * rows * 6 * 720896, bytes_accessed=rows * 14000, transcendentals=0),
    )(pos, *args)


def event_kernel(n_groups, pos, *refs):
    highs, lows = refs[:n_groups], refs[n_groups : 2 * n_groups]
    winh, winl = refs[2 * n_groups : 3 * n_groups], refs[3 * n_groups : 4 * n_groups]
    dlogits, gw_ref, out, gw = refs[4 * n_groups :]
    gw[...] = jnp.zeros_like(gw)
    gw[:GATE_COLS, :] = gw_ref[...]
    total = dot3(split(dlogits[...]), split(gw[...]), NN)
    for g in range(n_groups):
        total = total + dot3((highs[g][...], lows[g][...]), (winh[g][...], winl[g][...]), NN)
    out[...] = total


def event_grads(pos, rows, highs, lows, winh, winl, dlogits, gate_w):
    n_groups = len(highs)
    block = lambda width: pl.BlockSpec((RB, width), lambda i, pos: (i, 0))
    whole = lambda shape: pl.BlockSpec(shape, lambda i, pos: (0, 0))
    return pl.pallas_call(
        functools.partial(event_kernel, n_groups),
        grid_spec=pltpu.PrefetchScalarGridSpec(
            num_scalar_prefetch=1,
            grid=(rows // RB,),
            in_specs=[block(v.shape[1]) for v in (*highs, *lows)]
            + [whole(v.shape) for v in (*winh, *winl)]
            + [block(LANES), whole((GATE_COLS, D))],
            out_specs=block(D),
            scratch_shapes=[pltpu.VMEM((LANES, D), F32)],
        ),
        out_shape=jax.ShapeDtypeStruct((rows, D), F32),
        compiler_params=params(40),
        cost_estimate=pl.CostEstimate(flops=6 * rows * D * E * H, bytes_accessed=rows * 10000, transcendentals=0),
    )(pos, *highs, *lows, *winh, *winl, dlogits, gate_w)


def place_kernel(pos, own, other, out):
    mine = (pl.program_id(0) >= pl.num_programs(0) // 2) == ((pos[0] & 1) == 1)

    @pl.when(mine)
    def _():
        out[...] = own[...]

    @pl.when(jnp.logical_not(mine))
    def _():
        out[...] = other[...]


def place(pos, own, other):
    rows, width = own.shape
    steps = rows // RB

    def source(which):
        def index(i, pos):
            start = ((pos[0] & 1) ^ which) * steps
            return (jnp.clip(i - start, 0, steps - 1), 0)

        return pl.BlockSpec((RB, width), index)

    return pl.pallas_call(
        place_kernel,
        grid_spec=pltpu.PrefetchScalarGridSpec(
            num_scalar_prefetch=1,
            grid=(2 * steps,),
            in_specs=[source(0), source(1)],
            out_specs=pl.BlockSpec((RB, width), lambda i, pos: (i, 0)),
        ),
        out_shape=jax.ShapeDtypeStruct((2 * rows, width), F32),
        compiler_params=params(24),
        cost_estimate=pl.CostEstimate(flops=0, bytes_accessed=rows * width * 16, transcendentals=0),
    )(pos, own, other)


def in_vmem(kernel, out_shape, scratch, *args):
    total = sum(a.size * 4 for a in args)
    return pl.pallas_call(
        kernel,
        in_specs=[pl.BlockSpec(memory_space=pltpu.SMEM)] + [pl.BlockSpec(memory_space=pltpu.VMEM)] * (len(args) - 1),
        out_specs=[pl.BlockSpec(memory_space=pltpu.VMEM)] * len(out_shape),
        out_shape=out_shape,
        scratch_shapes=scratch,
        compiler_params=params(16),
        cost_estimate=pl.CostEstimate(flops=0, bytes_accessed=2 * total, transcendentals=0),
    )(*args)


def padded(rows, parts):
    unit = 8 * parts
    return -(-rows // unit) * unit


def halves_kernel(n_parts, total, pos, *refs):
    own, got = refs[:n_parts], refs[n_parts : 2 * n_parts]
    keep, send, both = refs[2 * n_parts :]
    at = 0
    for a, b in zip(own, got):
        both[at : at + a.shape[0], :] = a[...] + b[...]
        at += a.shape[0]
    if at < total:
        both[at:, :] = jnp.zeros((total - at, LANES), F32)
    half = total // 2
    mine = pl.multiple_of((pos[2] & 1) * half, 8)
    keep[...] = both[pl.ds(mine, half), :]
    send[...] = both[pl.ds(half - mine, half), :]


def chunks_kernel(outer, keep, got, pos, *refs):
    pass


def split_kernel(outer, pos, own, got, *refs):
    outs, both = refs[:outer], refs[outer]
    both[...] = own[...] + got[...]
    rows = outs[0].shape[0]
    for k in range(outer):
        outs[k][...] = both[pl.ds(pl.multiple_of(((pos[2] >> 1) ^ k) * rows, 8), rows), :]


def join_kernel(outer, pos, *refs):
    out = refs[outer]
    rows = refs[0].shape[0]
    for k in range(outer):
        out[pl.ds(pl.multiple_of(((pos[2] >> 1) ^ k) * rows, 8), rows), :] = refs[k][...]


def summed_over_dp(pos, parts, partner_parts, n_dp):
    outer = n_dp // 2
    got = [lax.ppermute(v, "tp", [(i, i ^ 1) for i in range(4)]) for v in partner_parts]
    total = padded(sum(v.shape[0] for v in parts), 2 * outer)
    half = jax.ShapeDtypeStruct((total // 2, LANES), F32)
    chunk = jax.ShapeDtypeStruct((total // 2 // outer, LANES), F32)
    over_x = [(i, i ^ 1) for i in range(n_dp)]
    over_z = [[(i, i ^ (2 * k)) for i in range(n_dp)] for k in range(outer)]
    keep, send = in_vmem(
        functools.partial(halves_kernel, len(parts), total), [half, half], [pltpu.VMEM((total, LANES), F32)], pos, *parts, *got
    )
    got = lax.ppermute(send, "dp", over_x)
    chunks = in_vmem(
        functools.partial(split_kernel, outer), [chunk] * outer, [pltpu.VMEM((total // 2, LANES), F32)], pos, keep, got
    )
    mine = chunks[0]
    for v in [lax.ppermute(chunks[k], "dp", over_z[k]) for k in range(1, outer)]:
        mine = mine + v
    chunks = [mine] + [lax.ppermute(mine, "dp", over_z[k]) for k in range(1, outer)]
    (done,) = in_vmem(functools.partial(join_kernel, outer), [half], [], pos, *chunks)
    return done, lax.ppermute(done, "dp", over_x)


def finish_kernel(groups, pos, *refs):
    n = len(groups)
    halves = refs[: 2 * n]
    in_grad, in_bias, out_grad, out_bias, gain, shift, gate = refs[2 * n : 2 * n + 7]
    both = refs[2 * n + 7 :]
    odd = (pos[0] & 1) == 1
    for g, group in enumerate(groups):
        half = halves[2 * g].shape[0]
        mine = pl.multiple_of((pos[2] & 1) * half, 8)
        both[g][pl.ds(mine, half), :] = halves[2 * g][...]
        both[g][pl.ds(half - mine, half), :] = halves[2 * g + 1][...]
        for i, e in enumerate(group):
            for t in range(WIDE // LANES):
                at = (t * len(group) + i) * SLICE
                tile = both[g][at : at + SLICE, :]
                if t < D // LANES:
                    in_grad[e, :, t * LANES : (t + 1) * LANES] = tile
                else:
                    out_grad[e, :, t * LANES - D : (t + 1) * LANES - D] = tile
    rest = WIDE // LANES * len(groups[-1]) * SLICE
    sums = both[-1][rest : rest + 24, :]
    sums = jnp.where(odd, sums[:, SLICE:], sums[:, :SLICE])
    for g, group in enumerate(groups):
        for i, e in enumerate(group):
            for k, ref in enumerate((in_bias, out_bias, gain, shift)):
                ref[e : e + 1, :] = sums[8 * g + 4 * i + k : 8 * g + 4 * i + k + 1, :]
    for t in range(D // LANES):
        gate[:, t * LANES : (t + 1) * LANES] = both[-1][rest + 64 + 16 * t : rest + 64 + 16 * t + GATE_COLS, :]


def per_device(
    events,
    valid_counts,
    mix_cotangent,
    expert_in,
    expert_in_bias,
    expert_out,
    expert_out_bias,
    norm_gain,
    norm_shift,
    gate_weight,
):
    n_dp = lax.axis_size("dp")
    rank = lax.axis_index("dp")
    me = lax.axis_index("tp")
    rows = events.shape[0] // 2
    pos = jnp.stack([me, valid_counts[rank], rank]).astype(jnp.int32)
    w_in = jnp.swapaxes(expert_in, 1, 2)
    w_out = jnp.swapaxes(expert_out, 1, 2)
    gate_w = jnp.swapaxes(gate_weight, 0, 1)
    core = [(i, i ^ 1) for i in range(4)]
    across = [(i, i ^ 2) for i in range(4)]
    small = lax.all_gather(jnp.stack([expert_in_bias, expert_out_bias, norm_gain, norm_shift]), "tp")
    shards = []
    ready = None
    for group in GROUPS:
        lo, hi = group[0], group[-1] + 1
        own = jnp.concatenate([w_in[lo:hi], w_out[lo:hi]], axis=2)
        beside = lax.ppermute(own, "tp", core)
        if ready is not None:
            own, _ = lax.optimization_barrier((own, ready))
        ready = lax.ppermute(own, "tp", across)
        shards.append((own, beside, ready, lax.ppermute(ready, "tp", core)))
    high, low, p = gates(pos, events, gate_w, rows)
    mix = None
    dps, sums, highs, lows, winh, winl, summed = [], [], [], [], [], [], []
    for g, group in enumerate(GROUPS):
        before = (dps, sums) if g == len(GROUPS) - 1 else None
        mix, dp, h, l, wh, wl, own, part, s = experts(
            pos, group, rows, high, low, mix_cotangent, p, shards[g], small, mix, before
        )
        for held, v in zip((dps, sums, highs, lows, winh, winl), (dp, s, h, l, wh, wl)):
            held.append(v)
        if before is None:
            summed.append(summed_over_dp(pos, [own], [part], n_dp))
        else:
            summed.append(summed_over_dp(pos, [own, s], [part, s], n_dp))
    x_grad = event_grads(pos, rows, highs, lows, winh, winl, dps[-1], gate_w)
    mixtures = place(pos, mix, lax.ppermute(mix, "tp", core))
    x_grad = place(pos, x_grad, lax.ppermute(x_grad, "tp", core))
    flat = [v for pair in summed for v in pair]
    per_expert = jax.ShapeDtypeStruct((E, SLICE), F32)
    in_grad, in_bias, out_grad, out_bias, gain, shift, gate = in_vmem(
        functools.partial(finish_kernel, GROUPS),
        [
            jax.ShapeDtypeStruct((E, SLICE, D), F32),
            per_expert,
            jax.ShapeDtypeStruct((E, SLICE, H), F32),
            per_expert,
            per_expert,
            per_expert,
            jax.ShapeDtypeStruct((GATE_COLS, D), F32),
        ],
        [pltpu.VMEM((2 * a.shape[0], LANES), F32) for a, _ in summed],
        pos,
        *flat,
    )
    return (
        mixtures,
        x_grad,
        jnp.swapaxes(in_grad, 1, 2),
        in_bias,
        jnp.swapaxes(out_grad, 1, 2),
        out_bias,
        gain,
        shift,
        jnp.swapaxes(gate, 0, 1),
    )


def solution(mesh):
    return jax.shard_map(
        per_device,
        mesh=mesh,
        in_specs=(
            P("dp", None),
            P(),
            P("dp", None),
            P(None, None, "tp"),
            P(None, "tp"),
            P(None, None, "tp"),
            P(None, "tp"),
            P(None, "tp"),
            P(None, "tp"),
            P(),
        ),
        out_specs=(
            P("dp", None),
            P("dp", None),
            P(None, None, "tp"),
            P(None, "tp"),
            P(None, None, "tp"),
            P(None, "tp"),
            P(None, "tp"),
            P(None, "tp"),
            P(),
        ),
        check_vma=False,
    )
```

time: 728 us -> 183 us (0.25)
  waiting for transfers between devices: 312 us -> 36.4 us
  blocking collectives: 140 us -> 8.52 us
  local copies, waits for them, and re-layouts: 110 us -> 17.6 us
  matrix products: 77.8 us -> 0 us
  Pallas kernels: 0 us -> 74.5 us
  other arithmetic: 40.5 us -> 0.86 us
  starting transfers between devices: 23.5 us -> 43.7 us
  between operations: 16.6 us -> 0.97 us
    all_to_all x4 -> x0, waiting for transfers between devices: 219 us -> none  [the longest x1 114 us: per_device(): lax.all_to_all(sent_cot, 'dp', split_axis=1, concat_axis=1, tiled=True)]
    psum x3 -> x0, blocking collectives: 140 us -> none  [the longest x1 117 us: per_device(): lax.psum((in_grad, in_bias_grad, out_grad, out_bias_grad, gain_grad, shif...]
    dot_general x11 -> x0, matrix products: 75.1 us -> none  [the longest x1 11.4 us: expert_pass(): dy = jnp.einsum('rte,rto->reo', coef, cot_local, precision=highest)]
    pallas_call x0 -> x17, Pallas kernels: none -> 74.5 us  [the longest x3 48.8 us: experts(): pl.pallas_call(functools.partial(expert_kernel, group, first, last), grid...]
    psum x2 -> x0, waiting for transfers between devices: 53.3 us -> none  [the longest x1 53.3 us: expert_pass(): x_grad = lax.psum(x_grad, 'tp')]
    ppermute x0 -> x39, starting transfers between devices: none -> 43.7 us  [the longest x9 14.7 us: summed_over_dp(): lax.ppermute(chunks[k], 'dp', over_z[k])]
    ppermute x0 -> x39, waiting for transfers between devices: none -> 36.4 us  [the longest x3 8.51 us: per_device(): ready = lax.ppermute(own, 'tp', across)]
    all_to_all x4 -> x0, local copies, waits for them, and re-layouts: 27 us -> none  [the longest x1 9.13 us: per_device(): lax.all_to_all(sent_cot, 'dp', split_axis=1, concat_axis=1, tiled=True)]
  transfers between devices with their start and end apart: 9 -> 39, of which waited for: 6 -> 16; matrix products, arithmetic and copies ran while one was open for 25% -> 1% of each run, Pallas kernels for 0% -> 29%
where the time goes in v1:
time: 183 us
  Pallas kernels  74.5 us (41%)
  starting transfers between devices  43.7 us (24%)
  waiting for transfers between devices  36.4 us (20%)
  local copies, waits for them, and re-layouts  17.6 us (10%)
  blocking collectives  8.52 us (5%)
    pallas_call x3, Pallas kernels, experts(): pl.pallas_call(functools.partial(expert_kernel, group, first, last), grid...  48.8 us
    unnamed x52, local copies, waits for them, and re-layouts  14.8 us
    ppermute x9, starting transfers between devices, summed_over_dp(): lax.ppermute(chunks[k], 'dp', over_z[k])  14.7 us
    ppermute x9, starting transfers between devices, summed_over_dp(): lax.ppermute(mine, 'dp', over_z[k])  13 us
    pallas_call x2, Pallas kernels, place(): pl.pallas_call(place_kernel, grid_spec=pltpu.PrefetchScalarGridSpec(num_s...  8.62 us
    all_gather x1, blocking collectives, per_device(): lax.all_gather(jnp.stack([expert_in_bias, expert_out_bias, norm_gain, nor...  8.52 us
    ppermute x3, waiting for transfers between devices, per_device(): ready = lax.ppermute(own, 'tp', across)  8.51 us
    pallas_call x1, Pallas kernels, event_grads(): pl.pallas_call(functools.partial(event_kernel, n_groups), grid_spec=pltpu...  7.03 us
  transfers between devices with their start and end apart: 39, of which 16 were waited for; matrix products, arithmetic and copies ran while one was open for 1% of the time, Pallas kernels for 29%

profile of v1, /device:TPU:0, one launch (start us, length us, event | category | flops | bytes accessed | tf_op | source)
XLA Modules:
  0.0 182.5 jit_solution(12667260554414381315)
XLA Ops:
  3.0 3.0 %collective-permute-start = (f32[2,64,768]{2,1,0:T(8,128)S(1)}, f32[2,64,768]{2,1,0:T(8,128)S(1)}, u32[]{:S(2)}, u32[]{:S(2)}) collective-permute-start(f32[2,64,768]{2,1,0:T(8,128)S(1)} %pad_maximum_fusion.2.refs_5_), channel_id=1, source_target_pairs={{0,2},{1,3},{2,0},{3,1},{4,6},{5,7},{6,4},{7,5},{8,10},{9,11},{10,... | collective-permute-start | bytes 1179656 | tf_op jit(solution)/shard_map/ppermute | solution.py:501
  6.6 8.5 %collective-permute-done.refs_7_ = f32[2,64,768]{2,1,0:T(8,128)S(1)} collective-permute-done((f32[2,64,768]{2,1,0:T(8,128)S(1)}, f32[2,64,768]{2,1,0:T(8,128)S(1)}, u32[]{:S(2)}, u32[]{:S(2)}) %collective-permute-start) | collective-permute-done | bytes 393248 | tf_op jit(solution)/shard_map/ppermute | solution.py:501
  15.1 1.7 collective-permute-start.1
  18.1 8.5 %all-gather = f32[16,6,64]{2,1,0:T(8,128)S(1)} all-gather(f32[4,6,64]{2,1,0:T(8,128)S(1)} %pad_maximum_fusion.3), channel_id=2, replica_groups=mesh['dp'=8,'tp'=4] {'tp'}, dimensions={0}, use_global_device_ids=true | all-gather | bytes 30720 | tf_op jit(solution)/shard_map/all_gather | solution.py:492
  27.4 2.2 %copy-done = f32[2048,512]{1,0:T(8,128)S(1)} copy-done((f32[2048,512]{1,0:T(8,128)S(1)}, f32[2048,512]{1,0:T(8,128)}, u32[]{:S(2)}) %copy-start) | copy-done | bytes 4194328
  29.5 3.0 %shard_map.169 = (bf16[1024,512]{1,0:T(8,128)(2,1)S(1)}, bf16[1024,512]{1,0:T(8,128)(2,1)S(1)}, f32[1024,128]{1,0:T(8,128)S(1)}) custom-call(s32[3]{0:T(128)S(1)} %pad_add_fusion.pos.refs_0_, f32[2048,512]{1,0:T(8,128)S(1)} %copy-done, f32[14,512]{1,0:T(8,128)S(1)} %bitcast.16), custom_call_target="tpu_custom_call" | custom-call | flops 402653184 | bytes 4194304 | tf_op jit(solution)/shard_map/pallas_call | solution.py:78
  36.0 15.7 %shard_map.170 = (f32[1024,768]{1,0:T(8,128)}, f32[1024,128]{1,0:T(8,128)S(1)}, bf16[1024,512]{1,0:T(8,128)(2,1)S(1)}, bf16[1024,512]{1,0:T(8,128)(2,1)}, bf16[5...) custom-call(s32[3]{0:T(128)S(1)} %pad_add_fusion.pos.refs_0_, ...), custom_call_target="tpu_custom_call" | custom-call | flops 8858370048 | bytes 14336000 | tf_op jit(solution)/shard_map/pallas_call | solution.py:259
  52.9 15.7 %shard_map.171 = (f32[1024,768]{1,0:T(8,128)}, f32[1024,128]{1,0:T(8,128)S(1)}, bf16[1024,512]{1,0:T(8,128)(2,1)S(1)}, bf16[1024,512]{1,0:T(8,128)(2,1)}, bf16[5...) custom-call(s32[3]{0:T(128)S(1)} %pad_add_fusion.pos.refs_0_, ...), custom_call_target="tpu_custom_call", output_to_operand_aliasing={{0}: (10, {})} | custom-call | flops 8858370048 | bytes 14336000 | tf_op jit(solution)/shard_map/pallas_call | solution.py:259
  69.5 17.4 %shard_map.172 = (f32[1024,768]{1,0:T(8,128)}, f32[1024,128]{1,0:T(8,128)S(1)}, bf16[1024,512]{1,0:T(8,128)(2,1)}, bf16[1024,512]{1,0:T(8,128)(2,1)}, bf16[512,5...) custom-call(s32[3]{0:T(128)S(1)} %pad_add_fusion.pos.refs_0_, ...), custom_call_target="tpu_custom_call", output_to_operand_aliasing={{0}: (10, {})} | custom-call | flops 8858370048 | bytes 14336000 | tf_op jit(solution)/shard_map/pallas_call | solution.py:259
  96.0 7.0 %shard_map.174.own = f32[1024,512]{1,0:T(8,128)S(1)} custom-call(s32[3]{0:T(128)S(1)} %pad_add_fusion.pos.refs_0_, bf16[1024,512]{1,0:T(8,128)(2,1)S(1)} %get-tuple-element.78.refs_0_, bf16[1024,512]{1,0:T(8,128)(2,1)S(1)} %get-tuple-element.79.refs_1_, bf16[1024,512]{1,0:T(8,128)(2,1)S(1)} %copy-done.7, bf16[1024,512]{1,0:T(8,128)(2,1)S(1)} %copy-done.5, ...), custom_call_target="tpu_custom_call" | custom-call | flops 4831838208 | bytes 10240000 | tf_op jit(solution)/shard_map/pallas_call | solution.py:311
  104.1 3.8 %collective-permute-done.11.refs_1_ = f32[768,128]{1,0:T(8,128)S(1)} collective-permute-done((f32[768,128]{1,0:T(8,128)S(1)}, f32[768,128]{1,0:T(8,128)S(1)}, u32[]{:S(2)}, u32[]{:S(2)}) %collective-permute-start.11) | collective-permute-done | bytes 393248 | tf_op jit(solution)/shard_map/ppermute | solution.py:419
  108.5 1.6 collective-permute-start.12
  110.1 5.7 %collective-permute-done.12.got = f32[384,128]{1,0:T(8,128)S(1)} collective-permute-done((f32[384,128]{1,0:T(8,128)S(1)}, f32[384,128]{1,0:T(8,128)S(1)}, u32[]{:S(2)}, u32[]{:S(2)}) %collective-permute-start.12) | collective-permute-done | bytes 196640 | tf_op jit(solution)/shard_map/ppermute | solution.py:428
  116.3 1.6 collective-permute-start.13
  118.0 2.6 %collective-permute-start.14 = (f32[96,128]{1,0:T(8,128)S(1)}, f32[96,128]{1,0:T(8,128)S(1)}, u32[]{:S(2)}, u32[]{:S(2)}) collective-permute-start(f32[96,128]{1,0:T(8,128)S(1)} %get-tuple-element.97), channel_id=1, source_target_pairs={{0,16},{4,20},{8,24},{12,28},{16,0},{20,4},{24,8},{28,12},{1,17},{... | collective-permute-start | bytes 147464 | tf_op jit(solution)/shard_map/ppermute | solution.py:433
  122.2 1.6 collective-permute-start.21
  126.5 3.0 %collective-permute-start.18 = (f32[96,128]{1,0:T(8,128)S(1)}, f32[96,128]{1,0:T(8,128)S(1)}, u32[]{:S(2)}, u32[]{:S(2)}) collective-permute-start(f32[96,128]{1,0:T(8,128)S(1)} %add_add_fusion.2.refs_0_), channel_id=1, source_target_pairs={{0,24},{4,28},{8,16},{12,20},{16,8},{20,12},{24,0},{28,4},{1,25},{... | collective-permute-start | bytes 147464 | tf_op jit(solution)/shard_map/ppermute | solution.py:435
  129.5 2.9 %collective-permute-done.18.refs_3_ = f32[96,128]{1,0:T(8,128)S(1)} collective-permute-done((f32[96,128]{1,0:T(8,128)S(1)}, f32[96,128]{1,0:T(8,128)S(1)}, u32[]{:S(2)}, u32[]{:S(2)}) %collective-permute-start.18) | collective-permute-done | bytes 49184 | tf_op jit(solution)/shard_map/ppermute | solution.py:435
  133.6 3.0 %collective-permute-start.16 = (f32[96,128]{1,0:T(8,128)S(1)}, f32[96,128]{1,0:T(8,128)S(1)}, u32[]{:S(2)}, u32[]{:S(2)}) collective-permute-start(f32[96,128]{1,0:T(8,128)S(1)} %add_add_fusion.2.refs_0_), channel_id=1, source_target_pairs={{0,8},{4,12},{8,0},{12,4},{16,24},{20,28},{24,16},{28,20},{1,9},{5... | collective-permute-start | bytes 147464 | tf_op jit(solution)/shard_map/ppermute | solution.py:435
  138.6 2.9 %collective-permute-start.33 = (f32[112,128]{1,0:T(8,128)S(1)}, f32[112,128]{1,0:T(8,128)S(1)}, u32[]{:S(2)}, u32[]{:S(2)}) collective-permute-start(f32[112,128]{1,0:T(8,128)S(1)} %get-tuple-element.114), channel_id=1, source_target_pairs={{0,16},{4,20},{8,24},{12,28},{16,0},{20,4},{24,8},{28,12},{1,17},{... | collective-permute-start | bytes 172040 | tf_op jit(solution)/shard_map/ppermute | solution.py:433
  141.5 1.8 collective-permute-start.34
  144.1 2.7 %collective-permute-start.23 = (f32[96,128]{1,0:T(8,128)S(1)}, f32[96,128]{1,0:T(8,128)S(1)}, u32[]{:S(2)}, u32[]{:S(2)}) collective-permute-start(f32[96,128]{1,0:T(8,128)S(1)} %get-tuple-element.105), channel_id=1, source_target_pairs={{0,16},{4,20},{8,24},{12,28},{16,0},{20,4},{24,8},{28,12},{1,17},{... | collective-permute-start | bytes 147464 | tf_op jit(solution)/shard_map/ppermute | solution.py:433
  149.5 2.3 %collective-permute-start.37 = (f32[112,128]{1,0:T(8,128)S(1)}, f32[112,128]{1,0:T(8,128)S(1)}, u32[]{:S(2)}, u32[]{:S(2)}) collective-permute-start(f32[112,128]{1,0:T(8,128)S(1)} %add_add_fusion.refs_0_), channel_id=1, source_target_pairs={{0,24},{4,28},{8,16},{12,20},{16,8},{20,12},{24,0},{28,4},{1,25},{... | collective-permute-start | bytes 172040 | tf_op jit(solution)/shard_map/ppermute | solution.py:435
  151.9 2.0 %collective-permute-done.24 = f32[96,128]{1,0:T(8,128)S(1)} collective-permute-done((f32[96,128]{1,0:T(8,128)S(1)}, f32[96,128]{1,0:T(8,128)S(1)}, u32[]{:S(2)}, u32[]{:S(2)}) %collective-permute-start.24) | collective-permute-done | bytes 49184 | tf_op jit(solution)/shard_map/ppermute | solution.py:433
  154.2 1.8 collective-permute-done.37.refs_3_
  156.0 2.1 %collective-permute-start.27 = (f32[96,128]{1,0:T(8,128)S(1)}, f32[96,128]{1,0:T(8,128)S(1)}, u32[]{:S(2)}, u32[]{:S(2)}) collective-permute-start(f32[96,128]{1,0:T(8,128)S(1)} %add_add_fusion.1.refs_0_), channel_id=1, source_target_pairs={{0,24},{4,28},{8,16},{12,20},{16,8},{20,12},{24,0},{28,4},{1,25},{... | collective-permute-start | bytes 147464 | tf_op jit(solution)/shard_map/ppermute | solution.py:435
  158.5 1.9 %collective-permute-start.25 = (f32[96,128]{1,0:T(8,128)S(1)}, f32[96,128]{1,0:T(8,128)S(1)}, u32[]{:S(2)}, u32[]{:S(2)}) collective-permute-start(f32[96,128]{1,0:T(8,128)S(1)} %add_add_fusion.1.refs_0_), channel_id=1, source_target_pairs={{0,8},{4,12},{8,0},{12,4},{16,24},{20,28},{24,16},{28,20},{1,9},{5... | collective-permute-start | bytes 147464 | tf_op jit(solution)/shard_map/ppermute | solution.py:435
  165.8 4.2 %collective-permute-done.19.refs_1_ = f32[384,128]{1,0:T(8,128)S(1)} collective-permute-done((f32[384,128]{1,0:T(8,128)S(1)}, f32[384,128]{1,0:T(8,128)S(1)}, u32[]{:S(2)}, u32[]{:S(2)}) %collective-permute-start.19) | collective-permute-done | bytes 196640 | tf_op jit(solution)/shard_map/ppermute | solution.py:437
  170.0 2.1 %collective-permute-done.28.refs_3_ = f32[384,128]{1,0:T(8,128)S(1)} collective-permute-done((f32[384,128]{1,0:T(8,128)S(1)}, f32[384,128]{1,0:T(8,128)S(1)}, u32[]{:S(2)}, u32[]{:S(2)}) %collective-permute-start.28) | collective-permute-done | bytes 196640 | tf_op jit(solution)/shard_map/ppermute | solution.py:437
  172.1 1.8 shard_map.185
  173.9 4.1 %shard_map.175 = f32[2048,512]{1,0:T(8,128)} custom-call(s32[3]{0:T(128)S(1)} %pad_add_fusion.pos.refs_0_, f32[1024,512]{1,0:T(8,128)S(1)} %shard_map.174.own, f32[1024,512]{1,0:T(8,128)S(1)} %collective-permute-done.10.other), custom_call_target="tpu_custom_call" | custom-call | bytes 8388608 | tf_op jit(solution)/shard_map/pallas_call | solution.py:351
  178.0 4.6 %shard_map.173 = f32[2048,768]{1,0:T(8,128)} custom-call(s32[3]{0:T(128)S(1)} %pad_add_fusion.pos.refs_0_, f32[1024,768]{1,0:T(8,128)S(1)} %copy-done.1, f32[1024,768]{1,0:T(8,128)S(1)} %collective-permute-done.9.other), custom_call_target="tpu_custom_call" | custom-call | bytes 12582912 | tf_op jit(solution)/shard_map/pallas_call | solution.py:351
  (127 shorter events, 38.7 us)
Async XLA Ops:
  3.0 12.1 %collective-permute-start = (f32[2,64,768]{2,1,0:T(8,128)S(1)}, f32[2,64,768]{2,1,0:T(8,128)S(1)}, u32[]{:S(2)}, u32[]{:S(2)}) collective-permute-start(f32[2,64,768]{2,1,0:T(8,128)S(1)} %pad_maximum_fusion.2.refs_5_), channel_id=1, source_target_pairs={{0,2},{1,3},{2,0},{3,1},{4,6},{5,7},{6,4},{7,5},{8,10},{9,11},{10,... | collective-permute-start | bytes 1179656 | tf_op jit(solution)/shard_map/ppermute | solution.py:501
  6.0 29.9 %collective-permute-start.7 = (f32[2,64,768]{2,1,0:T(8,128)S(1)}, f32[2,64,768]{2,1,0:T(8,128)S(1)}, u32[]{:S(2)}, u32[]{:S(2)}) collective-permute-start(f32[2,64,768]{2,1,0:T(8,128)S(1)} %pad_maximum_fusion.2.refs_5_), channel_id=1, source_target_pairs={{0,1},{1,0},{2,3},{3,2},{4,5},{5,4},{6,7},{7,6},{8,9},{9,8},{10,11... | collective-permute-start | bytes 1179656 | tf_op jit(solution)/shard_map/ppermute | solution.py:498
  6.1 46.9 %collective-permute-start.5 = (f32[2,64,768]{2,1,0:T(8,128)S(1)}, f32[2,64,768]{2,1,0:T(8,128)S(1)}, u32[]{:S(2)}, u32[]{:S(2)}) collective-permute-start(f32[2,64,768]{2,1,0:T(8,128)S(1)} %pad_maximum_fusion.1.refs_5_), channel_id=1, source_target_pairs={{0,1},{1,0},{2,3},{3,2},{4,5},{5,4},{6,7},{7,6},{8,9},{9,8},{10,11... | collective-permute-start | bytes 1179656 | tf_op jit(solution)/shard_map/ppermute | solution.py:498
  15.1 19.4 %collective-permute-start.1 = (f32[2,64,768]{2,1,0:T(8,128)S(1)}, f32[2,64,768]{2,1,0:T(8,128)S(1)}, u32[]{:S(2)}, u32[]{:S(2)}) collective-permute-start(f32[2,64,768]{2,1,0:T(8,128)S(1)} %pad_maximum_fusion.1.refs_5_), channel_id=1, source_target_pairs={{0,2},{1,3},{2,0},{3,1},{4,6},{5,7},{6,4},{7,5},{8,10},{9,11},{10,... | collective-permute-start | bytes 1179656 | tf_op jit(solution)/shard_map/ppermute | solution.py:501
  16.9 19.1 %collective-permute-start.8 = (f32[2,64,768]{2,1,0:T(8,128)S(1)}, f32[2,64,768]{2,1,0:T(8,128)}, u32[]{:S(2)}, u32[]{:S(2)}) collective-permute-start(f32[2,64,768]{2,1,0:T(8,128)S(1)} %collective-permute-done.refs_7_), channel_id=1, source_target_pairs={{0,1},{1,0},{2,3},{3,2},{4,5},{5,4},{6,7},{7,6},{8,9},{9,8},{10,11... | collective-permute-start | bytes 1179656 | tf_op jit(solution)/shard_map/ppermute | solution.py:502
  16.9 52.5 %collective-permute-start.2 = (f32[2,64,768]{2,1,0:T(8,128)S(1)}, f32[2,64,768]{2,1,0:T(8,128)S(1)}, u32[]{:S(2)}, u32[]{:S(2)}) collective-permute-start(f32[2,64,768]{2,1,0:T(8,128)S(1)} %pad_maximum_fusion.refs_5_), channel_id=1, source_target_pairs={{0,1},{1,0},{2,3},{3,2},{4,5},{5,4},{6,7},{7,6},{8,9},{9,8},{10,11... | collective-permute-start | bytes 1179656 | tf_op jit(solution)/shard_map/ppermute | solution.py:498
  34.5 18.0 %collective-permute-start.3 = (f32[2,64,768]{2,1,0:T(8,128)S(1)}, f32[2,64,768]{2,1,0:T(8,128)S(1)}, u32[]{:S(2)}, u32[]{:S(2)}) collective-permute-start(f32[2,64,768]{2,1,0:T(8,128)S(1)} %pad_maximum_fusion.refs_5_), channel_id=1, source_target_pairs={{0,2},{1,3},{2,0},{3,1},{4,6},{5,7},{6,4},{7,5},{8,10},{9,11},{10,... | collective-permute-start | bytes 1179656 | tf_op jit(solution)/shard_map/ppermute | solution.py:501
  36.0 17.0 %collective-permute-start.6 = (f32[2,64,768]{2,1,0:T(8,128)S(1)}, f32[2,64,768]{2,1,0:T(8,128)S(1)}, u32[]{:S(2)}, u32[]{:S(2)}) collective-permute-start(f32[2,64,768]{2,1,0:T(8,128)S(1)} %collective-permute-done.1.refs_7_), channel_id=1, source_target_pairs={{0,1},{1,0},{2,3},{3,2},{4,5},{5,4},{6,7},{7,6},{8,9},{9,8},{10,11... | collective-permute-start | bytes 1179656 | tf_op jit(solution)/shard_map/ppermute | solution.py:502
  52.5 17.0 %collective-permute-start.4 = (f32[2,64,768]{2,1,0:T(8,128)S(1)}, f32[2,64,768]{2,1,0:T(8,128)S(1)}, u32[]{:S(2)}, u32[]{:S(2)}) collective-permute-start(f32[2,64,768]{2,1,0:T(8,128)S(1)} %collective-permute-done.3.refs_7_), channel_id=1, source_target_pairs={{0,1},{1,0},{2,3},{3,2},{4,5},{5,4},{6,7},{7,6},{8,9},{9,8},{10,11... | collective-permute-start | bytes 1179656 | tf_op jit(solution)/shard_map/ppermute | solution.py:502
  89.3 88.7 %collective-permute-start.9 = (f32[1024,768]{1,0:T(8,128)}, f32[1024,768]{1,0:T(8,128)S(1)}, u32[]{:S(2)}, u32[]{:S(2)}) collective-permute-start(f32[1024,768]{1,0:T(8,128)} %get-tuple-element.77.own), channel_id=1, source_target_pairs={{0,1},{1,0},{2,3},{3,2},{4,5},{5,4},{6,7},{7,6},{8,9},{9,8},{10,11... | collective-permute-start | bytes 9437192 | tf_op jit(solution)/shard_map/ppermute | solution.py:518
  103.0 70.9 %collective-permute-start.10 = (f32[1024,512]{1,0:T(8,128)S(1)}, f32[1024,512]{1,0:T(8,128)S(1)}, u32[]{:S(2)}, u32[]{:S(2)}) collective-permute-start(f32[1024,512]{1,0:T(8,128)S(1)} %shard_map.174.own), channel_id=1, source_target_pairs={{0,1},{1,0},{2,3},{3,2},{4,5},{5,4},{6,7},{7,6},{8,9},{9,8},{10,11... | collective-permute-start | bytes 6291464 | tf_op jit(solution)/shard_map/ppermute | solution.py:519
  103.6 12.7 %collective-permute-start.20 = (f32[768,128]{1,0:T(8,128)S(1)}, f32[768,128]{1,0:T(8,128)S(1)}, u32[]{:S(2)}, u32[]{:S(2)}) collective-permute-start(f32[768,128]{1,0:T(8,128)S(1)} %get-tuple-element.100), channel_id=1, source_target_pairs={{0,1},{1,0},{2,3},{3,2},{4,5},{5,4},{6,7},{7,6},{8,9},{9,8},{10,11... | collective-permute-start | bytes 1179656 | tf_op jit(solution)/shard_map/ppermute | solution.py:419
  104.0 16.5 %collective-permute-start.29 = (f32[768,128]{1,0:T(8,128)S(1)}, f32[768,128]{1,0:T(8,128)S(1)}, u32[]{:S(2)}, u32[]{:S(2)}) collective-permute-start(f32[768,128]{1,0:T(8,128)S(1)} %get-tuple-element.109), channel_id=1, source_target_pairs={{0,1},{1,0},{2,3},{3,2},{4,5},{5,4},{6,7},{7,6},{8,9},{9,8},{10,11... | collective-permute-start | bytes 1179656 | tf_op jit(solution)/shard_map/ppermute | solution.py:419
  108.5 7.2 %collective-permute-start.12 = (f32[384,128]{1,0:T(8,128)S(1)}, f32[384,128]{1,0:T(8,128)S(1)}, u32[]{:S(2)}, u32[]{:S(2)}) collective-permute-start(f32[384,128]{1,0:T(8,128)S(1)} %get-tuple-element.94), channel_id=1, source_target_pairs={{0,4},{4,0},{8,12},{12,8},{16,20},{20,16},{24,28},{28,24},{1,5},{5... | collective-permute-start | bytes 589832 | tf_op jit(solution)/shard_map/ppermute | solution.py:428
  116.3 5.8 %collective-permute-start.13 = (f32[96,128]{1,0:T(8,128)S(1)}, f32[96,128]{1,0:T(8,128)S(1)}, u32[]{:S(2)}, u32[]{:S(2)}) collective-permute-start(f32[96,128]{1,0:T(8,128)S(1)} %get-tuple-element.96), channel_id=1, source_target_pairs={{0,8},{4,12},{8,0},{12,4},{16,24},{20,28},{24,16},{28,20},{1,9},{5... | collective-permute-start | bytes 147464 | tf_op jit(solution)/shard_map/ppermute | solution.py:433
  118.0 6.1 %collective-permute-start.14 = (f32[96,128]{1,0:T(8,128)S(1)}, f32[96,128]{1,0:T(8,128)S(1)}, u32[]{:S(2)}, u32[]{:S(2)}) collective-permute-start(f32[96,128]{1,0:T(8,128)S(1)} %get-tuple-element.97), channel_id=1, source_target_pairs={{0,16},{4,20},{8,24},{12,28},{16,0},{20,4},{24,8},{28,12},{1,17},{... | collective-permute-start | bytes 147464 | tf_op jit(solution)/shard_map/ppermute | solution.py:433
  120.6 5.9 %collective-permute-start.15 = (f32[96,128]{1,0:T(8,128)S(1)}, f32[96,128]{1,0:T(8,128)S(1)}, u32[]{:S(2)}, u32[]{:S(2)}) collective-permute-start(f32[96,128]{1,0:T(8,128)S(1)} %get-tuple-element.98), channel_id=1, source_target_pairs={{0,24},{4,28},{8,16},{12,20},{16,8},{20,12},{24,0},{28,4},{1,25},{... | collective-permute-start | bytes 147464 | tf_op jit(solution)/shard_map/ppermute | solution.py:433
  122.2 19.4 %collective-permute-start.21 = (f32[384,128]{1,0:T(8,128)S(1)}, f32[384,128]{1,0:T(8,128)S(1)}, u32[]{:S(2)}, u32[]{:S(2)}) collective-permute-start(f32[384,128]{1,0:T(8,128)S(1)} %get-tuple-element.102), channel_id=1, source_target_pairs={{0,4},{4,0},{8,12},{12,8},{16,20},{20,16},{24,28},{28,24},{1,5},{5... | collective-permute-start | bytes 589832 | tf_op jit(solution)/shard_map/ppermute | solution.py:428
  124.1 9.4 %collective-permute-start.31 = (f32[448,128]{1,0:T(8,128)S(1)}, f32[448,128]{1,0:T(8,128)S(1)}, u32[]{:S(2)}, u32[]{:S(2)}) collective-permute-start(f32[448,128]{1,0:T(8,128)S(1)} %get-tuple-element.111), channel_id=1, source_target_pairs={{0,4},{4,0},{8,12},{12,8},{16,20},{20,16},{24,28},{28,24},{1,5},{5... | collective-permute-start | bytes 688136 | tf_op jit(solution)/shard_map/ppermute | solution.py:428
  126.5 6.0 %collective-permute-start.18 = (f32[96,128]{1,0:T(8,128)S(1)}, f32[96,128]{1,0:T(8,128)S(1)}, u32[]{:S(2)}, u32[]{:S(2)}) collective-permute-start(f32[96,128]{1,0:T(8,128)S(1)} %add_add_fusion.2.refs_0_), channel_id=1, source_target_pairs={{0,24},{4,28},{8,16},{12,20},{16,8},{20,12},{24,0},{28,4},{1,25},{... | collective-permute-start | bytes 147464 | tf_op jit(solution)/shard_map/ppermute | solution.py:435
  137.5 6.4 %collective-permute-start.32 = (f32[112,128]{1,0:T(8,128)S(1)}, f32[112,128]{1,0:T(8,128)S(1)}, u32[]{:S(2)}, u32[]{:S(2)}) collective-permute-start(f32[112,128]{1,0:T(8,128)S(1)} %get-tuple-element.113), channel_id=1, source_target_pairs={{0,8},{4,12},{8,0},{12,4},{16,24},{20,28},{24,16},{28,20},{1,9},{5... | collective-permute-start | bytes 172040 | tf_op jit(solution)/shard_map/ppermute | solution.py:433
  141.5 6.4 %collective-permute-start.34 = (f32[112,128]{1,0:T(8,128)S(1)}, f32[112,128]{1,0:T(8,128)S(1)}, u32[]{:S(2)}, u32[]{:S(2)}) collective-permute-start(f32[112,128]{1,0:T(8,128)S(1)} %get-tuple-element.115), channel_id=1, source_target_pairs={{0,24},{4,28},{8,16},{12,20},{16,8},{20,12},{24,0},{28,4},{1,25},{... | collective-permute-start | bytes 172040 | tf_op jit(solution)/shard_map/ppermute | solution.py:433
  143.9 5.6 %collective-permute-start.22 = (f32[96,128]{1,0:T(8,128)S(1)}, f32[96,128]{1,0:T(8,128)S(1)}, u32[]{:S(2)}, u32[]{:S(2)}) collective-permute-start(f32[96,128]{1,0:T(8,128)S(1)} %get-tuple-element.104), channel_id=1, source_target_pairs={{0,8},{4,12},{8,0},{12,4},{16,24},{20,28},{24,16},{28,20},{1,9},{5... | collective-permute-start | bytes 147464 | tf_op jit(solution)/shard_map/ppermute | solution.py:433
  144.1 7.7 %collective-permute-start.23 = (f32[96,128]{1,0:T(8,128)S(1)}, f32[96,128]{1,0:T(8,128)S(1)}, u32[]{:S(2)}, u32[]{:S(2)}) collective-permute-start(f32[96,128]{1,0:T(8,128)S(1)} %get-tuple-element.105), channel_id=1, source_target_pairs={{0,16},{4,20},{8,24},{12,28},{16,0},{20,4},{24,8},{28,12},{1,17},{... | collective-permute-start | bytes 147464 | tf_op jit(solution)/shard_map/ppermute | solution.py:433
  147.9 6.0 %collective-permute-start.24 = (f32[96,128]{1,0:T(8,128)S(1)}, f32[96,128]{1,0:T(8,128)S(1)}, u32[]{:S(2)}, u32[]{:S(2)}) collective-permute-start(f32[96,128]{1,0:T(8,128)S(1)} %get-tuple-element.106), channel_id=1, source_target_pairs={{0,24},{4,28},{8,16},{12,20},{16,8},{20,12},{24,0},{28,4},{1,25},{... | collective-permute-start | bytes 147464 | tf_op jit(solution)/shard_map/ppermute | solution.py:433
  149.5 6.5 %collective-permute-start.37 = (f32[112,128]{1,0:T(8,128)S(1)}, f32[112,128]{1,0:T(8,128)S(1)}, u32[]{:S(2)}, u32[]{:S(2)}) collective-permute-start(f32[112,128]{1,0:T(8,128)S(1)} %add_add_fusion.refs_0_), channel_id=1, source_target_pairs={{0,24},{4,28},{8,16},{12,20},{16,8},{20,12},{24,0},{28,4},{1,25},{... | collective-permute-start | bytes 172040 | tf_op jit(solution)/shard_map/ppermute | solution.py:435
  151.8 6.2 %collective-permute-start.36 = (f32[112,128]{1,0:T(8,128)S(1)}, f32[112,128]{1,0:T(8,128)S(1)}, u32[]{:S(2)}, u32[]{:S(2)}) collective-permute-start(f32[112,128]{1,0:T(8,128)S(1)} %add_add_fusion.refs_0_), channel_id=1, source_target_pairs={{0,16},{4,20},{8,24},{12,28},{16,0},{20,4},{24,8},{28,12},{1,17},{... | collective-permute-start | bytes 172040 | tf_op jit(solution)/shard_map/ppermute | solution.py:435
  156.0 5.9 %collective-permute-start.27 = (f32[96,128]{1,0:T(8,128)S(1)}, f32[96,128]{1,0:T(8,128)S(1)}, u32[]{:S(2)}, u32[]{:S(2)}) collective-permute-start(f32[96,128]{1,0:T(8,128)S(1)} %add_add_fusion.1.refs_0_), channel_id=1, source_target_pairs={{0,24},{4,28},{8,16},{12,20},{16,8},{20,12},{24,0},{28,4},{1,25},{... | collective-permute-start | bytes 147464 | tf_op jit(solution)/shard_map/ppermute | solution.py:435
  158.5 6.1 %collective-permute-start.25 = (f32[96,128]{1,0:T(8,128)S(1)}, f32[96,128]{1,0:T(8,128)S(1)}, u32[]{:S(2)}, u32[]{:S(2)}) collective-permute-start(f32[96,128]{1,0:T(8,128)S(1)} %add_add_fusion.1.refs_0_), channel_id=1, source_target_pairs={{0,8},{4,12},{8,0},{12,4},{16,24},{20,28},{24,16},{28,20},{1,9},{5... | collective-permute-start | bytes 147464 | tf_op jit(solution)/shard_map/ppermute | solution.py:435
  161.9 10.2 %collective-permute-start.38 = (f32[448,128]{1,0:T(8,128)S(1)}, f32[448,128]{1,0:T(8,128)S(1)}, u32[]{:S(2)}, u32[]{:S(2)}) collective-permute-start(f32[448,128]{1,0:T(8,128)S(1)} %shard_map.184.refs_4_), channel_id=1, source_target_pairs={{0,4},{4,0},{8,12},{12,8},{16,20},{20,16},{24,28},{28,24},{1,5},{5... | collective-permute-start | bytes 688136 | tf_op jit(solution)/shard_map/ppermute | solution.py:437
  163.1 6.9 %collective-permute-start.19 = (f32[384,128]{1,0:T(8,128)S(1)}, f32[384,128]{1,0:T(8,128)S(1)}, u32[]{:S(2)}, u32[]{:S(2)}) collective-permute-start(f32[384,128]{1,0:T(8,128)S(1)} %shard_map.178.refs_0_), channel_id=1, source_target_pairs={{0,4},{4,0},{8,12},{12,8},{16,20},{20,16},{24,28},{28,24},{1,5},{5... | collective-permute-start | bytes 589832 | tf_op jit(solution)/shard_map/ppermute | solution.py:437
  165.1 7.0 %collective-permute-start.28 = (f32[384,128]{1,0:T(8,128)S(1)}, f32[384,128]{1,0:T(8,128)S(1)}, u32[]{:S(2)}, u32[]{:S(2)}) collective-permute-start(f32[384,128]{1,0:T(8,128)S(1)} %shard_map.181.refs_2_), channel_id=1, source_target_pairs={{0,4},{4,0},{8,12},{12,8},{16,20},{20,16},{24,28},{28,24},{1,5},{5... | collective-permute-start | bytes 589832 | tf_op jit(solution)/shard_map/ppermute | solution.py:437
  (33 other events, 259.6 us)

commit v2 on v1

v2 whole, which is shorter than its diff:
```python
import functools

import jax
import jax.numpy as jnp
from jax import lax
from jax.experimental import pallas as pl
from jax.experimental.pallas import tpu as pltpu
from jax.sharding import PartitionSpec as P

D = 512
H = 256
O = 256
E = 6
GATE_COLS = 14
SLICE = 64
WIDE = D + H
LANES = 128
TOKEN = (8, LANES)
RB = 512
ROW_BLOCK = 256
SUB = 256
LAG = 1
EPSILON = 1e-05
GROUPS = ((0, 1), (2, 3), (4, 5))
COLUMN = (
    {0: 0, 1: 1, 4: 2, 5: 3},
    {2: 4, 3: 5, 4: 6, 5: 7},
    {e: 8 + e for e in range(E)},
)
F32 = jnp.float32
BF16 = jnp.bfloat16
NN = (((1,), (0,)), ((), ()))
NT = (((1,), (1,)), ((), ()))
TN = (((0,), (0,)), ((), ()))


def split(v):
    high = v.astype(BF16)
    return high, (v - high.astype(F32)).astype(BF16)


def dot3(a, b, dims):
    def one(u, v):
        return lax.dot_general(u, v, dims, preferred_element_type=F32)

    return one(a[0], b[0]) + (one(a[0], b[1]) + one(a[1], b[0]))


def half_of(v, upper):
    return jnp.where(upper, v[:, LANES:], v[:, :LANES])


LARGE = 60


def params(mib):
    return pltpu.CompilerParams(vmem_limit_bytes=mib << 20)


def gate_kernel(n_deps, pos, ev_ref, gw_ref, *refs):
    high_ref, low_ref, p_ref, gw = refs[n_deps:]
    gw[...] = jnp.zeros_like(gw)
    gw[:GATE_COLS, :] = gw_ref[...]
    events = split(ev_ref[...])
    high_ref[...], low_ref[...] = events
    logits = dot3(events, split(gw[...]), NT)
    lane = lax.broadcasted_iota(jnp.int32, logits.shape, 1)
    sets = (lane < 4, (lane >= 4) & (lane < 8), (lane >= 8) & (lane < GATE_COLS))

    def per_set(values, empty, reduce):
        a, b, s = (reduce(jnp.where(m, values, empty), axis=1, keepdims=True) for m in sets)
        return jnp.where(sets[0], a, jnp.where(sets[1], b, s))

    top = per_set(logits, -3e38, jnp.max)
    shares = jnp.where(lane < GATE_COLS, jnp.exp(logits - top), 0.0)
    p = shares / per_set(shares, 0.0, jnp.sum)
    rows = pl.num_programs(0) * ROW_BLOCK
    row = (pos[0] & 1) * rows + pl.program_id(0) * ROW_BLOCK
    row = row + lax.broadcasted_iota(jnp.int32, logits.shape, 0)
    p_ref[...] = jnp.where((row < pos[1]) & (lane < GATE_COLS), p, 0.0)


def gates(pos, events, gate_w, rows, deps):
    steps = rows // ROW_BLOCK
    spec = lambda width: pl.BlockSpec((ROW_BLOCK, width), lambda i, pos: (i, 0))
    return pl.pallas_call(
        functools.partial(gate_kernel, len(deps)),
        grid_spec=pltpu.PrefetchScalarGridSpec(
            num_scalar_prefetch=1,
            grid=(steps,),
            in_specs=[
                pl.BlockSpec((ROW_BLOCK, D), lambda i, pos: ((pos[0] & 1) * steps + i, 0)),
                pl.BlockSpec((GATE_COLS, D), lambda i, pos: (0, 0)),
            ]
            + [pl.BlockSpec(memory_space=pl.ANY)] * len(deps),
            out_specs=[spec(D), spec(D), spec(LANES)],
            scratch_shapes=[pltpu.VMEM((LANES, D), F32)],
        ),
        out_shape=[
            jax.ShapeDtypeStruct((rows, D), BF16),
            jax.ShapeDtypeStruct((rows, D), BF16),
            jax.ShapeDtypeStruct((rows, LANES), F32),
        ],
        compiler_params=params(LARGE),
        cost_estimate=pl.CostEstimate(flops=6 * rows * D * LANES, bytes_accessed=rows * D * 8, transcendentals=0),
    )(pos, events, gate_w, *deps)


def payload_kernel(n_deps, w_in, w_out, *refs):
    out = refs[n_deps]
    out[:, :, :D] = w_in[...]
    out[:, :, D:] = w_out[...]


def payload(group, w_in, w_out, deps):
    n = len(group)
    return pl.pallas_call(
        functools.partial(payload_kernel, len(deps)),
        grid=(n,),
        in_specs=[
            pl.BlockSpec((1, SLICE, D), lambda i: (group[0] + i, 0, 0)),
            pl.BlockSpec((1, SLICE, H), lambda i: (group[0] + i, 0, 0)),
        ]
        + [pl.BlockSpec(memory_space=pl.ANY)] * len(deps),
        out_specs=pl.BlockSpec((1, SLICE, WIDE), lambda i: (i, 0, 0)),
        out_shape=jax.ShapeDtypeStruct((n, SLICE, WIDE), F32),
        compiler_params=params(LARGE),
        cost_estimate=pl.CostEstimate(flops=0, bytes_accessed=n * SLICE * WIDE * 8, transcendentals=0),
    )(w_in, w_out, *deps)


def expert_kernel(group, first, last, n_deps, *refs):
    n = len(group)
    refs = list(refs)
    pos, evh_ref, evl_ref, cot_ref, p_ref = refs[:5]
    shards, smalls = refs[5:9], refs[9:13]
    del refs[:13]
    mix_in = None if first else refs.pop(0)
    if last:
        dp_before, sums_before = refs[: len(GROUPS) - 1], refs[len(GROUPS) - 1 : 2 * len(GROUPS) - 2]
        del refs[: 2 * len(GROUPS) - 2]
    del refs[:n_deps]
    mix_ref, dp_ref, dph_ref, dpl_ref, winh, winl, own_ref, part_ref, sums_ref = refs[:9]
    del refs[:9]
    wouth, woutl, small, acc, sums = refs[:5]
    gate_acc = refs[5] if last else None
    step, steps = pl.program_id(0), pl.num_programs(0)
    odd = pos[0] & 1
    chip = pos[0] >> 1

    def tile(start, other):
        return pl.ds(pl.multiple_of(start + (chip ^ other) * LANES, LANES), LANES)

    @pl.when(step == 0)
    def _():
        acc[...] = jnp.zeros_like(acc)
        sums[...] = jnp.zeros_like(sums)
        if last:
            gate_acc[...] = jnp.zeros_like(gate_acc)
        orders = (jnp.concatenate([smalls[k ^ c][...] for k in range(4)], axis=1) for c in range(2))
        even_order, odd_order = orders
        small[...] = jnp.where(odd == 1, odd_order, even_order)
        for i, e in enumerate(group):
            parts = [
                (shard[i, :, :D], jnp.concatenate([shard[i, :, tile(D, 0)], shard[i, :, tile(D, 1)]], axis=1))
                for shard in shards
            ]
            centre = sum(jnp.sum(out, axis=0, keepdims=True) for _, out in parts) / O
            for k, (into, out) in enumerate(parts):
                at = pl.multiple_of((odd ^ k) * SLICE, SLICE)
                winh[pl.ds(i * H + at, SLICE), :], winl[pl.ds(i * H + at, SLICE), :] = split(into)
                wouth[i, pl.ds(at, SLICE), :], woutl[i, pl.ds(at, SLICE), :] = split(out - centre)
            row = E + e
            small[row : row + 1, :] = small[row : row + 1, :] - jnp.mean(small[row : row + 1, :], axis=1, keepdims=True)

    subs = RB // SUB
    rows_of = [slice(s * SUB, (s + 1) * SUB) for s in range(subs)]
    lane = lax.broadcasted_iota(jnp.int32, (SUB, LANES), 1)
    vector = lambda k, e: small[k * E + e : k * E + e + 1, :]
    state = [dict() for _ in range(subs)]

    def m1(s):
        events = evh_ref[rows_of[s], :], evl_ref[rows_of[s], :]
        state[s]["events"] = events
        pre = dot3(events, (winh[...], winl[...]), NT)
        state[s]["pre"] = [pre[:, i * H : (i + 1) * H] for i in range(n)]

    def v1(s):
        st = state[s]
        st["sigma"], st["hidden"], st["hidden_parts"] = [], [], []
        for i, e in enumerate(group):
            pre = st["pre"][i] + vector(0, e)
            sigma = jax.nn.sigmoid(pre)
            hidden = pre * sigma
            st["sigma"].append(sigma)
            st["hidden"].append(hidden)
            st["hidden_parts"].append(split(hidden))

    def m2(s):
        st = state[s]
        st["centred"] = [dot3(st["hidden_parts"][i], (wouth[i], woutl[i]), NT) for i in range(n)]

    def v2(s):
        st = state[s]
        p = p_ref[rows_of[s], :]
        dp = jnp.zeros_like(p)
        mixed = {}
        cots = [
            jnp.concatenate([cot_ref[rows_of[s], tile(t * O, 0)], cot_ref[rows_of[s], tile(t * O, 1)]], axis=1)
            for t in range(3)
        ]
        st["dnormed"] = []
        for i, e in enumerate(group):
            gain, shift = vector(2, e), vector(3, e)
            centred = st["centred"][i] + vector(1, e)
            rstd = lax.rsqrt(jnp.mean(centred * centred, axis=1, keepdims=True) + EPSILON)
            unit = centred * rstd
            y = unit * gain + shift
            dy = None
            for t in range(3):
                if e not in COLUMN[t]:
                    continue
                column = COLUMN[t][e]
                coef = p[:, column : column + 1]
                mixed[t] = coef * y + mixed[t] if t in mixed else coef * y
                dp = jnp.where(lane == column, jnp.sum(cots[t] * y, axis=1, keepdims=True), dp)
                dy = coef * cots[t] if dy is None else dy + coef * cots[t]
            dunit = dy * gain
            back_first = jnp.mean(dunit, axis=1, keepdims=True)
            back_second = jnp.mean(dunit * unit, axis=1, keepdims=True)
            dnormed = rstd * (dunit - back_first - unit * back_second)
            st["dnormed"].append(split(dnormed))
            dy_half = dy[:, :LANES]
            for k, v in enumerate((dnormed[:, :LANES], dy_half * unit[:, :LANES], dy_half)):
                sums[4 * i + k + 1 : 4 * i + k + 2, :] += jnp.sum(v, axis=0, keepdims=True)
        for t in range(3):
            for other in range(2):
                at = tile(t * O, other)
                if t in mixed:
                    value = mixed[t][:, other * LANES : (other + 1) * LANES]
                    mix_ref[rows_of[s], at] = value if first else mix_in[rows_of[s], at] + value
                elif first:
                    mix_ref[rows_of[s], at] = jnp.zeros((SUB, LANES), F32)
                else:
                    mix_ref[rows_of[s], at] = mix_in[rows_of[s], at]
        if last:
            for other in dp_before:
                dp = dp + other[rows_of[s], :]
            weighted = p * dp
            sets = (lane < 4, (lane >= 4) & (lane < 8), (lane >= 8) & (lane < GATE_COLS))
            a, b, c = (jnp.sum(jnp.where(m, weighted, 0.0), axis=1, keepdims=True) for m in sets)
            dp = weighted - p * jnp.where(sets[0], a, jnp.where(sets[1], b, c))
            st["dlogits"] = dp
        dp_ref[rows_of[s], :] = dp

    def m3(s):
        st = state[s]
        st["dhidden"] = [dot3(st["dnormed"][i], (wouth[i], woutl[i]), NN) for i in range(n)]

    def v3(s):
        st = state[s]
        st["dpre"] = []
        for i, e in enumerate(group):
            sigma, hidden = st["sigma"][i], st["hidden"][i]
            dpre = st["dhidden"][i] * (sigma + hidden * (1.0 - sigma))
            parts = split(dpre)
            dph_ref[rows_of[s], i * H : (i + 1) * H], dpl_ref[rows_of[s], i * H : (i + 1) * H] = parts
            st["dpre"].append(tuple(v[:, :LANES] for v in parts))
            sums[4 * i : 4 * i + 1, :] += jnp.sum(dpre[:, :LANES], axis=0, keepdims=True)

    def m4(s):
        st = state[s]
        for i in range(n):
            halves = tuple(v[:, :LANES] for v in st["dnormed"][i])
            acc[i * LANES : (i + 1) * LANES, D:] += dot3(halves, st["hidden_parts"][i], TN)
        beside = [split(st["dlogits"])] if last else []
        left = tuple(jnp.concatenate([h[k] for h in st["dpre"] + beside], axis=1) for k in range(2))
        both = dot3(left, st["events"], TN)
        acc[:, :D] += both[: n * LANES]
        if last:
            gate_acc[...] += both[n * LANES : n * LANES + 16]

    stages = (m1, v1, m2, v2, m3, v3, m4)
    for turn in range(len(stages) + LAG * (subs - 1)):
        for s in range(subs):
            if 0 <= turn - LAG * s < len(stages):
                stages[turn - LAG * s](s)

    @pl.when(step == steps - 1)
    def _():
        mine = pl.multiple_of(odd * SLICE, SLICE)
        other = pl.multiple_of(SLICE - mine, SLICE)
        for i in range(n):
            for t in range(WIDE // LANES):
                at = slice((t * n + i) * SLICE, (t * n + i + 1) * SLICE)
                lanes = slice(t * LANES, (t + 1) * LANES) if t < D // LANES else tile(D, t - D // LANES)
                own_ref[at, :] = acc[pl.ds(i * LANES + mine, SLICE), lanes]
                part_ref[at, :] = acc[pl.ds(i * LANES + other, SLICE), lanes]
        if last:
            sums_ref[...] = jnp.zeros_like(sums_ref)
            for g, before in enumerate(sums_before):
                sums_ref[8 * g : 8 * g + 8, :] = before[...]
            g = len(GROUPS) - 1
            sums_ref[8 * g : 8 * g + 8, :] = sums[...]
            for t in range(D // LANES):
                sums_ref[64 + 16 * t : 80 + 16 * t, :] = gate_acc[:, t * LANES : (t + 1) * LANES]
        else:
            sums_ref[...] = sums[...]


def experts(pos, group, rows, high, low, cot, p, shards, smalls, mix, before, deps):
    n = len(group)
    first, last = mix is None, before is not None
    steps = rows // RB
    block = lambda width: pl.BlockSpec((RB, width), lambda i, pos: (i, 0))
    whole = lambda shape: pl.BlockSpec(shape, lambda i, pos: (0,) * len(shape))
    in_specs = [
        block(D),
        block(D),
        pl.BlockSpec((RB, 3 * O), lambda i, pos: ((pos[0] & 1) * steps + i, 0)),
        block(LANES),
        *[whole((n, SLICE, WIDE))] * 4,
        *[whole(smalls[0].shape)] * 4,
    ]
    args = [high, low, cot, p, *shards, *smalls]
    aliases = {}
    if not first:
        aliases = {len(args) + 1: 0}
        in_specs.append(block(3 * O))
        args.append(mix)
    if last:
        in_specs += [block(LANES)] * len(before[0]) + [whole((8, LANES))] * len(before[1])
        args += [*before[0], *before[1]]
    in_specs += [pl.BlockSpec(memory_space=pl.ANY)] * len(deps)
    args += deps
    payload = WIDE // LANES * n * SLICE
    sums_shape = (2 * LANES // 2, LANES) if last else (8, LANES)
    scratch = [
        pltpu.VMEM((n, O, H), BF16),
        pltpu.VMEM((n, O, H), BF16),
        pltpu.VMEM((4 * E, H), F32),
        pltpu.VMEM((n * LANES, WIDE), F32),
        pltpu.VMEM((8, LANES), F32),
    ]
    if last:
        scratch.append(pltpu.VMEM((16, D), F32))
    return pl.pallas_call(
        functools.partial(expert_kernel, group, first, last, len(deps)),
        grid_spec=pltpu.PrefetchScalarGridSpec(
            num_scalar_prefetch=1,
            grid=(steps,),
            in_specs=in_specs,
            out_specs=[
                block(3 * O),
                block(LANES),
                block(n * H),
                block(n * H),
                whole((n * H, D)),
                whole((n * H, D)),
                whole((payload, LANES)),
                whole((payload, LANES)),
                whole(sums_shape),
            ],
            scratch_shapes=scratch,
        ),
        out_shape=[
            jax.ShapeDtypeStruct((rows, 3 * O), F32),
            jax.ShapeDtypeStruct((rows, LANES), F32),
            jax.ShapeDtypeStruct((rows, n * H), BF16),
            jax.ShapeDtypeStruct((rows, n * H), BF16),
            jax.ShapeDtypeStruct((n * H, D), BF16),
            jax.ShapeDtypeStruct((n * H, D), BF16),
            jax.ShapeDtypeStruct((payload, LANES), F32),
            jax.ShapeDtypeStruct((payload, LANES), F32),
            jax.ShapeDtypeStruct(sums_shape, F32),
        ],
        input_output_aliases=aliases,
        compiler_params=params(LARGE),
        cost_estimate=pl.CostEstimate(flops=n * rows * 6 * 720896, bytes_accessed=rows * 14000, transcendentals=0),
    )(pos, *args)


def event_kernel(gated, added, pos, high, low, winh, winl, *refs):
    total = dot3((high[...], low[...]), (winh[...], winl[...]), NN)
    if gated:
        dlogits, gw_ref, gw = refs[0], refs[1], refs[-1]
        refs = refs[2:]
        gw[...] = jnp.zeros_like(gw)
        gw[:GATE_COLS, :] = gw_ref[...]
        total = total + dot3(split(dlogits[...]), split(gw[...]), NN)
    if added:
        total = total + refs[0][...]
    refs[-3][...] = total
    refs[-2][...] = jnp.zeros_like(refs[-2])


def event_grads(pos, rows, high, low, winh, winl, gating, before, deps):
    block = lambda width: pl.BlockSpec((ROW_BLOCK, width), lambda i, pos: (i, 0))
    whole = lambda shape: pl.BlockSpec(shape, lambda i, pos: (0, 0))
    args = [high, low, winh, winl]
    in_specs = [block(high.shape[1])] * 2 + [whole(winh.shape)] * 2
    aliases = {}
    if gating:
        args += gating
        in_specs += [block(LANES), whole((GATE_COLS, D))]
    if before is not None:
        aliases = {len(args) + 1: 0}
        args.append(before)
        in_specs.append(block(D))
    return pl.pallas_call(
        functools.partial(event_kernel, bool(gating), before is not None),
        grid_spec=pltpu.PrefetchScalarGridSpec(
            num_scalar_prefetch=1,
            grid=(rows // ROW_BLOCK,),
            in_specs=in_specs + [pl.BlockSpec(memory_space=pl.ANY)] * len(deps),
            out_specs=[block(D), whole(TOKEN)],
            scratch_shapes=[pltpu.VMEM((LANES, D), F32)],
        ),
        out_shape=[jax.ShapeDtypeStruct((rows, D), F32), jax.ShapeDtypeStruct(TOKEN, F32)],
        input_output_aliases=aliases,
        compiler_params=params(LARGE),
        cost_estimate=pl.CostEstimate(flops=6 * rows * D * winh.shape[0], bytes_accessed=rows * 6000, transcendentals=0),
    )(pos, *args, *deps)


def place_kernel(pos, own, other, *refs):
    out, token = refs[-2:]
    token[...] = jnp.zeros_like(token)
    mine = (pl.program_id(0) >= pl.num_programs(0) // 2) == ((pos[0] & 1) == 1)

    @pl.when(mine)
    def _():
        out[...] = own[...]

    @pl.when(jnp.logical_not(mine))
    def _():
        out[...] = other[...]


def place(pos, own, other, deps):
    rows, width = own.shape
    steps = rows // ROW_BLOCK

    def source(which):
        def index(i, pos):
            start = ((pos[0] & 1) ^ which) * steps
            return (jnp.clip(i - start, 0, steps - 1), 0)

        return pl.BlockSpec((ROW_BLOCK, width), index)

    return pl.pallas_call(
        place_kernel,
        grid_spec=pltpu.PrefetchScalarGridSpec(
            num_scalar_prefetch=1,
            grid=(2 * steps,),
            in_specs=[source(0), source(1)] + [pl.BlockSpec(memory_space=pl.ANY)] * len(deps),
            out_specs=[
                pl.BlockSpec((ROW_BLOCK, width), lambda i, pos: (i, 0)),
                pl.BlockSpec(TOKEN, lambda i, pos: (0, 0)),
            ],
        ),
        out_shape=[jax.ShapeDtypeStruct((2 * rows, width), F32), jax.ShapeDtypeStruct(TOKEN, F32)],
        compiler_params=params(LARGE),
        cost_estimate=pl.CostEstimate(flops=0, bytes_accessed=rows * width * 16, transcendentals=0),
    )(pos, own, other, *deps)


class Job:
    def __init__(self, args, shapes, body, scratch=()):
        self.args, self.body, self.scratch = args, body, list(scratch)
        self.shapes = [jax.ShapeDtypeStruct(shape, F32) for shape in shapes]


def copy_job(*arrays):
    def body(pos, ins, outs, scratch):
        for a, b in zip(ins, outs):
            b[...] = a[...]

    return Job(arrays, [a.shape for a in arrays], body)


def run(pos, jobs, deps=(), through=()):
    args = [a for job in jobs for a in job.args]
    shapes = [o for job in jobs for o in job.shapes]
    scratch = [v for job in jobs for v in job.scratch]
    first = 1 + len(args)

    def kernel(pos_ref, *refs):
        ins, refs = refs[: len(args)], refs[len(args) + len(through) + len(deps) :]
        outs, token, kept = refs[: len(shapes)], refs[len(shapes) + len(through)], refs[len(shapes) + len(through) + 1 :]
        token[...] = jnp.zeros_like(token)
        i = o = k = 0
        for job in jobs:
            ni, no, nk = len(job.args), len(job.shapes), len(job.scratch)
            job.body(pos_ref, ins[i : i + ni], outs[o : o + no], kept[k : k + nk])
            i, o, k = i + ni, o + no, k + nk

    vmem, anywhere = pl.BlockSpec(memory_space=pltpu.VMEM), pl.BlockSpec(memory_space=pl.ANY)
    flat = pl.pallas_call(
        kernel,
        in_specs=[pl.BlockSpec(memory_space=pltpu.SMEM)] + [vmem] * len(args) + [anywhere] * (len(through) + len(deps)),
        out_specs=[vmem] * len(shapes) + [anywhere] * len(through) + [vmem],
        out_shape=shapes
        + [jax.ShapeDtypeStruct(v.shape, v.dtype) for v in through]
        + [jax.ShapeDtypeStruct(TOKEN, F32)],
        scratch_shapes=scratch,
        input_output_aliases={first + k: len(shapes) + k for k in range(len(through))},
        compiler_params=params(LARGE),
        cost_estimate=pl.CostEstimate(flops=0, bytes_accessed=sum(8 * a.size for a in args), transcendentals=0),
    )(pos, *args, *through, *deps)
    result = []
    for job in jobs:
        result.append(list(flat[: len(job.shapes)]))
        flat = flat[len(job.shapes) :]
    return result, list(flat[:-1]), flat[-1]


def part_of(ref, index, rows):
    return ref.at[pl.ds(pl.multiple_of(index * rows, 8), rows), :]


class Reduction:
    def __init__(self, pos, own, partner, n_dp):
        self.pos, self.own, self.partner = pos, own, partner
        self.bits = n_dp.bit_length() - 1
        unit = 8 << (self.bits - 1)
        self.rows = -(-sum(v.shape[0] for v in own) // unit) * unit
        self.swap = [[(i, i ^ (1 << b)) for i in range(n_dp)] for b in range(self.bits)]
        self.stage = -1

    def over(self, values, bit):
        return [lax.ppermute(v, "dp", self.swap[bit]) for v in values]

    @property
    def finished(self):
        return self.stage == 2 * self.bits

    def job(self):
        stage, bits = self.stage, self.bits
        if stage < 0:
            return copy_job(*self.partner)
        if stage == 0:
            args = [*self.own, *self.got]
            rows = self.rows
        elif stage <= bits:
            args = [self.keep, *self.got]
            rows = self.keep.shape[0]
        else:
            args = [self.keep, *self.got]
            rows = 2 * self.keep.shape[0]
        n = len(args) // 2
        gather = stage > bits
        bit = stage if stage < bits else 2 * bits - 1 - stage
        halving = stage < bits - 1

        def body(pos, ins, outs, scratch):
            to = scratch[0] if halving else outs[0]
            if gather:
                side = (pos[2] >> bit) & 1
                part_of(to, side, rows // 2)[...] = ins[0][...]
                part_of(to, 1 - side, rows // 2)[...] = ins[1][...]
                return
            at = 0
            for a, b in zip(ins[:n], ins[n:]):
                to[at : at + a.shape[0], :] = a[...] + b[...]
                at += a.shape[0]
            if at < rows:
                to[at:, :] = jnp.zeros((rows - at, LANES), F32)
            if halving:
                side = (pos[2] >> bit) & 1
                outs[0][...] = part_of(to, side, rows // 2)[...]
                outs[1][...] = part_of(to, 1 - side, rows // 2)[...]

        if halving:
            return Job(args, [(rows // 2, LANES)] * 2, body, [pltpu.VMEM((rows, LANES), F32)])
        return Job(args, [(rows, LANES)], body)

    def take(self, outs):
        stage, bits = self.stage, self.bits
        if stage < 0:
            self.got = [lax.ppermute(v, "tp", [(i, i ^ 1) for i in range(4)]) for v in outs]
        else:
            self.keep = outs[0]
            bit = stage if stage < bits else 2 * bits - 2 - stage
            if bit >= 0:
                self.got = self.over([outs[-1]], bit)
        self.stage += 1


def finish_body(groups, pos, halves, outs, both):
    in_grad, in_bias, out_grad, out_bias, gain, shift, gate = outs
    n, whole = len(groups), []
    odd = (pos[0] & 1) == 1
    for g, group in enumerate(groups):
        if g < n - 1:
            whole.append(halves[g])
        else:
            half = halves[g].shape[0]
            whole.append(both[0])
            part_of(both[0], pos[2] & 1, half)[...] = halves[g][...]
            part_of(both[0], 1 - (pos[2] & 1), half)[...] = halves[g + 1][...]
        for i, e in enumerate(group):
            for t in range(WIDE // LANES):
                at = (t * len(group) + i) * SLICE
                tile = whole[g][at : at + SLICE, :]
                if t < D // LANES:
                    in_grad[e, :, t * LANES : (t + 1) * LANES] = tile
                else:
                    out_grad[e, :, t * LANES - D : (t + 1) * LANES - D] = tile
    rest = WIDE // LANES * len(groups[-1]) * SLICE
    sums = whole[-1][rest : rest + 24, :]
    sums = jnp.where(odd, sums[:, SLICE:], sums[:, :SLICE])
    for g, group in enumerate(groups):
        for i, e in enumerate(group):
            for k, ref in enumerate((in_bias, out_bias, gain, shift)):
                ref[e : e + 1, :] = sums[8 * g + 4 * i + k : 8 * g + 4 * i + k + 1, :]
    for t in range(D // LANES):
        gate[:, t * LANES : (t + 1) * LANES] = whole[-1][rest + 64 + 16 * t : rest + 64 + 16 * t + GATE_COLS, :]


def per_device(
    events,
    valid_counts,
    mix_cotangent,
    expert_in,
    expert_in_bias,
    expert_out,
    expert_out_bias,
    norm_gain,
    norm_shift,
    gate_weight,
):
    n_dp = lax.axis_size("dp")
    rank = lax.axis_index("dp")
    me = lax.axis_index("tp")
    rows = events.shape[0] // 2
    pos = jnp.stack([me, valid_counts[rank], rank]).astype(jnp.int32)
    w_in = jnp.swapaxes(expert_in, 1, 2)
    w_out = jnp.swapaxes(expert_out, 1, 2)
    gate_w = jnp.swapaxes(gate_weight, 0, 1)
    core = [(i, i ^ 1) for i in range(4)]
    across = [(i, i ^ 2) for i in range(4)]
    small = jnp.concatenate([expert_in_bias, expert_out_bias, norm_gain, norm_shift], axis=0)
    smalls = [small] + [lax.ppermute(small, "tp", [(i, i ^ k) for i in range(4)]) for k in range(1, 4)]
    own = [payload(GROUPS[0], w_in, w_out, [])]
    far = [lax.ppermute(own[0], "tp", across)]
    beside = [lax.ppermute(own[0], "tp", core)]
    relayed = []
    summing = []
    high, low, p = gates(pos, events, gate_w, rows, own)

    def between(deps, through=(), others=()):
        active = [r for r in summing if not r.finished]
        jobs = [r.job() for r in active] + list(others)
        fetched = len(relayed)
        fetching = fetched < len(far)
        if fetching:
            jobs.append(copy_job(far[fetched]))
        outs, through, token = run(pos, jobs, deps, through)
        if fetching:
            relayed.append(lax.ppermute(outs[-1][0], "tp", core))
        for r, o in zip(active, outs):
            r.take(o)
        if len(own) < len(GROUPS):
            own.append(payload(GROUPS[len(own)], w_in, w_out, [token]))
            far.append(lax.ppermute(own[-1], "tp", across))
            beside.append(lax.ppermute(own[-1], "tp", core))
            token = own[-1]
        return [token], through, outs[len(active) :]

    deps, _, outs = between([p], others=[copy_job(*smalls[1:])])
    smalls = smalls[:1] + outs[0]
    mix = x_grad = None
    dps, sums = [], []
    for g, group in enumerate(GROUPS):
        last = g == len(GROUPS) - 1
        shards = (own[g], beside[g], far[g], relayed[g])
        mix, dp, h, l, wh, wl, mine, part, s = experts(
            pos, group, rows, high, low, mix_cotangent, p, shards, smalls, mix, (dps, sums) if last else None, deps
        )
        dps.append(dp)
        sums.append(s)
        summing.append(Reduction(pos, *(([mine, s], [part, s]) if last else ([mine], [part])), n_dp))
        deps, _, _ = between([s])
        x_grad, token = event_grads(pos, rows, h, l, wh, wl, [dp, gate_w] if last else [], x_grad, deps)
        deps = [token]
    deps, (mix, x_grad), _ = between(deps, [mix, x_grad])
    other_mix, other_grad = lax.ppermute(mix, "tp", core), lax.ppermute(x_grad, "tp", core)
    deps, _, _ = between(deps)
    mixtures, token = place(pos, mix, other_mix, deps)
    deps, _, _ = between([token])
    x_grad, token = place(pos, x_grad, other_grad, deps)
    deps = [token]
    while summing[-1].stage < 2 * summing[-1].bits - 1:
        deps, _, _ = between(deps)
    halves = [r.keep for r in summing] + summing[-1].got
    per_expert = (E, SLICE)
    shapes = [(E, SLICE, D), per_expert, (E, SLICE, H), per_expert, per_expert, per_expert, (GATE_COLS, D)]
    scratch = [pltpu.VMEM((summing[-1].rows, LANES), F32)]
    job = Job(halves, shapes, functools.partial(finish_body, GROUPS), scratch)
    (((in_grad, in_bias, out_grad, out_bias, gain, shift, gate),), _, _) = run(pos, [job], deps)
    return (
        mixtures,
        x_grad,
        jnp.swapaxes(in_grad, 1, 2),
        in_bias,
        jnp.swapaxes(out_grad, 1, 2),
        out_bias,
        gain,
        shift,
        jnp.swapaxes(gate, 0, 1),
    )


def solution(mesh):
    return jax.shard_map(
        per_device,
        mesh=mesh,
        in_specs=(
            P("dp", None),
            P(),
            P("dp", None),
            P(None, None, "tp"),
            P(None, "tp"),
            P(None, None, "tp"),
            P(None, "tp"),
            P(None, "tp"),
            P(None, "tp"),
            P(),
        ),
        out_specs=(
            P("dp", None),
            P("dp", None),
            P(None, None, "tp"),
            P(None, "tp"),
            P(None, None, "tp"),
            P(None, "tp"),
            P(None, "tp"),
            P(None, "tp"),
            P(),
        ),
        check_vma=False,
    )
```

time: 183 us -> 171 us (0.934)
  Pallas kernels: 74.5 us -> 111 us
  waiting for transfers between devices: 36.4 us -> 15.2 us
  starting transfers between devices: 43.7 us -> 27.9 us
  blocking collectives: 8.52 us -> 0 us
  local copies, waits for them, and re-layouts: 17.6 us -> 13 us
    pallas_call x15 -> x20, Pallas kernels: 65.9 us -> 94 us  [the longest x3 42.6 us: experts(): pl.pallas_call(functools.partial(expert_kernel, group, first, last, len(d...]
    ppermute x39 -> x33, waiting for transfers between devices: 36.4 us -> 15.2 us  [the longest x15 15.2 us: over(): return [lax.ppermute(v, 'dp', self.swap[bit]) for v in values]]
    ppermute x39 -> x33, starting transfers between devices: 43.7 us -> 27.9 us  [the longest x15 18 us: over(): return [lax.ppermute(v, 'dp', self.swap[bit]) for v in values]]
    all_gather x1 -> x0, blocking collectives: 8.52 us -> none  [per_device(): lax.all_gather(jnp.stack([expert_in_bias, expert_out_bias, norm_gain, nor...]
    pallas_call x2, Pallas kernels: 8.62 us -> 16.7 us  [place(): pl.pallas_call(place_kernel, grid_spec=pltpu.PrefetchScalarGridSpec(num_s...]
    unnamed x52 -> x66, local copies, waits for them, and re-layouts: 14.8 us -> 11.7 us
    slice x2 -> x0, local copies, waits for them, and re-layouts: 2.25 us -> none  [per_device(): own = jnp.concatenate([w_in[lo:hi], w_out[lo:hi]], axis=2)]
  transfers between devices with their start and end apart: 39 -> 33, of which waited for: 16 -> 4; matrix products, arithmetic and copies ran while one was open for 1% -> 2% of each run, Pallas kernels for 29% -> 58%
where the time goes in v2:
time: 171 us; the launch traced here: 170 us
  Pallas kernels  111 us (65%)
  starting transfers between devices  27.9 us (16%)
  waiting for transfers between devices  15.2 us (9%)
  local copies, waits for them, and re-layouts  13 us (8%)
  other arithmetic  1.97 us (1%)
    pallas_call x3, Pallas kernels, experts(): pl.pallas_call(functools.partial(expert_kernel, group, first, last, len(d...  42.6 us
    pallas_call x10, Pallas kernels, run(): pl.pallas_call(kernel, in_specs=[pl.BlockSpec(memory_space=pltpu.SMEM)] +...  21.5 us
    pallas_call x3, Pallas kernels, event_grads(): pl.pallas_call(functools.partial(event_kernel, bool(gating), before is no...  19.3 us
    ppermute x15, starting transfers between devices, over(): return [lax.ppermute(v, 'dp', self.swap[bit]) for v in values]  18 us
    pallas_call x2, Pallas kernels, place(): pl.pallas_call(place_kernel, grid_spec=pltpu.PrefetchScalarGridSpec(num_s...  16.7 us
    ppermute x15, waiting for transfers between devices, over(): return [lax.ppermute(v, 'dp', self.swap[bit]) for v in values]  15.2 us
    unnamed x66, local copies, waits for them, and re-layouts  11.7 us
    pallas_call x1, Pallas kernels, gates(): pl.pallas_call(functools.partial(gate_kernel, len(deps)), grid_spec=pltpu...  5.53 us
  transfers between devices with their start and end apart: 33, of which 4 were waited for; matrix products, arithmetic and copies ran while one was open for 2% of the time, Pallas kernels for 58%

profile of v2, /device:TPU:0, one launch (start us, length us, event | category | flops | bytes accessed | tf_op | source)
XLA Modules:
  0.0 169.9 jit_solution(2477933824397691066)
XLA Ops:
  0.6 1.7 %shard_map.169.refs_0_.refs_5_ = f32[2,64,768]{2,1,0:T(8,128)} custom-call(f32[6,64,512]{2,1,0:T(8,128)} %bitcast.8, f32[6,64,256]{2,1,0:T(8,128)} %bitcast.11), custom_call_target="tpu_custom_call" | custom-call | bytes 786432 | tf_op jit(solution)/shard_map/pallas_call | solution.py:117
  2.4 3.0 %collective-permute-start.1 = (f32[2,64,768]{2,1,0:T(8,128)}, f32[2,64,768]{2,1,0:T(8,128)S(1)}, u32[]{:S(2)}, u32[]{:S(2)}) collective-permute-start(f32[2,64,768]{2,1,0:T(8,128)} %shard_map.169.refs_0_.refs_5_), channel_id=1, source_target_pairs={{0,2},{1,3},{2,0},{3,1},{4,6},{5,7},{6,4},{7,5},{8,10},{9,11},{10,... | collective-permute-start | bytes 1179656 | tf_op jit(solution)/shard_map/ppermute | solution.py:646
  10.5 5.5 %shard_map.170 = (bf16[1024,512]{1,0:T(8,128)(2,1)}, bf16[1024,512]{1,0:T(8,128)(2,1)}, f32[1024,128]{1,0:T(8,128)}) custom-call(s32[3]{0:T(128)} %pad_add_fusion.pos.pos_ref.refs_0_, f32[2048,512]{1,0:T(8,128)} %ev_ref.1, f32[14,512]{1,0:T(8,128)} %bitcast.14, f32[2,64,768]{2,1,0:T(8,128)} %shard_map.169.refs_0_.refs_5_), custom_call_target="tpu_custom_call" | custom-call | flops 402653184 | bytes 4194304 | tf_op jit(solution)/shard_map/pallas_call | solution.py:86
  16.9 1.8 %shard_map.171 = (f32[24,64]{1,0:T(8,128)}, f32[24,64]{1,0:T(8,128)}, f32[24,64]{1,0:T(8,128)}, f32[2,64,768]{2,1,0:T(8,128)}, f32[8,128]{1,0:T(8,128)}) custom-call(s32[3]{0:T(128)} %pad_add_fusion.pos.pos_ref.refs_0_, f32[24,64]{1,0:T(8,128)} %copy-done.23, f32[24,64]{1,0:T(8,128)} %copy-done.24, f32[24,64]{1,0:T(8,128)} %copy-done.25, ...), custom_call_target="tpu_custom_call" | custom-call | bytes 823296 | tf_op jit(solution)/shard_map/pallas_call | solution.py:499
  19.5 1.7 shard_map.172.refs_13_.refs_5_
  22.3 13.0 %shard_map.173 = (f32[1024,768]{1,0:T(8,128)}, f32[1024,128]{1,0:T(8,128)}, bf16[1024,512]{1,0:T(8,128)(2,1)}, bf16[1024,512]{1,0:T(8,128)(2,1)}, bf16[512,512]{...) custom-call(s32[3]{0:T(128)} %pad_add_fusion.pos.pos_ref.refs_0_, ...), custom_call_target="tpu_custom_call" | custom-call | flops 8858370048 | bytes 14336000 | tf_op jit(solution)/shard_map/pallas_call | solution.py:347
  36.0 2.1 %shard_map.174 = (f32[768,128]{1,0:T(8,128)}, f32[2,64,768]{2,1,0:T(8,128)}, f32[8,128]{1,0:T(8,128)}) custom-call(s32[3]{0:T(128)} %pad_add_fusion.pos.pos_ref.refs_0_, f32[768,128]{1,0:T(8,128)} %get-tuple-element.109.refs_0_, f32[2,64,768]{2,1,0:T(8,128)} %copy-done.4, f32[8,128]{1,0:T(8,128)} %get-tuple-element.110.refs_2_.refs_16_), custom_call_target="tpu_custom_call" | custom-call | bytes 1572864 | tf_op jit(solution)/shard_map/pallas_call | solution.py:499
  38.5 1.7 %shard_map.175.refs_0_.refs_5_ = f32[2,64,768]{2,1,0:T(8,128)} custom-call(f32[6,64,512]{2,1,0:T(8,128)} %bitcast.10, f32[6,64,256]{2,1,0:T(8,128)} %bitcast.13, f32[8,128]{1,0:T(8,128)} %get-tuple-element.118.refs_0_), custom_call_target="tpu_custom_call" | custom-call | bytes 786432 | tf_op jit(solution)/shard_map/pallas_call | solution.py:117
  40.2 2.0 %collective-permute-start.10 = (f32[2,64,768]{2,1,0:T(8,128)}, f32[2,64,768]{2,1,0:T(8,128)S(1)}, u32[]{:S(2)}, u32[]{:S(2)}) collective-permute-start(f32[2,64,768]{2,1,0:T(8,128)} %shard_map.175.refs_0_.refs_5_), channel_id=1, source_target_pairs={{0,2},{1,3},{2,0},{3,1},{4,6},{5,7},{6,4},{7,5},{8,10},{9,11},{10,... | collective-permute-start | bytes 1179656 | tf_op jit(solution)/shard_map/ppermute | solution.py:666
  42.7 5.9 %shard_map.176 = (f32[1024,512]{1,0:T(8,128)}, f32[8,128]{1,0:T(8,128)}) custom-call(s32[3]{0:T(128)} %pad_add_fusion.pos.pos_ref.refs_0_, bf16[1024,512]{1,0:T(8,128)(2,1)} %get-tuple-element.114.high, bf16[1024,512]{1,0:T(8,128)(2,1)} %get-tuple-element.115.low, bf16[512,512]{1,0:T(8,128)(2,1)} %get-tuple-element.116.winh, ...), custom_call_target="tpu_custom_call" | custom-call | flops 1610612736 | bytes 6144000 | tf_op jit(solution)/shard_map/pallas_call | solution.py:410
  49.5 13.9 %shard_map.177 = (f32[1024,768]{1,0:T(8,128)}, f32[1024,128]{1,0:T(8,128)}, bf16[1024,512]{1,0:T(8,128)(2,1)}, bf16[1024,512]{1,0:T(8,128)(2,1)}, bf16[512,512]{...) custom-call(s32[3]{0:T(128)} %pad_add_fusion.pos.pos_ref.refs_0_, ...), custom_call_target="tpu_custom_call", output_to_operand_aliasing={{0}: (13, {})} | custom-call | flops 8858370048 | bytes 14336000 | tf_op jit(solution)/shard_map/pallas_call | solution.py:347
  64.3 2.4 %shard_map.178 = (f32[384,128]{1,0:T(8,128)}, f32[384,128]{1,0:T(8,128)}, f32[768,128]{1,0:T(8,128)}, f32[2,64,768]{2,1,0:T(8,128)}, f32[8,128]{1,0:T(8,128)}) custom-call(s32[3]{0:T(128)} %pad_add_fusion.pos.pos_ref.refs_0_, f32[768,128]{1,0:T(8,128)} %get-tuple-element.108.refs_0_, f32[768,128]{1,0:T(8,128)} %copy-done.6, ...), custom_call_target="tpu_custom_call" | custom-call | bytes 3145728 | tf_op jit(solution)/shard_map/pallas_call | solution.py:499
  68.4 6.4 %shard_map.179 = (f32[1024,512]{1,0:T(8,128)}, f32[8,128]{1,0:T(8,128)}) custom-call(s32[3]{0:T(128)} %pad_add_fusion.pos.pos_ref.refs_0_, bf16[1024,512]{1,0:T(8,128)(2,1)} %get-tuple-element.130.high, bf16[1024,512]{1,0:T(8,128)(2,1)} %get-tuple-element.131.low, bf16[512,512]{1,0:T(8,128)(2,1)} %get-tuple-element.132.winh, ...), custom_call_target="tpu_custom_call", output_to_operand_aliasing={{0}: (5, {})} | custom-call | flops 1610612736 | bytes 6144000 | tf_op jit(solution)/shard_map/pallas_call | solution.py:410
  75.7 15.7 %shard_map.180 = (f32[1024,768]{1,0:T(8,128)}, f32[1024,128]{1,0:T(8,128)}, bf16[1024,512]{1,0:T(8,128)(2,1)}, bf16[1024,512]{1,0:T(8,128)(2,1)}, bf16[512,512]{...) custom-call(s32[3]{0:T(128)} %pad_add_fusion.pos.pos_ref.refs_0_, ...), custom_call_target="tpu_custom_call", output_to_operand_aliasing={{0}: (13, {})} | custom-call | flops 8858370048 | bytes 14336000 | tf_op jit(solution)/shard_map/pallas_call | solution.py:347
  92.2 2.4 %shard_map.181 = (f32[192,128]{1,0:T(8,128)}, f32[192,128]{1,0:T(8,128)}, f32[384,128]{1,0:T(8,128)}, f32[384,128]{1,0:T(8,128)}, f32[768,128]{1,0:T(8,128)}, /*index=5*/f32[128,128]{1,0:T(8,128)}, f32[8,128]{1,0:T(8,128)}) custom-call(s32[3]{0:T(128)} %pad_add_fusion.pos.pos_ref.refs_0_, f32[384,128]{1,0:T(8,128)} %get-tuple-element.122.refs_0_, ...), custom_call_target="tpu_custom_call" | custom-call | bytes 3276800 | tf_op jit(solution)/shard_map/pallas_call | solution.py:499
  97.1 7.0 %shard_map.182 = (f32[1024,512]{1,0:T(8,128)}, f32[8,128]{1,0:T(8,128)}) custom-call(s32[3]{0:T(128)} %pad_add_fusion.pos.pos_ref.refs_0_, bf16[1024,512]{1,0:T(8,128)(2,1)} %get-tuple-element.147.high, bf16[1024,512]{1,0:T(8,128)(2,1)} %get-tuple-element.148.low, bf16[512,512]{1,0:T(8,128)(2,1)} %get-tuple-element.149.winh, ...), custom_call_target="tpu_custom_call", output_to_operand_aliasing={{0}: (7, {})} | custom-call | flops 1610612736 | bytes 6144000 | tf_op jit(solution)/shard_map/pallas_call | solution.py:410
  105.0 2.3 %shard_map.183 = (f32[192,128]{1,0:T(8,128)}, f32[192,128]{1,0:T(8,128)}, f32[192,128]{1,0:T(8,128)}, f32[448,128]{1,0:T(8,128)}, f32[448,128]{1,0:T(8,128)}, /*...) custom-call(s32[3]{0:T(128)} %pad_add_fusion.pos.pos_ref.refs_0_, ...), custom_call_target="tpu_custom_call", output_to_operand_aliasing={{5}: (9, {}), {6}: (10, {})} | custom-call | bytes 3014656 | tf_op jit(solution)/shard_map/pallas_call | solution.py:499
  109.3 2.6 %collective-permute-start.20 = (f32[192,128]{1,0:T(8,128)}, f32[192,128]{1,0:T(8,128)S(1)}, u32[]{:S(2)}, u32[]{:S(2)}) collective-permute-start(f32[192,128]{1,0:T(8,128)} %get-tuple-element.157.refs_0_), channel_id=1, source_target_pairs={{0,16},{4,20},{8,24},{12,28},{16,0},{20,4},{24,8},{28,12},{1,17},{... | collective-permute-start | bytes 294920 | tf_op jit(solution)/shard_map/ppermute | solution.py:532
  112.4 5.0 %collective-permute-done.20.refs_1_ = f32[192,128]{1,0:T(8,128)S(1)} collective-permute-done((f32[192,128]{1,0:T(8,128)}, f32[192,128]{1,0:T(8,128)S(1)}, u32[]{:S(2)}, u32[]{:S(2)}) %collective-permute-start.20) | collective-permute-done | bytes 98336 | tf_op jit(solution)/shard_map/ppermute | solution.py:532
  119.5 2.0 %shard_map.184 = (f32[192,128]{1,0:T(8,128)}, f32[192,128]{1,0:T(8,128)}, f32[224,128]{1,0:T(8,128)}, f32[224,128]{1,0:T(8,128)}, f32[8,128]{1,0:T(8,128)}) custom-call(s32[3]{0:T(128)} %pad_add_fusion.pos.pos_ref.refs_0_, f32[192,128]{1,0:T(8,128)} %get-tuple-element.157.refs_0_, f32[192,128]{1,0:T(8,128)} %copy-done.16, ...), custom_call_target="tpu_custom_call" | custom-call | bytes 1703936 | tf_op jit(solution)/shard_map/pallas_call | solution.py:499
  121.9 1.6 collective-permute-start.24
  123.5 1.6 copy-done
  125.2 9.0 %shard_map.185 = (f32[2048,768]{1,0:T(8,128)}, f32[8,128]{1,0:T(8,128)}) custom-call(s32[3]{0:T(128)} %pad_add_fusion.pos.pos_ref.refs_0_, f32[1024,768]{1,0:T(8,128)} %get-tuple-element.156.own, f32[1024,768]{1,0:T(8,128)} %copy-done, f32[8,128]{1,0:T(8,128)} %get-tuple-element.163.refs_0_), custom_call_target="tpu_custom_call" | custom-call | bytes 12582912 | tf_op jit(solution)/shard_map/pallas_call | solution.py:451
  134.8 1.9 %shard_map.186 = (f32[384,128]{1,0:T(8,128)}, f32[192,128]{1,0:T(8,128)}, f32[224,128]{1,0:T(8,128)}, f32[8,128]{1,0:T(8,128)}) custom-call(s32[3]{0:T(128)} %pad_add_fusion.pos.pos_ref.refs_0_, f32[192,128]{1,0:T(8,128)} %get-tuple-element.166.refs_0_, f32[192,128]{1,0:T(8,128)} %copy-done.18, f32[192,128]{1,0:T(8,128)} %get-tuple-element.167.refs_2_, ...), custom_call_target="tpu_custom_call" | custom-call | bytes 1245184 | tf_op jit(solution)/shard_map/pallas_call | solution.py:499
  138.1 2.1 %collective-permute-start.29 = (f32[224,128]{1,0:T(8,128)}, f32[224,128]{1,0:T(8,128)S(1)}, u32[]{:S(2)}, u32[]{:S(2)}) collective-permute-start(f32[224,128]{1,0:T(8,128)} %get-tuple-element.175.refs_4_), channel_id=1, source_target_pairs={{0,16},{4,20},{8,24},{12,28},{16,0},{20,4},{24,8},{28,12},{1,17},{... | collective-permute-start | bytes 344072 | tf_op jit(solution)/shard_map/ppermute | solution.py:532
  140.6 7.8 %shard_map.187 = (f32[2048,512]{1,0:T(8,128)}, f32[8,128]{1,0:T(8,128)}) custom-call(s32[3]{0:T(128)} %pad_add_fusion.pos.pos_ref.refs_0_, f32[1024,512]{1,0:T(8,128)} %get-tuple-element.165.own, f32[1024,512]{1,0:T(8,128)} %collective-permute-done.23.other, f32[8,128]{1,0:T(8,128)} %get-tuple-element.171.refs_0_), custom_call_target="tpu_custom_call" | custom-call | bytes 8388608 | tf_op jit(solution)/shard_map/pallas_call | solution.py:451
  149.2 2.1 %shard_map.188 = (f32[768,128]{1,0:T(8,128)}, f32[384,128]{1,0:T(8,128)}, f32[224,128]{1,0:T(8,128)}, f32[8,128]{1,0:T(8,128)}) custom-call(s32[3]{0:T(128)} %pad_add_fusion.pos.pos_ref.refs_0_, f32[384,128]{1,0:T(8,128)} %get-tuple-element.173.refs_0_, f32[384,128]{1,0:T(8,128)} %copy-done.11, f32[192,128]{1,0:T(8,128)} %get-tuple-element.174.refs_2_, ...), custom_call_target="tpu_custom_call" | custom-call | bytes 1638400 | tf_op jit(solution)/shard_map/pallas_call | solution.py:499
  152.7 1.6 collective-permute-start.31
  154.3 3.4 %collective-permute-done.31.refs_3_ = f32[224,128]{1,0:T(8,128)S(1)} collective-permute-done((f32[224,128]{1,0:T(8,128)}, f32[224,128]{1,0:T(8,128)S(1)}, u32[]{:S(2)}, u32[]{:S(2)}) %collective-permute-start.31) | collective-permute-done | bytes 114720 | tf_op jit(solution)/shard_map/ppermute | solution.py:532
  158.5 2.0 %shard_map.189 = (f32[768,128]{1,0:T(8,128)}, f32[448,128]{1,0:T(8,128)}, f32[8,128]{1,0:T(8,128)}) custom-call(s32[3]{0:T(128)} %pad_add_fusion.pos.pos_ref.refs_0_, f32[384,128]{1,0:T(8,128)} %get-tuple-element.178.refs_0_, f32[384,128]{1,0:T(8,128)} %copy-done.12, f32[224,128]{1,0:T(8,128)} %get-tuple-element.179.refs_2_, f32[224,128]{1,0:T(8,128)} %copy-done.15, ...), custom_call_target="tpu_custom_call" | custom-call | bytes 1245184 | tf_op jit(solution)/shard_map/pallas_call | solution.py:499
  161.3 5.4 %collective-permute-done.32.refs_3_ = f32[448,128]{1,0:T(8,128)S(1)} collective-permute-done((f32[448,128]{1,0:T(8,128)}, f32[448,128]{1,0:T(8,128)S(1)}, u32[]{:S(2)}, u32[]{:S(2)}) %collective-permute-start.32) | collective-permute-done | bytes 229408 | tf_op jit(solution)/shard_map/ppermute | solution.py:532
  167.4 2.4 %shard_map.190 = (f32[6,64,512]{2,1,0:T(8,128)}, f32[6,64]{1,0:T(8,128)}, f32[6,64,256]{2,1,0:T(8,128)}, f32[6,64]{1,0:T(8,128)}, f32[6,64]{1,0:T(8,128)}, /*ind...) custom-call(s32[3]{0:T(128)} %pad_add_fusion.pos.pos_ref.refs_0_, f32[768,128]{1,0:T(8,128)} %get-tuple-element.177.refs_0_, ...), custom_call_target="tpu_custom_call" | custom-call | bytes 2490368 | tf_op jit(solution)/shard_map/pallas_call | solution.py:499
  (125 shorter events, 29.7 us)
Async XLA Ops:
  2.4 13.8 %collective-permute-start.1 = (f32[2,64,768]{2,1,0:T(8,128)}, f32[2,64,768]{2,1,0:T(8,128)S(1)}, u32[]{:S(2)}, u32[]{:S(2)}) collective-permute-start(f32[2,64,768]{2,1,0:T(8,128)} %shard_map.169.refs_0_.refs_5_), channel_id=1, source_target_pairs={{0,2},{1,3},{2,0},{3,1},{4,6},{5,7},{6,4},{7,5},{8,10},{9,11},{10,... | collective-permute-start | bytes 1179656 | tf_op jit(solution)/shard_map/ppermute | solution.py:646
  5.3 16.1 %collective-permute-start = (f32[2,64,768]{2,1,0:T(8,128)}, f32[2,64,768]{2,1,0:T(8,128)S(1)}, u32[]{:S(2)}, u32[]{:S(2)}) collective-permute-start(f32[2,64,768]{2,1,0:T(8,128)} %shard_map.169.refs_0_.refs_5_), channel_id=1, source_target_pairs={{0,1},{1,0},{2,3},{3,2},{4,5},{5,4},{6,7},{7,6},{8,9},{9,8},{10,11... | collective-permute-start | bytes 1179656 | tf_op jit(solution)/shard_map/ppermute | solution.py:647
  6.1 10.0 %collective-permute-start.2 = (f32[24,64]{1,0:T(8,128)S(1)}, f32[24,64]{1,0:T(8,128)S(1)}, u32[]{:S(2)}, u32[]{:S(2)}) collective-permute-start(f32[24,64]{1,0:T(8,128)S(1)} %pad_maximum_fusion.refs_9_), channel_id=1, source_target_pairs={{0,1},{1,0},{2,3},{3,2},{4,5},{5,4},{6,7},{7,6},{8,9},{9,8},{10,11... | collective-permute-start | bytes 18440 | tf_op jit(solution)/shard_map/ppermute | solution.py:644
  6.6 9.4 %collective-permute-start.3 = (f32[24,64]{1,0:T(8,128)S(1)}, f32[24,64]{1,0:T(8,128)S(1)}, u32[]{:S(2)}, u32[]{:S(2)}) collective-permute-start(f32[24,64]{1,0:T(8,128)S(1)} %pad_maximum_fusion.refs_9_), channel_id=1, source_target_pairs={{0,2},{1,3},{2,0},{3,1},{4,6},{5,7},{6,4},{7,5},{8,10},{9,11},{10,... | collective-permute-start | bytes 18440 | tf_op jit(solution)/shard_map/ppermute | solution.py:644
  6.6 9.5 %collective-permute-start.4 = (f32[24,64]{1,0:T(8,128)S(1)}, f32[24,64]{1,0:T(8,128)S(1)}, u32[]{:S(2)}, u32[]{:S(2)}) collective-permute-start(f32[24,64]{1,0:T(8,128)S(1)} %pad_maximum_fusion.refs_9_), channel_id=1, source_target_pairs={{0,3},{1,2},{2,1},{3,0},{4,7},{5,6},{6,5},{7,4},{8,11},{9,10},{10,... | collective-permute-start | bytes 18440 | tf_op jit(solution)/shard_map/ppermute | solution.py:644
  21.2 14.1 %collective-permute-start.6 = (f32[2,64,768]{2,1,0:T(8,128)}, f32[2,64,768]{2,1,0:T(8,128)S(1)}, u32[]{:S(2)}, u32[]{:S(2)}) collective-permute-start(f32[2,64,768]{2,1,0:T(8,128)} %shard_map.172.refs_13_.refs_5_), channel_id=1, source_target_pairs={{0,2},{1,3},{2,0},{3,1},{4,6},{5,7},{6,4},{7,5},{8,10},{9,11},{10,... | collective-permute-start | bytes 1179656 | tf_op jit(solution)/shard_map/ppermute | solution.py:666
  21.2 27.3 %collective-permute-start.8 = (f32[2,64,768]{2,1,0:T(8,128)}, f32[2,64,768]{2,1,0:T(8,128)S(1)}, u32[]{:S(2)}, u32[]{:S(2)}) collective-permute-start(f32[2,64,768]{2,1,0:T(8,128)} %shard_map.172.refs_13_.refs_5_), channel_id=1, source_target_pairs={{0,1},{1,0},{2,3},{3,2},{4,5},{5,4},{6,7},{7,6},{8,9},{9,8},{10,11... | collective-permute-start | bytes 1179656 | tf_op jit(solution)/shard_map/ppermute | solution.py:667
  38.1 10.5 %collective-permute-start.9 = (f32[2,64,768]{2,1,0:T(8,128)}, f32[2,64,768]{2,1,0:T(8,128)S(1)}, u32[]{:S(2)}, u32[]{:S(2)}) collective-permute-start(f32[2,64,768]{2,1,0:T(8,128)} %get-tuple-element.112), channel_id=1, source_target_pairs={{0,1},{1,0},{2,3},{3,2},{4,5},{5,4},{6,7},{7,6},{8,9},{9,8},{10,11... | collective-permute-start | bytes 1179656 | tf_op jit(solution)/shard_map/ppermute | solution.py:661
  40.2 23.2 %collective-permute-start.10 = (f32[2,64,768]{2,1,0:T(8,128)}, f32[2,64,768]{2,1,0:T(8,128)S(1)}, u32[]{:S(2)}, u32[]{:S(2)}) collective-permute-start(f32[2,64,768]{2,1,0:T(8,128)} %shard_map.175.refs_0_.refs_5_), channel_id=1, source_target_pairs={{0,2},{1,3},{2,0},{3,1},{4,6},{5,7},{6,4},{7,5},{8,10},{9,11},{10,... | collective-permute-start | bytes 1179656 | tf_op jit(solution)/shard_map/ppermute | solution.py:666
  42.2 32.6 %collective-permute-start.13 = (f32[2,64,768]{2,1,0:T(8,128)}, f32[2,64,768]{2,1,0:T(8,128)S(1)}, u32[]{:S(2)}, u32[]{:S(2)}) collective-permute-start(f32[2,64,768]{2,1,0:T(8,128)} %shard_map.175.refs_0_.refs_5_), channel_id=1, source_target_pairs={{0,1},{1,0},{2,3},{3,2},{4,5},{5,4},{6,7},{7,6},{8,9},{9,8},{10,11... | collective-permute-start | bytes 1179656 | tf_op jit(solution)/shard_map/ppermute | solution.py:667
  42.2 21.2 %collective-permute-start.7 = (f32[768,128]{1,0:T(8,128)}, f32[768,128]{1,0:T(8,128)S(1)}, u32[]{:S(2)}, u32[]{:S(2)}) collective-permute-start(f32[768,128]{1,0:T(8,128)} %get-tuple-element.111), channel_id=1, source_target_pairs={{0,1},{1,0},{2,3},{3,2},{4,5},{5,4},{6,7},{7,6},{8,9},{9,8},{10,11... | collective-permute-start | bytes 1179656 | tf_op jit(solution)/shard_map/ppermute | solution.py:581
  66.7 8.1 %collective-permute-start.14 = (f32[2,64,768]{2,1,0:T(8,128)}, f32[2,64,768]{2,1,0:T(8,128)S(1)}, u32[]{:S(2)}, u32[]{:S(2)}) collective-permute-start(f32[2,64,768]{2,1,0:T(8,128)} %get-tuple-element.126), channel_id=1, source_target_pairs={{0,1},{1,0},{2,3},{3,2},{4,5},{5,4},{6,7},{7,6},{8,9},{9,8},{10,11... | collective-permute-start | bytes 1179656 | tf_op jit(solution)/shard_map/ppermute | solution.py:661
  66.7 24.7 %collective-permute-start.11 = (f32[384,128]{1,0:T(8,128)}, f32[384,128]{1,0:T(8,128)S(1)}, u32[]{:S(2)}, u32[]{:S(2)}) collective-permute-start(f32[384,128]{1,0:T(8,128)} %get-tuple-element.123), channel_id=1, source_target_pairs={{0,4},{4,0},{8,12},{12,8},{16,20},{20,16},{24,28},{28,24},{1,5},{5... | collective-permute-start | bytes 589832 | tf_op jit(solution)/shard_map/ppermute | solution.py:532
  68.2 23.2 %collective-permute-start.12 = (f32[768,128]{1,0:T(8,128)}, f32[768,128]{1,0:T(8,128)S(1)}, u32[]{:S(2)}, u32[]{:S(2)}) collective-permute-start(f32[768,128]{1,0:T(8,128)} %get-tuple-element.125), channel_id=1, source_target_pairs={{0,1},{1,0},{2,3},{3,2},{4,5},{5,4},{6,7},{7,6},{8,9},{9,8},{10,11... | collective-permute-start | bytes 1179656 | tf_op jit(solution)/shard_map/ppermute | solution.py:581
  94.6 9.5 %collective-permute-start.17 = (f32[768,128]{1,0:T(8,128)}, f32[768,128]{1,0:T(8,128)S(1)}, u32[]{:S(2)}, u32[]{:S(2)}) collective-permute-start(f32[768,128]{1,0:T(8,128)} %get-tuple-element.144), channel_id=1, source_target_pairs={{0,1},{1,0},{2,3},{3,2},{4,5},{5,4},{6,7},{7,6},{8,9},{9,8},{10,11... | collective-permute-start | bytes 1179656 | tf_op jit(solution)/shard_map/ppermute | solution.py:581
  94.9 9.2 %collective-permute-start.16 = (f32[384,128]{1,0:T(8,128)}, f32[384,128]{1,0:T(8,128)S(1)}, u32[]{:S(2)}, u32[]{:S(2)}) collective-permute-start(f32[384,128]{1,0:T(8,128)} %get-tuple-element.142), channel_id=1, source_target_pairs={{0,4},{4,0},{8,12},{12,8},{16,20},{20,16},{24,28},{28,24},{1,5},{5... | collective-permute-start | bytes 589832 | tf_op jit(solution)/shard_map/ppermute | solution.py:532
  95.5 8.6 %collective-permute-start.15 = (f32[192,128]{1,0:T(8,128)}, f32[192,128]{1,0:T(8,128)S(1)}, u32[]{:S(2)}, u32[]{:S(2)}) collective-permute-start(f32[192,128]{1,0:T(8,128)} %get-tuple-element.140), channel_id=1, source_target_pairs={{0,8},{4,12},{8,0},{12,4},{16,24},{20,28},{24,16},{28,20},{1,9},{5... | collective-permute-start | bytes 294920 | tf_op jit(solution)/shard_map/ppermute | solution.py:532
  97.1 7.0 %collective-permute-start.18 = (f32[128,128]{1,0:T(8,128)}, f32[128,128]{1,0:T(8,128)S(1)}, u32[]{:S(2)}, u32[]{:S(2)}) collective-permute-start(f32[128,128]{1,0:T(8,128)} %get-tuple-element.145), channel_id=1, source_target_pairs={{0,1},{1,0},{2,3},{3,2},{4,5},{5,4},{6,7},{7,6},{8,9},{9,8},{10,11... | collective-permute-start | bytes 196616 | tf_op jit(solution)/shard_map/ppermute | solution.py:581
  107.3 16.3 %collective-permute-start.19 = (f32[1024,768]{1,0:T(8,128)}, f32[1024,768]{1,0:T(8,128)S(1)}, u32[]{:S(2)}, u32[]{:S(2)}) collective-permute-start(f32[1024,768]{1,0:T(8,128)} %get-tuple-element.156.own), channel_id=1, source_target_pairs={{0,1},{1,0},{2,3},{3,2},{4,5},{5,4},{6,7},{7,6},{8,9},{9,8},{10,11... | collective-permute-start | bytes 9437192 | tf_op jit(solution)/shard_map/ppermute | solution.py:688
  107.8 32.8 %collective-permute-start.23 = (f32[1024,512]{1,0:T(8,128)}, f32[1024,512]{1,0:T(8,128)}, u32[]{:S(2)}, u32[]{:S(2)}) collective-permute-start(f32[1024,512]{1,0:T(8,128)} %get-tuple-element.165.own), channel_id=1, source_target_pairs={{0,1},{1,0},{2,3},{3,2},{4,5},{5,4},{6,7},{7,6},{8,9},{9,8},{10,11... | collective-permute-start | bytes 6291464 | tf_op jit(solution)/shard_map/ppermute | solution.py:688
  107.9 10.9 %collective-permute-start.22 = (f32[448,128]{1,0:T(8,128)}, f32[448,128]{1,0:T(8,128)S(1)}, u32[]{:S(2)}, u32[]{:S(2)}) collective-permute-start(f32[448,128]{1,0:T(8,128)} %get-tuple-element.161), channel_id=1, source_target_pairs={{0,4},{4,0},{8,12},{12,8},{16,20},{20,16},{24,28},{28,24},{1,5},{5... | collective-permute-start | bytes 688136 | tf_op jit(solution)/shard_map/ppermute | solution.py:532
  109.3 8.1 %collective-permute-start.20 = (f32[192,128]{1,0:T(8,128)}, f32[192,128]{1,0:T(8,128)S(1)}, u32[]{:S(2)}, u32[]{:S(2)}) collective-permute-start(f32[192,128]{1,0:T(8,128)} %get-tuple-element.157.refs_0_), channel_id=1, source_target_pairs={{0,16},{4,20},{8,24},{12,28},{16,0},{20,4},{24,8},{28,12},{1,17},{... | collective-permute-start | bytes 294920 | tf_op jit(solution)/shard_map/ppermute | solution.py:532
  111.9 6.8 %collective-permute-start.21 = (f32[192,128]{1,0:T(8,128)}, f32[192,128]{1,0:T(8,128)S(1)}, u32[]{:S(2)}, u32[]{:S(2)}) collective-permute-start(f32[192,128]{1,0:T(8,128)} %get-tuple-element.159), channel_id=1, source_target_pairs={{0,8},{4,12},{8,0},{12,4},{16,24},{20,28},{24,16},{28,20},{1,9},{5... | collective-permute-start | bytes 294920 | tf_op jit(solution)/shard_map/ppermute | solution.py:532
  121.5 12.7 %collective-permute-start.26 = (f32[224,128]{1,0:T(8,128)}, f32[224,128]{1,0:T(8,128)S(1)}, u32[]{:S(2)}, u32[]{:S(2)}) collective-permute-start(f32[224,128]{1,0:T(8,128)} %get-tuple-element.169), channel_id=1, source_target_pairs={{0,8},{4,12},{8,0},{12,4},{16,24},{20,28},{24,16},{28,20},{1,9},{5... | collective-permute-start | bytes 344072 | tf_op jit(solution)/shard_map/ppermute | solution.py:532
  121.9 12.2 %collective-permute-start.24 = (f32[192,128]{1,0:T(8,128)}, f32[192,128]{1,0:T(8,128)S(1)}, u32[]{:S(2)}, u32[]{:S(2)}) collective-permute-start(f32[192,128]{1,0:T(8,128)} %get-tuple-element.166.refs_0_), channel_id=1, source_target_pairs={{0,8},{4,12},{8,0},{12,4},{16,24},{20,28},{24,16},{28,20},{1,9},{5... | collective-permute-start | bytes 294920 | tf_op jit(solution)/shard_map/ppermute | solution.py:532
  123.5 10.6 %collective-permute-start.25 = (f32[192,128]{1,0:T(8,128)}, f32[192,128]{1,0:T(8,128)S(1)}, u32[]{:S(2)}, u32[]{:S(2)}) collective-permute-start(f32[192,128]{1,0:T(8,128)} %get-tuple-element.167.refs_2_), channel_id=1, source_target_pairs={{0,16},{4,20},{8,24},{12,28},{16,0},{20,4},{24,8},{28,12},{1,17},{... | collective-permute-start | bytes 294920 | tf_op jit(solution)/shard_map/ppermute | solution.py:532
  136.8 11.7 %collective-permute-start.27 = (f32[384,128]{1,0:T(8,128)}, f32[384,128]{1,0:T(8,128)S(1)}, u32[]{:S(2)}, u32[]{:S(2)}) collective-permute-start(f32[384,128]{1,0:T(8,128)} %get-tuple-element.173.refs_0_), channel_id=1, source_target_pairs={{0,4},{4,0},{8,12},{12,8},{16,20},{20,16},{24,28},{28,24},{1,5},{5... | collective-permute-start | bytes 589832 | tf_op jit(solution)/shard_map/ppermute | solution.py:532
  138.1 10.4 %collective-permute-start.29 = (f32[224,128]{1,0:T(8,128)}, f32[224,128]{1,0:T(8,128)S(1)}, u32[]{:S(2)}, u32[]{:S(2)}) collective-permute-start(f32[224,128]{1,0:T(8,128)} %get-tuple-element.175.refs_4_), channel_id=1, source_target_pairs={{0,16},{4,20},{8,24},{12,28},{16,0},{20,4},{24,8},{28,12},{1,17},{... | collective-permute-start | bytes 344072 | tf_op jit(solution)/shard_map/ppermute | solution.py:532
  140.2 8.2 %collective-permute-start.28 = (f32[192,128]{1,0:T(8,128)}, f32[192,128]{1,0:T(8,128)S(1)}, u32[]{:S(2)}, u32[]{:S(2)}) collective-permute-start(f32[192,128]{1,0:T(8,128)} %get-tuple-element.174.refs_2_), channel_id=1, source_target_pairs={{0,8},{4,12},{8,0},{12,4},{16,24},{20,28},{24,16},{28,20},{1,9},{5... | collective-permute-start | bytes 294920 | tf_op jit(solution)/shard_map/ppermute | solution.py:532
  151.3 6.5 %collective-permute-start.30 = (f32[384,128]{1,0:T(8,128)}, f32[384,128]{1,0:T(8,128)S(1)}, u32[]{:S(2)}, u32[]{:S(2)}) collective-permute-start(f32[384,128]{1,0:T(8,128)} %get-tuple-element.178.refs_0_), channel_id=1, source_target_pairs={{0,4},{4,0},{8,12},{12,8},{16,20},{20,16},{24,28},{28,24},{1,5},{5... | collective-permute-start | bytes 589832 | tf_op jit(solution)/shard_map/ppermute | solution.py:532
  152.7 5.0 %collective-permute-start.31 = (f32[224,128]{1,0:T(8,128)}, f32[224,128]{1,0:T(8,128)S(1)}, u32[]{:S(2)}, u32[]{:S(2)}) collective-permute-start(f32[224,128]{1,0:T(8,128)} %get-tuple-element.179.refs_2_), channel_id=1, source_target_pairs={{0,8},{4,12},{8,0},{12,4},{16,24},{20,28},{24,16},{28,20},{1,9},{5... | collective-permute-start | bytes 344072 | tf_op jit(solution)/shard_map/ppermute | solution.py:532
  160.5 6.2 %collective-permute-start.32 = (f32[448,128]{1,0:T(8,128)}, f32[448,128]{1,0:T(8,128)S(1)}, u32[]{:S(2)}, u32[]{:S(2)}) collective-permute-start(f32[448,128]{1,0:T(8,128)} %get-tuple-element.182.refs_2_), channel_id=1, source_target_pairs={{0,4},{4,0},{8,12},{12,8},{16,20},{20,16},{24,28},{28,24},{1,5},{5... | collective-permute-start | bytes 688136 | tf_op jit(solution)/shard_map/ppermute | solution.py:532
  (34 other events, 42.2 us)

commit v3 on v2

v3 whole, which is shorter than its diff:
```python
import functools

import jax
import jax.numpy as jnp
from jax import lax
from jax.experimental import pallas as pl
from jax.experimental.pallas import tpu as pltpu
from jax.sharding import PartitionSpec as P

D = 512
H = 256
O = 256
E = 6
GATE_COLS = 14
SLICE = 64
WIDE = D + H
LANES = 128
TOKEN = (8, LANES)
RB = 512
ROW_BLOCK = 256
SUB = 256
LAG = 1
EPSILON = 1e-05
GROUPS = ((0,), (1, 2), (3, 4), (5,))
UNITS = ((0, 1), (2,), (3,))
COLUMN = (
    {0: 0, 1: 1, 4: 2, 5: 3},
    {2: 4, 3: 5, 4: 6, 5: 7},
    {e: 8 + e for e in range(E)},
)
F32 = jnp.float32
BF16 = jnp.bfloat16
NN = (((1,), (0,)), ((), ()))
NT = (((1,), (1,)), ((), ()))
TN = (((0,), (0,)), ((), ()))


def split(v):
    high = v.astype(BF16)
    return high, (v - high.astype(F32)).astype(BF16)


def dot3(a, b, dims):
    def one(u, v):
        return lax.dot_general(u, v, dims, preferred_element_type=F32)

    return one(a[0], b[0]) + (one(a[0], b[1]) + one(a[1], b[0]))


def half_of(v, upper):
    return jnp.where(upper, v[:, LANES:], v[:, :LANES])


LARGE = 60
EXPERT_MIB, EVENT_MIB, GATE_MIB, PAYLOAD_MIB, SMALL_MIB = 28, 16, 54, 62, 8


def params(mib):
    return pltpu.CompilerParams(vmem_limit_bytes=mib << 20)


def gate_kernel(n_deps, counts, ev_ref, cot_ref, gw_ref, *refs):
    high_ref, low_ref, p_ref, cot_out, gw, held, sems = refs[n_deps:]
    rows = held.shape[0]
    steps = rows // ROW_BLOCK
    start = pl.multiple_of((lax.axis_index("tp") & 1) * rows, ROW_BLOCK)
    valid = counts[lax.axis_index("dp")]
    blocks = [slice(i * ROW_BLOCK, (i + 1) * ROW_BLOCK) for i in range(steps)]
    copies = [
        pltpu.make_async_copy(ev_ref.at[pl.ds(start + at.start, ROW_BLOCK), :], held.at[at, :], sems.at[i])
        for i, at in enumerate(blocks)
    ]
    copies.append(pltpu.make_async_copy(cot_ref.at[pl.ds(start, rows), :], cot_out, sems.at[steps]))
    for copy in copies:
        copy.start()
    gw[...] = jnp.zeros_like(gw)
    gw[:GATE_COLS, :] = gw_ref[...]
    gate = split(gw[...])
    lane = lax.broadcasted_iota(jnp.int32, (ROW_BLOCK, LANES), 1)
    sets = (lane < 4, (lane >= 4) & (lane < 8), (lane >= 8) & (lane < GATE_COLS))

    def per_set(values, empty, reduce):
        a, b, s = (reduce(jnp.where(m, values, empty), axis=1, keepdims=True) for m in sets)
        return jnp.where(sets[0], a, jnp.where(sets[1], b, s))

    for i, at in enumerate(blocks):
        copies[i].wait()
        events = split(held[at, :])
        high_ref[at, :], low_ref[at, :] = events
        logits = dot3(events, gate, NT)
        top = per_set(logits, -3e38, jnp.max)
        shares = jnp.where(lane < GATE_COLS, jnp.exp(logits - top), 0.0)
        p = shares / per_set(shares, 0.0, jnp.sum)
        row = start + at.start + lax.broadcasted_iota(jnp.int32, logits.shape, 0)
        p_ref[at, :] = jnp.where((row < valid) & (lane < GATE_COLS), p, 0.0)
    copies[-1].wait()


def gates(counts, events, cot, gate_w, rows, deps):
    vmem, hbm = pl.BlockSpec(memory_space=pltpu.VMEM), pl.BlockSpec(memory_space=pltpu.HBM)
    steps = rows // ROW_BLOCK
    return pl.pallas_call(
        functools.partial(gate_kernel, len(deps)),
        in_specs=[pl.BlockSpec(memory_space=pltpu.SMEM), hbm, hbm, vmem]
        + [pl.BlockSpec(memory_space=pl.ANY)] * len(deps),
        out_specs=[vmem] * 4,
        out_shape=[
            jax.ShapeDtypeStruct((rows, D), BF16),
            jax.ShapeDtypeStruct((rows, D), BF16),
            jax.ShapeDtypeStruct((rows, LANES), F32),
            jax.ShapeDtypeStruct((rows, 3 * O), F32),
        ],
        scratch_shapes=[
            pltpu.VMEM((LANES, D), F32),
            pltpu.VMEM((rows, D), F32),
            pltpu.SemaphoreType.DMA((steps + 1,)),
        ],
        compiler_params=params(GATE_MIB),
        cost_estimate=pl.CostEstimate(flops=6 * rows * D * LANES, bytes_accessed=rows * D * 8, transcendentals=0),
    )(counts, events, cot, gate_w, *deps)


def payload_kernel(groups, vectors, n_deps, w_in, w_out, *refs):
    given = refs[:4] if vectors else ()
    outs, sems = refs[len(given) + n_deps :][: len(groups)], refs[-1]
    copies = []
    for out, group in zip(outs, groups):
        experts_of, rows = pl.ds(group[0], len(group)), slice(0, SLICE)
        for part, lanes in ((w_in, slice(0, D)), (w_out, slice(D, WIDE))):
            copies.append(pltpu.make_async_copy(part.at[experts_of], out.at[:, rows, lanes], sems.at[len(copies)]))
    for copy in copies:
        copy.start()
    if vectors:
        held = refs[-2]
        for k, v in enumerate(given):
            held[k * E : (k + 1) * E, :] = v[...]
        outs[0][:, SLICE:, :] = jnp.zeros((len(groups[0]), 8, WIDE), F32)
        for j in range(4 * E // 8):
            outs[0][0, SLICE:, j * LANES : j * LANES + SLICE] = held[8 * j : 8 * j + 8, :]
    for copy in copies:
        copy.wait()


def payload(groups, w_in, w_out, vectors, deps):
    vmem, hbm = pl.BlockSpec(memory_space=pltpu.VMEM), pl.BlockSpec(memory_space=pltpu.HBM)
    rows = SLICE + 8 if vectors else SLICE
    return pl.pallas_call(
        functools.partial(payload_kernel, groups, bool(vectors), len(deps)),
        in_specs=[hbm, hbm] + [vmem] * len(vectors) + [pl.BlockSpec(memory_space=pl.ANY)] * len(deps),
        out_specs=[vmem] * len(groups),
        out_shape=[jax.ShapeDtypeStruct((len(group), rows, WIDE), F32) for group in groups],
        scratch_shapes=[pltpu.VMEM((4 * E, SLICE), F32), pltpu.SemaphoreType.DMA((2 * len(groups),))],
        compiler_params=params(PAYLOAD_MIB),
        cost_estimate=pl.CostEstimate(flops=0, bytes_accessed=SLICE * WIDE * 16, transcendentals=0),
    )(w_in, w_out, *vectors, *deps)


def expert_kernel(group, first, last, n_deps, *refs):
    n = len(group)
    refs = list(refs)
    evh_ref, evl_ref, cot_ref, p_ref = refs[:4]
    shards = refs[4:8]
    del refs[:8]
    small = None if first else refs.pop(0)
    mix_in = None if first else refs.pop(0)
    if last:
        dp_before, sums_before = refs[: len(GROUPS) - 1], refs[len(GROUPS) - 1 : 2 * len(GROUPS) - 2]
        del refs[: 2 * len(GROUPS) - 2]
    del refs[:n_deps]
    mix_ref, dp_ref, dph_ref, dpl_ref, winh, winl, own_ref, part_ref, sums_ref = refs[:9]
    del refs[:9]
    if first:
        small = refs.pop(0)
    wouth, woutl, acc, sums = refs[:4]
    gate_acc = refs[4] if last else None
    step, steps = pl.program_id(0), pl.num_programs(0)
    odd = lax.axis_index("tp") & 1
    chip = lax.axis_index("tp") >> 1

    def tile(start, other):
        return pl.ds(pl.multiple_of(start + (chip ^ other) * LANES, LANES), LANES)

    @pl.when(step == 0)
    def _():
        acc[...] = jnp.zeros_like(acc)
        sums[...] = jnp.zeros_like(sums)
        if last:
            gate_acc[...] = jnp.zeros_like(gate_acc)
        for j in range(4 * E // 8 if first else 0):
            vectors = [shard[0, SLICE:, j * LANES : j * LANES + SLICE] for shard in shards]
            even_order, odd_order = (jnp.concatenate([vectors[k ^ c] for k in range(4)], axis=1) for c in range(2))
            small[8 * j : 8 * j + 8, :] = jnp.where(odd == 1, odd_order, even_order)
        if first:
            bias = small[E : 2 * E, :]
            small[E : 2 * E, :] = bias - jnp.mean(bias, axis=1, keepdims=True)
        own_rows = slice(0, SLICE)
        for i, e in enumerate(group):
            parts = [
                (shard[i, own_rows, :D], jnp.concatenate([shard[i, own_rows, tile(D, k)] for k in range(2)], axis=1))
                for shard in shards
            ]
            centre = sum(jnp.sum(out, axis=0, keepdims=True) for _, out in parts) / O
            for k, (into, out) in enumerate(parts):
                at = pl.multiple_of((odd ^ k) * SLICE, SLICE)
                winh[pl.ds(i * H + at, SLICE), :], winl[pl.ds(i * H + at, SLICE), :] = split(into)
                wouth[i, pl.ds(at, SLICE), :], woutl[i, pl.ds(at, SLICE), :] = split(out - centre)

    subs = RB // SUB
    rows_of = [slice(s * SUB, (s + 1) * SUB) for s in range(subs)]
    lane = lax.broadcasted_iota(jnp.int32, (SUB, LANES), 1)
    vector = lambda k, e: small[k * E + e : k * E + e + 1, :]
    state = [dict() for _ in range(subs)]

    def m1(s):
        events = evh_ref[rows_of[s], :], evl_ref[rows_of[s], :]
        state[s]["events"] = events
        pre = dot3(events, (winh[...], winl[...]), NT)
        state[s]["pre"] = [pre[:, i * H : (i + 1) * H] for i in range(n)]

    def v1(s):
        st = state[s]
        st["sigma"], st["hidden"], st["hidden_parts"] = [], [], []
        for i, e in enumerate(group):
            pre = st["pre"][i] + vector(0, e)
            sigma = jax.nn.sigmoid(pre)
            hidden = pre * sigma
            st["sigma"].append(sigma)
            st["hidden"].append(hidden)
            st["hidden_parts"].append(split(hidden))

    def m2(s):
        st = state[s]
        st["centred"] = [dot3(st["hidden_parts"][i], (wouth[i], woutl[i]), NT) for i in range(n)]

    def v2(s):
        st = state[s]
        p = p_ref[rows_of[s], :]
        dp = jnp.zeros_like(p)
        mixed = {}
        cots = [
            jnp.concatenate([cot_ref[rows_of[s], tile(t * O, 0)], cot_ref[rows_of[s], tile(t * O, 1)]], axis=1)
            for t in range(3)
        ]
        st["dnormed"] = []
        for i, e in enumerate(group):
            gain, shift = vector(2, e), vector(3, e)
            centred = st["centred"][i] + vector(1, e)
            rstd = lax.rsqrt(jnp.mean(centred * centred, axis=1, keepdims=True) + EPSILON)
            unit = centred * rstd
            y = unit * gain + shift
            dy = None
            for t in range(3):
                if e not in COLUMN[t]:
                    continue
                column = COLUMN[t][e]
                coef = p[:, column : column + 1]
                mixed[t] = coef * y + mixed[t] if t in mixed else coef * y
                dp = jnp.where(lane == column, jnp.sum(cots[t] * y, axis=1, keepdims=True), dp)
                dy = coef * cots[t] if dy is None else dy + coef * cots[t]
            dunit = dy * gain
            back_first = jnp.mean(dunit, axis=1, keepdims=True)
            back_second = jnp.mean(dunit * unit, axis=1, keepdims=True)
            dnormed = rstd * (dunit - back_first - unit * back_second)
            st["dnormed"].append(split(dnormed))
            dy_half = dy[:, :LANES]
            for k, v in enumerate((dnormed[:, :LANES], dy_half * unit[:, :LANES], dy_half)):
                sums[4 * i + k + 1 : 4 * i + k + 2, :] += jnp.sum(v, axis=0, keepdims=True)
        for t in range(3):
            for other in range(2):
                at = tile(t * O, other)
                if t in mixed:
                    value = mixed[t][:, other * LANES : (other + 1) * LANES]
                    mix_ref[rows_of[s], at] = value if first else mix_in[rows_of[s], at] + value
                elif first:
                    mix_ref[rows_of[s], at] = jnp.zeros((SUB, LANES), F32)
                else:
                    mix_ref[rows_of[s], at] = mix_in[rows_of[s], at]
        if last:
            for other in dp_before:
                dp = dp + other[rows_of[s], :]
            weighted = p * dp
            sets = (lane < 4, (lane >= 4) & (lane < 8), (lane >= 8) & (lane < GATE_COLS))
            a, b, c = (jnp.sum(jnp.where(m, weighted, 0.0), axis=1, keepdims=True) for m in sets)
            dp = weighted - p * jnp.where(sets[0], a, jnp.where(sets[1], b, c))
            st["dlogits"] = dp
        dp_ref[rows_of[s], :] = dp

    def m3(s):
        st = state[s]
        st["dhidden"] = [dot3(st["dnormed"][i], (wouth[i], woutl[i]), NN) for i in range(n)]

    def v3(s):
        st = state[s]
        st["dpre"] = []
        for i, e in enumerate(group):
            sigma, hidden = st["sigma"][i], st["hidden"][i]
            dpre = st["dhidden"][i] * (sigma + hidden * (1.0 - sigma))
            parts = split(dpre)
            dph_ref[rows_of[s], i * H : (i + 1) * H], dpl_ref[rows_of[s], i * H : (i + 1) * H] = parts
            st["dpre"].append(tuple(v[:, :LANES] for v in parts))
            sums[4 * i : 4 * i + 1, :] += jnp.sum(dpre[:, :LANES], axis=0, keepdims=True)

    def m4(s):
        st = state[s]
        for i in range(n):
            halves = tuple(v[:, :LANES] for v in st["dnormed"][i])
            acc[i * LANES : (i + 1) * LANES, D:] += dot3(halves, st["hidden_parts"][i], TN)
        beside = [split(st["dlogits"])] if last else []
        left = tuple(jnp.concatenate([h[k] for h in st["dpre"] + beside], axis=1) for k in range(2))
        both = dot3(left, st["events"], TN)
        acc[:, :D] += both[: n * LANES]
        if last:
            gate_acc[...] += both[n * LANES : n * LANES + 16]

    stages = (m1, v1, m2, v2, m3, v3, m4)
    for turn in range(len(stages) + LAG * (subs - 1)):
        for s in range(subs):
            if 0 <= turn - LAG * s < len(stages):
                stages[turn - LAG * s](s)

    @pl.when(step == steps - 1)
    def _():
        mine = pl.multiple_of(odd * SLICE, SLICE)
        other = pl.multiple_of(SLICE - mine, SLICE)
        for i in range(n):
            for t in range(WIDE // LANES):
                at = slice((t * n + i) * SLICE, (t * n + i + 1) * SLICE)
                lanes = slice(t * LANES, (t + 1) * LANES) if t < D // LANES else tile(D, t - D // LANES)
                own_ref[at, :] = acc[pl.ds(i * LANES + mine, SLICE), lanes]
                part_ref[at, :] = acc[pl.ds(i * LANES + other, SLICE), lanes]
        if last:
            sums_ref[...] = jnp.zeros_like(sums_ref)
            for g, before in enumerate(sums_before):
                sums_ref[8 * g : 8 * g + 8, :] = before[...]
            g = len(GROUPS) - 1
            sums_ref[8 * g : 8 * g + 8, :] = sums[...]
            for t in range(D // LANES):
                sums_ref[64 + 16 * t : 80 + 16 * t, :] = gate_acc[:, t * LANES : (t + 1) * LANES]
        else:
            sums_ref[...] = sums[...]


def experts(group, rows, high, low, cot, p, shards, small, mix, before, deps):
    n = len(group)
    first, last = mix is None, before is not None
    steps = rows // RB
    block = lambda width: pl.BlockSpec((RB, width), lambda i: (i, 0))
    whole = lambda shape: pl.BlockSpec(shape, lambda i: (0,) * len(shape))
    in_specs = [
        block(D),
        block(D),
        block(3 * O),
        block(LANES),
        *[whole(shards[0].shape)] * 4,
    ]
    args = [high, low, cot, p, *shards]
    aliases = {}
    if not first:
        aliases = {len(args) + 1: 0}
        in_specs += [whole((4 * E, H)), block(3 * O)]
        args += [small, mix]
    if last:
        in_specs += [block(LANES)] * len(before[0]) + [whole((8, LANES))] * len(before[1])
        args += [*before[0], *before[1]]
    in_specs += [pl.BlockSpec(memory_space=pl.ANY)] * len(deps)
    args += deps
    payload = WIDE // LANES * n * SLICE
    sums_shape = (2 * LANES // 2, LANES) if last else (8, LANES)
    scratch = [
        pltpu.VMEM((n, O, H), BF16),
        pltpu.VMEM((n, O, H), BF16),
        pltpu.VMEM((n * LANES, WIDE), F32),
        pltpu.VMEM((8, LANES), F32),
    ]
    if last:
        scratch.append(pltpu.VMEM((16, D), F32))
    return pl.pallas_call(
        functools.partial(expert_kernel, group, first, last, len(deps)),
        grid=(steps,),
        in_specs=in_specs,
        out_specs=[
                block(3 * O),
                block(LANES),
                block(n * H),
                block(n * H),
                whole((n * H, D)),
                whole((n * H, D)),
                whole((payload, LANES)),
                whole((payload, LANES)),
                whole(sums_shape),
        ]
        + [whole((4 * E, H))] * first,
        scratch_shapes=scratch,
        out_shape=[
            jax.ShapeDtypeStruct((rows, 3 * O), F32),
            jax.ShapeDtypeStruct((rows, LANES), F32),
            jax.ShapeDtypeStruct((rows, n * H), BF16),
            jax.ShapeDtypeStruct((rows, n * H), BF16),
            jax.ShapeDtypeStruct((n * H, D), BF16),
            jax.ShapeDtypeStruct((n * H, D), BF16),
            jax.ShapeDtypeStruct((payload, LANES), F32),
            jax.ShapeDtypeStruct((payload, LANES), F32),
            jax.ShapeDtypeStruct(sums_shape, F32),
        ]
        + [jax.ShapeDtypeStruct((4 * E, H), F32)] * first,
        input_output_aliases=aliases,
        compiler_params=params(EXPERT_MIB),
        cost_estimate=pl.CostEstimate(flops=n * rows * 6 * 720896, bytes_accessed=rows * 14000, transcendentals=0),
    )(*args)


def event_kernel(n, *refs):
    highs, lows, winh, winl = (refs[k * n : (k + 1) * n] for k in range(4))
    dlogits, gw_ref = refs[4 * n : 4 * n + 2]
    out, token, gw = refs[-3:]
    gw[...] = jnp.zeros_like(gw)
    gw[:GATE_COLS, :] = gw_ref[...]
    total = dot3(split(dlogits[...]), split(gw[...]), NN)
    for g in range(n):
        total = total + dot3((highs[g][...], lows[g][...]), (winh[g][...], winl[g][...]), NN)
    out[...] = total
    token[...] = jnp.zeros_like(token)


def event_grads(rows, highs, lows, winh, winl, dlogits, gate_w, deps):
    block = lambda width: pl.BlockSpec((ROW_BLOCK, width), lambda i: (i, 0))
    whole = lambda shape: pl.BlockSpec(shape, lambda i: (0, 0))
    return pl.pallas_call(
        functools.partial(event_kernel, len(highs)),
        grid=(rows // ROW_BLOCK,),
        in_specs=[block(v.shape[1]) for v in (*highs, *lows)]
        + [whole(v.shape) for v in (*winh, *winl)]
        + [block(LANES), whole((GATE_COLS, D))]
        + [pl.BlockSpec(memory_space=pl.ANY)] * len(deps),
        out_specs=[block(D), whole(TOKEN)],
        scratch_shapes=[pltpu.VMEM((LANES, D), F32)],
        out_shape=[jax.ShapeDtypeStruct((rows, D), F32), jax.ShapeDtypeStruct(TOKEN, F32)],
        compiler_params=params(EVENT_MIB),
        cost_estimate=pl.CostEstimate(flops=6 * rows * D * E * H, bytes_accessed=rows * 10000, transcendentals=0),
    )(*highs, *lows, *winh, *winl, dlogits, gate_w, *deps)


def place_kernel(own, other, *refs):
    out, token, sems = refs[-3:]
    rows = own.shape[0]
    side = lax.axis_index("tp") & 1
    copies = [
        pltpu.make_async_copy(v, out.at[pl.ds(pl.multiple_of(at * rows, ROW_BLOCK), rows), :], sems.at[k])
        for k, (v, at) in enumerate(((own, side), (other, 1 - side)))
    ]
    for copy in copies:
        copy.start()
    token[...] = jnp.zeros_like(token)
    for copy in copies:
        copy.wait()


def place(own, other, deps):
    rows, width = own.shape
    anywhere = pl.BlockSpec(memory_space=pl.ANY)
    return pl.pallas_call(
        place_kernel,
        in_specs=[anywhere] * (2 + len(deps)),
        out_specs=[pl.BlockSpec(memory_space=pltpu.HBM), pl.BlockSpec(memory_space=pltpu.VMEM)],
        scratch_shapes=[pltpu.SemaphoreType.DMA((2,))],
        out_shape=[jax.ShapeDtypeStruct((2 * rows, width), F32), jax.ShapeDtypeStruct(TOKEN, F32)],
        compiler_params=params(SMALL_MIB),
        cost_estimate=pl.CostEstimate(flops=0, bytes_accessed=rows * width * 16, transcendentals=0),
    )(own, other, *deps)


class Job:
    def __init__(self, args, shapes, body, scratch=()):
        self.args, self.body, self.scratch = args, body, list(scratch)
        self.shapes = [jax.ShapeDtypeStruct(shape, F32) for shape in shapes]


def copy_job(*arrays):
    def body(ins, outs, scratch):
        for a, b in zip(ins, outs):
            b[...] = a[...]

    return Job(arrays, [a.shape for a in arrays], body)


def run(jobs, deps=(), through=()):
    args = [a for job in jobs for a in job.args]
    shapes = [o for job in jobs for o in job.shapes]
    scratch = [v for job in jobs for v in job.scratch]

    def kernel(*refs):
        ins, refs = refs[: len(args)], refs[len(args) + len(through) + len(deps) :]
        outs, token, kept = refs[: len(shapes)], refs[len(shapes) + len(through)], refs[len(shapes) + len(through) + 1 :]
        token[...] = jnp.zeros_like(token)
        i = o = k = 0
        for job in jobs:
            ni, no, nk = len(job.args), len(job.shapes), len(job.scratch)
            job.body(ins[i : i + ni], outs[o : o + no], kept[k : k + nk])
            i, o, k = i + ni, o + no, k + nk

    vmem, anywhere = pl.BlockSpec(memory_space=pltpu.VMEM), pl.BlockSpec(memory_space=pl.ANY)
    flat = pl.pallas_call(
        kernel,
        in_specs=[vmem] * len(args) + [anywhere] * (len(through) + len(deps)),
        out_specs=[vmem] * len(shapes) + [anywhere] * len(through) + [vmem],
        out_shape=shapes
        + [jax.ShapeDtypeStruct(v.shape, v.dtype) for v in through]
        + [jax.ShapeDtypeStruct(TOKEN, F32)],
        scratch_shapes=scratch,
        input_output_aliases={len(args) + k: len(shapes) + k for k in range(len(through))},
        compiler_params=params(SMALL_MIB),
        cost_estimate=pl.CostEstimate(flops=0, bytes_accessed=sum(8 * a.size for a in args), transcendentals=0),
    )(*args, *through, *deps)
    result = []
    for job in jobs:
        result.append(list(flat[: len(job.shapes)]))
        flat = flat[len(job.shapes) :]
    return result, list(flat[:-1]), flat[-1]


def part_of(ref, index, rows):
    return ref.at[pl.ds(pl.multiple_of(index * rows, 8), rows), :]


class Reduction:
    def __init__(self, own, got, n_dp):
        self.own, self.got = own, got
        self.bits = n_dp.bit_length() - 1
        unit = 8 << (self.bits - 1)
        self.rows = -(-sum(v.shape[0] for v in own) // unit) * unit
        self.swap = [[(i, i ^ (1 << b)) for i in range(n_dp)] for b in range(self.bits)]
        self.stage = 0

    def over(self, values, bit):
        return [lax.ppermute(v, "dp", self.swap[bit]) for v in values]

    @property
    def finished(self):
        return self.stage == 2 * self.bits

    def job(self):
        stage, bits = self.stage, self.bits
        if stage == 0:
            args = [*self.own, *self.got]
            rows = self.rows
        elif stage <= bits:
            args = [self.keep, *self.got]
            rows = self.keep.shape[0]
        else:
            args = [self.keep, *self.got]
            rows = 2 * self.keep.shape[0]
        n = len(args) // 2
        gather = stage > bits
        bit = stage if stage < bits else 2 * bits - 1 - stage
        halving = stage < bits - 1

        def body(ins, outs, scratch):
            to = scratch[0] if halving else outs[0]
            if gather:
                side = (lax.axis_index("dp") >> bit) & 1
                part_of(to, side, rows // 2)[...] = ins[0][...]
                part_of(to, 1 - side, rows // 2)[...] = ins[1][...]
                return
            at = 0
            for a, b in zip(ins[:n], ins[n:]):
                to[at : at + a.shape[0], :] = a[...] + b[...]
                at += a.shape[0]
            if at < rows:
                to[at:, :] = jnp.zeros((rows - at, LANES), F32)
            if halving:
                side = (lax.axis_index("dp") >> bit) & 1
                outs[0][...] = part_of(to, side, rows // 2)[...]
                outs[1][...] = part_of(to, 1 - side, rows // 2)[...]

        if halving:
            return Job(args, [(rows // 2, LANES)] * 2, body, [pltpu.VMEM((rows, LANES), F32)])
        return Job(args, [(rows, LANES)], body)

    def take(self, outs):
        stage, bits = self.stage, self.bits
        self.keep = outs[0]
        bit = stage if stage < bits else 2 * bits - 2 - stage
        if bit >= 0:
            self.got = self.over([outs[-1]], bit)
        self.stage += 1


def finish_body(ins, outs, both):
    in_grad, in_bias, out_grad, out_bias, gain, shift, gate = outs
    odd = (lax.axis_index("tp") & 1) == 1
    side = lax.axis_index("dp") & 1
    whole = list(ins[:-2])
    half = ins[-1].shape[0]
    part_of(both[0], side, half)[...] = ins[-2][...]
    part_of(both[0], 1 - side, half)[...] = ins[-1][...]
    whole.append(both[0])
    for u, unit in enumerate(UNITS):
        at = 0
        for g in unit:
            group = GROUPS[g]
            for t in range(WIDE // LANES):
                for e in group:
                    tile = whole[u][at : at + SLICE, :]
                    at += SLICE
                    if t < D // LANES:
                        in_grad[e, :, t * LANES : (t + 1) * LANES] = tile
                    else:
                        out_grad[e, :, t * LANES - D : (t + 1) * LANES - D] = tile
    sums = whole[-1][at : at + 8 * len(GROUPS), :]
    sums = jnp.where(odd, sums[:, SLICE:], sums[:, :SLICE])
    for g, group in enumerate(GROUPS):
        for i, e in enumerate(group):
            for k, ref in enumerate((in_bias, out_bias, gain, shift)):
                ref[e : e + 1, :] = sums[8 * g + 4 * i + k : 8 * g + 4 * i + k + 1, :]
    for t in range(D // LANES):
        gate[:, t * LANES : (t + 1) * LANES] = whole[-1][at + 64 + 16 * t : at + 64 + 16 * t + GATE_COLS, :]


def per_device(
    events,
    valid_counts,
    mix_cotangent,
    expert_in,
    expert_in_bias,
    expert_out,
    expert_out_bias,
    norm_gain,
    norm_shift,
    gate_weight,
):
    n_dp = lax.axis_size("dp")
    rows = events.shape[0] // 2
    w_in = jnp.swapaxes(expert_in, 1, 2)
    w_out = jnp.swapaxes(expert_out, 1, 2)
    gate_w = jnp.swapaxes(gate_weight, 0, 1)
    core = [(i, i ^ 1) for i in range(4)]
    across = [(i, i ^ 2) for i in range(4)]
    vectors = [expert_in_bias, expert_out_bias, norm_gain, norm_shift]
    own = list(payload(GROUPS[:1], w_in, w_out, vectors, []))
    far = [lax.ppermute(own[0], "tp", across)]
    beside = [lax.ppermute(own[0], "tp", core)]
    own += payload(GROUPS[1:], w_in, w_out, [], own)
    high, low, p, cot = gates(valid_counts, events, mix_cotangent, gate_w, rows, own[1:2])
    relayed = []
    summing = []
    partial = []

    def between(deps, through=(), sent=()):
        for unit in UNITS[len(summing) :]:
            if unit[-1] < len(partial):
                both = [partial[g] for g in unit]
                summing.append(Reduction([v for b in both for v in b[0]], [v for b in both for v in b[1]], n_dp))
        active = [r for r in summing if not r.finished]
        jobs = [r.job() for r in active] + [copy_job(*sent)]
        fetched = len(relayed)
        fetching = fetched < len(far)
        if fetching:
            jobs.append(copy_job(far[fetched], *own[fetched + 1 : fetched + 2]))
        outs, through, token = run(jobs, deps, through)
        if fetching:
            relayed.append(lax.ppermute(outs[-1][0], "tp", core))
            if len(outs[-1]) > 1:
                far.append(lax.ppermute(outs[-1][1], "tp", across))
                beside.append(lax.ppermute(outs[-1][1], "tp", core))
        for r, o in zip(active, outs):
            r.take(o)
        return [token], through, [lax.ppermute(v, "tp", core) for v in outs[len(active)]]

    deps, _, _ = between([p])
    mix = small = None
    dps, sums, highs, lows, winh, winl = [], [], [], [], [], []
    for g, group in enumerate(GROUPS):
        last = g == len(GROUPS) - 1
        shards = (own[g], beside[g], far[g], relayed[g])
        mix, dp, h, l, wh, wl, mine, part, s, *made = experts(
            group, rows, high, low, cot, p, shards, small, mix, (dps, sums) if last else None, deps
        )
        small = made[0] if made else small
        for held, v in zip((dps, sums, highs, lows, winh, winl), (dp, s, h, l, wh, wl)):
            held.append(v)
        extra = [s] if last else []
        deps, _, got = between([s], sent=[part, *extra])
        partial.append(([mine, *extra], got))
    deps, (mix,), _ = between(deps, [mix])
    other_mix = lax.ppermute(mix, "tp", core)
    x_grad, token = event_grads(rows, highs, lows, winh, winl, dps[-1], gate_w, deps)
    deps, (x_grad,), _ = between([token], [x_grad])
    other_grad = lax.ppermute(x_grad, "tp", core)
    mixtures, token = place(mix, other_mix, deps)
    deps, _, _ = between([token])
    x_grad, token = place(x_grad, other_grad, deps)
    deps = [token]
    while summing[-1].stage < 2 * summing[-1].bits - 1:
        deps, _, _ = between(deps)
    halves = [r.keep for r in summing] + summing[-1].got
    per_expert = (E, SLICE)
    shapes = [(E, SLICE, D), per_expert, (E, SLICE, H), per_expert, per_expert, per_expert, (GATE_COLS, D)]
    scratch = [pltpu.VMEM((summing[-1].rows, LANES), F32)]
    job = Job(halves, shapes, finish_body, scratch)
    (((in_grad, in_bias, out_grad, out_bias, gain, shift, gate),), _, _) = run([job], deps)
    return (
        mixtures,
        x_grad,
        jnp.swapaxes(in_grad, 1, 2),
        in_bias,
        jnp.swapaxes(out_grad, 1, 2),
        out_bias,
        gain,
        shift,
        jnp.swapaxes(gate, 0, 1),
    )


def solution(mesh):
    return jax.shard_map(
        per_device,
        mesh=mesh,
        in_specs=(
            P("dp", None),
            P(),
            P("dp", None),
            P(None, None, "tp"),
            P(None, "tp"),
            P(None, None, "tp"),
            P(None, "tp"),
            P(None, "tp"),
            P(None, "tp"),
            P(),
        ),
        out_specs=(
            P("dp", None),
            P("dp", None),
            P(None, None, "tp"),
            P(None, "tp"),
            P(None, None, "tp"),
            P(None, "tp"),
            P(None, "tp"),
            P(None, "tp"),
            P(),
        ),
        check_vma=False,
    )
```

time: 171 us -> 112 us (0.65)
  Pallas kernels: 111 us -> 52.8 us
  waiting for transfers between devices: 15.2 us -> 22.7 us
  local copies, waits for them, and re-layouts: 13 us -> 6.45 us
  other arithmetic: 1.97 us -> 0 us
    pallas_call x19 -> x17, Pallas kernels: 68.2 us -> 25 us  [the longest x1 7.56 us: gates(): pl.pallas_call(functools.partial(gate_kernel, len(deps)), in_specs=[pl.Bl...]
    pallas_call x3 -> x4, Pallas kernels: 42.6 us -> 27.9 us  [experts(): pl.pallas_call(functools.partial(expert_kernel, group, first, last, len(d...]
    unnamed x66 -> x26, local copies, waits for them, and re-layouts: 11.7 us -> 6.45 us
    ppermute x13, waiting for transfers between devices: 0.03 us -> 3.18 us  [the longest x3 2.13 us: between(): far.append(lax.ppermute(outs[-1][1], 'tp', across))]
    ppermute x15, waiting for transfers between devices: 15.2 us -> 18.3 us  [over(): return [lax.ppermute(v, 'dp', self.swap[bit]) for v in values]]
    ppermute x15, starting transfers between devices: 18 us -> 20.7 us  [over(): return [lax.ppermute(v, 'dp', self.swap[bit]) for v in values]]
    ppermute x13, starting transfers between devices: 5.82 us -> 3.42 us  [the longest x3 2.1 us: between(): far.append(lax.ppermute(outs[-1][1], 'tp', across))]
  transfers between devices with their start and end apart: 33 -> 34, of which waited for: 4 -> 12; matrix products, arithmetic and copies ran while one was open for 2% -> 0% of each run, Pallas kernels for 58% -> 44%
where the time goes in v3:
time: 112 us
  Pallas kernels  52.8 us (47%)
  starting transfers between devices  28.6 us (26%)
  waiting for transfers between devices  22.7 us (20%)
  local copies, waits for them, and re-layouts  6.45 us (6%)
    pallas_call x4, Pallas kernels, experts(): pl.pallas_call(functools.partial(expert_kernel, group, first, last, len(d...  27.9 us
    ppermute x15, starting transfers between devices, over(): return [lax.ppermute(v, 'dp', self.swap[bit]) for v in values]  20.7 us
    ppermute x15, waiting for transfers between devices, over(): return [lax.ppermute(v, 'dp', self.swap[bit]) for v in values]  18.3 us
    pallas_call x1, Pallas kernels, gates(): pl.pallas_call(functools.partial(gate_kernel, len(deps)), in_specs=[pl.Bl...  7.56 us
    unnamed x26, local copies, waits for them, and re-layouts  6.45 us
    pallas_call x1, Pallas kernels, event_grads(): pl.pallas_call(functools.partial(event_kernel, len(highs)), grid=(rows //...  6.29 us
    pallas_call x2, Pallas kernels, place(): pl.pallas_call(place_kernel, in_specs=[anywhere] * (2 + len(deps)), out_s...  4.74 us
    pallas_call x2, Pallas kernels, payload(): pl.pallas_call(functools.partial(payload_kernel, groups, bool(vectors), l...  4.49 us
  transfers between devices with their start and end apart: 34, of which 12 were waited for; matrix products, arithmetic and copies ran while one was open for 0% of the time, Pallas kernels for 44%

profile of v3, /device:TPU:0, one launch (start us, length us, event | category | flops | bytes accessed | tf_op | source)
XLA Modules:
  0.0 111.5 jit_solution(6817913670339132359)
XLA Ops:
  0.6 2.3 %shard_map.169.refs_0_.refs_4_ = f32[1,72,768]{2,1,0:T(8,128)} custom-call(f32[6,64,512]{2,1,0:T(8,128)} %bitcast.8, f32[6,64,256]{2,1,0:T(8,128)} %bitcast.10, f32[6,64]{1,0:T(8,128)} %refs_0_.1, f32[6,64]{1,0:T(8,128)} %refs_1_.1, f32[6,64]{1,0:T(8,128)} %refs_2_.1, f32[6,64]{1,0:T(8,128)} %refs_3_.1), custom_call_target="tpu_custom_call" | custom-call | bytes 786432 | tf_op jit(solution)/shard_map/pallas_call | solution.py:147
  3.0 3.0 %collective-permute-start.1 = (f32[1,72,768]{2,1,0:T(8,128)}, f32[1,72,768]{2,1,0:T(8,128)S(1)}, u32[]{:S(2)}, u32[]{:S(2)}) collective-permute-start(f32[1,72,768]{2,1,0:T(8,128)} %shard_map.169.refs_0_.refs_4_), channel_id=1, source_target_pairs={{0,2},{1,3},{2,0},{3,1},{4,6},{5,7},{6,4},{7,5},{8,10},{9,11},{10,... | collective-permute-start | bytes 663560 | tf_op jit(solution)/shard_map/ppermute | solution.py:640
  6.0 2.1 %shard_map.170 = (f32[2,64,768]{2,1,0:T(8,128)}, f32[2,64,768]{2,1,0:T(8,128)}, f32[1,64,768]{2,1,0:T(8,128)}) custom-call(f32[6,64,512]{2,1,0:T(8,128)} %bitcast.9, f32[6,64,256]{2,1,0:T(8,128)} %bitcast.11, f32[1,72,768]{2,1,0:T(8,128)} %shard_map.169.refs_0_.refs_4_), custom_call_target="tpu_custom_call" | custom-call | bytes 786432 | tf_op jit(solution)/shard_map/pallas_call | solution.py:147
  8.2 7.6 %shard_map.171 = (bf16[1024,512]{1,0:T(8,128)(2,1)}, bf16[1024,512]{1,0:T(8,128)(2,1)}, f32[1024,128]{1,0:T(8,128)}, f32[1024,768]{1,0:T(8,128)}) custom-call(s32[8]{0:T(128)} %counts.1, f32[2048,512]{1,0:T(8,128)} %ev_ref.1, f32[2048,768]{1,0:T(8,128)} %cot_ref.1, f32[14,512]{1,0:T(8,128)} %bitcast.6, f32[2,64,768]{2,1,0:T(8,128)} %get-tuple-element.113.refs_0_.refs_1_.refs_4_), custom_call_target="tpu_custom_call" | custom-call | flops 402653184 | bytes 4194304 | tf_op jit(solution)/shard_map/pallas_call | solution.py:102
  19.6 1.9 %copy-done.8 = f32[1024,768]{1,0:T(8,128)S(1)} copy-done((f32[1024,768]{1,0:T(8,128)S(1)}, f32[1024,768]{1,0:T(8,128)}, u32[]{:S(2)}) %copy-start.8) | copy-done | bytes 3145752
  21.5 1.2 %copy-done.10 = bf16[1024,512]{1,0:T(8,128)(2,1)S(1)} copy-done((bf16[1024,512]{1,0:T(8,128)(2,1)S(1)}, bf16[1024,512]{1,0:T(8,128)(2,1)}, u32[]{:S(2)}) %copy-start.10) | copy-done | bytes 1048600
  22.7 1.2 %copy-done.12 = bf16[1024,512]{1,0:T(8,128)(2,1)S(1)} copy-done((bf16[1024,512]{1,0:T(8,128)(2,1)S(1)}, bf16[1024,512]{1,0:T(8,128)(2,1)}, u32[]{:S(2)}) %copy-start.12) | copy-done | bytes 1048600
  24.0 4.9 %shard_map.173 = (f32[1024,768]{1,0:T(8,128)S(1)}, f32[1024,128]{1,0:T(8,128)S(1)}, bf16[1024,256]{1,0:T(8,128)(2,1)S(1)}, bf16[1024,256]{1,0:T(8,128)(2,1)S(1)}...) custom-call(bf16[1024,512]{1,0:T(8,128)(2,1)S(1)} %copy-done.10, ...), custom_call_target="tpu_custom_call" | custom-call | flops 4429185024 | bytes 14336000 | tf_op jit(solution)/shard_map/pallas_call | solution.py:377
  30.8 8.0 %shard_map.175 = (f32[1024,768]{1,0:T(8,128)S(1)}, f32[1024,128]{1,0:T(8,128)S(1)}, bf16[1024,512]{1,0:T(8,128)(2,1)S(1)}, bf16[1024,512]{1,0:T(8,128)(2,1)S(1)}...) custom-call(bf16[1024,512]{1,0:T(8,128)(2,1)S(1)} %copy-done.11, ...), custom_call_target="tpu_custom_call", output_to_operand_aliasing={{0}: (9, {})} | custom-call | flops 8858370048 | bytes 14336000 | tf_op jit(solution)/shard_map/pallas_call | solution.py:377
  38.8 2.1 %collective-permute-done.7.refs_1_.refs_6_ = f32[2,64,768]{2,1,0:T(8,128)S(1)} collective-permute-done((f32[2,64,768]{2,1,0:T(8,128)S(1)}, f32[2,64,768]{2,1,0:T(8,128)S(1)}, u32[]{:S(2)}, u32[]{:S(2)}) %collective-permute-start.7) | collective-permute-done | bytes 393248 | tf_op jit(solution)/shard_map/ppermute | solution.py:663
  41.7 1.0 collective-permute-start.11
  42.9 8.2 %shard_map.177 = (f32[1024,768]{1,0:T(8,128)S(1)}, f32[1024,128]{1,0:T(8,128)S(1)}, bf16[1024,512]{1,0:T(8,128)(2,1)S(1)}, bf16[1024,512]{1,0:T(8,128)(2,1)S(1)}...) custom-call(bf16[1024,512]{1,0:T(8,128)(2,1)S(1)} %copy-done.11, ...), custom_call_target="tpu_custom_call", output_to_operand_aliasing={{0}: (9, {})} | custom-call | flops 8858370048 | bytes 14336000 | tf_op jit(solution)/shard_map/pallas_call | solution.py:377
  51.7 1.5 %collective-permute-start.12 = (f32[576,128]{1,0:T(8,128)S(1)}, f32[576,128]{1,0:T(8,128)S(1)}, u32[]{:S(2)}, u32[]{:S(2)}) collective-permute-start(f32[576,128]{1,0:T(8,128)S(1)} %get-tuple-element.143), channel_id=1, source_target_pairs={{0,4},{4,0},{8,12},{12,8},{16,20},{20,16},{24,28},{28,24},{1,5},{5... | collective-permute-start | bytes 884744 | tf_op jit(solution)/shard_map/ppermute | solution.py:535
  53.2 6.7 %shard_map.179 = (f32[1024,768]{1,0:T(8,128)S(1)}, f32[1024,128]{1,0:T(8,128)S(1)}, bf16[1024,256]{1,0:T(8,128)(2,1)S(1)}, bf16[1024,256]{1,0:T(8,128)(2,1)S(1)}...) custom-call(bf16[1024,512]{1,0:T(8,128)(2,1)S(1)} %copy-done.11, ...), custom_call_target="tpu_custom_call", output_to_operand_aliasing={{0}: (9, {})} | custom-call | flops 4429185024 | bytes 14336000 | tf_op jit(solution)/shard_map/pallas_call | solution.py:377
  60.9 1.6 %collective-permute-start.17 = (f32[384,128]{1,0:T(8,128)S(1)}, f32[384,128]{1,0:T(8,128)S(1)}, u32[]{:S(2)}, u32[]{:S(2)}) collective-permute-start(f32[384,128]{1,0:T(8,128)S(1)} %get-tuple-element.157), channel_id=1, source_target_pairs={{0,4},{4,0},{8,12},{12,8},{16,20},{20,16},{24,28},{28,24},{1,5},{5... | collective-permute-start | bytes 589832 | tf_op jit(solution)/shard_map/ppermute | solution.py:535
  62.5 1.6 %collective-permute-start.16 = (f32[288,128]{1,0:T(8,128)S(1)}, f32[288,128]{1,0:T(8,128)S(1)}, u32[]{:S(2)}, u32[]{:S(2)}) collective-permute-start(f32[288,128]{1,0:T(8,128)S(1)} %get-tuple-element.155), channel_id=1, source_target_pairs={{0,8},{4,12},{8,0},{12,4},{16,24},{20,28},{24,16},{28,20},{1,9},{5... | collective-permute-start | bytes 442376 | tf_op jit(solution)/shard_map/ppermute | solution.py:535
  65.3 3.5 %collective-permute-done.16.refs_1_ = f32[288,128]{1,0:T(8,128)S(1)} collective-permute-done((f32[288,128]{1,0:T(8,128)S(1)}, f32[288,128]{1,0:T(8,128)S(1)}, u32[]{:S(2)}, u32[]{:S(2)}) %collective-permute-start.16) | collective-permute-done | bytes 147488 | tf_op jit(solution)/shard_map/ppermute | solution.py:535
  68.9 1.6 %collective-permute-start.22 = (f32[192,128]{1,0:T(8,128)S(1)}, f32[192,128]{1,0:T(8,128)S(1)}, u32[]{:S(2)}, u32[]{:S(2)}) collective-permute-start(f32[192,128]{1,0:T(8,128)S(1)} %get-tuple-element.166), channel_id=1, source_target_pairs={{0,8},{4,12},{8,0},{12,4},{16,24},{20,28},{24,16},{28,20},{1,9},{5... | collective-permute-start | bytes 294920 | tf_op jit(solution)/shard_map/ppermute | solution.py:535
  71.1 2.6 %collective-permute-start.21 = (f32[288,128]{1,0:T(8,128)S(1)}, f32[288,128]{1,0:T(8,128)S(1)}, u32[]{:S(2)}, u32[]{:S(2)}) collective-permute-start(f32[288,128]{1,0:T(8,128)S(1)} %get-tuple-element.164.refs_0_), channel_id=1, source_target_pairs={{0,16},{4,20},{8,24},{12,28},{16,0},{20,4},{24,8},{28,12},{1,17},{... | collective-permute-start | bytes 442376 | tf_op jit(solution)/shard_map/ppermute | solution.py:535
  73.7 6.3 %shard_map.182 = (f32[1024,512]{1,0:T(8,128)S(1)}, f32[8,128]{1,0:T(8,128)S(1)}) custom-call(bf16[1024,256]{1,0:T(8,128)(2,1)S(1)} %get-tuple-element.169.refs_0_, bf16[1024,512]{1,0:T(8,128)(2,1)S(1)} %get-tuple-element.170.refs_1_, bf16[1024,512]{1,0:T(8,128)(2,1)S(1)} %get-tuple-element.171.refs_2_, bf16[1024,256]{1,0:T(8,128)(2,1)S(1)} %get-tuple-element.172.refs_3_, ...), custom_call_target="tpu_custom_call" | custom-call | flops 4831838208 | bytes 10240000 | tf_op jit(solution)/shard_map/pallas_call | solution.py:428
  81.0 3.1 %collective-permute-start.26 = (f32[192,128]{1,0:T(8,128)S(1)}, f32[192,128]{1,0:T(8,128)S(1)}, u32[]{:S(2)}, u32[]{:S(2)}) collective-permute-start(f32[192,128]{1,0:T(8,128)S(1)} %get-tuple-element.193.refs_2_), channel_id=1, source_target_pairs={{0,16},{4,20},{8,24},{12,28},{16,0},{20,4},{24,8},{28,12},{1,17},{... | collective-permute-start | bytes 294920 | tf_op jit(solution)/shard_map/ppermute | solution.py:535
  84.2 2.7 %shard_map.184 = (f32[2048,768]{1,0:T(8,128)}, f32[8,128]{1,0:T(8,128)S(1)}) custom-call(f32[1024,768]{1,0:T(8,128)S(1)} %get-tuple-element.163.own, f32[1024,768]{1,0:T(8,128)S(1)} %collective-permute-done.20.other, f32[8,128]{1,0:T(8,128)S(1)} %get-tuple-element.189.refs_0_), custom_call_target="tpu_custom_call" | custom-call | bytes 12582912 | tf_op jit(solution)/shard_map/pallas_call | solution.py:461
  86.9 3.8 %collective-permute-done.27.refs_5_ = f32[128,128]{1,0:T(8,128)S(1)} collective-permute-done((f32[128,128]{1,0:T(8,128)S(1)}, f32[128,128]{1,0:T(8,128)S(1)}, u32[]{:S(2)}, u32[]{:S(2)}) %collective-permute-start.27) | collective-permute-done | bytes 65568 | tf_op jit(solution)/shard_map/ppermute | solution.py:535
  90.8 1.5 %collective-permute-start.28 = (f32[576,128]{1,0:T(8,128)S(1)}, f32[576,128]{1,0:T(8,128)S(1)}, u32[]{:S(2)}, u32[]{:S(2)}) collective-permute-start(f32[576,128]{1,0:T(8,128)S(1)} %get-tuple-element.199.refs_0_), channel_id=1, source_target_pairs={{0,4},{4,0},{8,12},{12,8},{16,20},{20,16},{24,28},{28,24},{1,5},{5... | collective-permute-start | bytes 884744 | tf_op jit(solution)/shard_map/ppermute | solution.py:535
  92.6 2.8 %collective-permute-start.30 = (f32[128,128]{1,0:T(8,128)S(1)}, f32[128,128]{1,0:T(8,128)S(1)}, u32[]{:S(2)}, u32[]{:S(2)}) collective-permute-start(f32[128,128]{1,0:T(8,128)S(1)} %get-tuple-element.201.refs_4_), channel_id=1, source_target_pairs={{0,16},{4,20},{8,24},{12,28},{16,0},{20,4},{24,8},{28,12},{1,17},{... | collective-permute-start | bytes 196616 | tf_op jit(solution)/shard_map/ppermute | solution.py:535
  95.4 2.0 %shard_map.186 = (f32[2048,512]{1,0:T(8,128)}, f32[8,128]{1,0:T(8,128)S(1)}) custom-call(f32[1024,512]{1,0:T(8,128)S(1)} %get-tuple-element.191.own, f32[1024,512]{1,0:T(8,128)S(1)} %collective-permute-done.24.other, f32[8,128]{1,0:T(8,128)S(1)} %get-tuple-element.197.refs_0_), custom_call_target="tpu_custom_call" | custom-call | bytes 8388608 | tf_op jit(solution)/shard_map/pallas_call | solution.py:461
  98.0 1.4 %collective-permute-done.28.refs_1_ = f32[576,128]{1,0:T(8,128)S(1)} collective-permute-done((f32[576,128]{1,0:T(8,128)S(1)}, f32[576,128]{1,0:T(8,128)S(1)}, u32[]{:S(2)}, u32[]{:S(2)}) %collective-permute-start.28) | collective-permute-done | bytes 294944 | tf_op jit(solution)/shard_map/ppermute | solution.py:535
  99.5 1.5 %collective-permute-start.31 = (f32[384,128]{1,0:T(8,128)S(1)}, f32[384,128]{1,0:T(8,128)S(1)}, u32[]{:S(2)}, u32[]{:S(2)}) collective-permute-start(f32[384,128]{1,0:T(8,128)S(1)} %get-tuple-element.204.refs_0_), channel_id=1, source_target_pairs={{0,4},{4,0},{8,12},{12,8},{16,20},{20,16},{24,28},{28,24},{1,5},{5... | collective-permute-start | bytes 589832 | tf_op jit(solution)/shard_map/ppermute | solution.py:535
  101.5 3.8 %collective-permute-done.32.refs_3_ = f32[128,128]{1,0:T(8,128)S(1)} collective-permute-done((f32[128,128]{1,0:T(8,128)S(1)}, f32[128,128]{1,0:T(8,128)S(1)}, u32[]{:S(2)}, u32[]{:S(2)}) %collective-permute-start.32) | collective-permute-done | bytes 65568 | tf_op jit(solution)/shard_map/ppermute | solution.py:535
  105.4 1.5 %collective-permute-start.33 = (f32[256,128]{1,0:T(8,128)S(1)}, f32[256,128]{1,0:T(8,128)S(1)}, u32[]{:S(2)}, u32[]{:S(2)}) collective-permute-start(f32[256,128]{1,0:T(8,128)S(1)} %get-tuple-element.208.refs_2_), channel_id=1, source_target_pairs={{0,4},{4,0},{8,12},{12,8},{16,20},{20,16},{24,28},{28,24},{1,5},{5... | collective-permute-start | bytes 393224 | tf_op jit(solution)/shard_map/ppermute | solution.py:535
  106.8 3.6 %collective-permute-done.33.refs_3_ = f32[256,128]{1,0:T(8,128)S(1)} collective-permute-done((f32[256,128]{1,0:T(8,128)S(1)}, f32[256,128]{1,0:T(8,128)S(1)}, u32[]{:S(2)}, u32[]{:S(2)}) %collective-permute-start.33) | collective-permute-done | bytes 131104 | tf_op jit(solution)/shard_map/ppermute | solution.py:535
  110.4 1.1 %shard_map.189 = (f32[6,64,512]{2,1,0:T(8,128)}, f32[6,64]{1,0:T(8,128)}, f32[6,64,256]{2,1,0:T(8,128)}, f32[6,64]{1,0:T(8,128)}, f32[6,64]{1,0:T(8,128)}, /*ind...) custom-call(f32[1152,128]{1,0:T(8,128)S(1)} %get-tuple-element.203.refs_0_, ...), custom_call_target="tpu_custom_call" | custom-call | bytes 2490368 | tf_op jit(solution)/shard_map/pallas_call | solution.py:502
  (83 shorter events, 12.8 us)
Async XLA Ops:
  3.0 12.8 %collective-permute-start.1 = (f32[1,72,768]{2,1,0:T(8,128)}, f32[1,72,768]{2,1,0:T(8,128)S(1)}, u32[]{:S(2)}, u32[]{:S(2)}) collective-permute-start(f32[1,72,768]{2,1,0:T(8,128)} %shard_map.169.refs_0_.refs_4_), channel_id=1, source_target_pairs={{0,2},{1,3},{2,0},{3,1},{4,6},{5,7},{6,4},{7,5},{8,10},{9,11},{10,... | collective-permute-start | bytes 663560 | tf_op jit(solution)/shard_map/ppermute | solution.py:640
  6.0 11.6 %collective-permute-start = (f32[1,72,768]{2,1,0:T(8,128)}, f32[1,72,768]{2,1,0:T(8,128)S(1)}, u32[]{:S(2)}, u32[]{:S(2)}) collective-permute-start(f32[1,72,768]{2,1,0:T(8,128)} %shard_map.169.refs_0_.refs_4_), channel_id=1, source_target_pairs={{0,1},{1,0},{2,3},{3,2},{4,5},{5,4},{6,7},{7,6},{8,9},{9,8},{10,11... | collective-permute-start | bytes 663560 | tf_op jit(solution)/shard_map/ppermute | solution.py:641
  17.5 11.4 %collective-permute-start.4 = (f32[2,64,768]{2,1,0:T(8,128)S(1)}, f32[2,64,768]{2,1,0:T(8,128)S(1)}, u32[]{:S(2)}, u32[]{:S(2)}) collective-permute-start(f32[2,64,768]{2,1,0:T(8,128)S(1)} %get-tuple-element.121), channel_id=1, source_target_pairs={{0,2},{1,3},{2,0},{3,1},{4,6},{5,7},{6,4},{7,5},{8,10},{9,11},{10,... | collective-permute-start | bytes 1179656 | tf_op jit(solution)/shard_map/ppermute | solution.py:663
  17.5 13.0 %collective-permute-start.3 = (f32[2,64,768]{2,1,0:T(8,128)S(1)}, f32[2,64,768]{2,1,0:T(8,128)S(1)}, u32[]{:S(2)}, u32[]{:S(2)}) collective-permute-start(f32[2,64,768]{2,1,0:T(8,128)S(1)} %get-tuple-element.121), channel_id=1, source_target_pairs={{0,1},{1,0},{2,3},{3,2},{4,5},{5,4},{6,7},{7,6},{8,9},{9,8},{10,11... | collective-permute-start | bytes 1179656 | tf_op jit(solution)/shard_map/ppermute | solution.py:664
  29.0 1.8 %collective-permute-start.5 = (f32[2,64,768]{2,1,0:T(8,128)S(1)}, f32[2,64,768]{2,1,0:T(8,128)S(1)}, u32[]{:S(2)}, u32[]{:S(2)}) collective-permute-start(f32[2,64,768]{2,1,0:T(8,128)S(1)} %get-tuple-element.125), channel_id=1, source_target_pairs={{0,1},{1,0},{2,3},{3,2},{4,5},{5,4},{6,7},{7,6},{8,9},{9,8},{10,11... | collective-permute-start | bytes 1179656 | tf_op jit(solution)/shard_map/ppermute | solution.py:661
  29.4 13.3 %collective-permute-start.9 = (f32[2,64,768]{2,1,0:T(8,128)S(1)}, f32[2,64,768]{2,1,0:T(8,128)S(1)}, u32[]{:S(2)}, u32[]{:S(2)}) collective-permute-start(f32[2,64,768]{2,1,0:T(8,128)S(1)} %get-tuple-element.132), channel_id=1, source_target_pairs={{0,1},{1,0},{2,3},{3,2},{4,5},{5,4},{6,7},{7,6},{8,9},{9,8},{10,11... | collective-permute-start | bytes 1179656 | tf_op jit(solution)/shard_map/ppermute | solution.py:664
  29.5 11.4 %collective-permute-start.7 = (f32[2,64,768]{2,1,0:T(8,128)S(1)}, f32[2,64,768]{2,1,0:T(8,128)S(1)}, u32[]{:S(2)}, u32[]{:S(2)}) collective-permute-start(f32[2,64,768]{2,1,0:T(8,128)S(1)} %get-tuple-element.132), channel_id=1, source_target_pairs={{0,2},{1,3},{2,0},{3,1},{4,6},{5,7},{6,4},{7,5},{8,10},{9,11},{10,... | collective-permute-start | bytes 1179656 | tf_op jit(solution)/shard_map/ppermute | solution.py:663
  41.0 1.9 %collective-permute-start.10 = (f32[2,64,768]{2,1,0:T(8,128)S(1)}, f32[2,64,768]{2,1,0:T(8,128)S(1)}, u32[]{:S(2)}, u32[]{:S(2)}) collective-permute-start(f32[2,64,768]{2,1,0:T(8,128)S(1)} %get-tuple-element.136), channel_id=1, source_target_pairs={{0,1},{1,0},{2,3},{3,2},{4,5},{5,4},{6,7},{7,6},{8,9},{9,8},{10,11... | collective-permute-start | bytes 1179656 | tf_op jit(solution)/shard_map/ppermute | solution.py:661
  41.1 10.0 %collective-permute-start.6 = (f32[384,128]{1,0:T(8,128)S(1)}, f32[384,128]{1,0:T(8,128)S(1)}, u32[]{:S(2)}, u32[]{:S(2)}) collective-permute-start(f32[384,128]{1,0:T(8,128)S(1)} %get-tuple-element.130), channel_id=1, source_target_pairs={{0,1},{1,0},{2,3},{3,2},{4,5},{5,4},{6,7},{7,6},{8,9},{9,8},{10,11... | collective-permute-start | bytes 589832 | tf_op jit(solution)/shard_map/ppermute | solution.py:667
  41.6 11.6 %collective-permute-start.14 = (f32[1,64,768]{2,1,0:T(8,128)S(1)}, f32[1,64,768]{2,1,0:T(8,128)S(1)}, u32[]{:S(2)}, u32[]{:S(2)}) collective-permute-start(f32[1,64,768]{2,1,0:T(8,128)S(1)} %get-tuple-element.140), channel_id=1, source_target_pairs={{0,1},{1,0},{2,3},{3,2},{4,5},{5,4},{6,7},{7,6},{8,9},{9,8},{10,11... | collective-permute-start | bytes 589832 | tf_op jit(solution)/shard_map/ppermute | solution.py:664
  41.7 9.5 %collective-permute-start.11 = (f32[1,64,768]{2,1,0:T(8,128)S(1)}, f32[1,64,768]{2,1,0:T(8,128)S(1)}, u32[]{:S(2)}, u32[]{:S(2)}) collective-permute-start(f32[1,64,768]{2,1,0:T(8,128)S(1)} %get-tuple-element.140), channel_id=1, source_target_pairs={{0,2},{1,3},{2,0},{3,1},{4,6},{5,7},{6,4},{7,5},{8,10},{9,11},{10,... | collective-permute-start | bytes 589832 | tf_op jit(solution)/shard_map/ppermute | solution.py:663
  42.7 8.4 %collective-permute-start.8 = (f32[768,128]{1,0:T(8,128)S(1)}, f32[768,128]{1,0:T(8,128)S(1)}, u32[]{:S(2)}, u32[]{:S(2)}) collective-permute-start(f32[768,128]{1,0:T(8,128)S(1)} %get-tuple-element.135), channel_id=1, source_target_pairs={{0,1},{1,0},{2,3},{3,2},{4,5},{5,4},{6,7},{7,6},{8,9},{9,8},{10,11... | collective-permute-start | bytes 1179656 | tf_op jit(solution)/shard_map/ppermute | solution.py:667
  51.3 1.9 %collective-permute-start.15 = (f32[1,64,768]{2,1,0:T(8,128)S(1)}, f32[1,64,768]{2,1,0:T(8,128)S(1)}, u32[]{:S(2)}, u32[]{:S(2)}) collective-permute-start(f32[1,64,768]{2,1,0:T(8,128)S(1)} %get-tuple-element.146), channel_id=1, source_target_pairs={{0,1},{1,0},{2,3},{3,2},{4,5},{5,4},{6,7},{7,6},{8,9},{9,8},{10,11... | collective-permute-start | bytes 589832 | tf_op jit(solution)/shard_map/ppermute | solution.py:661
  51.7 9.1 %collective-permute-start.12 = (f32[576,128]{1,0:T(8,128)S(1)}, f32[576,128]{1,0:T(8,128)S(1)}, u32[]{:S(2)}, u32[]{:S(2)}) collective-permute-start(f32[576,128]{1,0:T(8,128)S(1)} %get-tuple-element.143), channel_id=1, source_target_pairs={{0,4},{4,0},{8,12},{12,8},{16,20},{20,16},{24,28},{28,24},{1,5},{5... | collective-permute-start | bytes 884744 | tf_op jit(solution)/shard_map/ppermute | solution.py:535
  53.2 7.6 %collective-permute-start.13 = (f32[768,128]{1,0:T(8,128)S(1)}, f32[768,128]{1,0:T(8,128)S(1)}, u32[]{:S(2)}, u32[]{:S(2)}) collective-permute-start(f32[768,128]{1,0:T(8,128)S(1)} %get-tuple-element.145), channel_id=1, source_target_pairs={{0,1},{1,0},{2,3},{3,2},{4,5},{5,4},{6,7},{7,6},{8,9},{9,8},{10,11... | collective-permute-start | bytes 1179656 | tf_op jit(solution)/shard_map/ppermute | solution.py:667
  60.9 7.8 %collective-permute-start.17 = (f32[384,128]{1,0:T(8,128)S(1)}, f32[384,128]{1,0:T(8,128)S(1)}, u32[]{:S(2)}, u32[]{:S(2)}) collective-permute-start(f32[384,128]{1,0:T(8,128)S(1)} %get-tuple-element.157), channel_id=1, source_target_pairs={{0,4},{4,0},{8,12},{12,8},{16,20},{20,16},{24,28},{28,24},{1,5},{5... | collective-permute-start | bytes 589832 | tf_op jit(solution)/shard_map/ppermute | solution.py:535
  62.5 6.3 %collective-permute-start.18 = (f32[384,128]{1,0:T(8,128)S(1)}, f32[384,128]{1,0:T(8,128)S(1)}, u32[]{:S(2)}, u32[]{:S(2)}) collective-permute-start(f32[384,128]{1,0:T(8,128)S(1)} %get-tuple-element.159), channel_id=1, source_target_pairs={{0,1},{1,0},{2,3},{3,2},{4,5},{5,4},{6,7},{7,6},{8,9},{9,8},{10,11... | collective-permute-start | bytes 589832 | tf_op jit(solution)/shard_map/ppermute | solution.py:667
  62.5 6.3 %collective-permute-start.16 = (f32[288,128]{1,0:T(8,128)S(1)}, f32[288,128]{1,0:T(8,128)S(1)}, u32[]{:S(2)}, u32[]{:S(2)}) collective-permute-start(f32[288,128]{1,0:T(8,128)S(1)} %get-tuple-element.155), channel_id=1, source_target_pairs={{0,8},{4,12},{8,0},{12,4},{16,24},{20,28},{24,16},{28,20},{1,9},{5... | collective-permute-start | bytes 442376 | tf_op jit(solution)/shard_map/ppermute | solution.py:535
  68.9 15.3 %collective-permute-start.20 = (f32[1024,768]{1,0:T(8,128)S(1)}, f32[1024,768]{1,0:T(8,128)S(1)}, u32[]{:S(2)}, u32[]{:S(2)}) collective-permute-start(f32[1024,768]{1,0:T(8,128)S(1)} %get-tuple-element.163.own), channel_id=1, source_target_pairs={{0,1},{1,0},{2,3},{3,2},{4,5},{5,4},{6,7},{7,6},{8,9},{9,8},{10,11... | collective-permute-start | bytes 9437192 | tf_op jit(solution)/shard_map/ppermute | solution.py:685
  68.9 11.1 %collective-permute-start.22 = (f32[192,128]{1,0:T(8,128)S(1)}, f32[192,128]{1,0:T(8,128)S(1)}, u32[]{:S(2)}, u32[]{:S(2)}) collective-permute-start(f32[192,128]{1,0:T(8,128)S(1)} %get-tuple-element.166), channel_id=1, source_target_pairs={{0,8},{4,12},{8,0},{12,4},{16,24},{20,28},{24,16},{28,20},{1,9},{5... | collective-permute-start | bytes 294920 | tf_op jit(solution)/shard_map/ppermute | solution.py:535
  70.6 9.5 %collective-permute-start.23 = (f32[256,128]{1,0:T(8,128)S(1)}, f32[256,128]{1,0:T(8,128)S(1)}, u32[]{:S(2)}, u32[]{:S(2)}) collective-permute-start(f32[256,128]{1,0:T(8,128)S(1)} %get-tuple-element.168), channel_id=1, source_target_pairs={{0,4},{4,0},{8,12},{12,8},{16,20},{20,16},{24,28},{28,24},{1,5},{5... | collective-permute-start | bytes 393224 | tf_op jit(solution)/shard_map/ppermute | solution.py:535
  71.1 9.7 %collective-permute-start.21 = (f32[288,128]{1,0:T(8,128)S(1)}, f32[288,128]{1,0:T(8,128)S(1)}, u32[]{:S(2)}, u32[]{:S(2)}) collective-permute-start(f32[288,128]{1,0:T(8,128)S(1)} %get-tuple-element.164.refs_0_), channel_id=1, source_target_pairs={{0,16},{4,20},{8,24},{12,28},{16,0},{20,4},{24,8},{28,12},{1,17},{... | collective-permute-start | bytes 442376 | tf_op jit(solution)/shard_map/ppermute | solution.py:535
  80.9 14.5 %collective-permute-start.24 = (f32[1024,512]{1,0:T(8,128)S(1)}, f32[1024,512]{1,0:T(8,128)S(1)}, u32[]{:S(2)}, u32[]{:S(2)}) collective-permute-start(f32[1024,512]{1,0:T(8,128)S(1)} %get-tuple-element.191.own), channel_id=1, source_target_pairs={{0,1},{1,0},{2,3},{3,2},{4,5},{5,4},{6,7},{7,6},{8,9},{9,8},{10,11... | collective-permute-start | bytes 6291464 | tf_op jit(solution)/shard_map/ppermute | solution.py:688
  81.0 9.8 %collective-permute-start.25 = (f32[288,128]{1,0:T(8,128)S(1)}, f32[288,128]{1,0:T(8,128)S(1)}, u32[]{:S(2)}, u32[]{:S(2)}) collective-permute-start(f32[288,128]{1,0:T(8,128)S(1)} %get-tuple-element.192.refs_0_), channel_id=1, source_target_pairs={{0,8},{4,12},{8,0},{12,4},{16,24},{20,28},{24,16},{28,20},{1,9},{5... | collective-permute-start | bytes 442376 | tf_op jit(solution)/shard_map/ppermute | solution.py:535
  81.0 9.7 %collective-permute-start.26 = (f32[192,128]{1,0:T(8,128)S(1)}, f32[192,128]{1,0:T(8,128)S(1)}, u32[]{:S(2)}, u32[]{:S(2)}) collective-permute-start(f32[192,128]{1,0:T(8,128)S(1)} %get-tuple-element.193.refs_2_), channel_id=1, source_target_pairs={{0,16},{4,20},{8,24},{12,28},{16,0},{20,4},{24,8},{28,12},{1,17},{... | collective-permute-start | bytes 294920 | tf_op jit(solution)/shard_map/ppermute | solution.py:535
  84.1 6.6 %collective-permute-start.27 = (f32[128,128]{1,0:T(8,128)S(1)}, f32[128,128]{1,0:T(8,128)S(1)}, u32[]{:S(2)}, u32[]{:S(2)}) collective-permute-start(f32[128,128]{1,0:T(8,128)S(1)} %get-tuple-element.195), channel_id=1, source_target_pairs={{0,8},{4,12},{8,0},{12,4},{16,24},{20,28},{24,16},{28,20},{1,9},{5... | collective-permute-start | bytes 196616 | tf_op jit(solution)/shard_map/ppermute | solution.py:535
  90.8 8.6 %collective-permute-start.28 = (f32[576,128]{1,0:T(8,128)S(1)}, f32[576,128]{1,0:T(8,128)S(1)}, u32[]{:S(2)}, u32[]{:S(2)}) collective-permute-start(f32[576,128]{1,0:T(8,128)S(1)} %get-tuple-element.199.refs_0_), channel_id=1, source_target_pairs={{0,4},{4,0},{8,12},{12,8},{16,20},{20,16},{24,28},{28,24},{1,5},{5... | collective-permute-start | bytes 884744 | tf_op jit(solution)/shard_map/ppermute | solution.py:535
  92.3 5.7 %collective-permute-start.29 = (f32[192,128]{1,0:T(8,128)S(1)}, f32[192,128]{1,0:T(8,128)S(1)}, u32[]{:S(2)}, u32[]{:S(2)}) collective-permute-start(f32[192,128]{1,0:T(8,128)S(1)} %get-tuple-element.200.refs_2_), channel_id=1, source_target_pairs={{0,8},{4,12},{8,0},{12,4},{16,24},{20,28},{24,16},{28,20},{1,9},{5... | collective-permute-start | bytes 294920 | tf_op jit(solution)/shard_map/ppermute | solution.py:535
  92.6 5.4 %collective-permute-start.30 = (f32[128,128]{1,0:T(8,128)S(1)}, f32[128,128]{1,0:T(8,128)S(1)}, u32[]{:S(2)}, u32[]{:S(2)}) collective-permute-start(f32[128,128]{1,0:T(8,128)S(1)} %get-tuple-element.201.refs_4_), channel_id=1, source_target_pairs={{0,16},{4,20},{8,24},{12,28},{16,0},{20,4},{24,8},{28,12},{1,17},{... | collective-permute-start | bytes 196616 | tf_op jit(solution)/shard_map/ppermute | solution.py:535
  99.5 5.8 %collective-permute-start.31 = (f32[384,128]{1,0:T(8,128)S(1)}, f32[384,128]{1,0:T(8,128)S(1)}, u32[]{:S(2)}, u32[]{:S(2)}) collective-permute-start(f32[384,128]{1,0:T(8,128)S(1)} %get-tuple-element.204.refs_0_), channel_id=1, source_target_pairs={{0,4},{4,0},{8,12},{12,8},{16,20},{20,16},{24,28},{28,24},{1,5},{5... | collective-permute-start | bytes 589832 | tf_op jit(solution)/shard_map/ppermute | solution.py:535
  101.0 4.3 %collective-permute-start.32 = (f32[128,128]{1,0:T(8,128)S(1)}, f32[128,128]{1,0:T(8,128)S(1)}, u32[]{:S(2)}, u32[]{:S(2)}) collective-permute-start(f32[128,128]{1,0:T(8,128)S(1)} %get-tuple-element.205.refs_2_), channel_id=1, source_target_pairs={{0,8},{4,12},{8,0},{12,4},{16,24},{20,28},{24,16},{28,20},{1,9},{5... | collective-permute-start | bytes 196616 | tf_op jit(solution)/shard_map/ppermute | solution.py:535
  105.4 5.0 %collective-permute-start.33 = (f32[256,128]{1,0:T(8,128)S(1)}, f32[256,128]{1,0:T(8,128)S(1)}, u32[]{:S(2)}, u32[]{:S(2)}) collective-permute-start(f32[256,128]{1,0:T(8,128)S(1)} %get-tuple-element.208.refs_2_), channel_id=1, source_target_pairs={{0,4},{4,0},{8,12},{12,8},{16,20},{20,16},{24,28},{28,24},{1,5},{5... | collective-permute-start | bytes 393224 | tf_op jit(solution)/shard_map/ppermute | solution.py:535
  (15 other events, 82.0 us)

commit v4 on v3

--- a/solution.py
+++ b/solution.py
@@ -21,8 +21,31 @@
 SUB = 256
 LAG = 1
 EPSILON = 1e-05
-GROUPS = ((0,), (1, 2), (3, 4), (5,))
-UNITS = ((0, 1), (2,), (3,))
+GROUPS = ((0, 1), (2, 3), (4,), (5,))
+UNITS = ((0,), (1,), (2, 3))
+WIDTH = (1, 1, 2)
+PLAN = (
+    ("small", "fetch", ()),
+    ("experts", 0, ()),
+    ("small", "send", ()),
+    ("events", (0,), ()),
+    ("small", "fetch", (0,)),
+    ("experts", 1, ()),
+    ("small", "send fetch", (0,)),
+    ("events", (1,), ()),
+    ("small", "", (1,)),
+    ("experts", 2, ()),
+    ("small", "send fetch", (0, 1)),
+    ("experts", 3, ()),
+    ("small", "send", (0, 1)),
+    ("events", (2,), ()),
+    ("small", "mix", (2,)),
+    ("events", (3,), ()),
+    ("small", "grad", (0, 1, 2)),
+    ("place", None, ()),
+    ("small", "", (0, 1, 2)),
+    ("place", None, ()),
+)
 COLUMN = (
     {0: 0, 1: 1, 4: 2, 5: 3},
     {2: 4, 3: 5, 4: 6, 5: 7},
@@ -47,12 +70,12 @@
     return one(a[0], b[0]) + (one(a[0], b[1]) + one(a[1], b[0]))
 
 
-def half_of(v, upper):
-    return jnp.where(upper, v[:, LANES:], v[:, :LANES])
+def in_hbm(v):
+    return pltpu.with_memory_space_constraint(v, pltpu.HBM)
 
 
 LARGE = 60
-EXPERT_MIB, EVENT_MIB, GATE_MIB, PAYLOAD_MIB, SMALL_MIB = 28, 16, 54, 62, 8
+EXPERT_MIB, EVENT_MIB, GATE_MIB, SMALL_MIB = 28, 16, 16, 8
 
 
 def params(mib):
@@ -105,10 +128,10 @@
         + [pl.BlockSpec(memory_space=pl.ANY)] * len(deps),
         out_specs=[vmem] * 4,
         out_shape=[
-            jax.ShapeDtypeStruct((rows, D), BF16),
-            jax.ShapeDtypeStruct((rows, D), BF16),
-            jax.ShapeDtypeStruct((rows, LANES), F32),
-            jax.ShapeDtypeStruct((rows, 3 * O), F32),
+            pltpu.VMEM((rows, D), BF16),
+            pltpu.VMEM((rows, D), BF16),
+            pltpu.VMEM((rows, LANES), F32),
+            pltpu.VMEM((rows, 3 * O), F32),
         ],
         scratch_shapes=[
             pltpu.VMEM((LANES, D), F32),
@@ -117,7 +140,7 @@
         ],
         compiler_params=params(GATE_MIB),
         cost_estimate=pl.CostEstimate(flops=6 * rows * D * LANES, bytes_accessed=rows * D * 8, transcendentals=0),
-    )(counts, events, cot, gate_w, *deps)
+    )(counts, in_hbm(events), in_hbm(cot), in_hbm(gate_w), *deps)
 
 
 def payload_kernel(groups, vectors, n_deps, w_in, w_out, *refs):
@@ -148,11 +171,11 @@
         functools.partial(payload_kernel, groups, bool(vectors), len(deps)),
         in_specs=[hbm, hbm] + [vmem] * len(vectors) + [pl.BlockSpec(memory_space=pl.ANY)] * len(deps),
         out_specs=[vmem] * len(groups),
-        out_shape=[jax.ShapeDtypeStruct((len(group), rows, WIDE), F32) for group in groups],
+        out_shape=[pltpu.VMEM((len(group), rows, WIDE), F32) for group in groups],
         scratch_shapes=[pltpu.VMEM((4 * E, SLICE), F32), pltpu.SemaphoreType.DMA((2 * len(groups),))],
-        compiler_params=params(PAYLOAD_MIB),
+        compiler_params=params(SMALL_MIB),
         cost_estimate=pl.CostEstimate(flops=0, bytes_accessed=SLICE * WIDE * 16, transcendentals=0),
-    )(w_in, w_out, *vectors, *deps)
+    )(in_hbm(w_in), in_hbm(w_out), *[in_hbm(v) for v in vectors], *deps)
 
 
 def expert_kernel(group, first, last, n_deps, *refs):
@@ -409,35 +432,49 @@
     )(*args)
 
 
-def event_kernel(n, *refs):
+def event_kernel(n, last, added, n_deps, *refs):
     highs, lows, winh, winl = (refs[k * n : (k + 1) * n] for k in range(4))
-    dlogits, gw_ref = refs[4 * n : 4 * n + 2]
-    out, token, gw = refs[-3:]
-    gw[...] = jnp.zeros_like(gw)
-    gw[:GATE_COLS, :] = gw_ref[...]
-    total = dot3(split(dlogits[...]), split(gw[...]), NN)
+    refs = list(refs[4 * n :])
+    total = 0.0
+    if last:
+        dlogits, gw_ref, gw = refs.pop(0), refs.pop(0), refs[-1]
+        gw[...] = jnp.zeros_like(gw)
+        gw[:GATE_COLS, :] = gw_ref[...]
+        total = dot3(split(dlogits[...]), split(gw[...]), NN)
+    before = refs.pop(0) if added else None
+    out, token = refs[n_deps : n_deps + 2]
     for g in range(n):
         total = total + dot3((highs[g][...], lows[g][...]), (winh[g][...], winl[g][...]), NN)
-    out[...] = total
+    out[...] = total + before[...] if added else total
     token[...] = jnp.zeros_like(token)
 
 
-def event_grads(rows, highs, lows, winh, winl, dlogits, gate_w, deps):
+def event_grads(rows, highs, lows, winh, winl, gating, before, deps):
     block = lambda width: pl.BlockSpec((ROW_BLOCK, width), lambda i: (i, 0))
     whole = lambda shape: pl.BlockSpec(shape, lambda i: (0, 0))
+    args = [*highs, *lows, *winh, *winl]
+    in_specs = [block(v.shape[1]) for v in (*highs, *lows)] + [whole(v.shape) for v in (*winh, *winl)]
+    aliases = {}
+    if gating:
+        args += gating
+        in_specs += [block(LANES), whole((GATE_COLS, D))]
+    if before is not None:
+        aliases = {len(args): 0}
+        args.append(before)
+        in_specs.append(block(D))
     return pl.pallas_call(
-        functools.partial(event_kernel, len(highs)),
+        functools.partial(event_kernel, len(highs), bool(gating), before is not None, len(deps)),
         grid=(rows // ROW_BLOCK,),
-        in_specs=[block(v.shape[1]) for v in (*highs, *lows)]
-        + [whole(v.shape) for v in (*winh, *winl)]
-        + [block(LANES), whole((GATE_COLS, D))]
-        + [pl.BlockSpec(memory_space=pl.ANY)] * len(deps),
+        in_specs=in_specs + [pl.BlockSpec(memory_space=pl.ANY)] * len(deps),
         out_specs=[block(D), whole(TOKEN)],
         scratch_shapes=[pltpu.VMEM((LANES, D), F32)],
-        out_shape=[jax.ShapeDtypeStruct((rows, D), F32), jax.ShapeDtypeStruct(TOKEN, F32)],
+        out_shape=[pltpu.VMEM((rows, D), F32), jax.ShapeDtypeStruct(TOKEN, F32)],
+        input_output_aliases=aliases,
         compiler_params=params(EVENT_MIB),
-        cost_estimate=pl.CostEstimate(flops=6 * rows * D * E * H, bytes_accessed=rows * 10000, transcendentals=0),
-    )(*highs, *lows, *winh, *winl, dlogits, gate_w, *deps)
+        cost_estimate=pl.CostEstimate(
+            flops=6 * rows * D * sum(v.shape[1] for v in highs), bytes_accessed=rows * 4000, transcendentals=0
+        ),
+    )(*args, *deps)
 
 
 def place_kernel(own, other, *refs):
@@ -523,97 +560,113 @@
 
 
 class Reduction:
-    def __init__(self, own, got, n_dp):
+    def __init__(self, own, got, n_dp, width):
         self.own, self.got = own, got
-        self.bits = n_dp.bit_length() - 1
-        unit = 8 << (self.bits - 1)
+        left, start = n_dp.bit_length() - 1, 0
+        self.groups = []
+        while left > width:
+            self.groups.append((start, width))
+            start, left = start + width, left - width
+        self.scattered = len(self.groups)
+        self.order = [*self.groups, (start, left), *reversed(self.groups)]
+        unit = 8 << start
         self.rows = -(-sum(v.shape[0] for v in own) // unit) * unit
-        self.swap = [[(i, i ^ (1 << b)) for i in range(n_dp)] for b in range(self.bits)]
+        self.n_dp = n_dp
         self.stage = 0
-
-    def over(self, values, bit):
-        return [lax.ppermute(v, "dp", self.swap[bit]) for v in values]
 
     @property
     def finished(self):
-        return self.stage == 2 * self.bits
+        return self.stage > len(self.order)
+
+    @property
+    def joining(self):
+        return self.stage == len(self.order)
 
     def job(self):
-        stage, bits = self.stage, self.bits
-        if stage == 0:
-            args = [*self.own, *self.got]
-            rows = self.rows
-        elif stage <= bits:
-            args = [self.keep, *self.got]
-            rows = self.keep.shape[0]
-        else:
-            args = [self.keep, *self.got]
-            rows = 2 * self.keep.shape[0]
-        n = len(args) // 2
-        gather = stage > bits
-        bit = stage if stage < bits else 2 * bits - 1 - stage
-        halving = stage < bits - 1
+        stage = self.stage
+        gather, scatter = stage > self.scattered + 1, stage < self.scattered
+        keeps = self.own if stage == 0 else [self.keep]
+        args = [*keeps, *self.got]
+        came = self.order[stage - 1]
+        goes = self.order[stage] if stage < len(self.order) else None
+        rows = self.rows if stage == 0 else self.keep.shape[0] * ((1 << came[1]) if gather else 1)
+        parts = 1 << goes[1] if scatter else 1
 
         def body(ins, outs, scratch):
-            to = scratch[0] if halving else outs[0]
+            to = scratch[0] if scatter else outs[0]
             if gather:
-                side = (lax.axis_index("dp") >> bit) & 1
-                part_of(to, side, rows // 2)[...] = ins[0][...]
-                part_of(to, 1 - side, rows // 2)[...] = ins[1][...]
+                join(ins, to, came)
                 return
             at = 0
-            for a, b in zip(ins[:n], ins[n:]):
-                to[at : at + a.shape[0], :] = a[...] + b[...]
+            for k, a in enumerate(keeps):
+                total = ins[k][...]
+                for v in ins[k + len(keeps) :: len(keeps)]:
+                    total = total + v[...]
+                to[at : at + a.shape[0], :] = total
                 at += a.shape[0]
             if at < rows:
                 to[at:, :] = jnp.zeros((rows - at, LANES), F32)
-            if halving:
-                side = (lax.axis_index("dp") >> bit) & 1
-                outs[0][...] = part_of(to, side, rows // 2)[...]
-                outs[1][...] = part_of(to, 1 - side, rows // 2)[...]
-
-        if halving:
-            return Job(args, [(rows // 2, LANES)] * 2, body, [pltpu.VMEM((rows, LANES), F32)])
+            if scatter:
+                side = side_of(goes)
+                for m in range(parts):
+                    outs[m][...] = part_of(to, side ^ m, rows // parts)[...]
+
+        if scatter:
+            return Job(args, [(rows // parts, LANES)] * parts, body, [pltpu.VMEM((rows, LANES), F32)])
         return Job(args, [(rows, LANES)], body)
 
     def take(self, outs):
-        stage, bits = self.stage, self.bits
         self.keep = outs[0]
-        bit = stage if stage < bits else 2 * bits - 2 - stage
-        if bit >= 0:
-            self.got = self.over([outs[-1]], bit)
+        if self.stage < len(self.order):
+            start, bits = self.order[self.stage]
+            self.got = []
+            for m in range(1, 1 << bits):
+                v = outs[m] if self.stage < self.scattered else outs[0]
+                self.got.append(lax.ppermute(v, "dp", [(i, i ^ (m << start)) for i in range(self.n_dp)]))
         self.stage += 1
 
 
-def finish_body(ins, outs, both):
+def side_of(bits):
+    return (lax.axis_index("dp") >> bits[0]) & ((1 << bits[1]) - 1)
+
+
+def join(ins, to, bits):
+    for m, v in enumerate(ins):
+        part_of(to, side_of(bits) ^ m, v.shape[0])[...] = v[...]
+
+
+def finish_body(joining, ins, outs, both):
     in_grad, in_bias, out_grad, out_bias, gain, shift, gate = outs
     odd = (lax.axis_index("tp") & 1) == 1
-    side = lax.axis_index("dp") & 1
-    whole = list(ins[:-2])
-    half = ins[-1].shape[0]
-    part_of(both[0], side, half)[...] = ins[-2][...]
-    part_of(both[0], 1 - side, half)[...] = ins[-1][...]
-    whole.append(both[0])
+    ins, both, summed = list(ins), list(both), []
+    for bits in joining:
+        if bits:
+            n = 1 << bits[1]
+            join(ins[:n], both[0], bits)
+            summed.append(both.pop(0))
+            del ins[:n]
+        else:
+            summed.append(ins.pop(0))
     for u, unit in enumerate(UNITS):
         at = 0
         for g in unit:
             group = GROUPS[g]
             for t in range(WIDE // LANES):
                 for e in group:
-                    tile = whole[u][at : at + SLICE, :]
+                    tile = summed[u][at : at + SLICE, :]
                     at += SLICE
                     if t < D // LANES:
                         in_grad[e, :, t * LANES : (t + 1) * LANES] = tile
                     else:
                         out_grad[e, :, t * LANES - D : (t + 1) * LANES - D] = tile
-    sums = whole[-1][at : at + 8 * len(GROUPS), :]
+    sums = summed[-1][at : at + 8 * len(GROUPS), :]
     sums = jnp.where(odd, sums[:, SLICE:], sums[:, :SLICE])
     for g, group in enumerate(GROUPS):
         for i, e in enumerate(group):
             for k, ref in enumerate((in_bias, out_bias, gain, shift)):
                 ref[e : e + 1, :] = sums[8 * g + 4 * i + k : 8 * g + 4 * i + k + 1, :]
     for t in range(D // LANES):
-        gate[:, t * LANES : (t + 1) * LANES] = whole[-1][at + 64 + 16 * t : at + 64 + 16 * t + GATE_COLS, :]
+        gate[:, t * LANES : (t + 1) * LANES] = summed[-1][at + 64 + 16 * t : at + 64 + 16 * t + GATE_COLS, :]
 
 
 def per_device(
@@ -642,61 +695,75 @@
     own += payload(GROUPS[1:], w_in, w_out, [], own)
     high, low, p, cot = gates(valid_counts, events, mix_cotangent, gate_w, rows, own[1:2])
     relayed = []
-    summing = []
+    summing = {}
     partial = []
-
-    def between(deps, through=(), sent=()):
-        for unit in UNITS[len(summing) :]:
-            if unit[-1] < len(partial):
-                both = [partial[g] for g in unit]
-                summing.append(Reduction([v for b in both for v in b[0]], [v for b in both for v in b[1]], n_dp))
-        active = [r for r in summing if not r.finished]
-        jobs = [r.job() for r in active] + [copy_job(*sent)]
-        fetched = len(relayed)
-        fetching = fetched < len(far)
-        if fetching:
-            jobs.append(copy_job(far[fetched], *own[fetched + 1 : fetched + 2]))
-        outs, through, token = run(jobs, deps, through)
-        if fetching:
-            relayed.append(lax.ppermute(outs[-1][0], "tp", core))
-            if len(outs[-1]) > 1:
-                far.append(lax.ppermute(outs[-1][1], "tp", across))
-                beside.append(lax.ppermute(outs[-1][1], "tp", core))
-        for r, o in zip(active, outs):
-            r.take(o)
-        return [token], through, [lax.ppermute(v, "tp", core) for v in outs[len(active)]]
-
-    deps, _, _ = between([p])
-    mix = small = None
-    dps, sums, highs, lows, winh, winl = [], [], [], [], [], []
-    for g, group in enumerate(GROUPS):
-        last = g == len(GROUPS) - 1
-        shards = (own[g], beside[g], far[g], relayed[g])
-        mix, dp, h, l, wh, wl, mine, part, s, *made = experts(
-            group, rows, high, low, cot, p, shards, small, mix, (dps, sums) if last else None, deps
-        )
-        small = made[0] if made else small
-        for held, v in zip((dps, sums, highs, lows, winh, winl), (dp, s, h, l, wh, wl)):
-            held.append(v)
-        extra = [s] if last else []
-        deps, _, got = between([s], sent=[part, *extra])
-        partial.append(([mine, *extra], got))
-    deps, (mix,), _ = between(deps, [mix])
-    other_mix = lax.ppermute(mix, "tp", core)
-    x_grad, token = event_grads(rows, highs, lows, winh, winl, dps[-1], gate_w, deps)
-    deps, (x_grad,), _ = between([token], [x_grad])
-    other_grad = lax.ppermute(x_grad, "tp", core)
-    mixtures, token = place(mix, other_mix, deps)
-    deps, _, _ = between([token])
-    x_grad, token = place(x_grad, other_grad, deps)
-    deps = [token]
-    while summing[-1].stage < 2 * summing[-1].bits - 1:
-        deps, _, _ = between(deps)
-    halves = [r.keep for r in summing] + summing[-1].got
+    made = []
+    placed, unplaced = [], []
+    mix = small = x_grad = None
+    deps = [p]
+    for kind, what, units in PLAN:
+        if kind == "experts":
+            last = what == len(GROUPS) - 1
+            shards = (own[what], beside[what], far[what], relayed[what])
+            before = ([m[1] for m in made], [m[8] for m in made]) if last else None
+            made.append(experts(GROUPS[what], rows, high, low, cot, p, shards, small, mix, before, deps))
+            mix = made[what][0]
+            small = made[0][9]
+            deps = [made[what][8]]
+        elif kind == "events":
+            ours = [[made[g][k] for g in what] for k in (2, 3, 4, 5)]
+            gating = [made[-1][1], gate_w] if what[-1] == len(GROUPS) - 1 else []
+            x_grad, token = event_grads(rows, *ours, gating, x_grad, deps)
+            deps = [token]
+        elif kind == "place":
+            v, token = place(*unplaced.pop(0), deps)
+            placed.append(v)
+            deps = [token]
+        else:
+            jobs = [summing[u].job() for u in units]
+            sent, fetched, through = [], [], []
+            if "send" in what:
+                sent = [made[-1][7]] + ([made[-1][8]] if len(made) == len(GROUPS) else [])
+                jobs.append(copy_job(*sent))
+            if "fetch" in what:
+                group = len(relayed)
+                fetched = [far[group], *own[group + 1 : group + 2]]
+                jobs.append(copy_job(*fetched))
+            if "mix" in what:
+                through.append(mix)
+            if "grad" in what:
+                through.append(x_grad)
+            outs, through, token = run(jobs, deps, through)
+            deps = [token]
+            for u, o in zip(units, outs):
+                summing[u].take(o)
+            if fetched:
+                relayed.append(lax.ppermute(outs[-1][0], "tp", core))
+                if len(fetched) > 1:
+                    far.append(lax.ppermute(outs[-1][1], "tp", across))
+                    beside.append(lax.ppermute(outs[-1][1], "tp", core))
+            if sent:
+                got = [lax.ppermute(v, "tp", core) for v in outs[len(units)]]
+                partial.append(([made[-1][6], *sent[1:]], got))
+                for u, (unit, width) in enumerate(zip(UNITS, WIDTH)):
+                    if unit[-1] == len(partial) - 1:
+                        both = [partial[g] for g in unit]
+                        summing[u] = Reduction([v for b in both for v in b[0]], [v for b in both for v in b[1]], n_dp, width)
+            unplaced += [(v, lax.ppermute(v, "tp", core)) for v in through]
+    mixtures, x_grad = placed
+    summing = [summing[u] for u in range(len(UNITS))]
+    while not all(u.finished or u.joining for u in summing):
+        ours = [u for u in summing if not u.finished and not u.joining]
+        outs, _, token = run([u.job() for u in ours], deps)
+        deps = [token]
+        for u, o in zip(ours, outs):
+            u.take(o)
+    joining = [u.order[-1] if u.joining else None for u in summing]
+    halves = [v for u in summing for v in ([u.keep, *u.got] if u.joining else [u.keep])]
     per_expert = (E, SLICE)
     shapes = [(E, SLICE, D), per_expert, (E, SLICE, H), per_expert, per_expert, per_expert, (GATE_COLS, D)]
-    scratch = [pltpu.VMEM((summing[-1].rows, LANES), F32)]
-    job = Job(halves, shapes, finish_body, scratch)
+    scratch = [pltpu.VMEM((u.rows, LANES), F32) for u in summing if u.joining]
+    job = Job(halves, shapes, functools.partial(finish_body, joining), scratch)
     (((in_grad, in_bias, out_grad, out_bias, gain, shift, gate),), _, _) = run([job], deps)
     return (
         mixtures,

time: 112 us -> 100 us (0.89)
  local copies, waits for them, and re-layouts: 6.45 us -> 0.01 us
  waiting for transfers between devices: 22.7 us -> 17.7 us
  Pallas kernels: 52.8 us -> 50.2 us
  starting transfers between devices: 28.6 us -> 30.8 us
    ppermute x32 -> x34, waiting for transfers between devices: 22.6 us -> 13.7 us  [the longest x17 13.7 us: take(): lax.ppermute(v, 'dp', [(i, i ^ m << start) for i in range(self.n_dp)])]
    unnamed x26 -> x4, local copies, waits for them, and re-layouts: 6.45 us -> 0.01 us
    ppermute x1, waiting for transfers between devices: 0.01 us -> 3.98 us  [per_device(): far = [lax.ppermute(own[0], 'tp', across)]]
    pallas_call x1, Pallas kernels: 7.56 us -> 4.97 us  [gates(): pl.pallas_call(functools.partial(gate_kernel, len(deps)), in_specs=[pl.Bl...]
    ppermute x32 -> x34, starting transfers between devices: 25.6 us -> 27.8 us  [the longest x17 20.9 us: take(): lax.ppermute(v, 'dp', [(i, i ^ m << start) for i in range(self.n_dp)])]
    pallas_call x1 -> x4, Pallas kernels: 6.29 us -> 8.38 us  [event_grads(): pl.pallas_call(functools.partial(event_kernel, len(highs), bool(gating),...]
    pallas_call x2, Pallas kernels: 4.49 us -> 2.92 us  [payload(): pl.pallas_call(functools.partial(payload_kernel, groups, bool(vectors), l...]
  transfers between devices with their start and end apart: 34 -> 36, of which waited for: 12 -> 5; matrix products, arithmetic and copies ran while one was open for 0% -> 0% of each run, Pallas kernels for 44% -> 47%
where the time goes in v4:
time: 100 us; the launch traced here: 99.8 us
  Pallas kernels  50.2 us (50%)
  starting transfers between devices  30.8 us (31%)
  waiting for transfers between devices  17.7 us (18%)
  between operations  1 us (1%)
    pallas_call x4, Pallas kernels, experts(): pl.pallas_call(functools.partial(expert_kernel, group, first, last, len(d...  27.3 us
    ppermute x17, starting transfers between devices, take(): lax.ppermute(v, 'dp', [(i, i ^ m << start) for i in range(self.n_dp)])  20.9 us
    ppermute x17, waiting for transfers between devices, take(): lax.ppermute(v, 'dp', [(i, i ^ m << start) for i in range(self.n_dp)])  13.7 us
    pallas_call x4, Pallas kernels, event_grads(): pl.pallas_call(functools.partial(event_kernel, len(highs), bool(gating),...  8.38 us
    pallas_call x1, Pallas kernels, gates(): pl.pallas_call(functools.partial(gate_kernel, len(deps)), in_specs=[pl.Bl...  4.97 us
    pallas_call x2, Pallas kernels, place(): pl.pallas_call(place_kernel, in_specs=[anywhere] * (2 + len(deps)), out_s...  4.74 us
    ppermute x3, starting transfers between devices, per_device(): far.append(lax.ppermute(outs[-1][1], 'tp', across))  3.99 us
    ppermute x1, waiting for transfers between devices, per_device(): far = [lax.ppermute(own[0], 'tp', across)]  3.98 us
  transfers between devices with their start and end apart: 36, of which 5 were waited for; matrix products, arithmetic and copies ran while one was open for 0% of the time, Pallas kernels for 47%

profile of v4, /device:TPU:0, one launch (start us, length us, event | category | flops | bytes accessed | tf_op | source)
XLA Modules:
  0.0 99.8 jit_solution(13443582895220189031)
XLA Ops:
  0.7 1.7 %shard_map.169.refs_0_.refs_4_ = f32[2,72,768]{2,1,0:T(8,128)S(1)} custom-call(f32[6,64,512]{2,1,0:T(8,128)} %bitcast.8, f32[6,64,256]{2,1,0:T(8,128)} %bitcast.10, f32[6,64]{1,0:T(8,128)} %refs_0_.1, f32[6,64]{1,0:T(8,128)} %refs_1_.1, f32[6,64]{1,0:T(8,128)} %refs_2_.1, f32[6,64]{1,0:T(8,128)} %refs_3_.1), custom_call_target="tpu_custom_call" | custom-call | bytes 786432 | tf_op jit(solution)/shard_map/pallas_call | solution.py:170
  2.4 3.0 %collective-permute-start.1 = (f32[2,72,768]{2,1,0:T(8,128)S(1)}, f32[2,72,768]{2,1,0:T(8,128)S(1)}, u32[]{:S(2)}, u32[]{:S(2)}) collective-permute-start(f32[2,72,768]{2,1,0:T(8,128)S(1)} %shard_map.169.refs_0_.refs_4_), channel_id=1, source_target_pairs={{0,2},{1,3},{2,0},{3,1},{4,6},{5,7},{6,4},{7,5},{8,10},{9,11},{10,... | collective-permute-start | bytes 1327112 | tf_op jit(solution)/shard_map/ppermute | solution.py:693
  5.4 1.2 %shard_map.170 = (f32[2,64,768]{2,1,0:T(8,128)S(1)}, f32[1,64,768]{2,1,0:T(8,128)S(1)}, f32[1,64,768]{2,1,0:T(8,128)S(1)}) custom-call(f32[6,64,512]{2,1,0:T(8,128)} %bitcast.9, f32[6,64,256]{2,1,0:T(8,128)} %bitcast.11, f32[2,72,768]{2,1,0:T(8,128)S(1)} %shard_map.169.refs_0_.refs_4_), custom_call_target="tpu_custom_call" | custom-call | bytes 786432 | tf_op jit(solution)/shard_map/pallas_call | solution.py:170
  6.6 5.0 %shard_map.171 = (bf16[1024,512]{1,0:T(8,128)(2,1)S(1)}, bf16[1024,512]{1,0:T(8,128)(2,1)S(1)}, f32[1024,128]{1,0:T(8,128)S(1)}, f32[1024,768]{1,0:T(8,128)S(1)}) custom-call(s32[8]{0:T(128)S(1)} %copy-done.1, f32[2048,512]{1,0:T(8,128)} %ev_ref.1, f32[2048,768]{1,0:T(8,128)} %cot_ref.1, f32[14,512]{1,0:T(8,128)} %bitcast.6, ...), custom_call_target="tpu_custom_call" | custom-call | flops 402653184 | bytes 4194304 | tf_op jit(solution)/shard_map/pallas_call | solution.py:125
  11.6 4.0 %collective-permute-done.1.refs_0_.refs_6_ = f32[2,72,768]{2,1,0:T(8,128)S(1)} collective-permute-done((f32[2,72,768]{2,1,0:T(8,128)S(1)}, f32[2,72,768]{2,1,0:T(8,128)S(1)}, u32[]{:S(2)}, u32[]{:S(2)}) %collective-permute-start.1) | collective-permute-done | bytes 442400 | tf_op jit(solution)/shard_map/ppermute | solution.py:693
  15.7 1.8 %collective-permute-start.4 = (f32[2,64,768]{2,1,0:T(8,128)S(1)}, f32[2,64,768]{2,1,0:T(8,128)S(1)}, u32[]{:S(2)}, u32[]{:S(2)}) collective-permute-start(f32[2,64,768]{2,1,0:T(8,128)S(1)} %get-tuple-element.129), channel_id=1, source_target_pairs={{0,2},{1,3},{2,0},{3,1},{4,6},{5,7},{6,4},{7,5},{8,10},{9,11},{10,... | collective-permute-start | bytes 1179656 | tf_op jit(solution)/shard_map/ppermute | solution.py:743
  17.6 7.5 %shard_map.173 = (f32[1024,768]{1,0:T(8,128)S(1)}, f32[1024,128]{1,0:T(8,128)S(1)}, bf16[1024,512]{1,0:T(8,128)(2,1)S(1)}, bf16[1024,512]{1,0:T(8,128)(2,1)S(1)}...) custom-call(bf16[1024,512]{1,0:T(8,128)(2,1)S(1)} %get-tuple-element, ...), custom_call_target="tpu_custom_call" | custom-call | flops 8858370048 | bytes 14336000 | tf_op jit(solution)/shard_map/pallas_call | solution.py:400
  25.7 2.3 %shard_map.175 = (f32[1024,512]{1,0:T(8,128)S(1)}, f32[8,128]{1,0:T(8,128)S(1)}) custom-call(bf16[1024,512]{1,0:T(8,128)(2,1)S(1)} %get-tuple-element.130.refs_0_, bf16[1024,512]{1,0:T(8,128)(2,1)S(1)} %get-tuple-element.131.refs_1_, bf16[512,512]{1,0:T(8,128)(2,1)S(1)} %get-tuple-element.132.refs_2_, bf16[512,512]{1,0:T(8,128)(2,1)S(1)} %get-tuple-element.133.refs_3_, ...), custom_call_target="tpu_custom_call" | custom-call | flops 1610612736 | bytes 4096000 | tf_op jit(solution)/shard_map/pallas_call | solution.py:465
  28.4 1.7 %collective-permute-start.6 = (f32[1,64,768]{2,1,0:T(8,128)S(1)}, f32[1,64,768]{2,1,0:T(8,128)S(1)}, u32[]{:S(2)}, u32[]{:S(2)}) collective-permute-start(f32[1,64,768]{2,1,0:T(8,128)S(1)} %get-tuple-element.136), channel_id=1, source_target_pairs={{0,2},{1,3},{2,0},{3,1},{4,6},{5,7},{6,4},{7,5},{8,10},{9,11},{10,... | collective-permute-start | bytes 589832 | tf_op jit(solution)/shard_map/ppermute | solution.py:743
  30.1 1.5 %collective-permute-start.7 = (f32[384,128]{1,0:T(8,128)S(1)}, f32[384,128]{1,0:T(8,128)S(1)}, u32[]{:S(2)}, u32[]{:S(2)}) collective-permute-start(f32[384,128]{1,0:T(8,128)S(1)} %get-tuple-element.138), channel_id=1, source_target_pairs={{0,4},{4,0},{8,12},{12,8},{16,20},{20,16},{24,28},{28,24},{1,5},{5... | collective-permute-start | bytes 589832 | tf_op jit(solution)/shard_map/ppermute | solution.py:625
  31.6 7.9 %shard_map.177 = (f32[1024,768]{1,0:T(8,128)S(1)}, f32[1024,128]{1,0:T(8,128)S(1)}, bf16[1024,512]{1,0:T(8,128)(2,1)S(1)}, bf16[1024,512]{1,0:T(8,128)(2,1)S(1)}...) custom-call(bf16[1024,512]{1,0:T(8,128)(2,1)S(1)} %get-tuple-element, ...), custom_call_target="tpu_custom_call", output_to_operand_aliasing={{0}: (9, {})} | custom-call | flops 8858370048 | bytes 14336000 | tf_op jit(solution)/shard_map/pallas_call | solution.py:400
  40.9 2.3 %shard_map.179 = (f32[1024,512]{1,0:T(8,128)S(1)}, f32[8,128]{1,0:T(8,128)S(1)}) custom-call(bf16[1024,512]{1,0:T(8,128)(2,1)S(1)} %get-tuple-element.150.refs_0_, bf16[1024,512]{1,0:T(8,128)(2,1)S(1)} %get-tuple-element.151.refs_1_, bf16[512,512]{1,0:T(8,128)(2,1)S(1)} %get-tuple-element.152.refs_2_, ...), custom_call_target="tpu_custom_call", output_to_operand_aliasing={{0}: (4, {})} | custom-call | flops 1610612736 | bytes 4096000 | tf_op jit(solution)/shard_map/pallas_call | solution.py:465
  43.3 1.6 %collective-permute-start.14 = (f32[192,128]{1,0:T(8,128)S(1)}, f32[192,128]{1,0:T(8,128)S(1)}, u32[]{:S(2)}, u32[]{:S(2)}) collective-permute-start(f32[192,128]{1,0:T(8,128)S(1)} %get-tuple-element.161), channel_id=1, source_target_pairs={{0,8},{4,12},{8,0},{12,4},{16,24},{20,28},{24,16},{28,20},{1,9},{5... | collective-permute-start | bytes 294920 | tf_op jit(solution)/shard_map/ppermute | solution.py:625
  45.0 1.1 %collective-permute-start.15 = (f32[384,128]{1,0:T(8,128)S(1)}, f32[384,128]{1,0:T(8,128)S(1)}, u32[]{:S(2)}, u32[]{:S(2)}) collective-permute-start(f32[384,128]{1,0:T(8,128)S(1)} %get-tuple-element.163), channel_id=1, source_target_pairs={{0,4},{4,0},{8,12},{12,8},{16,20},{20,16},{24,28},{28,24},{1,5},{5... | collective-permute-start | bytes 589832 | tf_op jit(solution)/shard_map/ppermute | solution.py:625
  46.1 5.3 %shard_map.181 = (f32[1024,768]{1,0:T(8,128)S(1)}, f32[1024,128]{1,0:T(8,128)S(1)}, bf16[1024,256]{1,0:T(8,128)(2,1)S(1)}, bf16[1024,256]{1,0:T(8,128)(2,1)S(1)}...) custom-call(bf16[1024,512]{1,0:T(8,128)(2,1)S(1)} %get-tuple-element, ...), custom_call_target="tpu_custom_call", output_to_operand_aliasing={{0}: (9, {})} | custom-call | flops 4429185024 | bytes 14336000 | tf_op jit(solution)/shard_map/pallas_call | solution.py:400
  52.1 2.7 %collective-permute-start.18 = (f32[192,128]{1,0:T(8,128)S(1)}, f32[192,128]{1,0:T(8,128)S(1)}, u32[]{:S(2)}, u32[]{:S(2)}) collective-permute-start(f32[192,128]{1,0:T(8,128)S(1)} %get-tuple-element.175.refs_0_), channel_id=1, source_target_pairs={{0,16},{4,20},{8,24},{12,28},{16,0},{20,4},{24,8},{28,12},{1,17},{... | collective-permute-start | bytes 294920 | tf_op jit(solution)/shard_map/ppermute | solution.py:625
  55.2 6.5 %shard_map.183 = (f32[1024,768]{1,0:T(8,128)S(1)}, f32[1024,128]{1,0:T(8,128)S(1)}, bf16[1024,256]{1,0:T(8,128)(2,1)S(1)}, bf16[1024,256]{1,0:T(8,128)(2,1)S(1)}...) custom-call(bf16[1024,512]{1,0:T(8,128)(2,1)S(1)} %get-tuple-element, ...), custom_call_target="tpu_custom_call", output_to_operand_aliasing={{0}: (9, {})} | custom-call | flops 4429185024 | bytes 14336000 | tf_op jit(solution)/shard_map/pallas_call | solution.py:400
  62.4 1.5 %shard_map.185 = (f32[1024,512]{1,0:T(8,128)S(1)}, f32[8,128]{1,0:T(8,128)S(1)}) custom-call(bf16[1024,256]{1,0:T(8,128)(2,1)S(1)} %get-tuple-element.182.refs_0_, bf16[1024,256]{1,0:T(8,128)(2,1)S(1)} %get-tuple-element.183.refs_1_, bf16[256,512]{1,0:T(8,128)(2,1)S(1)} %get-tuple-element.184.refs_2_, ...), custom_call_target="tpu_custom_call", output_to_operand_aliasing={{0}: (4, {})} | custom-call | flops 805306368 | bytes 4096000 | tf_op jit(solution)/shard_map/pallas_call | solution.py:465
  64.5 1.6 %collective-permute-start.23 = (f32[192,128]{1,0:T(8,128)S(1)}, f32[192,128]{1,0:T(8,128)S(1)}, u32[]{:S(2)}, u32[]{:S(2)}) collective-permute-start(f32[192,128]{1,0:T(8,128)S(1)} %get-tuple-element.190.refs_0_), channel_id=1, source_target_pairs={{0,8},{4,12},{8,0},{12,4},{16,24},{20,28},{24,16},{28,20},{1,9},{5... | collective-permute-start | bytes 294920 | tf_op jit(solution)/shard_map/ppermute | solution.py:625
  66.1 1.1 %collective-permute-start.25 = (f32[224,128]{1,0:T(8,128)S(1)}, f32[224,128]{1,0:T(8,128)S(1)}, u32[]{:S(2)}, u32[]{:S(2)}) collective-permute-start(f32[224,128]{1,0:T(8,128)S(1)} %get-tuple-element.193), channel_id=1, source_target_pairs={{0,4},{4,0},{8,12},{12,8},{16,20},{20,16},{24,28},{28,24},{1,5},{5... | collective-permute-start | bytes 344072 | tf_op jit(solution)/shard_map/ppermute | solution.py:625
  67.7 1.9 %collective-permute-start.27 = (f32[224,128]{1,0:T(8,128)S(1)}, f32[224,128]{1,0:T(8,128)S(1)}, u32[]{:S(2)}, u32[]{:S(2)}) collective-permute-start(f32[224,128]{1,0:T(8,128)S(1)} %get-tuple-element.195), channel_id=1, source_target_pairs={{0,12},{4,8},{8,4},{12,0},{16,28},{20,24},{24,20},{28,16},{1,13},{... | collective-permute-start | bytes 344072 | tf_op jit(solution)/shard_map/ppermute | solution.py:625
  70.5 2.3 %shard_map.187 = (f32[1024,512]{1,0:T(8,128)S(1)}, f32[8,128]{1,0:T(8,128)S(1)}) custom-call(bf16[1024,256]{1,0:T(8,128)(2,1)S(1)} %get-tuple-element.196.refs_0_, bf16[1024,256]{1,0:T(8,128)(2,1)S(1)} %get-tuple-element.197.refs_1_, bf16[256,512]{1,0:T(8,128)(2,1)S(1)} %get-tuple-element.198.refs_2_, ...), custom_call_target="tpu_custom_call", output_to_operand_aliasing={{0}: (6, {})} | custom-call | flops 805306368 | bytes 4096000 | tf_op jit(solution)/shard_map/pallas_call | solution.py:465
  72.8 4.0 %collective-permute-done.24.refs_3_ = f32[192,128]{1,0:T(8,128)S(1)} collective-permute-done((f32[192,128]{1,0:T(8,128)S(1)}, f32[192,128]{1,0:T(8,128)S(1)}, u32[]{:S(2)}, u32[]{:S(2)}) %collective-permute-start.24) | collective-permute-done | bytes 98336 | tf_op jit(solution)/shard_map/ppermute | solution.py:625
  77.0 1.3 %collective-permute-start.29 = (f32[384,128]{1,0:T(8,128)S(1)}, f32[384,128]{1,0:T(8,128)S(1)}, u32[]{:S(2)}, u32[]{:S(2)}) collective-permute-start(f32[384,128]{1,0:T(8,128)S(1)} %get-tuple-element.208.refs_0_), channel_id=1, source_target_pairs={{0,4},{4,0},{8,12},{12,8},{16,20},{20,16},{24,28},{28,24},{1,5},{5... | collective-permute-start | bytes 589832 | tf_op jit(solution)/shard_map/ppermute | solution.py:625
  78.3 1.8 %collective-permute-start.31 = (f32[224,128]{1,0:T(8,128)S(1)}, f32[224,128]{1,0:T(8,128)S(1)}, u32[]{:S(2)}, u32[]{:S(2)}) collective-permute-start(f32[224,128]{1,0:T(8,128)S(1)} %get-tuple-element.210.refs_4_), channel_id=1, source_target_pairs={{0,16},{4,20},{8,24},{12,28},{16,0},{20,4},{24,8},{28,12},{1,17},{... | collective-permute-start | bytes 344072 | tf_op jit(solution)/shard_map/ppermute | solution.py:625
  80.1 2.7 %shard_map.189 = (f32[2048,768]{1,0:T(8,128)}, f32[8,128]{1,0:T(8,128)S(1)}) custom-call(f32[1024,768]{1,0:T(8,128)S(1)} %get-tuple-element.189.own, f32[1024,768]{1,0:T(8,128)S(1)} %collective-permute-done.22.other, f32[8,128]{1,0:T(8,128)S(1)} %get-tuple-element.205.refs_0_), custom_call_target="tpu_custom_call" | custom-call | bytes 12582912 | tf_op jit(solution)/shard_map/pallas_call | solution.py:498
  82.8 4.3 %collective-permute-done.30.refs_3_ = f32[192,128]{1,0:T(8,128)S(1)} collective-permute-done((f32[192,128]{1,0:T(8,128)S(1)}, f32[192,128]{1,0:T(8,128)S(1)}, u32[]{:S(2)}, u32[]{:S(2)}) %collective-permute-start.30) | collective-permute-done | bytes 98336 | tf_op jit(solution)/shard_map/ppermute | solution.py:625
  88.1 1.1 %collective-permute-start.33 = (f32[224,128]{1,0:T(8,128)S(1)}, f32[224,128]{1,0:T(8,128)S(1)}, u32[]{:S(2)}, u32[]{:S(2)}) collective-permute-start(f32[224,128]{1,0:T(8,128)S(1)} %get-tuple-element.216.refs_3_), channel_id=1, source_target_pairs={{0,4},{4,0},{8,12},{12,8},{16,20},{20,16},{24,28},{28,24},{1,5},{5... | collective-permute-start | bytes 344072 | tf_op jit(solution)/shard_map/ppermute | solution.py:625
  89.6 2.0 %collective-permute-start.35 = (f32[224,128]{1,0:T(8,128)S(1)}, f32[224,128]{1,0:T(8,128)S(1)}, u32[]{:S(2)}, u32[]{:S(2)}) collective-permute-start(f32[224,128]{1,0:T(8,128)S(1)} %get-tuple-element.216.refs_3_), channel_id=1, source_target_pairs={{0,12},{4,8},{8,4},{12,0},{16,28},{20,24},{24,20},{28,16},{1,13},{... | collective-permute-start | bytes 344072 | tf_op jit(solution)/shard_map/ppermute | solution.py:625
  91.6 2.0 %shard_map.191 = (f32[2048,512]{1,0:T(8,128)}, f32[8,128]{1,0:T(8,128)S(1)}) custom-call(f32[1024,512]{1,0:T(8,128)S(1)} %get-tuple-element.207.own, f32[1024,512]{1,0:T(8,128)S(1)} %collective-permute-done.28.other, f32[8,128]{1,0:T(8,128)S(1)} %get-tuple-element.212.refs_0_), custom_call_target="tpu_custom_call" | custom-call | bytes 8388608 | tf_op jit(solution)/shard_map/pallas_call | solution.py:498
  93.6 4.9 %collective-permute-done.33.refs_4_ = f32[224,128]{1,0:T(8,128)S(1)} collective-permute-done((f32[224,128]{1,0:T(8,128)S(1)}, f32[224,128]{1,0:T(8,128)S(1)}, u32[]{:S(2)}, u32[]{:S(2)}) %collective-permute-start.33) | collective-permute-done | bytes 114720 | tf_op jit(solution)/shard_map/ppermute | solution.py:625
  98.5 1.2 %shard_map.192 = (f32[6,64,512]{2,1,0:T(8,128)}, f32[6,64]{1,0:T(8,128)}, f32[6,64,256]{2,1,0:T(8,128)}, f32[6,64]{1,0:T(8,128)}, f32[6,64]{1,0:T(8,128)}, /*ind...) custom-call(f32[768,128]{1,0:T(8,128)S(1)} %get-tuple-element.214.refs_0_, ...), custom_call_target="tpu_custom_call" | custom-call | bytes 2490368 | tf_op jit(solution)/shard_map/pallas_call | solution.py:539
  (68 shorter events, 7.9 us)
Async XLA Ops:
  2.4 13.2 %collective-permute-start.1 = (f32[2,72,768]{2,1,0:T(8,128)S(1)}, f32[2,72,768]{2,1,0:T(8,128)S(1)}, u32[]{:S(2)}, u32[]{:S(2)}) collective-permute-start(f32[2,72,768]{2,1,0:T(8,128)S(1)} %shard_map.169.refs_0_.refs_4_), channel_id=1, source_target_pairs={{0,2},{1,3},{2,0},{3,1},{4,6},{5,7},{6,4},{7,5},{8,10},{9,11},{10,... | collective-permute-start | bytes 1327112 | tf_op jit(solution)/shard_map/ppermute | solution.py:693
  5.4 12.1 %collective-permute-start = (f32[2,72,768]{2,1,0:T(8,128)S(1)}, f32[2,72,768]{2,1,0:T(8,128)S(1)}, u32[]{:S(2)}, u32[]{:S(2)}) collective-permute-start(f32[2,72,768]{2,1,0:T(8,128)S(1)} %shard_map.169.refs_0_.refs_4_), channel_id=1, source_target_pairs={{0,1},{1,0},{2,3},{3,2},{4,5},{5,4},{6,7},{7,6},{8,9},{9,8},{10,11... | collective-permute-start | bytes 1327112 | tf_op jit(solution)/shard_map/ppermute | solution.py:694
  15.7 12.3 %collective-permute-start.4 = (f32[2,64,768]{2,1,0:T(8,128)S(1)}, f32[2,64,768]{2,1,0:T(8,128)S(1)}, u32[]{:S(2)}, u32[]{:S(2)}) collective-permute-start(f32[2,64,768]{2,1,0:T(8,128)S(1)} %get-tuple-element.129), channel_id=1, source_target_pairs={{0,2},{1,3},{2,0},{3,1},{4,6},{5,7},{6,4},{7,5},{8,10},{9,11},{10,... | collective-permute-start | bytes 1179656 | tf_op jit(solution)/shard_map/ppermute | solution.py:743
  25.4 6.2 %collective-permute-start.8 = (f32[2,64,768]{2,1,0:T(8,128)S(1)}, f32[2,64,768]{2,1,0:T(8,128)S(1)}, u32[]{:S(2)}, u32[]{:S(2)}) collective-permute-start(f32[2,64,768]{2,1,0:T(8,128)S(1)} %get-tuple-element.129), channel_id=1, source_target_pairs={{0,1},{1,0},{2,3},{3,2},{4,5},{5,4},{6,7},{7,6},{8,9},{9,8},{10,11... | collective-permute-start | bytes 1179656 | tf_op jit(solution)/shard_map/ppermute | solution.py:744
  28.1 3.4 %collective-permute-start.9 = (f32[2,64,768]{2,1,0:T(8,128)S(1)}, f32[2,64,768]{2,1,0:T(8,128)S(1)}, u32[]{:S(2)}, u32[]{:S(2)}) collective-permute-start(f32[2,64,768]{2,1,0:T(8,128)S(1)} %get-tuple-element.139), channel_id=1, source_target_pairs={{0,1},{1,0},{2,3},{3,2},{4,5},{5,4},{6,7},{7,6},{8,9},{9,8},{10,11... | collective-permute-start | bytes 1179656 | tf_op jit(solution)/shard_map/ppermute | solution.py:741
  28.4 11.1 %collective-permute-start.6 = (f32[1,64,768]{2,1,0:T(8,128)S(1)}, f32[1,64,768]{2,1,0:T(8,128)S(1)}, u32[]{:S(2)}, u32[]{:S(2)}) collective-permute-start(f32[1,64,768]{2,1,0:T(8,128)S(1)} %get-tuple-element.136), channel_id=1, source_target_pairs={{0,2},{1,3},{2,0},{3,1},{4,6},{5,7},{6,4},{7,5},{8,10},{9,11},{10,... | collective-permute-start | bytes 589832 | tf_op jit(solution)/shard_map/ppermute | solution.py:743
  30.1 9.4 %collective-permute-start.7 = (f32[384,128]{1,0:T(8,128)S(1)}, f32[384,128]{1,0:T(8,128)S(1)}, u32[]{:S(2)}, u32[]{:S(2)}) collective-permute-start(f32[384,128]{1,0:T(8,128)S(1)} %get-tuple-element.138), channel_id=1, source_target_pairs={{0,4},{4,0},{8,12},{12,8},{16,20},{20,16},{24,28},{28,24},{1,5},{5... | collective-permute-start | bytes 589832 | tf_op jit(solution)/shard_map/ppermute | solution.py:625
  39.6 3.6 %collective-permute-start.11 = (f32[768,128]{1,0:T(8,128)S(1)}, f32[768,128]{1,0:T(8,128)S(1)}, u32[]{:S(2)}, u32[]{:S(2)}) collective-permute-start(f32[768,128]{1,0:T(8,128)S(1)} %get-tuple-element.149), channel_id=1, source_target_pairs={{0,1},{1,0},{2,3},{3,2},{4,5},{5,4},{6,7},{7,6},{8,9},{9,8},{10,11... | collective-permute-start | bytes 1179656 | tf_op jit(solution)/shard_map/ppermute | solution.py:746
  39.7 5.3 %collective-permute-start.5 = (f32[1,64,768]{2,1,0:T(8,128)S(1)}, f32[1,64,768]{2,1,0:T(8,128)S(1)}, u32[]{:S(2)}, u32[]{:S(2)}) collective-permute-start(f32[1,64,768]{2,1,0:T(8,128)S(1)} %get-tuple-element.136), channel_id=1, source_target_pairs={{0,1},{1,0},{2,3},{3,2},{4,5},{5,4},{6,7},{7,6},{8,9},{9,8},{10,11... | collective-permute-start | bytes 589832 | tf_op jit(solution)/shard_map/ppermute | solution.py:744
  40.2 5.9 %collective-permute-start.10 = (f32[1,64,768]{2,1,0:T(8,128)S(1)}, f32[1,64,768]{2,1,0:T(8,128)S(1)}, u32[]{:S(2)}, u32[]{:S(2)}) collective-permute-start(f32[1,64,768]{2,1,0:T(8,128)S(1)} %get-tuple-element.146), channel_id=1, source_target_pairs={{0,1},{1,0},{2,3},{3,2},{4,5},{5,4},{6,7},{7,6},{8,9},{9,8},{10,11... | collective-permute-start | bytes 589832 | tf_op jit(solution)/shard_map/ppermute | solution.py:741
  40.3 11.2 %collective-permute-start.13 = (f32[1,64,768]{2,1,0:T(8,128)S(1)}, f32[1,64,768]{2,1,0:T(8,128)S(1)}, u32[]{:S(2)}, u32[]{:S(2)}) collective-permute-start(f32[1,64,768]{2,1,0:T(8,128)S(1)} %get-tuple-element.159), channel_id=1, source_target_pairs={{0,2},{1,3},{2,0},{3,1},{4,6},{5,7},{6,4},{7,5},{8,10},{9,11},{10,... | collective-permute-start | bytes 589832 | tf_op jit(solution)/shard_map/ppermute | solution.py:743
  40.8 14.4 %collective-permute-start.12 = (f32[1,64,768]{2,1,0:T(8,128)S(1)}, f32[1,64,768]{2,1,0:T(8,128)S(1)}, u32[]{:S(2)}, u32[]{:S(2)}) collective-permute-start(f32[1,64,768]{2,1,0:T(8,128)S(1)} %get-tuple-element.159), channel_id=1, source_target_pairs={{0,1},{1,0},{2,3},{3,2},{4,5},{5,4},{6,7},{7,6},{8,9},{9,8},{10,11... | collective-permute-start | bytes 589832 | tf_op jit(solution)/shard_map/ppermute | solution.py:744
  43.3 8.2 %collective-permute-start.14 = (f32[192,128]{1,0:T(8,128)S(1)}, f32[192,128]{1,0:T(8,128)S(1)}, u32[]{:S(2)}, u32[]{:S(2)}) collective-permute-start(f32[192,128]{1,0:T(8,128)S(1)} %get-tuple-element.161), channel_id=1, source_target_pairs={{0,8},{4,12},{8,0},{12,4},{16,24},{20,28},{24,16},{28,20},{1,9},{5... | collective-permute-start | bytes 294920 | tf_op jit(solution)/shard_map/ppermute | solution.py:625
  45.0 6.9 %collective-permute-start.15 = (f32[384,128]{1,0:T(8,128)S(1)}, f32[384,128]{1,0:T(8,128)S(1)}, u32[]{:S(2)}, u32[]{:S(2)}) collective-permute-start(f32[384,128]{1,0:T(8,128)S(1)} %get-tuple-element.163), channel_id=1, source_target_pairs={{0,4},{4,0},{8,12},{12,8},{16,20},{20,16},{24,28},{28,24},{1,5},{5... | collective-permute-start | bytes 589832 | tf_op jit(solution)/shard_map/ppermute | solution.py:625
  52.0 3.2 %collective-permute-start.16 = (f32[1,64,768]{2,1,0:T(8,128)S(1)}, f32[1,64,768]{2,1,0:T(8,128)S(1)}, u32[]{:S(2)}, u32[]{:S(2)}) collective-permute-start(f32[1,64,768]{2,1,0:T(8,128)S(1)} %get-tuple-element.166), channel_id=1, source_target_pairs={{0,1},{1,0},{2,3},{3,2},{4,5},{5,4},{6,7},{7,6},{8,9},{9,8},{10,11... | collective-permute-start | bytes 589832 | tf_op jit(solution)/shard_map/ppermute | solution.py:741
  52.1 9.6 %collective-permute-start.18 = (f32[192,128]{1,0:T(8,128)S(1)}, f32[192,128]{1,0:T(8,128)S(1)}, u32[]{:S(2)}, u32[]{:S(2)}) collective-permute-start(f32[192,128]{1,0:T(8,128)S(1)} %get-tuple-element.175.refs_0_), channel_id=1, source_target_pairs={{0,16},{4,20},{8,24},{12,28},{16,0},{20,4},{24,8},{28,12},{1,17},{... | collective-permute-start | bytes 294920 | tf_op jit(solution)/shard_map/ppermute | solution.py:625
  54.7 7.0 %collective-permute-start.19 = (f32[192,128]{1,0:T(8,128)S(1)}, f32[192,128]{1,0:T(8,128)S(1)}, u32[]{:S(2)}, u32[]{:S(2)}) collective-permute-start(f32[192,128]{1,0:T(8,128)S(1)} %get-tuple-element.177), channel_id=1, source_target_pairs={{0,8},{4,12},{8,0},{12,4},{16,24},{20,28},{24,16},{28,20},{1,9},{5... | collective-permute-start | bytes 294920 | tf_op jit(solution)/shard_map/ppermute | solution.py:625
  55.2 8.7 %collective-permute-start.17 = (f32[384,128]{1,0:T(8,128)S(1)}, f32[384,128]{1,0:T(8,128)S(1)}, u32[]{:S(2)}, u32[]{:S(2)}) collective-permute-start(f32[384,128]{1,0:T(8,128)S(1)} %get-tuple-element.174), channel_id=1, source_target_pairs={{0,1},{1,0},{2,3},{3,2},{4,5},{5,4},{6,7},{7,6},{8,9},{9,8},{10,11... | collective-permute-start | bytes 589832 | tf_op jit(solution)/shard_map/ppermute | solution.py:746
  64.0 16.1 %collective-permute-start.22 = (f32[1024,768]{1,0:T(8,128)S(1)}, f32[1024,768]{1,0:T(8,128)S(1)}, u32[]{:S(2)}, u32[]{:S(2)}) collective-permute-start(f32[1024,768]{1,0:T(8,128)S(1)} %get-tuple-element.189.own), channel_id=1, source_target_pairs={{0,1},{1,0},{2,3},{3,2},{4,5},{5,4},{6,7},{7,6},{8,9},{9,8},{10,11... | collective-permute-start | bytes 9437192 | tf_op jit(solution)/shard_map/ppermute | solution.py:752
  64.5 5.1 %collective-permute-start.23 = (f32[192,128]{1,0:T(8,128)S(1)}, f32[192,128]{1,0:T(8,128)S(1)}, u32[]{:S(2)}, u32[]{:S(2)}) collective-permute-start(f32[192,128]{1,0:T(8,128)S(1)} %get-tuple-element.190.refs_0_), channel_id=1, source_target_pairs={{0,8},{4,12},{8,0},{12,4},{16,24},{20,28},{24,16},{28,20},{1,9},{5... | collective-permute-start | bytes 294920 | tf_op jit(solution)/shard_map/ppermute | solution.py:625
  66.1 10.8 %collective-permute-start.25 = (f32[224,128]{1,0:T(8,128)S(1)}, f32[224,128]{1,0:T(8,128)S(1)}, u32[]{:S(2)}, u32[]{:S(2)}) collective-permute-start(f32[224,128]{1,0:T(8,128)S(1)} %get-tuple-element.193), channel_id=1, source_target_pairs={{0,4},{4,0},{8,12},{12,8},{16,20},{20,16},{24,28},{28,24},{1,5},{5... | collective-permute-start | bytes 344072 | tf_op jit(solution)/shard_map/ppermute | solution.py:625
  67.2 9.7 %collective-permute-start.26 = (f32[224,128]{1,0:T(8,128)S(1)}, f32[224,128]{1,0:T(8,128)S(1)}, u32[]{:S(2)}, u32[]{:S(2)}) collective-permute-start(f32[224,128]{1,0:T(8,128)S(1)} %get-tuple-element.194), channel_id=1, source_target_pairs={{0,8},{4,12},{8,0},{12,4},{16,24},{20,28},{24,16},{28,20},{1,9},{5... | collective-permute-start | bytes 344072 | tf_op jit(solution)/shard_map/ppermute | solution.py:625
  67.7 9.2 %collective-permute-start.27 = (f32[224,128]{1,0:T(8,128)S(1)}, f32[224,128]{1,0:T(8,128)S(1)}, u32[]{:S(2)}, u32[]{:S(2)}) collective-permute-start(f32[224,128]{1,0:T(8,128)S(1)} %get-tuple-element.195), channel_id=1, source_target_pairs={{0,12},{4,8},{8,4},{12,0},{16,28},{20,24},{24,20},{28,16},{1,13},{... | collective-permute-start | bytes 344072 | tf_op jit(solution)/shard_map/ppermute | solution.py:625
  69.6 7.3 %collective-permute-start.24 = (f32[192,128]{1,0:T(8,128)S(1)}, f32[192,128]{1,0:T(8,128)S(1)}, u32[]{:S(2)}, u32[]{:S(2)}) collective-permute-start(f32[192,128]{1,0:T(8,128)S(1)} %get-tuple-element.191.refs_2_), channel_id=1, source_target_pairs={{0,16},{4,20},{8,24},{12,28},{16,0},{20,4},{24,8},{28,12},{1,17},{... | collective-permute-start | bytes 294920 | tf_op jit(solution)/shard_map/ppermute | solution.py:625
  76.9 14.7 %collective-permute-start.28 = (f32[1024,512]{1,0:T(8,128)S(1)}, f32[1024,512]{1,0:T(8,128)S(1)}, u32[]{:S(2)}, u32[]{:S(2)}) collective-permute-start(f32[1024,512]{1,0:T(8,128)S(1)} %get-tuple-element.207.own), channel_id=1, source_target_pairs={{0,1},{1,0},{2,3},{3,2},{4,5},{5,4},{6,7},{7,6},{8,9},{9,8},{10,11... | collective-permute-start | bytes 6291464 | tf_op jit(solution)/shard_map/ppermute | solution.py:752
  77.0 10.1 %collective-permute-start.29 = (f32[384,128]{1,0:T(8,128)S(1)}, f32[384,128]{1,0:T(8,128)S(1)}, u32[]{:S(2)}, u32[]{:S(2)}) collective-permute-start(f32[384,128]{1,0:T(8,128)S(1)} %get-tuple-element.208.refs_0_), channel_id=1, source_target_pairs={{0,4},{4,0},{8,12},{12,8},{16,20},{20,16},{24,28},{28,24},{1,5},{5... | collective-permute-start | bytes 589832 | tf_op jit(solution)/shard_map/ppermute | solution.py:625
  78.3 8.8 %collective-permute-start.31 = (f32[224,128]{1,0:T(8,128)S(1)}, f32[224,128]{1,0:T(8,128)S(1)}, u32[]{:S(2)}, u32[]{:S(2)}) collective-permute-start(f32[224,128]{1,0:T(8,128)S(1)} %get-tuple-element.210.refs_4_), channel_id=1, source_target_pairs={{0,16},{4,20},{8,24},{12,28},{16,0},{20,4},{24,8},{28,12},{1,17},{... | collective-permute-start | bytes 344072 | tf_op jit(solution)/shard_map/ppermute | solution.py:625
  80.1 7.0 %collective-permute-start.30 = (f32[192,128]{1,0:T(8,128)S(1)}, f32[192,128]{1,0:T(8,128)S(1)}, u32[]{:S(2)}, u32[]{:S(2)}) collective-permute-start(f32[192,128]{1,0:T(8,128)S(1)} %get-tuple-element.209.refs_2_), channel_id=1, source_target_pairs={{0,8},{4,12},{8,0},{12,4},{16,24},{20,28},{24,16},{28,20},{1,9},{5... | collective-permute-start | bytes 294920 | tf_op jit(solution)/shard_map/ppermute | solution.py:625
  87.2 11.4 %collective-permute-start.32 = (f32[384,128]{1,0:T(8,128)S(1)}, f32[384,128]{1,0:T(8,128)S(1)}, u32[]{:S(2)}, u32[]{:S(2)}) collective-permute-start(f32[384,128]{1,0:T(8,128)S(1)} %get-tuple-element.215.refs_1_), channel_id=1, source_target_pairs={{0,4},{4,0},{8,12},{12,8},{16,20},{20,16},{24,28},{28,24},{1,5},{5... | collective-permute-start | bytes 589832 | tf_op jit(solution)/shard_map/ppermute | solution.py:625
  88.1 10.4 %collective-permute-start.33 = (f32[224,128]{1,0:T(8,128)S(1)}, f32[224,128]{1,0:T(8,128)S(1)}, u32[]{:S(2)}, u32[]{:S(2)}) collective-permute-start(f32[224,128]{1,0:T(8,128)S(1)} %get-tuple-element.216.refs_3_), channel_id=1, source_target_pairs={{0,4},{4,0},{8,12},{12,8},{16,20},{20,16},{24,28},{28,24},{1,5},{5... | collective-permute-start | bytes 344072 | tf_op jit(solution)/shard_map/ppermute | solution.py:625
  89.3 9.3 %collective-permute-start.34 = (f32[224,128]{1,0:T(8,128)S(1)}, f32[224,128]{1,0:T(8,128)S(1)}, u32[]{:S(2)}, u32[]{:S(2)}) collective-permute-start(f32[224,128]{1,0:T(8,128)S(1)} %get-tuple-element.216.refs_3_), channel_id=1, source_target_pairs={{0,8},{4,12},{8,0},{12,4},{16,24},{20,28},{24,16},{28,20},{1,9},{5... | collective-permute-start | bytes 344072 | tf_op jit(solution)/shard_map/ppermute | solution.py:625
  89.6 8.9 %collective-permute-start.35 = (f32[224,128]{1,0:T(8,128)S(1)}, f32[224,128]{1,0:T(8,128)S(1)}, u32[]{:S(2)}, u32[]{:S(2)}) collective-permute-start(f32[224,128]{1,0:T(8,128)S(1)} %get-tuple-element.216.refs_3_), channel_id=1, source_target_pairs={{0,12},{4,8},{8,4},{12,0},{16,28},{20,24},{24,20},{28,16},{1,13},{... | collective-permute-start | bytes 344072 | tf_op jit(solution)/shard_map/ppermute | solution.py:625
  (6 other events, 22.7 us)

commit v5 on v4

--- a/solution.py
+++ b/solution.py
@@ -16,14 +16,14 @@
 WIDE = D + H
 LANES = 128
 TOKEN = (8, LANES)
-RB = 512
+RB = 1024
 ROW_BLOCK = 256
 SUB = 256
 LAG = 1
 EPSILON = 1e-05
 GROUPS = ((0, 1), (2, 3), (4,), (5,))
 UNITS = ((0,), (1,), (2, 3))
-WIDTH = (1, 1, 2)
+WAY = ("single", "single", "pair")
 PLAN = (
     ("small", "fetch", ()),
     ("experts", 0, ()),
@@ -33,17 +33,17 @@
     ("experts", 1, ()),
     ("small", "send fetch", (0,)),
     ("events", (1,), ()),
-    ("small", "", (1,)),
+    ("small", "", (0, 1)),
     ("experts", 2, ()),
     ("small", "send fetch", (0, 1)),
     ("experts", 3, ()),
     ("small", "send", (0, 1)),
     ("events", (2,), ()),
-    ("small", "mix", (2,)),
+    ("small", "", (2,)),
     ("events", (3,), ()),
-    ("small", "grad", (0, 1, 2)),
+    ("small", "mix grad", (0, 1, 2)),
+    ("small", "", (1, 2)),
     ("place", None, ()),
-    ("small", "", (0, 1, 2)),
     ("place", None, ()),
 )
 COLUMN = (
@@ -145,21 +145,25 @@
 
 def payload_kernel(groups, vectors, n_deps, w_in, w_out, *refs):
     given = refs[:4] if vectors else ()
+    held = refs[-2]
     outs, sems = refs[len(given) + n_deps :][: len(groups)], refs[-1]
     copies = []
     for out, group in zip(outs, groups):
         experts_of, rows = pl.ds(group[0], len(group)), slice(0, SLICE)
         for part, lanes in ((w_in, slice(0, D)), (w_out, slice(D, WIDE))):
             copies.append(pltpu.make_async_copy(part.at[experts_of], out.at[:, rows, lanes], sems.at[len(copies)]))
+    for k, v in enumerate(given):
+        copies.append(pltpu.make_async_copy(v, held.at[k, slice(0, E), :], sems.at[len(copies)]))
     for copy in copies:
         copy.start()
     if vectors:
-        held = refs[-2]
-        for k, v in enumerate(given):
-            held[k * E : (k + 1) * E, :] = v[...]
+        for copy in copies[-len(given) :]:
+            copy.wait()
+        copies = copies[: -len(given)]
+        rows = jnp.concatenate([held[k, :E, :] for k in range(4)], axis=0)
         outs[0][:, SLICE:, :] = jnp.zeros((len(groups[0]), 8, WIDE), F32)
         for j in range(4 * E // 8):
-            outs[0][0, SLICE:, j * LANES : j * LANES + SLICE] = held[8 * j : 8 * j + 8, :]
+            outs[0][0, SLICE:, j * LANES : j * LANES + SLICE] = rows[8 * j : 8 * j + 8, :]
     for copy in copies:
         copy.wait()
 
@@ -169,10 +173,10 @@
     rows = SLICE + 8 if vectors else SLICE
     return pl.pallas_call(
         functools.partial(payload_kernel, groups, bool(vectors), len(deps)),
-        in_specs=[hbm, hbm] + [vmem] * len(vectors) + [pl.BlockSpec(memory_space=pl.ANY)] * len(deps),
+        in_specs=[hbm, hbm] + [hbm] * len(vectors) + [pl.BlockSpec(memory_space=pl.ANY)] * len(deps),
         out_specs=[vmem] * len(groups),
         out_shape=[pltpu.VMEM((len(group), rows, WIDE), F32) for group in groups],
-        scratch_shapes=[pltpu.VMEM((4 * E, SLICE), F32), pltpu.SemaphoreType.DMA((2 * len(groups),))],
+        scratch_shapes=[pltpu.VMEM((4, 8, SLICE), F32), pltpu.SemaphoreType.DMA((2 * len(groups) + 4,))],
         compiler_params=params(SMALL_MIB),
         cost_estimate=pl.CostEstimate(flops=0, bytes_accessed=SLICE * WIDE * 16, transcendentals=0),
     )(in_hbm(w_in), in_hbm(w_out), *[in_hbm(v) for v in vectors], *deps)
@@ -559,18 +563,38 @@
     return ref.at[pl.ds(pl.multiple_of(index * rows, 8), rows), :]
 
 
+class Piece:
+    def __init__(self, array, at=0, rows=None):
+        self.array, self.at = array, at
+        self.rows = array.shape[0] if rows is None else rows
+
+    def of(self, ref):
+        return ref.at[pl.ds(self.at, self.rows), :]
+
+
+def bit_groups(bits, width):
+    groups, start = [], 0
+    while bits - start > width:
+        groups.append((start, width))
+        start += width
+    return groups, (start, bits - start)
+
+
 class Reduction:
-    def __init__(self, own, got, n_dp, width):
-        self.own, self.got = own, got
-        left, start = n_dp.bit_length() - 1, 0
-        self.groups = []
-        while left > width:
-            self.groups.append((start, width))
-            start, left = start + width, left - width
-        self.scattered = len(self.groups)
-        self.order = [*self.groups, (start, left), *reversed(self.groups)]
-        unit = 8 << start
-        self.rows = -(-sum(v.shape[0] for v in own) // unit) * unit
+    def __init__(self, own, got, n_dp, kind):
+        self.keep, self.got = [Piece(v) for v in own], [Piece(v) for v in got]
+        pairs, last = bit_groups(n_dp.bit_length() - 1, 2)
+        singles, lone = bit_groups(n_dp.bit_length() - 1, 1)
+        if kind == "single":
+            scatter, last, gather = singles, lone, singles
+        elif kind == "pair":
+            scatter, gather = pairs, pairs
+        else:
+            scatter, gather = [(b + k, 1) for b, n in pairs for k in reversed(range(n))], pairs
+        self.order = [*scatter, last, *reversed(gather)]
+        self.scattered = len(scatter)
+        unit = 8 << sum(n for _, n in scatter)
+        self.rows = -(-sum(p.rows for p in self.keep) // unit) * unit
         self.n_dp = n_dp
         self.stage = 0
 
@@ -585,45 +609,61 @@
     def job(self):
         stage = self.stage
         gather, scatter = stage > self.scattered + 1, stage < self.scattered
-        keeps = self.own if stage == 0 else [self.keep]
-        args = [*keeps, *self.got]
+        n = len(self.keep)
+        pieces = [*self.keep, *self.got]
         came = self.order[stage - 1]
         goes = self.order[stage] if stage < len(self.order) else None
-        rows = self.rows if stage == 0 else self.keep.shape[0] * ((1 << came[1]) if gather else 1)
+        rows = self.rows if stage == 0 else self.keep[0].rows * ((1 << came[1]) if gather else 1)
         parts = 1 << goes[1] if scatter else 1
 
         def body(ins, outs, scratch):
+            ins = [p.of(ref) for p, ref in zip(pieces, ins)]
             to = scratch[0] if scatter else outs[0]
             if gather:
                 join(ins, to, came)
                 return
             at = 0
-            for k, a in enumerate(keeps):
+            for k, piece in enumerate(pieces[:n]):
                 total = ins[k][...]
-                for v in ins[k + len(keeps) :: len(keeps)]:
+                for v in ins[k + n :: n]:
                     total = total + v[...]
-                to[at : at + a.shape[0], :] = total
-                at += a.shape[0]
+                to[at : at + piece.rows, :] = total
+                at += piece.rows
             if at < rows:
-                to[at:, :] = jnp.zeros((rows - at, LANES), F32)
+                to[at:rows, :] = jnp.zeros((rows - at, LANES), F32)
             if scatter:
                 side = side_of(goes)
                 for m in range(parts):
                     outs[m][...] = part_of(to, side ^ m, rows // parts)[...]
 
+        arrays = [p.array for p in pieces]
         if scatter:
-            return Job(args, [(rows // parts, LANES)] * parts, body, [pltpu.VMEM((rows, LANES), F32)])
-        return Job(args, [(rows, LANES)], body)
+            return Job(arrays, [(rows // parts, LANES)] * parts, body, [pltpu.VMEM((rows, LANES), F32)])
+        return Job(arrays, [(rows, LANES)], body)
 
     def take(self, outs):
-        self.keep = outs[0]
-        if self.stage < len(self.order):
-            start, bits = self.order[self.stage]
-            self.got = []
-            for m in range(1, 1 << bits):
-                v = outs[m] if self.stage < self.scattered else outs[0]
-                self.got.append(lax.ppermute(v, "dp", [(i, i ^ (m << start)) for i in range(self.n_dp)]))
         self.stage += 1
+        self.keep = [Piece(outs[0])]
+        if self.stage <= len(self.order):
+            sent = outs[1:] if self.stage <= self.scattered else None
+            self.got = [Piece(v) for v in exchange(outs[0], sent, self.order[self.stage - 1], self.n_dp)]
+
+    @staticmethod
+    def take_together(units, out, rows):
+        at = 0
+        came = exchange(out, None, units[0].order[units[0].stage], units[0].n_dp)
+        for unit, n in zip(units, rows):
+            unit.stage += 1
+            unit.keep, unit.got = [Piece(out, at, n)], [Piece(v, at, n) for v in came]
+            at += n
+
+
+def exchange(whole, parts, bits, n_dp):
+    start, n = bits
+    return [
+        lax.ppermute(whole if parts is None else parts[m - 1], "dp", [(i, i ^ (m << start)) for i in range(n_dp)])
+        for m in range(1, 1 << n)
+    ]
 
 
 def side_of(bits):
@@ -633,20 +673,31 @@
 def join(ins, to, bits):
     for m, v in enumerate(ins):
         part_of(to, side_of(bits) ^ m, v.shape[0])[...] = v[...]
+
+
+def together(jobs):
+    rows = [job.shapes[0].shape[0] for job in jobs]
+
+    def body(ins, outs, scratch):
+        at = i = 0
+        for job, n in zip(jobs, rows):
+            job.body(ins[i : i + len(job.args)], [outs[0].at[pl.ds(at, n), :]], [])
+            i, at = i + len(job.args), at + n
+
+    return Job([a for job in jobs for a in job.args], [(sum(rows), LANES)], body), rows
 
 
 def finish_body(joining, ins, outs, both):
     in_grad, in_bias, out_grad, out_bias, gain, shift, gate = outs
     odd = (lax.axis_index("tp") & 1) == 1
     ins, both, summed = list(ins), list(both), []
-    for bits in joining:
+    for bits, pieces in joining:
+        parts = [piece.of(ins.pop(0)) for piece in pieces]
         if bits:
-            n = 1 << bits[1]
-            join(ins[:n], both[0], bits)
+            join(parts, both[0], bits)
             summed.append(both.pop(0))
-            del ins[:n]
         else:
-            summed.append(ins.pop(0))
+            summed.append(parts[0])
     for u, unit in enumerate(UNITS):
         at = 0
         for g in unit:
@@ -720,7 +771,9 @@
             placed.append(v)
             deps = [token]
         else:
-            jobs = [summing[u].job() for u in units]
+            joint = units if "joint" in what else ()
+            alone = () if joint else units
+            jobs = [summing[u].job() for u in alone]
             sent, fetched, through = [], [], []
             if "send" in what:
                 sent = [made[-1][7]] + ([made[-1][8]] if len(made) == len(GROUPS) else [])
@@ -733,9 +786,14 @@
                 through.append(mix)
             if "grad" in what:
                 through.append(x_grad)
+            if joint:
+                job, rows_of = together([summing[u].job() for u in joint])
+                jobs.append(job)
             outs, through, token = run(jobs, deps, through)
             deps = [token]
-            for u, o in zip(units, outs):
+            if joint:
+                Reduction.take_together([summing[u] for u in joint], outs.pop()[0], rows_of)
+            for u, o in zip(alone, outs):
                 summing[u].take(o)
             if fetched:
                 relayed.append(lax.ppermute(outs[-1][0], "tp", core))
@@ -743,12 +801,12 @@
                     far.append(lax.ppermute(outs[-1][1], "tp", across))
                     beside.append(lax.ppermute(outs[-1][1], "tp", core))
             if sent:
-                got = [lax.ppermute(v, "tp", core) for v in outs[len(units)]]
+                got = [lax.ppermute(v, "tp", core) for v in outs[len(alone)]]
                 partial.append(([made[-1][6], *sent[1:]], got))
-                for u, (unit, width) in enumerate(zip(UNITS, WIDTH)):
+                for u, (unit, way) in enumerate(zip(UNITS, WAY)):
                     if unit[-1] == len(partial) - 1:
                         both = [partial[g] for g in unit]
-                        summing[u] = Reduction([v for b in both for v in b[0]], [v for b in both for v in b[1]], n_dp, width)
+                        summing[u] = Reduction([v for b in both for v in b[0]], [v for b in both for v in b[1]], n_dp, way)
             unplaced += [(v, lax.ppermute(v, "tp", core)) for v in through]
     mixtures, x_grad = placed
     summing = [summing[u] for u in range(len(UNITS))]
@@ -758,8 +816,8 @@
         deps = [token]
         for u, o in zip(ours, outs):
             u.take(o)
-    joining = [u.order[-1] if u.joining else None for u in summing]
-    halves = [v for u in summing for v in ([u.keep, *u.got] if u.joining else [u.keep])]
+    joining = [(u.order[-1], [*u.keep, *u.got]) if u.joining else (None, u.keep) for u in summing]
+    halves = [p.array for _, pieces in joining for p in pieces]
     per_expert = (E, SLICE)
     shapes = [(E, SLICE, D), per_expert, (E, SLICE, H), per_expert, per_expert, per_expert, (GATE_COLS, D)]
     scratch = [pltpu.VMEM((u.rows, LANES), F32) for u in summing if u.joining]

time: 100 us -> 97.6 us (0.976)
  waiting for transfers between devices: 17.7 us -> 14.9 us
  starting transfers between devices: 30.8 us -> 33.5 us
  Pallas kernels: 50.2 us -> 48 us
    ppermute x22, starting transfers between devices: 21.8 us -> 24.7 us  [the longest x17 23.9 us: exchange(): lax.ppermute(whole if parts is None else parts[m - 1], 'dp', [(i, i ^ m <...]
    ppermute x22, waiting for transfers between devices: 13.7 us -> 10.9 us  [the longest x17 10.9 us: exchange(): lax.ppermute(whole if parts is None else parts[m - 1], 'dp', [(i, i ^ m <...]
    pallas_call x4, Pallas kernels: 27.3 us -> 25.5 us  [experts(): pl.pallas_call(functools.partial(expert_kernel, group, first, last, len(d...]
  transfers between devices with their start and end apart: 36 -> 36, of which waited for: 5 -> 8; matrix products, arithmetic and copies ran while one was open for 0% -> 0% of each run, Pallas kernels for 47% -> 47%
where the time goes in v5:
time: 97.6 us; the launch traced here: 97.3 us
  Pallas kernels  48 us (49%)
  starting transfers between devices  33.5 us (34%)
  waiting for transfers between devices  14.9 us (15%)
    pallas_call x4, Pallas kernels, experts(): pl.pallas_call(functools.partial(expert_kernel, group, first, last, len(d...  25.5 us
    ppermute x17, starting transfers between devices, exchange(): lax.ppermute(whole if parts is None else parts[m - 1], 'dp', [(i, i ^ m <...  23.9 us
    ppermute x17, waiting for transfers between devices, exchange(): lax.ppermute(whole if parts is None else parts[m - 1], 'dp', [(i, i ^ m <...  10.9 us
    pallas_call x4, Pallas kernels, event_grads(): pl.pallas_call(functools.partial(event_kernel, len(highs), bool(gating),...  8.61 us
    pallas_call x1, Pallas kernels, gates(): pl.pallas_call(functools.partial(gate_kernel, len(deps)), in_specs=[pl.Bl...  4.97 us
    pallas_call x2, Pallas kernels, place(): pl.pallas_call(place_kernel, in_specs=[anywhere] * (2 + len(deps)), out_s...  4.75 us
    ppermute x1, waiting for transfers between devices, per_device(): far = [lax.ppermute(own[0], 'tp', across)]  3.95 us
    ppermute x3, starting transfers between devices, per_device(): far.append(lax.ppermute(outs[-1][1], 'tp', across))  3.85 us
  transfers between devices with their start and end apart: 36, of which 8 were waited for; matrix products, arithmetic and copies ran while one was open for 0% of the time, Pallas kernels for 47%

profile of v5, /device:TPU:0, one launch (start us, length us, event | category | flops | bytes accessed | tf_op | source)
XLA Modules:
  0.0 97.3 jit_solution(7779010392584527682)
XLA Ops:
  1.7 3.0 %collective-permute-start.1 = (f32[2,72,768]{2,1,0:T(8,128)S(1)}, f32[2,72,768]{2,1,0:T(8,128)S(1)}, u32[]{:S(2)}, u32[]{:S(2)}) collective-permute-start(f32[2,72,768]{2,1,0:T(8,128)S(1)} %shard_map.169.refs_0_.refs_4_), channel_id=1, source_target_pairs={{0,2},{1,3},{2,0},{3,1},{4,6},{5,7},{6,4},{7,5},{8,10},{9,11},{10,... | collective-permute-start | bytes 1327112 | tf_op jit(solution)/shard_map/ppermute | solution.py:744
  4.7 1.2 %shard_map.170 = (f32[2,64,768]{2,1,0:T(8,128)S(1)}, f32[1,64,768]{2,1,0:T(8,128)S(1)}, f32[1,64,768]{2,1,0:T(8,128)S(1)}) custom-call(f32[6,64,512]{2,1,0:T(8,128)} %bitcast.9, f32[6,64,256]{2,1,0:T(8,128)} %bitcast.11, f32[2,72,768]{2,1,0:T(8,128)S(1)} %shard_map.169.refs_0_.refs_4_), custom_call_target="tpu_custom_call" | custom-call | bytes 786432 | tf_op jit(solution)/shard_map/pallas_call | solution.py:174
  6.0 5.0 %shard_map.171 = (bf16[1024,512]{1,0:T(8,128)(2,1)S(1)}, bf16[1024,512]{1,0:T(8,128)(2,1)S(1)}, f32[1024,128]{1,0:T(8,128)S(1)}, f32[1024,768]{1,0:T(8,128)S(1)}) custom-call(s32[8]{0:T(128)S(1)} %copy-done.1, f32[2048,512]{1,0:T(8,128)} %ev_ref.1, f32[2048,768]{1,0:T(8,128)} %cot_ref.1, f32[14,512]{1,0:T(8,128)} %bitcast.6, ...), custom_call_target="tpu_custom_call" | custom-call | flops 402653184 | bytes 4194304 | tf_op jit(solution)/shard_map/pallas_call | solution.py:125
  11.0 3.9 %collective-permute-done.1.refs_0_.refs_6_ = f32[2,72,768]{2,1,0:T(8,128)S(1)} collective-permute-done((f32[2,72,768]{2,1,0:T(8,128)S(1)}, f32[2,72,768]{2,1,0:T(8,128)S(1)}, u32[]{:S(2)}, u32[]{:S(2)}) %collective-permute-start.1) | collective-permute-done | bytes 442400 | tf_op jit(solution)/shard_map/ppermute | solution.py:744
  15.0 1.8 %collective-permute-start.4 = (f32[2,64,768]{2,1,0:T(8,128)S(1)}, f32[2,64,768]{2,1,0:T(8,128)S(1)}, u32[]{:S(2)}, u32[]{:S(2)}) collective-permute-start(f32[2,64,768]{2,1,0:T(8,128)S(1)} %get-tuple-element.128), channel_id=1, source_target_pairs={{0,2},{1,3},{2,0},{3,1},{4,6},{5,7},{6,4},{7,5},{8,10},{9,11},{10,... | collective-permute-start | bytes 1179656 | tf_op jit(solution)/shard_map/ppermute | solution.py:801
  16.9 7.3 %shard_map.173 = (f32[1024,768]{1,0:T(8,128)S(1)}, f32[1024,128]{1,0:T(8,128)S(1)}, bf16[1024,512]{1,0:T(8,128)(2,1)S(1)}, bf16[1024,512]{1,0:T(8,128)(2,1)S(1)}...) custom-call(bf16[1024,512]{1,0:T(8,128)(2,1)S(1)} %get-tuple-element, ...), custom_call_target="tpu_custom_call" | custom-call | flops 8858370048 | bytes 14336000 | tf_op jit(solution)/shard_map/pallas_call | solution.py:404
  24.8 2.3 %shard_map.175 = (f32[1024,512]{1,0:T(8,128)S(1)}, f32[8,128]{1,0:T(8,128)S(1)}) custom-call(bf16[1024,512]{1,0:T(8,128)(2,1)S(1)} %get-tuple-element.130.refs_0_, bf16[1024,512]{1,0:T(8,128)(2,1)S(1)} %get-tuple-element.131.refs_1_, bf16[512,512]{1,0:T(8,128)(2,1)S(1)} %get-tuple-element.132.refs_2_, bf16[512,512]{1,0:T(8,128)(2,1)S(1)} %get-tuple-element.133.refs_3_, ...), custom_call_target="tpu_custom_call" | custom-call | flops 1610612736 | bytes 4096000 | tf_op jit(solution)/shard_map/pallas_call | solution.py:469
  27.5 1.7 %collective-permute-start.5 = (f32[384,128]{1,0:T(8,128)S(1)}, f32[384,128]{1,0:T(8,128)S(1)}, u32[]{:S(2)}, u32[]{:S(2)}) collective-permute-start(f32[384,128]{1,0:T(8,128)S(1)} %get-tuple-element.137), channel_id=1, source_target_pairs={{0,4},{4,0},{8,12},{12,8},{16,20},{20,16},{24,28},{28,24},{1,5},{5... | collective-permute-start | bytes 589832 | tf_op jit(solution)/shard_map/ppermute | solution.py:664
  29.1 1.5 %collective-permute-start.8 = (f32[1,64,768]{2,1,0:T(8,128)S(1)}, f32[1,64,768]{2,1,0:T(8,128)S(1)}, u32[]{:S(2)}, u32[]{:S(2)}) collective-permute-start(f32[1,64,768]{2,1,0:T(8,128)S(1)} %get-tuple-element.143), channel_id=1, source_target_pairs={{0,2},{1,3},{2,0},{3,1},{4,6},{5,7},{6,4},{7,5},{8,10},{9,11},{10,... | collective-permute-start | bytes 589832 | tf_op jit(solution)/shard_map/ppermute | solution.py:801
  30.6 7.8 %shard_map.177 = (f32[1024,768]{1,0:T(8,128)S(1)}, f32[1024,128]{1,0:T(8,128)S(1)}, bf16[1024,512]{1,0:T(8,128)(2,1)S(1)}, bf16[1024,512]{1,0:T(8,128)(2,1)S(1)}...) custom-call(bf16[1024,512]{1,0:T(8,128)(2,1)S(1)} %get-tuple-element, ...), custom_call_target="tpu_custom_call", output_to_operand_aliasing={{0}: (9, {})} | custom-call | flops 8858370048 | bytes 14336000 | tf_op jit(solution)/shard_map/pallas_call | solution.py:404
  39.3 1.6 %collective-permute-start.9 = (f32[192,128]{1,0:T(8,128)S(1)}, f32[192,128]{1,0:T(8,128)S(1)}, u32[]{:S(2)}, u32[]{:S(2)}) collective-permute-start(f32[192,128]{1,0:T(8,128)S(1)} %get-tuple-element.147), channel_id=1, source_target_pairs={{0,8},{4,12},{8,0},{12,4},{16,24},{20,28},{24,16},{28,20},{1,9},{5... | collective-permute-start | bytes 294920 | tf_op jit(solution)/shard_map/ppermute | solution.py:664
  41.4 2.5 %shard_map.179 = (f32[1024,512]{1,0:T(8,128)S(1)}, f32[8,128]{1,0:T(8,128)S(1)}) custom-call(bf16[1024,512]{1,0:T(8,128)(2,1)S(1)} %get-tuple-element.150.refs_0_, bf16[1024,512]{1,0:T(8,128)(2,1)S(1)} %get-tuple-element.151.refs_1_, bf16[512,512]{1,0:T(8,128)(2,1)S(1)} %get-tuple-element.152.refs_2_, ...), custom_call_target="tpu_custom_call", output_to_operand_aliasing={{0}: (4, {})} | custom-call | flops 1610612736 | bytes 4096000 | tf_op jit(solution)/shard_map/pallas_call | solution.py:469
  45.3 2.6 %collective-permute-start.11 = (f32[192,128]{1,0:T(8,128)S(1)}, f32[192,128]{1,0:T(8,128)S(1)}, u32[]{:S(2)}, u32[]{:S(2)}) collective-permute-start(f32[192,128]{1,0:T(8,128)S(1)} %get-tuple-element.157.refs_0_), channel_id=1, source_target_pairs={{0,16},{4,20},{8,24},{12,28},{16,0},{20,4},{24,8},{28,12},{1,17},{... | collective-permute-start | bytes 294920 | tf_op jit(solution)/shard_map/ppermute | solution.py:664
  47.9 4.6 %shard_map.181 = (f32[1024,768]{1,0:T(8,128)S(1)}, f32[1024,128]{1,0:T(8,128)S(1)}, bf16[1024,256]{1,0:T(8,128)(2,1)S(1)}, bf16[1024,256]{1,0:T(8,128)(2,1)S(1)}...) custom-call(bf16[1024,512]{1,0:T(8,128)(2,1)S(1)} %get-tuple-element, ...), custom_call_target="tpu_custom_call", output_to_operand_aliasing={{0}: (9, {})} | custom-call | flops 4429185024 | bytes 14336000 | tf_op jit(solution)/shard_map/pallas_call | solution.py:404
  54.1 1.3 %collective-permute-start.17 = (f32[192,128]{1,0:T(8,128)S(1)}, f32[192,128]{1,0:T(8,128)S(1)}, u32[]{:S(2)}, u32[]{:S(2)}) collective-permute-start(f32[192,128]{1,0:T(8,128)S(1)} %get-tuple-element.168), channel_id=1, source_target_pairs={{0,8},{4,12},{8,0},{12,4},{16,24},{20,28},{24,16},{28,20},{1,9},{5... | collective-permute-start | bytes 294920 | tf_op jit(solution)/shard_map/ppermute | solution.py:664
  55.4 5.8 %shard_map.183 = (f32[1024,768]{1,0:T(8,128)S(1)}, f32[1024,128]{1,0:T(8,128)S(1)}, bf16[1024,256]{1,0:T(8,128)(2,1)S(1)}, bf16[1024,256]{1,0:T(8,128)(2,1)S(1)}...) custom-call(bf16[1024,512]{1,0:T(8,128)(2,1)S(1)} %get-tuple-element, ...), custom_call_target="tpu_custom_call", output_to_operand_aliasing={{0}: (9, {})} | custom-call | flops 4429185024 | bytes 14336000 | tf_op jit(solution)/shard_map/pallas_call | solution.py:404
  61.9 1.3 %collective-permute-start.20 = (f32[384,128]{1,0:T(8,128)S(1)}, f32[384,128]{1,0:T(8,128)S(1)}, u32[]{:S(2)}, u32[]{:S(2)}) collective-permute-start(f32[384,128]{1,0:T(8,128)S(1)} %get-tuple-element.177.refs_0_), channel_id=1, source_target_pairs={{0,4},{4,0},{8,12},{12,8},{16,20},{20,16},{24,28},{28,24},{1,5},{5... | collective-permute-start | bytes 589832 | tf_op jit(solution)/shard_map/ppermute | solution.py:664
  63.2 1.5 %shard_map.185 = (f32[1024,512]{1,0:T(8,128)S(1)}, f32[8,128]{1,0:T(8,128)S(1)}) custom-call(bf16[1024,256]{1,0:T(8,128)(2,1)S(1)} %get-tuple-element.184.refs_0_, bf16[1024,256]{1,0:T(8,128)(2,1)S(1)} %get-tuple-element.185.refs_1_, bf16[256,512]{1,0:T(8,128)(2,1)S(1)} %get-tuple-element.186.refs_2_, ...), custom_call_target="tpu_custom_call", output_to_operand_aliasing={{0}: (4, {})} | custom-call | flops 805306368 | bytes 4096000 | tf_op jit(solution)/shard_map/pallas_call | solution.py:469
  66.3 2.1 %collective-permute-start.27 = (f32[224,128]{1,0:T(8,128)S(1)}, f32[224,128]{1,0:T(8,128)S(1)}, u32[]{:S(2)}, u32[]{:S(2)}) collective-permute-start(f32[224,128]{1,0:T(8,128)S(1)} %get-tuple-element.194), channel_id=1, source_target_pairs={{0,12},{4,8},{8,4},{12,0},{16,28},{20,24},{24,20},{28,16},{1,13},{... | collective-permute-start | bytes 344072 | tf_op jit(solution)/shard_map/ppermute | solution.py:664
  68.4 2.1 %collective-permute-start.21 = (f32[192,128]{1,0:T(8,128)S(1)}, f32[192,128]{1,0:T(8,128)S(1)}, u32[]{:S(2)}, u32[]{:S(2)}) collective-permute-start(f32[192,128]{1,0:T(8,128)S(1)} %get-tuple-element.178.refs_2_), channel_id=1, source_target_pairs={{0,16},{4,20},{8,24},{12,28},{16,0},{20,4},{24,8},{28,12},{1,17},{... | collective-permute-start | bytes 294920 | tf_op jit(solution)/shard_map/ppermute | solution.py:664
  70.5 2.3 %shard_map.187 = (f32[1024,512]{1,0:T(8,128)S(1)}, f32[8,128]{1,0:T(8,128)S(1)}) custom-call(bf16[1024,256]{1,0:T(8,128)(2,1)S(1)} %get-tuple-element.196.refs_0_, bf16[1024,256]{1,0:T(8,128)(2,1)S(1)} %get-tuple-element.197.refs_1_, bf16[256,512]{1,0:T(8,128)(2,1)S(1)} %get-tuple-element.198.refs_2_, ...), custom_call_target="tpu_custom_call", output_to_operand_aliasing={{0}: (6, {})} | custom-call | flops 805306368 | bytes 4096000 | tf_op jit(solution)/shard_map/pallas_call | solution.py:469
  72.8 1.1 %collective-permute-done.21.refs_3_ = f32[192,128]{1,0:T(8,128)S(1)} collective-permute-done((f32[192,128]{1,0:T(8,128)S(1)}, f32[192,128]{1,0:T(8,128)S(1)}, u32[]{:S(2)}, u32[]{:S(2)}) %collective-permute-start.21) | collective-permute-done | bytes 98336 | tf_op jit(solution)/shard_map/ppermute | solution.py:664
  73.9 2.3 %collective-permute-done.27.refs_7_ = f32[224,128]{1,0:T(8,128)S(1)} collective-permute-done((f32[224,128]{1,0:T(8,128)S(1)}, f32[224,128]{1,0:T(8,128)S(1)}, u32[]{:S(2)}, u32[]{:S(2)}) %collective-permute-start.27) | collective-permute-done | bytes 114720 | tf_op jit(solution)/shard_map/ppermute | solution.py:664
  77.9 3.1 %collective-permute-start.29 = (f32[192,128]{1,0:T(8,128)S(1)}, f32[192,128]{1,0:T(8,128)S(1)}, u32[]{:S(2)}, u32[]{:S(2)}) collective-permute-start(f32[192,128]{1,0:T(8,128)S(1)} %get-tuple-element.206.refs_0_), channel_id=1, source_target_pairs={{0,8},{4,12},{8,0},{12,4},{16,24},{20,28},{24,16},{28,20},{1,9},{5... | collective-permute-start | bytes 294920 | tf_op jit(solution)/shard_map/ppermute | solution.py:664
  80.9 3.3 %collective-permute-done.29.refs_1_ = f32[192,128]{1,0:T(8,128)S(1)} collective-permute-done((f32[192,128]{1,0:T(8,128)S(1)}, f32[192,128]{1,0:T(8,128)S(1)}, u32[]{:S(2)}, u32[]{:S(2)}) %collective-permute-start.29) | collective-permute-done | bytes 98336 | tf_op jit(solution)/shard_map/ppermute | solution.py:664
  84.2 1.2 %collective-permute-done.30.refs_3_ = f32[224,128]{1,0:T(8,128)S(1)} collective-permute-done((f32[224,128]{1,0:T(8,128)S(1)}, f32[224,128]{1,0:T(8,128)S(1)}, u32[]{:S(2)}, u32[]{:S(2)}) %collective-permute-start.30) | collective-permute-done | bytes 114720 | tf_op jit(solution)/shard_map/ppermute | solution.py:664
  86.0 1.5 %collective-permute-start.33 = (f32[224,128]{1,0:T(8,128)S(1)}, f32[224,128]{1,0:T(8,128)S(1)}, u32[]{:S(2)}, u32[]{:S(2)}) collective-permute-start(f32[224,128]{1,0:T(8,128)S(1)} %get-tuple-element.216.refs_3_), channel_id=1, source_target_pairs={{0,4},{4,0},{8,12},{12,8},{16,20},{20,16},{24,28},{28,24},{1,5},{5... | collective-permute-start | bytes 344072 | tf_op jit(solution)/shard_map/ppermute | solution.py:664
  87.7 1.8 %collective-permute-start.35 = (f32[224,128]{1,0:T(8,128)S(1)}, f32[224,128]{1,0:T(8,128)S(1)}, u32[]{:S(2)}, u32[]{:S(2)}) collective-permute-start(f32[224,128]{1,0:T(8,128)S(1)} %get-tuple-element.216.refs_3_), channel_id=1, source_target_pairs={{0,12},{4,8},{8,4},{12,0},{16,28},{20,24},{24,20},{28,16},{1,13},{... | collective-permute-start | bytes 344072 | tf_op jit(solution)/shard_map/ppermute | solution.py:664
  89.5 2.7 %shard_map.190 = (f32[2048,768]{1,0:T(8,128)}, f32[8,128]{1,0:T(8,128)S(1)}) custom-call(f32[1024,768]{1,0:T(8,128)S(1)} %get-tuple-element.205.own, f32[1024,768]{1,0:T(8,128)S(1)} %collective-permute-done.28.other, f32[8,128]{1,0:T(8,128)S(1)} %get-tuple-element.209.refs_0_), custom_call_target="tpu_custom_call" | custom-call | bytes 12582912 | tf_op jit(solution)/shard_map/pallas_call | solution.py:502
  92.3 2.0 %shard_map.191 = (f32[2048,512]{1,0:T(8,128)}, f32[8,128]{1,0:T(8,128)S(1)}) custom-call(f32[1024,512]{1,0:T(8,128)S(1)} %get-tuple-element.211.own, f32[1024,512]{1,0:T(8,128)S(1)} %collective-permute-done.31.other, f32[8,128]{1,0:T(8,128)S(1)} %get-tuple-element.212.refs_0_), custom_call_target="tpu_custom_call" | custom-call | bytes 8388608 | tf_op jit(solution)/shard_map/pallas_call | solution.py:502
  94.3 1.8 %collective-permute-done.33.refs_4_ = f32[224,128]{1,0:T(8,128)S(1)} collective-permute-done((f32[224,128]{1,0:T(8,128)S(1)}, f32[224,128]{1,0:T(8,128)S(1)}, u32[]{:S(2)}, u32[]{:S(2)}) %collective-permute-start.33) | collective-permute-done | bytes 114720 | tf_op jit(solution)/shard_map/ppermute | solution.py:664
  96.1 1.2 %shard_map.192 = (f32[6,64,512]{2,1,0:T(8,128)}, f32[6,64]{1,0:T(8,128)}, f32[6,64,256]{2,1,0:T(8,128)}, f32[6,64]{1,0:T(8,128)}, f32[6,64]{1,0:T(8,128)}, /*ind...) custom-call(f32[768,128]{1,0:T(8,128)S(1)} %get-tuple-element.214.refs_0_, ...), custom_call_target="tpu_custom_call" | custom-call | bytes 2490368 | tf_op jit(solution)/shard_map/pallas_call | solution.py:543
  (68 shorter events, 11.1 us)
Async XLA Ops:
  1.7 13.2 %collective-permute-start.1 = (f32[2,72,768]{2,1,0:T(8,128)S(1)}, f32[2,72,768]{2,1,0:T(8,128)S(1)}, u32[]{:S(2)}, u32[]{:S(2)}) collective-permute-start(f32[2,72,768]{2,1,0:T(8,128)S(1)} %shard_map.169.refs_0_.refs_4_), channel_id=1, source_target_pairs={{0,2},{1,3},{2,0},{3,1},{4,6},{5,7},{6,4},{7,5},{8,10},{9,11},{10,... | collective-permute-start | bytes 1327112 | tf_op jit(solution)/shard_map/ppermute | solution.py:744
  4.7 12.1 %collective-permute-start = (f32[2,72,768]{2,1,0:T(8,128)S(1)}, f32[2,72,768]{2,1,0:T(8,128)S(1)}, u32[]{:S(2)}, u32[]{:S(2)}) collective-permute-start(f32[2,72,768]{2,1,0:T(8,128)S(1)} %shard_map.169.refs_0_.refs_4_), channel_id=1, source_target_pairs={{0,1},{1,0},{2,3},{3,2},{4,5},{5,4},{6,7},{7,6},{8,9},{9,8},{10,11... | collective-permute-start | bytes 1327112 | tf_op jit(solution)/shard_map/ppermute | solution.py:745
  15.0 12.1 %collective-permute-start.4 = (f32[2,64,768]{2,1,0:T(8,128)S(1)}, f32[2,64,768]{2,1,0:T(8,128)S(1)}, u32[]{:S(2)}, u32[]{:S(2)}) collective-permute-start(f32[2,64,768]{2,1,0:T(8,128)S(1)} %get-tuple-element.128), channel_id=1, source_target_pairs={{0,2},{1,3},{2,0},{3,1},{4,6},{5,7},{6,4},{7,5},{8,10},{9,11},{10,... | collective-permute-start | bytes 1179656 | tf_op jit(solution)/shard_map/ppermute | solution.py:801
  24.5 6.2 %collective-permute-start.6 = (f32[2,64,768]{2,1,0:T(8,128)S(1)}, f32[2,64,768]{2,1,0:T(8,128)S(1)}, u32[]{:S(2)}, u32[]{:S(2)}) collective-permute-start(f32[2,64,768]{2,1,0:T(8,128)S(1)} %get-tuple-element.128), channel_id=1, source_target_pairs={{0,1},{1,0},{2,3},{3,2},{4,5},{5,4},{6,7},{7,6},{8,9},{9,8},{10,11... | collective-permute-start | bytes 1179656 | tf_op jit(solution)/shard_map/ppermute | solution.py:802
  27.2 3.4 %collective-permute-start.7 = (f32[2,64,768]{2,1,0:T(8,128)S(1)}, f32[2,64,768]{2,1,0:T(8,128)S(1)}, u32[]{:S(2)}, u32[]{:S(2)}) collective-permute-start(f32[2,64,768]{2,1,0:T(8,128)S(1)} %get-tuple-element.138), channel_id=1, source_target_pairs={{0,1},{1,0},{2,3},{3,2},{4,5},{5,4},{6,7},{7,6},{8,9},{9,8},{10,11... | collective-permute-start | bytes 1179656 | tf_op jit(solution)/shard_map/ppermute | solution.py:799
  27.5 11.0 %collective-permute-start.5 = (f32[384,128]{1,0:T(8,128)S(1)}, f32[384,128]{1,0:T(8,128)S(1)}, u32[]{:S(2)}, u32[]{:S(2)}) collective-permute-start(f32[384,128]{1,0:T(8,128)S(1)} %get-tuple-element.137), channel_id=1, source_target_pairs={{0,4},{4,0},{8,12},{12,8},{16,20},{20,16},{24,28},{28,24},{1,5},{5... | collective-permute-start | bytes 589832 | tf_op jit(solution)/shard_map/ppermute | solution.py:664
  29.1 9.4 %collective-permute-start.8 = (f32[1,64,768]{2,1,0:T(8,128)S(1)}, f32[1,64,768]{2,1,0:T(8,128)S(1)}, u32[]{:S(2)}, u32[]{:S(2)}) collective-permute-start(f32[1,64,768]{2,1,0:T(8,128)S(1)} %get-tuple-element.143), channel_id=1, source_target_pairs={{0,2},{1,3},{2,0},{3,1},{4,6},{5,7},{6,4},{7,5},{8,10},{9,11},{10,... | collective-permute-start | bytes 589832 | tf_op jit(solution)/shard_map/ppermute | solution.py:801
  38.6 5.8 %collective-permute-start.10 = (f32[768,128]{1,0:T(8,128)S(1)}, f32[768,128]{1,0:T(8,128)S(1)}, u32[]{:S(2)}, u32[]{:S(2)}) collective-permute-start(f32[768,128]{1,0:T(8,128)S(1)} %get-tuple-element.149), channel_id=1, source_target_pairs={{0,1},{1,0},{2,3},{3,2},{4,5},{5,4},{6,7},{7,6},{8,9},{9,8},{10,11... | collective-permute-start | bytes 1179656 | tf_op jit(solution)/shard_map/ppermute | solution.py:804
  38.7 6.6 %collective-permute-start.13 = (f32[1,64,768]{2,1,0:T(8,128)S(1)}, f32[1,64,768]{2,1,0:T(8,128)S(1)}, u32[]{:S(2)}, u32[]{:S(2)}) collective-permute-start(f32[1,64,768]{2,1,0:T(8,128)S(1)} %get-tuple-element.143), channel_id=1, source_target_pairs={{0,1},{1,0},{2,3},{3,2},{4,5},{5,4},{6,7},{7,6},{8,9},{9,8},{10,11... | collective-permute-start | bytes 589832 | tf_op jit(solution)/shard_map/ppermute | solution.py:802
  39.2 8.7 %collective-permute-start.14 = (f32[1,64,768]{2,1,0:T(8,128)S(1)}, f32[1,64,768]{2,1,0:T(8,128)S(1)}, u32[]{:S(2)}, u32[]{:S(2)}) collective-permute-start(f32[1,64,768]{2,1,0:T(8,128)S(1)} %get-tuple-element.160), channel_id=1, source_target_pairs={{0,1},{1,0},{2,3},{3,2},{4,5},{5,4},{6,7},{7,6},{8,9},{9,8},{10,11... | collective-permute-start | bytes 589832 | tf_op jit(solution)/shard_map/ppermute | solution.py:799
  39.3 5.1 %collective-permute-start.9 = (f32[192,128]{1,0:T(8,128)S(1)}, f32[192,128]{1,0:T(8,128)S(1)}, u32[]{:S(2)}, u32[]{:S(2)}) collective-permute-start(f32[192,128]{1,0:T(8,128)S(1)} %get-tuple-element.147), channel_id=1, source_target_pairs={{0,8},{4,12},{8,0},{12,4},{16,24},{20,28},{24,16},{28,20},{1,9},{5... | collective-permute-start | bytes 294920 | tf_op jit(solution)/shard_map/ppermute | solution.py:664
  40.8 11.6 %collective-permute-start.15 = (f32[1,64,768]{2,1,0:T(8,128)S(1)}, f32[1,64,768]{2,1,0:T(8,128)S(1)}, u32[]{:S(2)}, u32[]{:S(2)}) collective-permute-start(f32[1,64,768]{2,1,0:T(8,128)S(1)} %get-tuple-element.164), channel_id=1, source_target_pairs={{0,2},{1,3},{2,0},{3,1},{4,6},{5,7},{6,4},{7,5},{8,10},{9,11},{10,... | collective-permute-start | bytes 589832 | tf_op jit(solution)/shard_map/ppermute | solution.py:801
  44.4 11.0 %collective-permute-start.18 = (f32[1,64,768]{2,1,0:T(8,128)S(1)}, f32[1,64,768]{2,1,0:T(8,128)S(1)}, u32[]{:S(2)}, u32[]{:S(2)}) collective-permute-start(f32[1,64,768]{2,1,0:T(8,128)S(1)} %get-tuple-element.164), channel_id=1, source_target_pairs={{0,1},{1,0},{2,3},{3,2},{4,5},{5,4},{6,7},{7,6},{8,9},{9,8},{10,11... | collective-permute-start | bytes 589832 | tf_op jit(solution)/shard_map/ppermute | solution.py:802
  44.5 8.7 %collective-permute-start.12 = (f32[384,128]{1,0:T(8,128)S(1)}, f32[384,128]{1,0:T(8,128)S(1)}, u32[]{:S(2)}, u32[]{:S(2)}) collective-permute-start(f32[384,128]{1,0:T(8,128)S(1)} %get-tuple-element.159), channel_id=1, source_target_pairs={{0,4},{4,0},{8,12},{12,8},{16,20},{20,16},{24,28},{28,24},{1,5},{5... | collective-permute-start | bytes 589832 | tf_op jit(solution)/shard_map/ppermute | solution.py:664
  45.3 7.9 %collective-permute-start.11 = (f32[192,128]{1,0:T(8,128)S(1)}, f32[192,128]{1,0:T(8,128)S(1)}, u32[]{:S(2)}, u32[]{:S(2)}) collective-permute-start(f32[192,128]{1,0:T(8,128)S(1)} %get-tuple-element.157.refs_0_), channel_id=1, source_target_pairs={{0,16},{4,20},{8,24},{12,28},{16,0},{20,4},{24,8},{28,12},{1,17},{... | collective-permute-start | bytes 294920 | tf_op jit(solution)/shard_map/ppermute | solution.py:664
  53.3 7.9 %collective-permute-start.16 = (f32[192,128]{1,0:T(8,128)S(1)}, f32[192,128]{1,0:T(8,128)S(1)}, u32[]{:S(2)}, u32[]{:S(2)}) collective-permute-start(f32[192,128]{1,0:T(8,128)S(1)} %get-tuple-element.166.refs_0_), channel_id=1, source_target_pairs={{0,8},{4,12},{8,0},{12,4},{16,24},{20,28},{24,16},{28,20},{1,9},{5... | collective-permute-start | bytes 294920 | tf_op jit(solution)/shard_map/ppermute | solution.py:664
  54.1 7.1 %collective-permute-start.17 = (f32[192,128]{1,0:T(8,128)S(1)}, f32[192,128]{1,0:T(8,128)S(1)}, u32[]{:S(2)}, u32[]{:S(2)}) collective-permute-start(f32[192,128]{1,0:T(8,128)S(1)} %get-tuple-element.168), channel_id=1, source_target_pairs={{0,8},{4,12},{8,0},{12,4},{16,24},{20,28},{24,16},{28,20},{1,9},{5... | collective-permute-start | bytes 294920 | tf_op jit(solution)/shard_map/ppermute | solution.py:664
  55.4 9.3 %collective-permute-start.22 = (f32[384,128]{1,0:T(8,128)S(1)}, f32[384,128]{1,0:T(8,128)S(1)}, u32[]{:S(2)}, u32[]{:S(2)}) collective-permute-start(f32[384,128]{1,0:T(8,128)S(1)} %get-tuple-element.181), channel_id=1, source_target_pairs={{0,1},{1,0},{2,3},{3,2},{4,5},{5,4},{6,7},{7,6},{8,9},{9,8},{10,11... | collective-permute-start | bytes 589832 | tf_op jit(solution)/shard_map/ppermute | solution.py:804
  61.3 3.4 %collective-permute-start.23 = (f32[384,128]{1,0:T(8,128)S(1)}, f32[384,128]{1,0:T(8,128)S(1)}, u32[]{:S(2)}, u32[]{:S(2)}) collective-permute-start(f32[384,128]{1,0:T(8,128)S(1)} %get-tuple-element.182), channel_id=1, source_target_pairs={{0,1},{1,0},{2,3},{3,2},{4,5},{5,4},{6,7},{7,6},{8,9},{9,8},{10,11... | collective-permute-start | bytes 589832 | tf_op jit(solution)/shard_map/ppermute | solution.py:804
  61.9 12.1 %collective-permute-start.20 = (f32[384,128]{1,0:T(8,128)S(1)}, f32[384,128]{1,0:T(8,128)S(1)}, u32[]{:S(2)}, u32[]{:S(2)}) collective-permute-start(f32[384,128]{1,0:T(8,128)S(1)} %get-tuple-element.177.refs_0_), channel_id=1, source_target_pairs={{0,4},{4,0},{8,12},{12,8},{16,20},{20,16},{24,28},{28,24},{1,5},{5... | collective-permute-start | bytes 589832 | tf_op jit(solution)/shard_map/ppermute | solution.py:664
  64.9 9.1 %collective-permute-start.25 = (f32[224,128]{1,0:T(8,128)S(1)}, f32[224,128]{1,0:T(8,128)S(1)}, u32[]{:S(2)}, u32[]{:S(2)}) collective-permute-start(f32[224,128]{1,0:T(8,128)S(1)} %get-tuple-element.192), channel_id=1, source_target_pairs={{0,4},{4,0},{8,12},{12,8},{16,20},{20,16},{24,28},{28,24},{1,5},{5... | collective-permute-start | bytes 344072 | tf_op jit(solution)/shard_map/ppermute | solution.py:664
  65.6 8.3 %collective-permute-start.26 = (f32[224,128]{1,0:T(8,128)S(1)}, f32[224,128]{1,0:T(8,128)S(1)}, u32[]{:S(2)}, u32[]{:S(2)}) collective-permute-start(f32[224,128]{1,0:T(8,128)S(1)} %get-tuple-element.193), channel_id=1, source_target_pairs={{0,8},{4,12},{8,0},{12,4},{16,24},{20,28},{24,16},{28,20},{1,9},{5... | collective-permute-start | bytes 344072 | tf_op jit(solution)/shard_map/ppermute | solution.py:664
  66.3 9.9 %collective-permute-start.27 = (f32[224,128]{1,0:T(8,128)S(1)}, f32[224,128]{1,0:T(8,128)S(1)}, u32[]{:S(2)}, u32[]{:S(2)}) collective-permute-start(f32[224,128]{1,0:T(8,128)S(1)} %get-tuple-element.194), channel_id=1, source_target_pairs={{0,12},{4,8},{8,4},{12,0},{16,28},{20,24},{24,20},{28,16},{1,13},{... | collective-permute-start | bytes 344072 | tf_op jit(solution)/shard_map/ppermute | solution.py:664
  68.4 5.5 %collective-permute-start.21 = (f32[192,128]{1,0:T(8,128)S(1)}, f32[192,128]{1,0:T(8,128)S(1)}, u32[]{:S(2)}, u32[]{:S(2)}) collective-permute-start(f32[192,128]{1,0:T(8,128)S(1)} %get-tuple-element.178.refs_2_), channel_id=1, source_target_pairs={{0,16},{4,20},{8,24},{12,28},{16,0},{20,4},{24,8},{28,12},{1,17},{... | collective-permute-start | bytes 294920 | tf_op jit(solution)/shard_map/ppermute | solution.py:664
  76.3 11.4 %collective-permute-start.28 = (f32[1024,768]{1,0:T(8,128)S(1)}, f32[1024,768]{1,0:T(8,128)S(1)}, u32[]{:S(2)}, u32[]{:S(2)}) collective-permute-start(f32[1024,768]{1,0:T(8,128)S(1)} %get-tuple-element.205.own), channel_id=1, source_target_pairs={{0,1},{1,0},{2,3},{3,2},{4,5},{5,4},{6,7},{7,6},{8,9},{9,8},{10,11... | collective-permute-start | bytes 9437192 | tf_op jit(solution)/shard_map/ppermute | solution.py:810
  76.4 15.9 %collective-permute-start.31 = (f32[1024,512]{1,0:T(8,128)S(1)}, f32[1024,512]{1,0:T(8,128)S(1)}, u32[]{:S(2)}, u32[]{:S(2)}) collective-permute-start(f32[1024,512]{1,0:T(8,128)S(1)} %get-tuple-element.211.own), channel_id=1, source_target_pairs={{0,1},{1,0},{2,3},{3,2},{4,5},{5,4},{6,7},{7,6},{8,9},{9,8},{10,11... | collective-permute-start | bytes 6291464 | tf_op jit(solution)/shard_map/ppermute | solution.py:810
  76.9 8.5 %collective-permute-start.30 = (f32[224,128]{1,0:T(8,128)S(1)}, f32[224,128]{1,0:T(8,128)S(1)}, u32[]{:S(2)}, u32[]{:S(2)}) collective-permute-start(f32[224,128]{1,0:T(8,128)S(1)} %get-tuple-element.207.refs_2_), channel_id=1, source_target_pairs={{0,16},{4,20},{8,24},{12,28},{16,0},{20,4},{24,8},{28,12},{1,17},{... | collective-permute-start | bytes 344072 | tf_op jit(solution)/shard_map/ppermute | solution.py:664
  77.9 6.3 %collective-permute-start.29 = (f32[192,128]{1,0:T(8,128)S(1)}, f32[192,128]{1,0:T(8,128)S(1)}, u32[]{:S(2)}, u32[]{:S(2)}) collective-permute-start(f32[192,128]{1,0:T(8,128)S(1)} %get-tuple-element.206.refs_0_), channel_id=1, source_target_pairs={{0,8},{4,12},{8,0},{12,4},{16,24},{20,28},{24,16},{28,20},{1,9},{5... | collective-permute-start | bytes 294920 | tf_op jit(solution)/shard_map/ppermute | solution.py:664
  85.4 10.7 %collective-permute-start.32 = (f32[384,128]{1,0:T(8,128)S(1)}, f32[384,128]{1,0:T(8,128)S(1)}, u32[]{:S(2)}, u32[]{:S(2)}) collective-permute-start(f32[384,128]{1,0:T(8,128)S(1)} %get-tuple-element.215.refs_1_), channel_id=1, source_target_pairs={{0,4},{4,0},{8,12},{12,8},{16,20},{20,16},{24,28},{28,24},{1,5},{5... | collective-permute-start | bytes 589832 | tf_op jit(solution)/shard_map/ppermute | solution.py:664
  86.0 10.1 %collective-permute-start.33 = (f32[224,128]{1,0:T(8,128)S(1)}, f32[224,128]{1,0:T(8,128)S(1)}, u32[]{:S(2)}, u32[]{:S(2)}) collective-permute-start(f32[224,128]{1,0:T(8,128)S(1)} %get-tuple-element.216.refs_3_), channel_id=1, source_target_pairs={{0,4},{4,0},{8,12},{12,8},{16,20},{20,16},{24,28},{28,24},{1,5},{5... | collective-permute-start | bytes 344072 | tf_op jit(solution)/shard_map/ppermute | solution.py:664
  87.5 8.6 %collective-permute-start.34 = (f32[224,128]{1,0:T(8,128)S(1)}, f32[224,128]{1,0:T(8,128)S(1)}, u32[]{:S(2)}, u32[]{:S(2)}) collective-permute-start(f32[224,128]{1,0:T(8,128)S(1)} %get-tuple-element.216.refs_3_), channel_id=1, source_target_pairs={{0,8},{4,12},{8,0},{12,4},{16,24},{20,28},{24,16},{28,20},{1,9},{5... | collective-permute-start | bytes 344072 | tf_op jit(solution)/shard_map/ppermute | solution.py:664
  87.7 8.4 %collective-permute-start.35 = (f32[224,128]{1,0:T(8,128)S(1)}, f32[224,128]{1,0:T(8,128)S(1)}, u32[]{:S(2)}, u32[]{:S(2)}) collective-permute-start(f32[224,128]{1,0:T(8,128)S(1)} %get-tuple-element.216.refs_3_), channel_id=1, source_target_pairs={{0,12},{4,8},{8,4},{12,0},{16,28},{20,24},{24,20},{28,16},{1,13},{... | collective-permute-start | bytes 344072 | tf_op jit(solution)/shard_map/ppermute | solution.py:664
  (6 other events, 23.1 us)

commit v6 on v5

--- a/solution.py
+++ b/solution.py
@@ -24,6 +24,7 @@
 GROUPS = ((0, 1), (2, 3), (4,), (5,))
 UNITS = ((0,), (1,), (2, 3))
 WAY = ("single", "single", "pair")
+SPARE = (0, 0, 0)
 PLAN = (
     ("small", "fetch", ()),
     ("experts", 0, ()),
@@ -32,17 +33,16 @@
     ("small", "fetch", (0,)),
     ("experts", 1, ()),
     ("small", "send fetch", (0,)),
-    ("events", (1,), ()),
-    ("small", "", (0, 1)),
+    ("small", "", (1,)),
     ("experts", 2, ()),
     ("small", "send fetch", (0, 1)),
     ("experts", 3, ()),
     ("small", "send", (0, 1)),
     ("events", (2,), ()),
     ("small", "", (2,)),
-    ("events", (3,), ()),
+    ("events", (1, 3), ()),
     ("small", "mix grad", (0, 1, 2)),
-    ("small", "", (1, 2)),
+    ("small", "", (0, 1, 2)),
     ("place", None, ()),
     ("place", None, ()),
 )
@@ -332,7 +332,7 @@
         for i in range(n):
             halves = tuple(v[:, :LANES] for v in st["dnormed"][i])
             acc[i * LANES : (i + 1) * LANES, D:] += dot3(halves, st["hidden_parts"][i], TN)
-        beside = [split(st["dlogits"])] if last else []
+        beside = [split(st["dlogits"][:, :16])] if last else []
         left = tuple(jnp.concatenate([h[k] for h in st["dpre"] + beside], axis=1) for k in range(2))
         both = dot3(left, st["events"], TN)
         acc[:, :D] += both[: n * LANES]
@@ -356,13 +356,12 @@
                 own_ref[at, :] = acc[pl.ds(i * LANES + mine, SLICE), lanes]
                 part_ref[at, :] = acc[pl.ds(i * LANES + other, SLICE), lanes]
         if last:
-            sums_ref[...] = jnp.zeros_like(sums_ref)
             for g, before in enumerate(sums_before):
                 sums_ref[8 * g : 8 * g + 8, :] = before[...]
             g = len(GROUPS) - 1
             sums_ref[8 * g : 8 * g + 8, :] = sums[...]
             for t in range(D // LANES):
-                sums_ref[64 + 16 * t : 80 + 16 * t, :] = gate_acc[:, t * LANES : (t + 1) * LANES]
+                sums_ref[8 * g + 8 + 16 * t : 8 * g + 24 + 16 * t, :] = gate_acc[:, t * LANES : (t + 1) * LANES]
         else:
             sums_ref[...] = sums[...]
 
@@ -392,7 +391,7 @@
     in_specs += [pl.BlockSpec(memory_space=pl.ANY)] * len(deps)
     args += deps
     payload = WIDE // LANES * n * SLICE
-    sums_shape = (2 * LANES // 2, LANES) if last else (8, LANES)
+    sums_shape = (8 * len(GROUPS) + 16 * (D // LANES), LANES) if last else (8, LANES)
     scratch = [
         pltpu.VMEM((n, O, H), BF16),
         pltpu.VMEM((n, O, H), BF16),
@@ -581,7 +580,8 @@
 
 
 class Reduction:
-    def __init__(self, own, got, n_dp, kind):
+    def __init__(self, own, got, n_dp, kind, spare):
+        self.spare = spare
         self.keep, self.got = [Piece(v) for v in own], [Piece(v) for v in got]
         pairs, last = bit_groups(n_dp.bit_length() - 1, 2)
         singles, lone = bit_groups(n_dp.bit_length() - 1, 1)
@@ -629,8 +629,8 @@
                     total = total + v[...]
                 to[at : at + piece.rows, :] = total
                 at += piece.rows
-            if at < rows:
-                to[at:rows, :] = jnp.zeros((rows - at, LANES), F32)
+            if at < to.shape[0]:
+                to[at:, :] = jnp.zeros((to.shape[0] - at, LANES), F32)
             if scatter:
                 side = side_of(goes)
                 for m in range(parts):
@@ -639,14 +639,17 @@
         arrays = [p.array for p in pieces]
         if scatter:
             return Job(arrays, [(rows // parts, LANES)] * parts, body, [pltpu.VMEM((rows, LANES), F32)])
-        return Job(arrays, [(rows, LANES)], body)
+        self.used = rows
+        return Job(arrays, [(rows + (self.spare if stage == self.scattered else 0), LANES)], body)
 
     def take(self, outs):
         self.stage += 1
-        self.keep = [Piece(outs[0])]
+        scatters = self.stage <= self.scattered
+        rows = None if scatters else self.used
+        self.keep = [Piece(outs[0], 0, rows)]
         if self.stage <= len(self.order):
-            sent = outs[1:] if self.stage <= self.scattered else None
-            self.got = [Piece(v) for v in exchange(outs[0], sent, self.order[self.stage - 1], self.n_dp)]
+            sent = outs[1:] if scatters else None
+            self.got = [Piece(v, 0, rows) for v in exchange(outs[0], sent, self.order[self.stage - 1], self.n_dp)]
 
     @staticmethod
     def take_together(units, out, rows):
@@ -712,12 +715,13 @@
                         out_grad[e, :, t * LANES - D : (t + 1) * LANES - D] = tile
     sums = summed[-1][at : at + 8 * len(GROUPS), :]
     sums = jnp.where(odd, sums[:, SLICE:], sums[:, :SLICE])
+    start = at + 8 * len(GROUPS)
     for g, group in enumerate(GROUPS):
         for i, e in enumerate(group):
             for k, ref in enumerate((in_bias, out_bias, gain, shift)):
                 ref[e : e + 1, :] = sums[8 * g + 4 * i + k : 8 * g + 4 * i + k + 1, :]
     for t in range(D // LANES):
-        gate[:, t * LANES : (t + 1) * LANES] = summed[-1][at + 64 + 16 * t : at + 64 + 16 * t + GATE_COLS, :]
+        gate[:, t * LANES : (t + 1) * LANES] = summed[-1][start + 16 * t : start + 16 * t + GATE_COLS, :]
 
 
 def per_device(
@@ -752,7 +756,7 @@
     placed, unplaced = [], []
     mix = small = x_grad = None
     deps = [p]
-    for kind, what, units in PLAN:
+    for kind, what, units, *holding in PLAN:
         if kind == "experts":
             last = what == len(GROUPS) - 1
             shards = (own[what], beside[what], far[what], relayed[what])
@@ -773,7 +777,8 @@
         else:
             joint = units if "joint" in what else ()
             alone = () if joint else units
-            jobs = [summing[u].job() for u in alone]
+            held = holding[0] if holding else ()
+            jobs = [summing[u].job() for u in (*alone, *held)]
             sent, fetched, through = [], [], []
             if "send" in what:
                 sent = [made[-1][7]] + ([made[-1][8]] if len(made) == len(GROUPS) else [])
@@ -795,18 +800,20 @@
                 Reduction.take_together([summing[u] for u in joint], outs.pop()[0], rows_of)
             for u, o in zip(alone, outs):
                 summing[u].take(o)
+            for u, o in zip(held, outs[len(alone) :]):
+                summing[u].keep, summing[u].got = [Piece(o[0])], []
             if fetched:
                 relayed.append(lax.ppermute(outs[-1][0], "tp", core))
                 if len(fetched) > 1:
                     far.append(lax.ppermute(outs[-1][1], "tp", across))
                     beside.append(lax.ppermute(outs[-1][1], "tp", core))
             if sent:
-                got = [lax.ppermute(v, "tp", core) for v in outs[len(alone)]]
+                got = [lax.ppermute(v, "tp", core) for v in outs[len(alone) + len(held)]]
                 partial.append(([made[-1][6], *sent[1:]], got))
-                for u, (unit, way) in enumerate(zip(UNITS, WAY)):
+                for u, (unit, way, spare) in enumerate(zip(UNITS, WAY, SPARE)):
                     if unit[-1] == len(partial) - 1:
                         both = [partial[g] for g in unit]
-                        summing[u] = Reduction([v for b in both for v in b[0]], [v for b in both for v in b[1]], n_dp, way)
+                        summing[u] = Reduction([v for b in both for v in b[0]], [v for b in both for v in b[1]], n_dp, way, spare)
             unplaced += [(v, lax.ppermute(v, "tp", core)) for v in through]
     mixtures, x_grad = placed
     summing = [summing[u] for u in range(len(UNITS))]

time: 97.6 us -> 94.2 us (0.965)
  starting transfers between devices: 33.5 us -> 29.6 us
  waiting for transfers between devices: 14.9 us -> 16.8 us
  Pallas kernels: 48 us -> 46.6 us
    ppermute x17, starting transfers between devices: 23.9 us -> 19.9 us  [exchange(): lax.ppermute(whole if parts is None else parts[m - 1], 'dp', [(i, i ^ m <...]
    ppermute x17, waiting for transfers between devices: 10.9 us -> 12.3 us  [exchange(): lax.ppermute(whole if parts is None else parts[m - 1], 'dp', [(i, i ^ m <...]
    pallas_call x4 -> x3, Pallas kernels: 8.61 us -> 7.86 us  [event_grads(): pl.pallas_call(functools.partial(event_kernel, len(highs), bool(gating),...]
where the time goes in v6:
time: 94.2 us; the launch traced here: 94 us
  Pallas kernels  46.6 us (49%)
  starting transfers between devices  29.6 us (31%)
  waiting for transfers between devices  16.8 us (18%)
  between operations  0.99 us (1%)
    pallas_call x4, Pallas kernels, experts(): pl.pallas_call(functools.partial(expert_kernel, group, first, last, len(d...  24.8 us
    ppermute x17, starting transfers between devices, exchange(): lax.ppermute(whole if parts is None else parts[m - 1], 'dp', [(i, i ^ m <...  19.9 us
    ppermute x17, waiting for transfers between devices, exchange(): lax.ppermute(whole if parts is None else parts[m - 1], 'dp', [(i, i ^ m <...  12.3 us
    pallas_call x3, Pallas kernels, event_grads(): pl.pallas_call(functools.partial(event_kernel, len(highs), bool(gating),...  7.86 us
    pallas_call x1, Pallas kernels, gates(): pl.pallas_call(functools.partial(gate_kernel, len(deps)), in_specs=[pl.Bl...  4.97 us
    pallas_call x2, Pallas kernels, place(): pl.pallas_call(place_kernel, in_specs=[anywhere] * (2 + len(deps)), out_s...  4.75 us
    ppermute x1, waiting for transfers between devices, per_device(): far = [lax.ppermute(own[0], 'tp', across)]  3.95 us
    ppermute x3, starting transfers between devices, per_device(): far.append(lax.ppermute(outs[-1][1], 'tp', across))  3.82 us
  transfers between devices with their start and end apart: 36, of which 8 were waited for; matrix products, arithmetic and copies ran while one was open for 0% of the time, Pallas kernels for 47%

profile of v6, /device:TPU:0, one launch (start us, length us, event | category | flops | bytes accessed | tf_op | source)
XLA Modules:
  0.0 94.0 jit_solution(13149472256457399634)
XLA Ops:
  0.7 1.0 %shard_map.169.refs_0_.refs_4_ = f32[2,72,768]{2,1,0:T(8,128)S(1)} custom-call(f32[6,64,512]{2,1,0:T(8,128)} %bitcast.8, f32[6,64,256]{2,1,0:T(8,128)} %bitcast.10, f32[6,64]{1,0:T(8,128)} %refs_0_.1, f32[6,64]{1,0:T(8,128)} %refs_1_.1, f32[6,64]{1,0:T(8,128)} %refs_2_.1, f32[6,64]{1,0:T(8,128)} %refs_3_.1), custom_call_target="tpu_custom_call" | custom-call | bytes 786432 | tf_op jit(solution)/shard_map/pallas_call | solution.py:174
  1.7 3.0 %collective-permute-start.1 = (f32[2,72,768]{2,1,0:T(8,128)S(1)}, f32[2,72,768]{2,1,0:T(8,128)S(1)}, u32[]{:S(2)}, u32[]{:S(2)}) collective-permute-start(f32[2,72,768]{2,1,0:T(8,128)S(1)} %shard_map.169.refs_0_.refs_4_), channel_id=1, source_target_pairs={{0,2},{1,3},{2,0},{3,1},{4,6},{5,7},{6,4},{7,5},{8,10},{9,11},{10,... | collective-permute-start | bytes 1327112 | tf_op jit(solution)/shard_map/ppermute | solution.py:748
  4.7 1.2 %shard_map.170 = (f32[2,64,768]{2,1,0:T(8,128)S(1)}, f32[1,64,768]{2,1,0:T(8,128)S(1)}, f32[1,64,768]{2,1,0:T(8,128)S(1)}) custom-call(f32[6,64,512]{2,1,0:T(8,128)} %bitcast.9, f32[6,64,256]{2,1,0:T(8,128)} %bitcast.11, f32[2,72,768]{2,1,0:T(8,128)S(1)} %shard_map.169.refs_0_.refs_4_), custom_call_target="tpu_custom_call" | custom-call | bytes 786432 | tf_op jit(solution)/shard_map/pallas_call | solution.py:174
  6.0 5.0 %shard_map.171 = (bf16[1024,512]{1,0:T(8,128)(2,1)S(1)}, bf16[1024,512]{1,0:T(8,128)(2,1)S(1)}, f32[1024,128]{1,0:T(8,128)S(1)}, f32[1024,768]{1,0:T(8,128)S(1)}) custom-call(s32[8]{0:T(128)S(1)} %copy-done.1, f32[2048,512]{1,0:T(8,128)} %ev_ref.1, f32[2048,768]{1,0:T(8,128)} %cot_ref.1, f32[14,512]{1,0:T(8,128)} %bitcast.6, ...), custom_call_target="tpu_custom_call" | custom-call | flops 402653184 | bytes 4194304 | tf_op jit(solution)/shard_map/pallas_call | solution.py:125
  11.0 3.9 %collective-permute-done.1.refs_0_.refs_6_ = f32[2,72,768]{2,1,0:T(8,128)S(1)} collective-permute-done((f32[2,72,768]{2,1,0:T(8,128)S(1)}, f32[2,72,768]{2,1,0:T(8,128)S(1)}, u32[]{:S(2)}, u32[]{:S(2)}) %collective-permute-start.1) | collective-permute-done | bytes 442400 | tf_op jit(solution)/shard_map/ppermute | solution.py:748
  15.0 1.8 %collective-permute-start.4 = (f32[2,64,768]{2,1,0:T(8,128)S(1)}, f32[2,64,768]{2,1,0:T(8,128)S(1)}, u32[]{:S(2)}, u32[]{:S(2)}) collective-permute-start(f32[2,64,768]{2,1,0:T(8,128)S(1)} %get-tuple-element.126), channel_id=1, source_target_pairs={{0,2},{1,3},{2,0},{3,1},{4,6},{5,7},{6,4},{7,5},{8,10},{9,11},{10,... | collective-permute-start | bytes 1179656 | tf_op jit(solution)/shard_map/ppermute | solution.py:808
  16.9 7.3 %shard_map.173 = (f32[1024,768]{1,0:T(8,128)S(1)}, f32[1024,128]{1,0:T(8,128)S(1)}, bf16[1024,512]{1,0:T(8,128)(2,1)S(1)}, bf16[1024,512]{1,0:T(8,128)(2,1)S(1)}...) custom-call(bf16[1024,512]{1,0:T(8,128)(2,1)S(1)} %get-tuple-element, ...), custom_call_target="tpu_custom_call" | custom-call | flops 8858370048 | bytes 14336000 | tf_op jit(solution)/shard_map/pallas_call | solution.py:403
  24.8 2.5 %shard_map.175 = (f32[1024,512]{1,0:T(8,128)S(1)}, f32[8,128]{1,0:T(8,128)S(1)}) custom-call(bf16[1024,512]{1,0:T(8,128)(2,1)S(1)} %get-tuple-element.128.refs_0_, bf16[1024,512]{1,0:T(8,128)(2,1)S(1)} %get-tuple-element.129.refs_1_, bf16[512,512]{1,0:T(8,128)(2,1)S(1)} %get-tuple-element.130.refs_2_, bf16[512,512]{1,0:T(8,128)(2,1)S(1)} %get-tuple-element.131.refs_3_, ...), custom_call_target="tpu_custom_call" | custom-call | flops 1610612736 | bytes 4096000 | tf_op jit(solution)/shard_map/pallas_call | solution.py:468
  27.6 1.7 %collective-permute-start.5 = (f32[384,128]{1,0:T(8,128)S(1)}, f32[384,128]{1,0:T(8,128)S(1)}, u32[]{:S(2)}, u32[]{:S(2)}) collective-permute-start(f32[384,128]{1,0:T(8,128)S(1)} %get-tuple-element.135), channel_id=1, source_target_pairs={{0,4},{4,0},{8,12},{12,8},{16,20},{20,16},{24,28},{28,24},{1,5},{5... | collective-permute-start | bytes 589832 | tf_op jit(solution)/shard_map/ppermute | solution.py:667
  29.3 1.5 %collective-permute-start.8 = (f32[1,64,768]{2,1,0:T(8,128)S(1)}, f32[1,64,768]{2,1,0:T(8,128)S(1)}, u32[]{:S(2)}, u32[]{:S(2)}) collective-permute-start(f32[1,64,768]{2,1,0:T(8,128)S(1)} %get-tuple-element.141), channel_id=1, source_target_pairs={{0,2},{1,3},{2,0},{3,1},{4,6},{5,7},{6,4},{7,5},{8,10},{9,11},{10,... | collective-permute-start | bytes 589832 | tf_op jit(solution)/shard_map/ppermute | solution.py:808
  30.8 7.8 %shard_map.177 = (f32[1024,768]{1,0:T(8,128)S(1)}, f32[1024,128]{1,0:T(8,128)S(1)}, bf16[1024,512]{1,0:T(8,128)(2,1)S(1)}, bf16[1024,512]{1,0:T(8,128)(2,1)S(1)}...) custom-call(bf16[1024,512]{1,0:T(8,128)(2,1)S(1)} %get-tuple-element, ...), custom_call_target="tpu_custom_call", output_to_operand_aliasing={{0}: (9, {})} | custom-call | flops 8858370048 | bytes 14336000 | tf_op jit(solution)/shard_map/pallas_call | solution.py:403
  40.5 1.6 %collective-permute-start.9 = (f32[192,128]{1,0:T(8,128)S(1)}, f32[192,128]{1,0:T(8,128)S(1)}, u32[]{:S(2)}, u32[]{:S(2)}) collective-permute-start(f32[192,128]{1,0:T(8,128)S(1)} %get-tuple-element.145), channel_id=1, source_target_pairs={{0,8},{4,12},{8,0},{12,4},{16,24},{20,28},{24,16},{28,20},{1,9},{5... | collective-permute-start | bytes 294920 | tf_op jit(solution)/shard_map/ppermute | solution.py:667
  42.8 4.8 %shard_map.180 = (f32[1024,768]{1,0:T(8,128)S(1)}, f32[1024,128]{1,0:T(8,128)S(1)}, bf16[1024,256]{1,0:T(8,128)(2,1)S(1)}, bf16[1024,256]{1,0:T(8,128)(2,1)S(1)}...) custom-call(bf16[1024,512]{1,0:T(8,128)(2,1)S(1)} %get-tuple-element, ...), custom_call_target="tpu_custom_call", output_to_operand_aliasing={{0}: (9, {})} | custom-call | flops 4429185024 | bytes 14336000 | tf_op jit(solution)/shard_map/pallas_call | solution.py:403
  47.6 1.3 %collective-permute-done.11.refs_3_ = f32[384,128]{1,0:T(8,128)S(1)} collective-permute-done((f32[384,128]{1,0:T(8,128)S(1)}, f32[384,128]{1,0:T(8,128)S(1)}, u32[]{:S(2)}, u32[]{:S(2)}) %collective-permute-start.11) | collective-permute-done | bytes 196640 | tf_op jit(solution)/shard_map/ppermute | solution.py:667
  49.1 2.7 %collective-permute-start.15 = (f32[192,128]{1,0:T(8,128)S(1)}, f32[192,128]{1,0:T(8,128)S(1)}, u32[]{:S(2)}, u32[]{:S(2)}) collective-permute-start(f32[192,128]{1,0:T(8,128)S(1)} %get-tuple-element.157.refs_0_), channel_id=1, source_target_pairs={{0,16},{4,20},{8,24},{12,28},{16,0},{20,4},{24,8},{28,12},{1,17},{... | collective-permute-start | bytes 294920 | tf_op jit(solution)/shard_map/ppermute | solution.py:667
  52.2 4.9 %shard_map.182 = (f32[1024,768]{1,0:T(8,128)S(1)}, f32[1024,128]{1,0:T(8,128)S(1)}, bf16[1024,256]{1,0:T(8,128)(2,1)S(1)}, bf16[1024,256]{1,0:T(8,128)(2,1)S(1)}...) custom-call(bf16[1024,512]{1,0:T(8,128)(2,1)S(1)} %get-tuple-element, ...), custom_call_target="tpu_custom_call", output_to_operand_aliasing={{0}: (9, {})} | custom-call | flops 4429185024 | bytes 14336000 | tf_op jit(solution)/shard_map/pallas_call | solution.py:403
  57.3 1.3 %collective-permute-done.16.refs_3_ = f32[192,128]{1,0:T(8,128)S(1)} collective-permute-done((f32[192,128]{1,0:T(8,128)S(1)}, f32[192,128]{1,0:T(8,128)S(1)}, u32[]{:S(2)}, u32[]{:S(2)}) %collective-permute-start.16) | collective-permute-done | bytes 98336 | tf_op jit(solution)/shard_map/ppermute | solution.py:667
  59.6 1.4 %collective-permute-start.20 = (f32[192,128]{1,0:T(8,128)S(1)}, f32[192,128]{1,0:T(8,128)S(1)}, u32[]{:S(2)}, u32[]{:S(2)}) collective-permute-start(f32[192,128]{1,0:T(8,128)S(1)} %get-tuple-element.169.refs_2_), channel_id=1, source_target_pairs={{0,16},{4,20},{8,24},{12,28},{16,0},{20,4},{24,8},{28,12},{1,17},{... | collective-permute-start | bytes 294920 | tf_op jit(solution)/shard_map/ppermute | solution.py:667
  61.0 1.5 %shard_map.184 = (f32[1024,512]{1,0:T(8,128)S(1)}, f32[8,128]{1,0:T(8,128)S(1)}) custom-call(bf16[1024,256]{1,0:T(8,128)(2,1)S(1)} %get-tuple-element.175.refs_0_, bf16[1024,256]{1,0:T(8,128)(2,1)S(1)} %get-tuple-element.176.refs_1_, bf16[256,512]{1,0:T(8,128)(2,1)S(1)} %get-tuple-element.177.refs_2_, ...), custom_call_target="tpu_custom_call", output_to_operand_aliasing={{0}: (4, {})} | custom-call | flops 805306368 | bytes 4096000 | tf_op jit(solution)/shard_map/pallas_call | solution.py:468
  63.8 2.4 %collective-permute-start.26 = (f32[216,128]{1,0:T(8,128)S(1)}, f32[216,128]{1,0:T(8,128)S(1)}, u32[]{:S(2)}, u32[]{:S(2)}) collective-permute-start(f32[216,128]{1,0:T(8,128)S(1)} %get-tuple-element.185), channel_id=1, source_target_pairs={{0,12},{4,8},{8,4},{12,0},{16,28},{20,24},{24,20},{28,16},{1,13},{... | collective-permute-start | bytes 331784 | tf_op jit(solution)/shard_map/ppermute | solution.py:667
  66.2 3.9 %shard_map.186 = (f32[1024,512]{1,0:T(8,128)S(1)}, f32[8,128]{1,0:T(8,128)S(1)}) custom-call(bf16[1024,512]{1,0:T(8,128)(2,1)S(1)} %get-tuple-element.187.refs_0_, bf16[1024,256]{1,0:T(8,128)(2,1)S(1)} %get-tuple-element.188.refs_1_, bf16[1024,512]{1,0:T(8,128)(2,1)S(1)} %get-tuple-element.189.refs_2_, ...), custom_call_target="tpu_custom_call", output_to_operand_aliasing={{0}: (10, {})} | custom-call | flops 2415919104 | bytes 4096000 | tf_op jit(solution)/shard_map/pallas_call | solution.py:468
  70.1 1.7 %collective-permute-done.26.refs_7_ = f32[216,128]{1,0:T(8,128)S(1)} collective-permute-done((f32[216,128]{1,0:T(8,128)S(1)}, f32[216,128]{1,0:T(8,128)S(1)}, u32[]{:S(2)}, u32[]{:S(2)}) %collective-permute-start.26) | collective-permute-done | bytes 110624 | tf_op jit(solution)/shard_map/ppermute | solution.py:667
  73.3 1.0 %collective-permute-start.30 = (f32[216,128]{1,0:T(8,128)S(1)}, f32[216,128]{1,0:T(8,128)S(1)}, u32[]{:S(2)}, u32[]{:S(2)}) collective-permute-start(f32[216,128]{1,0:T(8,128)S(1)} %get-tuple-element.203.refs_4_), channel_id=1, source_target_pairs={{0,16},{4,20},{8,24},{12,28},{16,0},{20,4},{24,8},{28,12},{1,17},{... | collective-permute-start | bytes 331784 | tf_op jit(solution)/shard_map/ppermute | solution.py:667
  74.3 1.1 %collective-permute-start.29 = (f32[192,128]{1,0:T(8,128)S(1)}, f32[192,128]{1,0:T(8,128)S(1)}, u32[]{:S(2)}, u32[]{:S(2)}) collective-permute-start(f32[192,128]{1,0:T(8,128)S(1)} %get-tuple-element.202.refs_2_), channel_id=1, source_target_pairs={{0,8},{4,12},{8,0},{12,4},{16,24},{20,28},{24,16},{28,20},{1,9},{5... | collective-permute-start | bytes 294920 | tf_op jit(solution)/shard_map/ppermute | solution.py:667
  75.4 5.8 %collective-permute-done.29.refs_3_ = f32[192,128]{1,0:T(8,128)S(1)} collective-permute-done((f32[192,128]{1,0:T(8,128)S(1)}, f32[192,128]{1,0:T(8,128)S(1)}, u32[]{:S(2)}, u32[]{:S(2)}) %collective-permute-start.29) | collective-permute-done | bytes 98336 | tf_op jit(solution)/shard_map/ppermute | solution.py:667
  81.3 1.1 %collective-permute-start.32 = (f32[384,128]{1,0:T(8,128)S(1)}, f32[384,128]{1,0:T(8,128)S(1)}, u32[]{:S(2)}, u32[]{:S(2)}) collective-permute-start(f32[384,128]{1,0:T(8,128)S(1)} %get-tuple-element.211.refs_1_), channel_id=1, source_target_pairs={{0,4},{4,0},{8,12},{12,8},{16,20},{20,16},{24,28},{28,24},{1,5},{5... | collective-permute-start | bytes 589832 | tf_op jit(solution)/shard_map/ppermute | solution.py:667
  82.4 1.0 %collective-permute-start.33 = (f32[216,128]{1,0:T(8,128)S(1)}, f32[216,128]{1,0:T(8,128)S(1)}, u32[]{:S(2)}, u32[]{:S(2)}) collective-permute-start(f32[216,128]{1,0:T(8,128)S(1)} %get-tuple-element.212.refs_3_), channel_id=1, source_target_pairs={{0,4},{4,0},{8,12},{12,8},{16,20},{20,16},{24,28},{28,24},{1,5},{5... | collective-permute-start | bytes 331784 | tf_op jit(solution)/shard_map/ppermute | solution.py:667
  83.4 2.5 %collective-permute-start.35 = (f32[216,128]{1,0:T(8,128)S(1)}, f32[216,128]{1,0:T(8,128)S(1)}, u32[]{:S(2)}, u32[]{:S(2)}) collective-permute-start(f32[216,128]{1,0:T(8,128)S(1)} %get-tuple-element.212.refs_3_), channel_id=1, source_target_pairs={{0,12},{4,8},{8,4},{12,0},{16,28},{20,24},{24,20},{28,16},{1,13},{... | collective-permute-start | bytes 331784 | tf_op jit(solution)/shard_map/ppermute | solution.py:667
  85.9 2.7 %shard_map.189 = (f32[2048,768]{1,0:T(8,128)}, f32[8,128]{1,0:T(8,128)S(1)}) custom-call(f32[1024,768]{1,0:T(8,128)S(1)} %get-tuple-element.200.own, f32[1024,768]{1,0:T(8,128)S(1)} %collective-permute-done.27.other, f32[8,128]{1,0:T(8,128)S(1)} %get-tuple-element.205.refs_0_), custom_call_target="tpu_custom_call" | custom-call | bytes 12582912 | tf_op jit(solution)/shard_map/pallas_call | solution.py:501
  88.7 2.0 %shard_map.190 = (f32[2048,512]{1,0:T(8,128)}, f32[8,128]{1,0:T(8,128)S(1)}) custom-call(f32[1024,512]{1,0:T(8,128)S(1)} %get-tuple-element.207.own, f32[1024,512]{1,0:T(8,128)S(1)} %collective-permute-done.31.other, f32[8,128]{1,0:T(8,128)S(1)} %get-tuple-element.208.refs_0_), custom_call_target="tpu_custom_call" | custom-call | bytes 8388608 | tf_op jit(solution)/shard_map/pallas_call | solution.py:501
  90.7 2.0 %collective-permute-done.33.refs_4_ = f32[216,128]{1,0:T(8,128)S(1)} collective-permute-done((f32[216,128]{1,0:T(8,128)S(1)}, f32[216,128]{1,0:T(8,128)S(1)}, u32[]{:S(2)}, u32[]{:S(2)}) %collective-permute-start.33) | collective-permute-done | bytes 110624 | tf_op jit(solution)/shard_map/ppermute | solution.py:667
  92.7 1.2 %shard_map.191 = (f32[6,64,512]{2,1,0:T(8,128)}, f32[6,64]{1,0:T(8,128)}, f32[6,64,256]{2,1,0:T(8,128)}, f32[6,64]{1,0:T(8,128)}, f32[6,64]{1,0:T(8,128)}, /*ind...) custom-call(f32[768,128]{1,0:T(8,128)S(1)} %get-tuple-element.210.refs_0_, ...), custom_call_target="tpu_custom_call" | custom-call | bytes 2457600 | tf_op jit(solution)/shard_map/pallas_call | solution.py:542
  (67 shorter events, 8.4 us)
Async XLA Ops:
  1.7 13.2 %collective-permute-start.1 = (f32[2,72,768]{2,1,0:T(8,128)S(1)}, f32[2,72,768]{2,1,0:T(8,128)S(1)}, u32[]{:S(2)}, u32[]{:S(2)}) collective-permute-start(f32[2,72,768]{2,1,0:T(8,128)S(1)} %shard_map.169.refs_0_.refs_4_), channel_id=1, source_target_pairs={{0,2},{1,3},{2,0},{3,1},{4,6},{5,7},{6,4},{7,5},{8,10},{9,11},{10,... | collective-permute-start | bytes 1327112 | tf_op jit(solution)/shard_map/ppermute | solution.py:748
  4.7 12.1 %collective-permute-start = (f32[2,72,768]{2,1,0:T(8,128)S(1)}, f32[2,72,768]{2,1,0:T(8,128)S(1)}, u32[]{:S(2)}, u32[]{:S(2)}) collective-permute-start(f32[2,72,768]{2,1,0:T(8,128)S(1)} %shard_map.169.refs_0_.refs_4_), channel_id=1, source_target_pairs={{0,1},{1,0},{2,3},{3,2},{4,5},{5,4},{6,7},{7,6},{8,9},{9,8},{10,11... | collective-permute-start | bytes 1327112 | tf_op jit(solution)/shard_map/ppermute | solution.py:749
  15.0 12.2 %collective-permute-start.4 = (f32[2,64,768]{2,1,0:T(8,128)S(1)}, f32[2,64,768]{2,1,0:T(8,128)S(1)}, u32[]{:S(2)}, u32[]{:S(2)}) collective-permute-start(f32[2,64,768]{2,1,0:T(8,128)S(1)} %get-tuple-element.126), channel_id=1, source_target_pairs={{0,2},{1,3},{2,0},{3,1},{4,6},{5,7},{6,4},{7,5},{8,10},{9,11},{10,... | collective-permute-start | bytes 1179656 | tf_op jit(solution)/shard_map/ppermute | solution.py:808
  24.4 6.4 %collective-permute-start.6 = (f32[2,64,768]{2,1,0:T(8,128)S(1)}, f32[2,64,768]{2,1,0:T(8,128)S(1)}, u32[]{:S(2)}, u32[]{:S(2)}) collective-permute-start(f32[2,64,768]{2,1,0:T(8,128)S(1)} %get-tuple-element.126), channel_id=1, source_target_pairs={{0,1},{1,0},{2,3},{3,2},{4,5},{5,4},{6,7},{7,6},{8,9},{9,8},{10,11... | collective-permute-start | bytes 1179656 | tf_op jit(solution)/shard_map/ppermute | solution.py:809
  27.4 3.4 %collective-permute-start.7 = (f32[2,64,768]{2,1,0:T(8,128)S(1)}, f32[2,64,768]{2,1,0:T(8,128)S(1)}, u32[]{:S(2)}, u32[]{:S(2)}) collective-permute-start(f32[2,64,768]{2,1,0:T(8,128)S(1)} %get-tuple-element.136), channel_id=1, source_target_pairs={{0,1},{1,0},{2,3},{3,2},{4,5},{5,4},{6,7},{7,6},{8,9},{9,8},{10,11... | collective-permute-start | bytes 1179656 | tf_op jit(solution)/shard_map/ppermute | solution.py:806
  27.6 11.0 %collective-permute-start.5 = (f32[384,128]{1,0:T(8,128)S(1)}, f32[384,128]{1,0:T(8,128)S(1)}, u32[]{:S(2)}, u32[]{:S(2)}) collective-permute-start(f32[384,128]{1,0:T(8,128)S(1)} %get-tuple-element.135), channel_id=1, source_target_pairs={{0,4},{4,0},{8,12},{12,8},{16,20},{20,16},{24,28},{28,24},{1,5},{5... | collective-permute-start | bytes 589832 | tf_op jit(solution)/shard_map/ppermute | solution.py:667
  29.3 9.4 %collective-permute-start.8 = (f32[1,64,768]{2,1,0:T(8,128)S(1)}, f32[1,64,768]{2,1,0:T(8,128)S(1)}, u32[]{:S(2)}, u32[]{:S(2)}) collective-permute-start(f32[1,64,768]{2,1,0:T(8,128)S(1)} %get-tuple-element.141), channel_id=1, source_target_pairs={{0,2},{1,3},{2,0},{3,1},{4,6},{5,7},{6,4},{7,5},{8,10},{9,11},{10,... | collective-permute-start | bytes 589832 | tf_op jit(solution)/shard_map/ppermute | solution.py:808
  38.8 3.4 %collective-permute-start.12 = (f32[1,64,768]{2,1,0:T(8,128)S(1)}, f32[1,64,768]{2,1,0:T(8,128)S(1)}, u32[]{:S(2)}, u32[]{:S(2)}) collective-permute-start(f32[1,64,768]{2,1,0:T(8,128)S(1)} %get-tuple-element.141), channel_id=1, source_target_pairs={{0,1},{1,0},{2,3},{3,2},{4,5},{5,4},{6,7},{7,6},{8,9},{9,8},{10,11... | collective-permute-start | bytes 589832 | tf_op jit(solution)/shard_map/ppermute | solution.py:809
  39.3 3.5 %collective-permute-start.13 = (f32[1,64,768]{2,1,0:T(8,128)S(1)}, f32[1,64,768]{2,1,0:T(8,128)S(1)}, u32[]{:S(2)}, u32[]{:S(2)}) collective-permute-start(f32[1,64,768]{2,1,0:T(8,128)S(1)} %get-tuple-element.151), channel_id=1, source_target_pairs={{0,1},{1,0},{2,3},{3,2},{4,5},{5,4},{6,7},{7,6},{8,9},{9,8},{10,11... | collective-permute-start | bytes 589832 | tf_op jit(solution)/shard_map/ppermute | solution.py:806
  39.4 8.2 %collective-permute-start.14 = (f32[1,64,768]{2,1,0:T(8,128)S(1)}, f32[1,64,768]{2,1,0:T(8,128)S(1)}, u32[]{:S(2)}, u32[]{:S(2)}) collective-permute-start(f32[1,64,768]{2,1,0:T(8,128)S(1)} %get-tuple-element.155), channel_id=1, source_target_pairs={{0,2},{1,3},{2,0},{3,1},{4,6},{5,7},{6,4},{7,5},{8,10},{9,11},{10,... | collective-permute-start | bytes 589832 | tf_op jit(solution)/shard_map/ppermute | solution.py:808
  39.9 12.3 %collective-permute-start.17 = (f32[1,64,768]{2,1,0:T(8,128)S(1)}, f32[1,64,768]{2,1,0:T(8,128)S(1)}, u32[]{:S(2)}, u32[]{:S(2)}) collective-permute-start(f32[1,64,768]{2,1,0:T(8,128)S(1)} %get-tuple-element.155), channel_id=1, source_target_pairs={{0,1},{1,0},{2,3},{3,2},{4,5},{5,4},{6,7},{7,6},{8,9},{9,8},{10,11... | collective-permute-start | bytes 589832 | tf_op jit(solution)/shard_map/ppermute | solution.py:809
  40.5 7.1 %collective-permute-start.9 = (f32[192,128]{1,0:T(8,128)S(1)}, f32[192,128]{1,0:T(8,128)S(1)}, u32[]{:S(2)}, u32[]{:S(2)}) collective-permute-start(f32[192,128]{1,0:T(8,128)S(1)} %get-tuple-element.145), channel_id=1, source_target_pairs={{0,8},{4,12},{8,0},{12,4},{16,24},{20,28},{24,16},{28,20},{1,9},{5... | collective-permute-start | bytes 294920 | tf_op jit(solution)/shard_map/ppermute | solution.py:667
  42.2 6.7 %collective-permute-start.11 = (f32[384,128]{1,0:T(8,128)S(1)}, f32[384,128]{1,0:T(8,128)S(1)}, u32[]{:S(2)}, u32[]{:S(2)}) collective-permute-start(f32[384,128]{1,0:T(8,128)S(1)} %get-tuple-element.150), channel_id=1, source_target_pairs={{0,4},{4,0},{8,12},{12,8},{16,20},{20,16},{24,28},{28,24},{1,5},{5... | collective-permute-start | bytes 589832 | tf_op jit(solution)/shard_map/ppermute | solution.py:667
  49.1 8.2 %collective-permute-start.15 = (f32[192,128]{1,0:T(8,128)S(1)}, f32[192,128]{1,0:T(8,128)S(1)}, u32[]{:S(2)}, u32[]{:S(2)}) collective-permute-start(f32[192,128]{1,0:T(8,128)S(1)} %get-tuple-element.157.refs_0_), channel_id=1, source_target_pairs={{0,16},{4,20},{8,24},{12,28},{16,0},{20,4},{24,8},{28,12},{1,17},{... | collective-permute-start | bytes 294920 | tf_op jit(solution)/shard_map/ppermute | solution.py:667
  51.7 6.9 %collective-permute-start.16 = (f32[192,128]{1,0:T(8,128)S(1)}, f32[192,128]{1,0:T(8,128)S(1)}, u32[]{:S(2)}, u32[]{:S(2)}) collective-permute-start(f32[192,128]{1,0:T(8,128)S(1)} %get-tuple-element.159), channel_id=1, source_target_pairs={{0,8},{4,12},{8,0},{12,4},{16,24},{20,28},{24,16},{28,20},{1,9},{5... | collective-permute-start | bytes 294920 | tf_op jit(solution)/shard_map/ppermute | solution.py:667
  52.2 10.3 %collective-permute-start.21 = (f32[384,128]{1,0:T(8,128)S(1)}, f32[384,128]{1,0:T(8,128)S(1)}, u32[]{:S(2)}, u32[]{:S(2)}) collective-permute-start(f32[384,128]{1,0:T(8,128)S(1)} %get-tuple-element.172), channel_id=1, source_target_pairs={{0,1},{1,0},{2,3},{3,2},{4,5},{5,4},{6,7},{7,6},{8,9},{9,8},{10,11... | collective-permute-start | bytes 589832 | tf_op jit(solution)/shard_map/ppermute | solution.py:811
  58.6 3.9 %collective-permute-start.22 = (f32[384,128]{1,0:T(8,128)S(1)}, f32[384,128]{1,0:T(8,128)S(1)}, u32[]{:S(2)}, u32[]{:S(2)}) collective-permute-start(f32[384,128]{1,0:T(8,128)S(1)} %get-tuple-element.173), channel_id=1, source_target_pairs={{0,1},{1,0},{2,3},{3,2},{4,5},{5,4},{6,7},{7,6},{8,9},{9,8},{10,11... | collective-permute-start | bytes 589832 | tf_op jit(solution)/shard_map/ppermute | solution.py:811
  58.7 3.8 %collective-permute-start.23 = (f32[96,128]{1,0:T(8,128)S(1)}, f32[96,128]{1,0:T(8,128)S(1)}, u32[]{:S(2)}, u32[]{:S(2)}) collective-permute-start(f32[96,128]{1,0:T(8,128)S(1)} %get-tuple-element.174), channel_id=1, source_target_pairs={{0,1},{1,0},{2,3},{3,2},{4,5},{5,4},{6,7},{7,6},{8,9},{9,8},{10,11... | collective-permute-start | bytes 147464 | tf_op jit(solution)/shard_map/ppermute | solution.py:811
  59.2 10.9 %collective-permute-start.19 = (f32[192,128]{1,0:T(8,128)S(1)}, f32[192,128]{1,0:T(8,128)S(1)}, u32[]{:S(2)}, u32[]{:S(2)}) collective-permute-start(f32[192,128]{1,0:T(8,128)S(1)} %get-tuple-element.168.refs_0_), channel_id=1, source_target_pairs={{0,8},{4,12},{8,0},{12,4},{16,24},{20,28},{24,16},{28,20},{1,9},{5... | collective-permute-start | bytes 294920 | tf_op jit(solution)/shard_map/ppermute | solution.py:667
  59.6 10.5 %collective-permute-start.20 = (f32[192,128]{1,0:T(8,128)S(1)}, f32[192,128]{1,0:T(8,128)S(1)}, u32[]{:S(2)}, u32[]{:S(2)}) collective-permute-start(f32[192,128]{1,0:T(8,128)S(1)} %get-tuple-element.169.refs_2_), channel_id=1, source_target_pairs={{0,16},{4,20},{8,24},{12,28},{16,0},{20,4},{24,8},{28,12},{1,17},{... | collective-permute-start | bytes 294920 | tf_op jit(solution)/shard_map/ppermute | solution.py:667
  62.6 7.5 %collective-permute-start.24 = (f32[216,128]{1,0:T(8,128)S(1)}, f32[216,128]{1,0:T(8,128)S(1)}, u32[]{:S(2)}, u32[]{:S(2)}) collective-permute-start(f32[216,128]{1,0:T(8,128)S(1)} %get-tuple-element.183), channel_id=1, source_target_pairs={{0,4},{4,0},{8,12},{12,8},{16,20},{20,16},{24,28},{28,24},{1,5},{5... | collective-permute-start | bytes 331784 | tf_op jit(solution)/shard_map/ppermute | solution.py:667
  63.6 6.6 %collective-permute-start.25 = (f32[216,128]{1,0:T(8,128)S(1)}, f32[216,128]{1,0:T(8,128)S(1)}, u32[]{:S(2)}, u32[]{:S(2)}) collective-permute-start(f32[216,128]{1,0:T(8,128)S(1)} %get-tuple-element.184), channel_id=1, source_target_pairs={{0,8},{4,12},{8,0},{12,4},{16,24},{20,28},{24,16},{28,20},{1,9},{5... | collective-permute-start | bytes 331784 | tf_op jit(solution)/shard_map/ppermute | solution.py:667
  63.8 8.0 %collective-permute-start.26 = (f32[216,128]{1,0:T(8,128)S(1)}, f32[216,128]{1,0:T(8,128)S(1)}, u32[]{:S(2)}, u32[]{:S(2)}) collective-permute-start(f32[216,128]{1,0:T(8,128)S(1)} %get-tuple-element.185), channel_id=1, source_target_pairs={{0,12},{4,8},{8,4},{12,0},{16,28},{20,24},{24,20},{28,16},{1,13},{... | collective-permute-start | bytes 331784 | tf_op jit(solution)/shard_map/ppermute | solution.py:667
  71.9 11.6 %collective-permute-start.27 = (f32[1024,768]{1,0:T(8,128)S(1)}, f32[1024,768]{1,0:T(8,128)S(1)}, u32[]{:S(2)}, u32[]{:S(2)}) collective-permute-start(f32[1024,768]{1,0:T(8,128)S(1)} %get-tuple-element.200.own), channel_id=1, source_target_pairs={{0,1},{1,0},{2,3},{3,2},{4,5},{5,4},{6,7},{7,6},{8,9},{9,8},{10,11... | collective-permute-start | bytes 9437192 | tf_op jit(solution)/shard_map/ppermute | solution.py:817
  71.9 16.7 %collective-permute-start.31 = (f32[1024,512]{1,0:T(8,128)S(1)}, f32[1024,512]{1,0:T(8,128)S(1)}, u32[]{:S(2)}, u32[]{:S(2)}) collective-permute-start(f32[1024,512]{1,0:T(8,128)S(1)} %get-tuple-element.207.own), channel_id=1, source_target_pairs={{0,1},{1,0},{2,3},{3,2},{4,5},{5,4},{6,7},{7,6},{8,9},{9,8},{10,11... | collective-permute-start | bytes 6291464 | tf_op jit(solution)/shard_map/ppermute | solution.py:817
  72.4 8.8 %collective-permute-start.28 = (f32[384,128]{1,0:T(8,128)S(1)}, f32[384,128]{1,0:T(8,128)S(1)}, u32[]{:S(2)}, u32[]{:S(2)}) collective-permute-start(f32[384,128]{1,0:T(8,128)S(1)} %get-tuple-element.201.refs_0_), channel_id=1, source_target_pairs={{0,4},{4,0},{8,12},{12,8},{16,20},{20,16},{24,28},{28,24},{1,5},{5... | collective-permute-start | bytes 589832 | tf_op jit(solution)/shard_map/ppermute | solution.py:667
  73.3 7.9 %collective-permute-start.30 = (f32[216,128]{1,0:T(8,128)S(1)}, f32[216,128]{1,0:T(8,128)S(1)}, u32[]{:S(2)}, u32[]{:S(2)}) collective-permute-start(f32[216,128]{1,0:T(8,128)S(1)} %get-tuple-element.203.refs_4_), channel_id=1, source_target_pairs={{0,16},{4,20},{8,24},{12,28},{16,0},{20,4},{24,8},{28,12},{1,17},{... | collective-permute-start | bytes 331784 | tf_op jit(solution)/shard_map/ppermute | solution.py:667
  74.3 6.9 %collective-permute-start.29 = (f32[192,128]{1,0:T(8,128)S(1)}, f32[192,128]{1,0:T(8,128)S(1)}, u32[]{:S(2)}, u32[]{:S(2)}) collective-permute-start(f32[192,128]{1,0:T(8,128)S(1)} %get-tuple-element.202.refs_2_), channel_id=1, source_target_pairs={{0,8},{4,12},{8,0},{12,4},{16,24},{20,28},{24,16},{28,20},{1,9},{5... | collective-permute-start | bytes 294920 | tf_op jit(solution)/shard_map/ppermute | solution.py:667
  81.3 11.4 %collective-permute-start.32 = (f32[384,128]{1,0:T(8,128)S(1)}, f32[384,128]{1,0:T(8,128)S(1)}, u32[]{:S(2)}, u32[]{:S(2)}) collective-permute-start(f32[384,128]{1,0:T(8,128)S(1)} %get-tuple-element.211.refs_1_), channel_id=1, source_target_pairs={{0,4},{4,0},{8,12},{12,8},{16,20},{20,16},{24,28},{28,24},{1,5},{5... | collective-permute-start | bytes 589832 | tf_op jit(solution)/shard_map/ppermute | solution.py:667
  82.4 10.3 %collective-permute-start.33 = (f32[216,128]{1,0:T(8,128)S(1)}, f32[216,128]{1,0:T(8,128)S(1)}, u32[]{:S(2)}, u32[]{:S(2)}) collective-permute-start(f32[216,128]{1,0:T(8,128)S(1)} %get-tuple-element.212.refs_3_), channel_id=1, source_target_pairs={{0,4},{4,0},{8,12},{12,8},{16,20},{20,16},{24,28},{28,24},{1,5},{5... | collective-permute-start | bytes 331784 | tf_op jit(solution)/shard_map/ppermute | solution.py:667
  83.4 9.3 %collective-permute-start.34 = (f32[216,128]{1,0:T(8,128)S(1)}, f32[216,128]{1,0:T(8,128)S(1)}, u32[]{:S(2)}, u32[]{:S(2)}) collective-permute-start(f32[216,128]{1,0:T(8,128)S(1)} %get-tuple-element.212.refs_3_), channel_id=1, source_target_pairs={{0,8},{4,12},{8,0},{12,4},{16,24},{20,28},{24,16},{28,20},{1,9},{5... | collective-permute-start | bytes 331784 | tf_op jit(solution)/shard_map/ppermute | solution.py:667
  83.4 9.3 %collective-permute-start.35 = (f32[216,128]{1,0:T(8,128)S(1)}, f32[216,128]{1,0:T(8,128)S(1)}, u32[]{:S(2)}, u32[]{:S(2)}) collective-permute-start(f32[216,128]{1,0:T(8,128)S(1)} %get-tuple-element.212.refs_3_), channel_id=1, source_target_pairs={{0,12},{4,8},{8,4},{12,0},{16,28},{20,24},{24,20},{28,16},{1,13},{... | collective-permute-start | bytes 331784 | tf_op jit(solution)/shard_map/ppermute | solution.py:667
  (6 other events, 24.3 us)

commit v7 on v6

--- a/solution.py
+++ b/solution.py
@@ -17,7 +17,7 @@
 LANES = 128
 TOKEN = (8, LANES)
 RB = 1024
-ROW_BLOCK = 256
+ROW_BLOCK = 512
 SUB = 256
 LAG = 1
 EPSILON = 1e-05
@@ -184,6 +184,7 @@
 
 def expert_kernel(group, first, last, n_deps, *refs):
     n = len(group)
+    sub = SUB * n
     refs = list(refs)
     evh_ref, evl_ref, cot_ref, p_ref = refs[:4]
     shards = refs[4:8]
@@ -232,9 +233,9 @@
                 winh[pl.ds(i * H + at, SLICE), :], winl[pl.ds(i * H + at, SLICE), :] = split(into)
                 wouth[i, pl.ds(at, SLICE), :], woutl[i, pl.ds(at, SLICE), :] = split(out - centre)
 
-    subs = RB // SUB
-    rows_of = [slice(s * SUB, (s + 1) * SUB) for s in range(subs)]
-    lane = lax.broadcasted_iota(jnp.int32, (SUB, LANES), 1)
+    subs = RB // sub
+    rows_of = [slice(s * sub, (s + 1) * sub) for s in range(subs)]
+    lane = lax.broadcasted_iota(jnp.int32, (sub, LANES), 1)
     vector = lambda k, e: small[k * E + e : k * E + e + 1, :]
     state = [dict() for _ in range(subs)]
 
@@ -299,7 +300,7 @@
                     value = mixed[t][:, other * LANES : (other + 1) * LANES]
                     mix_ref[rows_of[s], at] = value if first else mix_in[rows_of[s], at] + value
                 elif first:
-                    mix_ref[rows_of[s], at] = jnp.zeros((SUB, LANES), F32)
+                    mix_ref[rows_of[s], at] = jnp.zeros((sub, LANES), F32)
                 else:
                     mix_ref[rows_of[s], at] = mix_in[rows_of[s], at]
         if last:

time: 94.2 us -> 93.5 us (level)
  Pallas kernels: 46.6 us -> 44.9 us
    pallas_call x3, Pallas kernels: 7.86 us -> 6.87 us  [event_grads(): pl.pallas_call(functools.partial(event_kernel, len(highs), bool(gating),...]
  transfers between devices with their start and end apart: 36 -> 36, of which waited for: 8 -> 10; matrix products, arithmetic and copies ran while one was open for 0% -> 0% of each run, Pallas kernels for 47% -> 46%
where the time goes in v7:
time: 93.5 us; the launch traced here: 93.2 us
  Pallas kernels  44.9 us (48%)
  starting transfers between devices  29.6 us (32%)
  waiting for transfers between devices  17.7 us (19%)
  between operations  0.98 us (1%)
    pallas_call x4, Pallas kernels, experts(): pl.pallas_call(functools.partial(expert_kernel, group, first, last, len(d...  24.5 us
    ppermute x17, starting transfers between devices, exchange(): lax.ppermute(whole if parts is None else parts[m - 1], 'dp', [(i, i ^ m <...  19.8 us
    ppermute x17, waiting for transfers between devices, exchange(): lax.ppermute(whole if parts is None else parts[m - 1], 'dp', [(i, i ^ m <...  12.9 us
    pallas_call x3, Pallas kernels, event_grads(): pl.pallas_call(functools.partial(event_kernel, len(highs), bool(gating),...  6.87 us
    pallas_call x2, Pallas kernels, place(): pl.pallas_call(place_kernel, in_specs=[anywhere] * (2 + len(deps)), out_s...  4.75 us
    pallas_call x1, Pallas kernels, gates(): pl.pallas_call(functools.partial(gate_kernel, len(deps)), in_specs=[pl.Bl...  4.67 us
    ppermute x1, waiting for transfers between devices, per_device(): far = [lax.ppermute(own[0], 'tp', across)]  4.26 us
    ppermute x3, starting transfers between devices, per_device(): far.append(lax.ppermute(outs[-1][1], 'tp', across))  3.82 us
  transfers between devices with their start and end apart: 36, of which 10 were waited for; matrix products, arithmetic and copies ran while one was open for 0% of the time, Pallas kernels for 46%

profile of v7, /device:TPU:0, one launch (start us, length us, event | category | flops | bytes accessed | tf_op | source)
XLA Modules:
  0.0 93.2 jit_solution(14022334770237226651)
XLA Ops:
  0.7 1.0 %shard_map.169.refs_0_.refs_4_ = f32[2,72,768]{2,1,0:T(8,128)S(1)} custom-call(f32[6,64,512]{2,1,0:T(8,128)} %bitcast.8, f32[6,64,256]{2,1,0:T(8,128)} %bitcast.10, f32[6,64]{1,0:T(8,128)} %refs_0_.1, f32[6,64]{1,0:T(8,128)} %refs_1_.1, f32[6,64]{1,0:T(8,128)} %refs_2_.1, f32[6,64]{1,0:T(8,128)} %refs_3_.1), custom_call_target="tpu_custom_call" | custom-call | bytes 786432 | tf_op jit(solution)/shard_map/pallas_call | solution.py:174
  1.7 3.0 %collective-permute-start.1 = (f32[2,72,768]{2,1,0:T(8,128)S(1)}, f32[2,72,768]{2,1,0:T(8,128)S(1)}, u32[]{:S(2)}, u32[]{:S(2)}) collective-permute-start(f32[2,72,768]{2,1,0:T(8,128)S(1)} %shard_map.169.refs_0_.refs_4_), channel_id=1, source_target_pairs={{0,2},{1,3},{2,0},{3,1},{4,6},{5,7},{6,4},{7,5},{8,10},{9,11},{10,... | collective-permute-start | bytes 1327112 | tf_op jit(solution)/shard_map/ppermute | solution.py:749
  4.7 1.2 %shard_map.170 = (f32[2,64,768]{2,1,0:T(8,128)S(1)}, f32[1,64,768]{2,1,0:T(8,128)S(1)}, f32[1,64,768]{2,1,0:T(8,128)S(1)}) custom-call(f32[6,64,512]{2,1,0:T(8,128)} %bitcast.9, f32[6,64,256]{2,1,0:T(8,128)} %bitcast.11, f32[2,72,768]{2,1,0:T(8,128)S(1)} %shard_map.169.refs_0_.refs_4_), custom_call_target="tpu_custom_call" | custom-call | bytes 786432 | tf_op jit(solution)/shard_map/pallas_call | solution.py:174
  6.0 4.7 %shard_map.171 = (bf16[1024,512]{1,0:T(8,128)(2,1)S(1)}, bf16[1024,512]{1,0:T(8,128)(2,1)S(1)}, f32[1024,128]{1,0:T(8,128)S(1)}, f32[1024,768]{1,0:T(8,128)S(1)}) custom-call(s32[8]{0:T(128)S(1)} %copy-done.1, f32[2048,512]{1,0:T(8,128)} %ev_ref.1, f32[2048,768]{1,0:T(8,128)} %cot_ref.1, f32[14,512]{1,0:T(8,128)} %bitcast.6, ...), custom_call_target="tpu_custom_call" | custom-call | flops 402653184 | bytes 4194304 | tf_op jit(solution)/shard_map/pallas_call | solution.py:125
  10.6 4.3 %collective-permute-done.1.refs_0_.refs_6_ = f32[2,72,768]{2,1,0:T(8,128)S(1)} collective-permute-done((f32[2,72,768]{2,1,0:T(8,128)S(1)}, f32[2,72,768]{2,1,0:T(8,128)S(1)}, u32[]{:S(2)}, u32[]{:S(2)}) %collective-permute-start.1) | collective-permute-done | bytes 442400 | tf_op jit(solution)/shard_map/ppermute | solution.py:749
  15.0 1.8 %collective-permute-start.4 = (f32[2,64,768]{2,1,0:T(8,128)S(1)}, f32[2,64,768]{2,1,0:T(8,128)S(1)}, u32[]{:S(2)}, u32[]{:S(2)}) collective-permute-start(f32[2,64,768]{2,1,0:T(8,128)S(1)} %get-tuple-element.126), channel_id=1, source_target_pairs={{0,2},{1,3},{2,0},{3,1},{4,6},{5,7},{6,4},{7,5},{8,10},{9,11},{10,... | collective-permute-start | bytes 1179656 | tf_op jit(solution)/shard_map/ppermute | solution.py:809
  16.9 7.1 %shard_map.173 = (f32[1024,768]{1,0:T(8,128)S(1)}, f32[1024,128]{1,0:T(8,128)S(1)}, bf16[1024,512]{1,0:T(8,128)(2,1)S(1)}, bf16[1024,512]{1,0:T(8,128)(2,1)S(1)}...) custom-call(bf16[1024,512]{1,0:T(8,128)(2,1)S(1)} %get-tuple-element, ...), custom_call_target="tpu_custom_call" | custom-call | flops 8858370048 | bytes 14336000 | tf_op jit(solution)/shard_map/pallas_call | solution.py:404
  24.6 2.1 %shard_map.175 = (f32[1024,512]{1,0:T(8,128)S(1)}, f32[8,128]{1,0:T(8,128)S(1)}) custom-call(bf16[1024,512]{1,0:T(8,128)(2,1)S(1)} %get-tuple-element.128.refs_0_, bf16[1024,512]{1,0:T(8,128)(2,1)S(1)} %get-tuple-element.129.refs_1_, bf16[512,512]{1,0:T(8,128)(2,1)S(1)} %get-tuple-element.130.refs_2_, bf16[512,512]{1,0:T(8,128)(2,1)S(1)} %get-tuple-element.131.refs_3_, ...), custom_call_target="tpu_custom_call" | custom-call | flops 1610612736 | bytes 4096000 | tf_op jit(solution)/shard_map/pallas_call | solution.py:469
  27.1 1.7 %collective-permute-start.5 = (f32[384,128]{1,0:T(8,128)S(1)}, f32[384,128]{1,0:T(8,128)S(1)}, u32[]{:S(2)}, u32[]{:S(2)}) collective-permute-start(f32[384,128]{1,0:T(8,128)S(1)} %get-tuple-element.135), channel_id=1, source_target_pairs={{0,4},{4,0},{8,12},{12,8},{16,20},{20,16},{24,28},{28,24},{1,5},{5... | collective-permute-start | bytes 589832 | tf_op jit(solution)/shard_map/ppermute | solution.py:668
  28.8 1.5 %collective-permute-start.8 = (f32[1,64,768]{2,1,0:T(8,128)S(1)}, f32[1,64,768]{2,1,0:T(8,128)S(1)}, u32[]{:S(2)}, u32[]{:S(2)}) collective-permute-start(f32[1,64,768]{2,1,0:T(8,128)S(1)} %get-tuple-element.141), channel_id=1, source_target_pairs={{0,2},{1,3},{2,0},{3,1},{4,6},{5,7},{6,4},{7,5},{8,10},{9,11},{10,... | collective-permute-start | bytes 589832 | tf_op jit(solution)/shard_map/ppermute | solution.py:809
  30.3 7.6 %shard_map.177 = (f32[1024,768]{1,0:T(8,128)S(1)}, f32[1024,128]{1,0:T(8,128)S(1)}, bf16[1024,512]{1,0:T(8,128)(2,1)S(1)}, bf16[1024,512]{1,0:T(8,128)(2,1)S(1)}...) custom-call(bf16[1024,512]{1,0:T(8,128)(2,1)S(1)} %get-tuple-element, ...), custom_call_target="tpu_custom_call", output_to_operand_aliasing={{0}: (9, {})} | custom-call | flops 8858370048 | bytes 14336000 | tf_op jit(solution)/shard_map/pallas_call | solution.py:404
  39.8 1.6 %collective-permute-start.9 = (f32[192,128]{1,0:T(8,128)S(1)}, f32[192,128]{1,0:T(8,128)S(1)}, u32[]{:S(2)}, u32[]{:S(2)}) collective-permute-start(f32[192,128]{1,0:T(8,128)S(1)} %get-tuple-element.145), channel_id=1, source_target_pairs={{0,8},{4,12},{8,0},{12,4},{16,24},{20,28},{24,16},{28,20},{1,9},{5... | collective-permute-start | bytes 294920 | tf_op jit(solution)/shard_map/ppermute | solution.py:668
  42.1 4.8 %shard_map.180 = (f32[1024,768]{1,0:T(8,128)S(1)}, f32[1024,128]{1,0:T(8,128)S(1)}, bf16[1024,256]{1,0:T(8,128)(2,1)S(1)}, bf16[1024,256]{1,0:T(8,128)(2,1)S(1)}...) custom-call(bf16[1024,512]{1,0:T(8,128)(2,1)S(1)} %get-tuple-element, ...), custom_call_target="tpu_custom_call", output_to_operand_aliasing={{0}: (9, {})} | custom-call | flops 4429185024 | bytes 14336000 | tf_op jit(solution)/shard_map/pallas_call | solution.py:404
  47.0 1.3 %collective-permute-done.11.refs_3_ = f32[384,128]{1,0:T(8,128)S(1)} collective-permute-done((f32[384,128]{1,0:T(8,128)S(1)}, f32[384,128]{1,0:T(8,128)S(1)}, u32[]{:S(2)}, u32[]{:S(2)}) %collective-permute-start.11) | collective-permute-done | bytes 196640 | tf_op jit(solution)/shard_map/ppermute | solution.py:668
  48.4 2.7 %collective-permute-start.15 = (f32[192,128]{1,0:T(8,128)S(1)}, f32[192,128]{1,0:T(8,128)S(1)}, u32[]{:S(2)}, u32[]{:S(2)}) collective-permute-start(f32[192,128]{1,0:T(8,128)S(1)} %get-tuple-element.157.refs_0_), channel_id=1, source_target_pairs={{0,16},{4,20},{8,24},{12,28},{16,0},{20,4},{24,8},{28,12},{1,17},{... | collective-permute-start | bytes 294920 | tf_op jit(solution)/shard_map/ppermute | solution.py:668
  51.5 4.9 %shard_map.182 = (f32[1024,768]{1,0:T(8,128)S(1)}, f32[1024,128]{1,0:T(8,128)S(1)}, bf16[1024,256]{1,0:T(8,128)(2,1)S(1)}, bf16[1024,256]{1,0:T(8,128)(2,1)S(1)}...) custom-call(bf16[1024,512]{1,0:T(8,128)(2,1)S(1)} %get-tuple-element, ...), custom_call_target="tpu_custom_call", output_to_operand_aliasing={{0}: (9, {})} | custom-call | flops 4429185024 | bytes 14336000 | tf_op jit(solution)/shard_map/pallas_call | solution.py:404
  56.6 1.3 %collective-permute-done.16.refs_3_ = f32[192,128]{1,0:T(8,128)S(1)} collective-permute-done((f32[192,128]{1,0:T(8,128)S(1)}, f32[192,128]{1,0:T(8,128)S(1)}, u32[]{:S(2)}, u32[]{:S(2)}) %collective-permute-start.16) | collective-permute-done | bytes 98336 | tf_op jit(solution)/shard_map/ppermute | solution.py:668
  59.0 1.4 %collective-permute-start.20 = (f32[192,128]{1,0:T(8,128)S(1)}, f32[192,128]{1,0:T(8,128)S(1)}, u32[]{:S(2)}, u32[]{:S(2)}) collective-permute-start(f32[192,128]{1,0:T(8,128)S(1)} %get-tuple-element.169.refs_2_), channel_id=1, source_target_pairs={{0,16},{4,20},{8,24},{12,28},{16,0},{20,4},{24,8},{28,12},{1,17},{... | collective-permute-start | bytes 294920 | tf_op jit(solution)/shard_map/ppermute | solution.py:668
  60.3 1.2 %shard_map.184 = (f32[1024,512]{1,0:T(8,128)S(1)}, f32[8,128]{1,0:T(8,128)S(1)}) custom-call(bf16[1024,256]{1,0:T(8,128)(2,1)S(1)} %get-tuple-element.175.refs_0_, bf16[1024,256]{1,0:T(8,128)(2,1)S(1)} %get-tuple-element.176.refs_1_, bf16[256,512]{1,0:T(8,128)(2,1)S(1)} %get-tuple-element.177.refs_2_, ...), custom_call_target="tpu_custom_call", output_to_operand_aliasing={{0}: (4, {})} | custom-call | flops 805306368 | bytes 4096000 | tf_op jit(solution)/shard_map/pallas_call | solution.py:469
  62.8 2.3 %collective-permute-start.26 = (f32[216,128]{1,0:T(8,128)S(1)}, f32[216,128]{1,0:T(8,128)S(1)}, u32[]{:S(2)}, u32[]{:S(2)}) collective-permute-start(f32[216,128]{1,0:T(8,128)S(1)} %get-tuple-element.185), channel_id=1, source_target_pairs={{0,12},{4,8},{8,4},{12,0},{16,28},{20,24},{24,20},{28,16},{1,13},{... | collective-permute-start | bytes 331784 | tf_op jit(solution)/shard_map/ppermute | solution.py:668
  65.2 3.6 %shard_map.186 = (f32[1024,512]{1,0:T(8,128)S(1)}, f32[8,128]{1,0:T(8,128)S(1)}) custom-call(bf16[1024,512]{1,0:T(8,128)(2,1)S(1)} %get-tuple-element.187.refs_0_, bf16[1024,256]{1,0:T(8,128)(2,1)S(1)} %get-tuple-element.188.refs_1_, bf16[1024,512]{1,0:T(8,128)(2,1)S(1)} %get-tuple-element.189.refs_2_, ...), custom_call_target="tpu_custom_call", output_to_operand_aliasing={{0}: (10, {})} | custom-call | flops 2415919104 | bytes 4096000 | tf_op jit(solution)/shard_map/pallas_call | solution.py:469
  69.0 1.7 %collective-permute-done.26.refs_7_ = f32[216,128]{1,0:T(8,128)S(1)} collective-permute-done((f32[216,128]{1,0:T(8,128)S(1)}, f32[216,128]{1,0:T(8,128)S(1)}, u32[]{:S(2)}, u32[]{:S(2)}) %collective-permute-start.26) | collective-permute-done | bytes 110624 | tf_op jit(solution)/shard_map/ppermute | solution.py:668
  73.3 1.1 %collective-permute-start.29 = (f32[192,128]{1,0:T(8,128)S(1)}, f32[192,128]{1,0:T(8,128)S(1)}, u32[]{:S(2)}, u32[]{:S(2)}) collective-permute-start(f32[192,128]{1,0:T(8,128)S(1)} %get-tuple-element.202.refs_2_), channel_id=1, source_target_pairs={{0,8},{4,12},{8,0},{12,4},{16,24},{20,28},{24,16},{28,20},{1,9},{5... | collective-permute-start | bytes 294920 | tf_op jit(solution)/shard_map/ppermute | solution.py:668
  74.4 4.5 %collective-permute-done.29.refs_3_ = f32[192,128]{1,0:T(8,128)S(1)} collective-permute-done((f32[192,128]{1,0:T(8,128)S(1)}, f32[192,128]{1,0:T(8,128)S(1)}, u32[]{:S(2)}, u32[]{:S(2)}) %collective-permute-start.29) | collective-permute-done | bytes 98336 | tf_op jit(solution)/shard_map/ppermute | solution.py:668
  78.9 1.4 %collective-permute-done.30.refs_5_ = f32[216,128]{1,0:T(8,128)S(1)} collective-permute-done((f32[216,128]{1,0:T(8,128)S(1)}, f32[216,128]{1,0:T(8,128)S(1)}, u32[]{:S(2)}, u32[]{:S(2)}) %collective-permute-start.30) | collective-permute-done | bytes 110624 | tf_op jit(solution)/shard_map/ppermute | solution.py:668
  80.4 1.1 %collective-permute-start.32 = (f32[384,128]{1,0:T(8,128)S(1)}, f32[384,128]{1,0:T(8,128)S(1)}, u32[]{:S(2)}, u32[]{:S(2)}) collective-permute-start(f32[384,128]{1,0:T(8,128)S(1)} %get-tuple-element.211.refs_1_), channel_id=1, source_target_pairs={{0,4},{4,0},{8,12},{12,8},{16,20},{20,16},{24,28},{28,24},{1,5},{5... | collective-permute-start | bytes 589832 | tf_op jit(solution)/shard_map/ppermute | solution.py:668
  81.4 1.0 %collective-permute-start.33 = (f32[216,128]{1,0:T(8,128)S(1)}, f32[216,128]{1,0:T(8,128)S(1)}, u32[]{:S(2)}, u32[]{:S(2)}) collective-permute-start(f32[216,128]{1,0:T(8,128)S(1)} %get-tuple-element.212.refs_3_), channel_id=1, source_target_pairs={{0,4},{4,0},{8,12},{12,8},{16,20},{20,16},{24,28},{28,24},{1,5},{5... | collective-permute-start | bytes 331784 | tf_op jit(solution)/shard_map/ppermute | solution.py:668
  82.5 2.5 %collective-permute-start.35 = (f32[216,128]{1,0:T(8,128)S(1)}, f32[216,128]{1,0:T(8,128)S(1)}, u32[]{:S(2)}, u32[]{:S(2)}) collective-permute-start(f32[216,128]{1,0:T(8,128)S(1)} %get-tuple-element.212.refs_3_), channel_id=1, source_target_pairs={{0,12},{4,8},{8,4},{12,0},{16,28},{20,24},{24,20},{28,16},{1,13},{... | collective-permute-start | bytes 331784 | tf_op jit(solution)/shard_map/ppermute | solution.py:668
  84.9 2.7 %shard_map.189 = (f32[2048,768]{1,0:T(8,128)}, f32[8,128]{1,0:T(8,128)S(1)}) custom-call(f32[1024,768]{1,0:T(8,128)S(1)} %get-tuple-element.200.own, f32[1024,768]{1,0:T(8,128)S(1)} %collective-permute-done.27.other, f32[8,128]{1,0:T(8,128)S(1)} %get-tuple-element.205.refs_0_), custom_call_target="tpu_custom_call" | custom-call | bytes 12582912 | tf_op jit(solution)/shard_map/pallas_call | solution.py:502
  87.7 2.0 %shard_map.190 = (f32[2048,512]{1,0:T(8,128)}, f32[8,128]{1,0:T(8,128)S(1)}) custom-call(f32[1024,512]{1,0:T(8,128)S(1)} %get-tuple-element.207.own, f32[1024,512]{1,0:T(8,128)S(1)} %collective-permute-done.31.other, f32[8,128]{1,0:T(8,128)S(1)} %get-tuple-element.208.refs_0_), custom_call_target="tpu_custom_call" | custom-call | bytes 8388608 | tf_op jit(solution)/shard_map/pallas_call | solution.py:502
  89.7 2.3 %collective-permute-done.33.refs_4_ = f32[216,128]{1,0:T(8,128)S(1)} collective-permute-done((f32[216,128]{1,0:T(8,128)S(1)}, f32[216,128]{1,0:T(8,128)S(1)}, u32[]{:S(2)}, u32[]{:S(2)}) %collective-permute-start.33) | collective-permute-done | bytes 110624 | tf_op jit(solution)/shard_map/ppermute | solution.py:668
  92.0 1.2 %shard_map.191 = (f32[6,64,512]{2,1,0:T(8,128)}, f32[6,64]{1,0:T(8,128)}, f32[6,64,256]{2,1,0:T(8,128)}, f32[6,64]{1,0:T(8,128)}, f32[6,64]{1,0:T(8,128)}, /*ind...) custom-call(f32[768,128]{1,0:T(8,128)S(1)} %get-tuple-element.210.refs_0_, ...), custom_call_target="tpu_custom_call" | custom-call | bytes 2457600 | tf_op jit(solution)/shard_map/pallas_call | solution.py:543
  (67 shorter events, 9.7 us)
Async XLA Ops:
  1.7 13.2 %collective-permute-start.1 = (f32[2,72,768]{2,1,0:T(8,128)S(1)}, f32[2,72,768]{2,1,0:T(8,128)S(1)}, u32[]{:S(2)}, u32[]{:S(2)}) collective-permute-start(f32[2,72,768]{2,1,0:T(8,128)S(1)} %shard_map.169.refs_0_.refs_4_), channel_id=1, source_target_pairs={{0,2},{1,3},{2,0},{3,1},{4,6},{5,7},{6,4},{7,5},{8,10},{9,11},{10,... | collective-permute-start | bytes 1327112 | tf_op jit(solution)/shard_map/ppermute | solution.py:749
  4.7 12.1 %collective-permute-start = (f32[2,72,768]{2,1,0:T(8,128)S(1)}, f32[2,72,768]{2,1,0:T(8,128)S(1)}, u32[]{:S(2)}, u32[]{:S(2)}) collective-permute-start(f32[2,72,768]{2,1,0:T(8,128)S(1)} %shard_map.169.refs_0_.refs_4_), channel_id=1, source_target_pairs={{0,1},{1,0},{2,3},{3,2},{4,5},{5,4},{6,7},{7,6},{8,9},{9,8},{10,11... | collective-permute-start | bytes 1327112 | tf_op jit(solution)/shard_map/ppermute | solution.py:750
  15.0 11.7 %collective-permute-start.4 = (f32[2,64,768]{2,1,0:T(8,128)S(1)}, f32[2,64,768]{2,1,0:T(8,128)S(1)}, u32[]{:S(2)}, u32[]{:S(2)}) collective-permute-start(f32[2,64,768]{2,1,0:T(8,128)S(1)} %get-tuple-element.126), channel_id=1, source_target_pairs={{0,2},{1,3},{2,0},{3,1},{4,6},{5,7},{6,4},{7,5},{8,10},{9,11},{10,... | collective-permute-start | bytes 1179656 | tf_op jit(solution)/shard_map/ppermute | solution.py:809
  24.2 6.1 %collective-permute-start.6 = (f32[2,64,768]{2,1,0:T(8,128)S(1)}, f32[2,64,768]{2,1,0:T(8,128)S(1)}, u32[]{:S(2)}, u32[]{:S(2)}) collective-permute-start(f32[2,64,768]{2,1,0:T(8,128)S(1)} %get-tuple-element.126), channel_id=1, source_target_pairs={{0,1},{1,0},{2,3},{3,2},{4,5},{5,4},{6,7},{7,6},{8,9},{9,8},{10,11... | collective-permute-start | bytes 1179656 | tf_op jit(solution)/shard_map/ppermute | solution.py:810
  26.9 3.4 %collective-permute-start.7 = (f32[2,64,768]{2,1,0:T(8,128)S(1)}, f32[2,64,768]{2,1,0:T(8,128)S(1)}, u32[]{:S(2)}, u32[]{:S(2)}) collective-permute-start(f32[2,64,768]{2,1,0:T(8,128)S(1)} %get-tuple-element.136), channel_id=1, source_target_pairs={{0,1},{1,0},{2,3},{3,2},{4,5},{5,4},{6,7},{7,6},{8,9},{9,8},{10,11... | collective-permute-start | bytes 1179656 | tf_op jit(solution)/shard_map/ppermute | solution.py:807
  27.1 10.8 %collective-permute-start.5 = (f32[384,128]{1,0:T(8,128)S(1)}, f32[384,128]{1,0:T(8,128)S(1)}, u32[]{:S(2)}, u32[]{:S(2)}) collective-permute-start(f32[384,128]{1,0:T(8,128)S(1)} %get-tuple-element.135), channel_id=1, source_target_pairs={{0,4},{4,0},{8,12},{12,8},{16,20},{20,16},{24,28},{28,24},{1,5},{5... | collective-permute-start | bytes 589832 | tf_op jit(solution)/shard_map/ppermute | solution.py:668
  28.8 9.2 %collective-permute-start.8 = (f32[1,64,768]{2,1,0:T(8,128)S(1)}, f32[1,64,768]{2,1,0:T(8,128)S(1)}, u32[]{:S(2)}, u32[]{:S(2)}) collective-permute-start(f32[1,64,768]{2,1,0:T(8,128)S(1)} %get-tuple-element.141), channel_id=1, source_target_pairs={{0,2},{1,3},{2,0},{3,1},{4,6},{5,7},{6,4},{7,5},{8,10},{9,11},{10,... | collective-permute-start | bytes 589832 | tf_op jit(solution)/shard_map/ppermute | solution.py:809
  38.1 3.4 %collective-permute-start.12 = (f32[1,64,768]{2,1,0:T(8,128)S(1)}, f32[1,64,768]{2,1,0:T(8,128)S(1)}, u32[]{:S(2)}, u32[]{:S(2)}) collective-permute-start(f32[1,64,768]{2,1,0:T(8,128)S(1)} %get-tuple-element.141), channel_id=1, source_target_pairs={{0,1},{1,0},{2,3},{3,2},{4,5},{5,4},{6,7},{7,6},{8,9},{9,8},{10,11... | collective-permute-start | bytes 589832 | tf_op jit(solution)/shard_map/ppermute | solution.py:810
  38.6 3.5 %collective-permute-start.13 = (f32[1,64,768]{2,1,0:T(8,128)S(1)}, f32[1,64,768]{2,1,0:T(8,128)S(1)}, u32[]{:S(2)}, u32[]{:S(2)}) collective-permute-start(f32[1,64,768]{2,1,0:T(8,128)S(1)} %get-tuple-element.151), channel_id=1, source_target_pairs={{0,1},{1,0},{2,3},{3,2},{4,5},{5,4},{6,7},{7,6},{8,9},{9,8},{10,11... | collective-permute-start | bytes 589832 | tf_op jit(solution)/shard_map/ppermute | solution.py:807
  38.7 8.2 %collective-permute-start.14 = (f32[1,64,768]{2,1,0:T(8,128)S(1)}, f32[1,64,768]{2,1,0:T(8,128)S(1)}, u32[]{:S(2)}, u32[]{:S(2)}) collective-permute-start(f32[1,64,768]{2,1,0:T(8,128)S(1)} %get-tuple-element.155), channel_id=1, source_target_pairs={{0,2},{1,3},{2,0},{3,1},{4,6},{5,7},{6,4},{7,5},{8,10},{9,11},{10,... | collective-permute-start | bytes 589832 | tf_op jit(solution)/shard_map/ppermute | solution.py:809
  39.2 12.3 %collective-permute-start.17 = (f32[1,64,768]{2,1,0:T(8,128)S(1)}, f32[1,64,768]{2,1,0:T(8,128)S(1)}, u32[]{:S(2)}, u32[]{:S(2)}) collective-permute-start(f32[1,64,768]{2,1,0:T(8,128)S(1)} %get-tuple-element.155), channel_id=1, source_target_pairs={{0,1},{1,0},{2,3},{3,2},{4,5},{5,4},{6,7},{7,6},{8,9},{9,8},{10,11... | collective-permute-start | bytes 589832 | tf_op jit(solution)/shard_map/ppermute | solution.py:810
  39.8 7.1 %collective-permute-start.9 = (f32[192,128]{1,0:T(8,128)S(1)}, f32[192,128]{1,0:T(8,128)S(1)}, u32[]{:S(2)}, u32[]{:S(2)}) collective-permute-start(f32[192,128]{1,0:T(8,128)S(1)} %get-tuple-element.145), channel_id=1, source_target_pairs={{0,8},{4,12},{8,0},{12,4},{16,24},{20,28},{24,16},{28,20},{1,9},{5... | collective-permute-start | bytes 294920 | tf_op jit(solution)/shard_map/ppermute | solution.py:668
  41.5 6.7 %collective-permute-start.11 = (f32[384,128]{1,0:T(8,128)S(1)}, f32[384,128]{1,0:T(8,128)S(1)}, u32[]{:S(2)}, u32[]{:S(2)}) collective-permute-start(f32[384,128]{1,0:T(8,128)S(1)} %get-tuple-element.150), channel_id=1, source_target_pairs={{0,4},{4,0},{8,12},{12,8},{16,20},{20,16},{24,28},{28,24},{1,5},{5... | collective-permute-start | bytes 589832 | tf_op jit(solution)/shard_map/ppermute | solution.py:668
  48.4 8.2 %collective-permute-start.15 = (f32[192,128]{1,0:T(8,128)S(1)}, f32[192,128]{1,0:T(8,128)S(1)}, u32[]{:S(2)}, u32[]{:S(2)}) collective-permute-start(f32[192,128]{1,0:T(8,128)S(1)} %get-tuple-element.157.refs_0_), channel_id=1, source_target_pairs={{0,16},{4,20},{8,24},{12,28},{16,0},{20,4},{24,8},{28,12},{1,17},{... | collective-permute-start | bytes 294920 | tf_op jit(solution)/shard_map/ppermute | solution.py:668
  51.0 6.9 %collective-permute-start.16 = (f32[192,128]{1,0:T(8,128)S(1)}, f32[192,128]{1,0:T(8,128)S(1)}, u32[]{:S(2)}, u32[]{:S(2)}) collective-permute-start(f32[192,128]{1,0:T(8,128)S(1)} %get-tuple-element.159), channel_id=1, source_target_pairs={{0,8},{4,12},{8,0},{12,4},{16,24},{20,28},{24,16},{28,20},{1,9},{5... | collective-permute-start | bytes 294920 | tf_op jit(solution)/shard_map/ppermute | solution.py:668
  51.5 10.0 %collective-permute-start.21 = (f32[384,128]{1,0:T(8,128)S(1)}, f32[384,128]{1,0:T(8,128)S(1)}, u32[]{:S(2)}, u32[]{:S(2)}) collective-permute-start(f32[384,128]{1,0:T(8,128)S(1)} %get-tuple-element.172), channel_id=1, source_target_pairs={{0,1},{1,0},{2,3},{3,2},{4,5},{5,4},{6,7},{7,6},{8,9},{9,8},{10,11... | collective-permute-start | bytes 589832 | tf_op jit(solution)/shard_map/ppermute | solution.py:812
  58.0 3.5 %collective-permute-start.22 = (f32[384,128]{1,0:T(8,128)S(1)}, f32[384,128]{1,0:T(8,128)S(1)}, u32[]{:S(2)}, u32[]{:S(2)}) collective-permute-start(f32[384,128]{1,0:T(8,128)S(1)} %get-tuple-element.173), channel_id=1, source_target_pairs={{0,1},{1,0},{2,3},{3,2},{4,5},{5,4},{6,7},{7,6},{8,9},{9,8},{10,11... | collective-permute-start | bytes 589832 | tf_op jit(solution)/shard_map/ppermute | solution.py:812
  58.0 3.5 %collective-permute-start.23 = (f32[96,128]{1,0:T(8,128)S(1)}, f32[96,128]{1,0:T(8,128)S(1)}, u32[]{:S(2)}, u32[]{:S(2)}) collective-permute-start(f32[96,128]{1,0:T(8,128)S(1)} %get-tuple-element.174), channel_id=1, source_target_pairs={{0,1},{1,0},{2,3},{3,2},{4,5},{5,4},{6,7},{7,6},{8,9},{9,8},{10,11... | collective-permute-start | bytes 147464 | tf_op jit(solution)/shard_map/ppermute | solution.py:812
  58.5 10.2 %collective-permute-start.19 = (f32[192,128]{1,0:T(8,128)S(1)}, f32[192,128]{1,0:T(8,128)S(1)}, u32[]{:S(2)}, u32[]{:S(2)}) collective-permute-start(f32[192,128]{1,0:T(8,128)S(1)} %get-tuple-element.168.refs_0_), channel_id=1, source_target_pairs={{0,8},{4,12},{8,0},{12,4},{16,24},{20,28},{24,16},{28,20},{1,9},{5... | collective-permute-start | bytes 294920 | tf_op jit(solution)/shard_map/ppermute | solution.py:668
  59.0 9.8 %collective-permute-start.20 = (f32[192,128]{1,0:T(8,128)S(1)}, f32[192,128]{1,0:T(8,128)S(1)}, u32[]{:S(2)}, u32[]{:S(2)}) collective-permute-start(f32[192,128]{1,0:T(8,128)S(1)} %get-tuple-element.169.refs_2_), channel_id=1, source_target_pairs={{0,16},{4,20},{8,24},{12,28},{16,0},{20,4},{24,8},{28,12},{1,17},{... | collective-permute-start | bytes 294920 | tf_op jit(solution)/shard_map/ppermute | solution.py:668
  61.6 7.2 %collective-permute-start.24 = (f32[216,128]{1,0:T(8,128)S(1)}, f32[216,128]{1,0:T(8,128)S(1)}, u32[]{:S(2)}, u32[]{:S(2)}) collective-permute-start(f32[216,128]{1,0:T(8,128)S(1)} %get-tuple-element.183), channel_id=1, source_target_pairs={{0,4},{4,0},{8,12},{12,8},{16,20},{20,16},{24,28},{28,24},{1,5},{5... | collective-permute-start | bytes 331784 | tf_op jit(solution)/shard_map/ppermute | solution.py:668
  62.6 6.5 %collective-permute-start.25 = (f32[216,128]{1,0:T(8,128)S(1)}, f32[216,128]{1,0:T(8,128)S(1)}, u32[]{:S(2)}, u32[]{:S(2)}) collective-permute-start(f32[216,128]{1,0:T(8,128)S(1)} %get-tuple-element.184), channel_id=1, source_target_pairs={{0,8},{4,12},{8,0},{12,4},{16,24},{20,28},{24,16},{28,20},{1,9},{5... | collective-permute-start | bytes 331784 | tf_op jit(solution)/shard_map/ppermute | solution.py:668
  62.8 8.0 %collective-permute-start.26 = (f32[216,128]{1,0:T(8,128)S(1)}, f32[216,128]{1,0:T(8,128)S(1)}, u32[]{:S(2)}, u32[]{:S(2)}) collective-permute-start(f32[216,128]{1,0:T(8,128)S(1)} %get-tuple-element.185), channel_id=1, source_target_pairs={{0,12},{4,8},{8,4},{12,0},{16,28},{20,24},{24,20},{28,16},{1,13},{... | collective-permute-start | bytes 331784 | tf_op jit(solution)/shard_map/ppermute | solution.py:668
  70.8 11.6 %collective-permute-start.27 = (f32[1024,768]{1,0:T(8,128)S(1)}, f32[1024,768]{1,0:T(8,128)S(1)}, u32[]{:S(2)}, u32[]{:S(2)}) collective-permute-start(f32[1024,768]{1,0:T(8,128)S(1)} %get-tuple-element.200.own), channel_id=1, source_target_pairs={{0,1},{1,0},{2,3},{3,2},{4,5},{5,4},{6,7},{7,6},{8,9},{9,8},{10,11... | collective-permute-start | bytes 9437192 | tf_op jit(solution)/shard_map/ppermute | solution.py:818
  70.9 16.7 %collective-permute-start.31 = (f32[1024,512]{1,0:T(8,128)S(1)}, f32[1024,512]{1,0:T(8,128)S(1)}, u32[]{:S(2)}, u32[]{:S(2)}) collective-permute-start(f32[1024,512]{1,0:T(8,128)S(1)} %get-tuple-element.207.own), channel_id=1, source_target_pairs={{0,1},{1,0},{2,3},{3,2},{4,5},{5,4},{6,7},{7,6},{8,9},{9,8},{10,11... | collective-permute-start | bytes 6291464 | tf_op jit(solution)/shard_map/ppermute | solution.py:818
  71.4 8.9 %collective-permute-start.28 = (f32[384,128]{1,0:T(8,128)S(1)}, f32[384,128]{1,0:T(8,128)S(1)}, u32[]{:S(2)}, u32[]{:S(2)}) collective-permute-start(f32[384,128]{1,0:T(8,128)S(1)} %get-tuple-element.201.refs_0_), channel_id=1, source_target_pairs={{0,4},{4,0},{8,12},{12,8},{16,20},{20,16},{24,28},{28,24},{1,5},{5... | collective-permute-start | bytes 589832 | tf_op jit(solution)/shard_map/ppermute | solution.py:668
  72.3 8.0 %collective-permute-start.30 = (f32[216,128]{1,0:T(8,128)S(1)}, f32[216,128]{1,0:T(8,128)S(1)}, u32[]{:S(2)}, u32[]{:S(2)}) collective-permute-start(f32[216,128]{1,0:T(8,128)S(1)} %get-tuple-element.203.refs_4_), channel_id=1, source_target_pairs={{0,16},{4,20},{8,24},{12,28},{16,0},{20,4},{24,8},{28,12},{1,17},{... | collective-permute-start | bytes 331784 | tf_op jit(solution)/shard_map/ppermute | solution.py:668
  73.3 5.6 %collective-permute-start.29 = (f32[192,128]{1,0:T(8,128)S(1)}, f32[192,128]{1,0:T(8,128)S(1)}, u32[]{:S(2)}, u32[]{:S(2)}) collective-permute-start(f32[192,128]{1,0:T(8,128)S(1)} %get-tuple-element.202.refs_2_), channel_id=1, source_target_pairs={{0,8},{4,12},{8,0},{12,4},{16,24},{20,28},{24,16},{28,20},{1,9},{5... | collective-permute-start | bytes 294920 | tf_op jit(solution)/shard_map/ppermute | solution.py:668
  80.4 11.6 %collective-permute-start.32 = (f32[384,128]{1,0:T(8,128)S(1)}, f32[384,128]{1,0:T(8,128)S(1)}, u32[]{:S(2)}, u32[]{:S(2)}) collective-permute-start(f32[384,128]{1,0:T(8,128)S(1)} %get-tuple-element.211.refs_1_), channel_id=1, source_target_pairs={{0,4},{4,0},{8,12},{12,8},{16,20},{20,16},{24,28},{28,24},{1,5},{5... | collective-permute-start | bytes 589832 | tf_op jit(solution)/shard_map/ppermute | solution.py:668
  81.4 10.6 %collective-permute-start.33 = (f32[216,128]{1,0:T(8,128)S(1)}, f32[216,128]{1,0:T(8,128)S(1)}, u32[]{:S(2)}, u32[]{:S(2)}) collective-permute-start(f32[216,128]{1,0:T(8,128)S(1)} %get-tuple-element.212.refs_3_), channel_id=1, source_target_pairs={{0,4},{4,0},{8,12},{12,8},{16,20},{20,16},{24,28},{28,24},{1,5},{5... | collective-permute-start | bytes 331784 | tf_op jit(solution)/shard_map/ppermute | solution.py:668
  82.5 9.5 %collective-permute-start.34 = (f32[216,128]{1,0:T(8,128)S(1)}, f32[216,128]{1,0:T(8,128)S(1)}, u32[]{:S(2)}, u32[]{:S(2)}) collective-permute-start(f32[216,128]{1,0:T(8,128)S(1)} %get-tuple-element.212.refs_3_), channel_id=1, source_target_pairs={{0,8},{4,12},{8,0},{12,4},{16,24},{20,28},{24,16},{28,20},{1,9},{5... | collective-permute-start | bytes 331784 | tf_op jit(solution)/shard_map/ppermute | solution.py:668
  82.5 9.5 %collective-permute-start.35 = (f32[216,128]{1,0:T(8,128)S(1)}, f32[216,128]{1,0:T(8,128)S(1)}, u32[]{:S(2)}, u32[]{:S(2)}) collective-permute-start(f32[216,128]{1,0:T(8,128)S(1)} %get-tuple-element.212.refs_3_), channel_id=1, source_target_pairs={{0,12},{4,8},{8,4},{12,0},{16,28},{20,24},{24,20},{28,16},{1,13},{... | collective-permute-start | bytes 331784 | tf_op jit(solution)/shard_map/ppermute | solution.py:668
  (6 other events, 23.7 us)

commit v8 on v7

--- a/solution.py
+++ b/solution.py
@@ -149,9 +149,10 @@
     outs, sems = refs[len(given) + n_deps :][: len(groups)], refs[-1]
     copies = []
     for out, group in zip(outs, groups):
-        experts_of, rows = pl.ds(group[0], len(group)), slice(0, SLICE)
         for part, lanes in ((w_in, slice(0, D)), (w_out, slice(D, WIDE))):
-            copies.append(pltpu.make_async_copy(part.at[experts_of], out.at[:, rows, lanes], sems.at[len(copies)]))
+            for i, e in enumerate(group):
+                to = out.at[pl.ds(i * SLICE, SLICE), lanes] if vectors else out.at[i, :, lanes]
+                copies.append(pltpu.make_async_copy(part.at[e], to, sems.at[len(copies)]))
     for k, v in enumerate(given):
         copies.append(pltpu.make_async_copy(v, held.at[k, slice(0, E), :], sems.at[len(copies)]))
     for copy in copies:
@@ -161,22 +162,23 @@
             copy.wait()
         copies = copies[: -len(given)]
         rows = jnp.concatenate([held[k, :E, :] for k in range(4)], axis=0)
-        outs[0][:, SLICE:, :] = jnp.zeros((len(groups[0]), 8, WIDE), F32)
+        end = len(groups[0]) * SLICE
+        outs[0][end:, :] = jnp.zeros((8, WIDE), F32)
         for j in range(4 * E // 8):
-            outs[0][0, SLICE:, j * LANES : j * LANES + SLICE] = rows[8 * j : 8 * j + 8, :]
+            outs[0][end:, j * LANES : j * LANES + SLICE] = rows[8 * j : 8 * j + 8, :]
     for copy in copies:
         copy.wait()
 
 
 def payload(groups, w_in, w_out, vectors, deps):
     vmem, hbm = pl.BlockSpec(memory_space=pltpu.VMEM), pl.BlockSpec(memory_space=pltpu.HBM)
-    rows = SLICE + 8 if vectors else SLICE
+    shapes = [(len(group) * SLICE + 8, WIDE) if vectors else (len(group), SLICE, WIDE) for group in groups]
     return pl.pallas_call(
         functools.partial(payload_kernel, groups, bool(vectors), len(deps)),
         in_specs=[hbm, hbm] + [hbm] * len(vectors) + [pl.BlockSpec(memory_space=pl.ANY)] * len(deps),
         out_specs=[vmem] * len(groups),
-        out_shape=[pltpu.VMEM((len(group), rows, WIDE), F32) for group in groups],
-        scratch_shapes=[pltpu.VMEM((4, 8, SLICE), F32), pltpu.SemaphoreType.DMA((2 * len(groups) + 4,))],
+        out_shape=[pltpu.VMEM(shape, F32) for shape in shapes],
+        scratch_shapes=[pltpu.VMEM((4, 8, SLICE), F32), pltpu.SemaphoreType.DMA((2 * E + 4,))],
         compiler_params=params(SMALL_MIB),
         cost_estimate=pl.CostEstimate(flops=0, bytes_accessed=SLICE * WIDE * 16, transcendentals=0),
     )(in_hbm(w_in), in_hbm(w_out), *[in_hbm(v) for v in vectors], *deps)
@@ -215,16 +217,16 @@
         if last:
             gate_acc[...] = jnp.zeros_like(gate_acc)
         for j in range(4 * E // 8 if first else 0):
-            vectors = [shard[0, SLICE:, j * LANES : j * LANES + SLICE] for shard in shards]
+            vectors = [shard[n * SLICE :, j * LANES : j * LANES + SLICE] for shard in shards]
             even_order, odd_order = (jnp.concatenate([vectors[k ^ c] for k in range(4)], axis=1) for c in range(2))
             small[8 * j : 8 * j + 8, :] = jnp.where(odd == 1, odd_order, even_order)
         if first:
             bias = small[E : 2 * E, :]
             small[E : 2 * E, :] = bias - jnp.mean(bias, axis=1, keepdims=True)
-        own_rows = slice(0, SLICE)
         for i, e in enumerate(group):
+            at = (slice(i * SLICE, (i + 1) * SLICE),) if first else (i, slice(0, SLICE))
             parts = [
-                (shard[i, own_rows, :D], jnp.concatenate([shard[i, own_rows, tile(D, k)] for k in range(2)], axis=1))
+                (shard[*at, slice(0, D)], jnp.concatenate([shard[*at, tile(D, k)] for k in range(2)], axis=1))
                 for shard in shards
             ]
             centre = sum(jnp.sum(out, axis=0, keepdims=True) for _, out in parts) / O

time: 93.5 us -> 93.2 us (level)
  transfers between devices with their start and end apart: 36 -> 36, of which waited for: 10 -> 9; matrix products, arithmetic and copies ran while one was open for 0% -> 0% of each run, Pallas kernels for 46% -> 46%
where the time goes in v8:
time: 93.2 us; the launch traced here: 93 us
  Pallas kernels  45.4 us (49%)
  starting transfers between devices  29.4 us (32%)
  waiting for transfers between devices  17.2 us (18%)
  between operations  0.98 us (1%)
    pallas_call x4, Pallas kernels, experts(): pl.pallas_call(functools.partial(expert_kernel, group, first, last, len(d...  24.7 us
    ppermute x17, starting transfers between devices, exchange(): lax.ppermute(whole if parts is None else parts[m - 1], 'dp', [(i, i ^ m <...  19.7 us
    ppermute x17, waiting for transfers between devices, exchange(): lax.ppermute(whole if parts is None else parts[m - 1], 'dp', [(i, i ^ m <...  13 us
    pallas_call x3, Pallas kernels, event_grads(): pl.pallas_call(functools.partial(event_kernel, len(highs), bool(gating),...  6.87 us
    pallas_call x2, Pallas kernels, place(): pl.pallas_call(place_kernel, in_specs=[anywhere] * (2 + len(deps)), out_s...  4.75 us
    pallas_call x1, Pallas kernels, gates(): pl.pallas_call(functools.partial(gate_kernel, len(deps)), in_specs=[pl.Bl...  4.66 us
    ppermute x3, starting transfers between devices, per_device(): far.append(lax.ppermute(outs[-1][1], 'tp', across))  3.84 us
    ppermute x1, waiting for transfers between devices, per_device(): far = [lax.ppermute(own[0], 'tp', across)]  3.62 us
  transfers between devices with their start and end apart: 36, of which 9 were waited for; matrix products, arithmetic and copies ran while one was open for 0% of the time, Pallas kernels for 46%

profile of v8, /device:TPU:0, one launch (start us, length us, event | category | flops | bytes accessed | tf_op | source)
XLA Modules:
  0.0 93.0 jit_solution(4882799492273403269)
XLA Ops:
  0.7 1.1 %shard_map.169.refs_0_.refs_4_ = f32[136,768]{1,0:T(8,128)S(1)} custom-call(f32[6,64,512]{2,1,0:T(8,128)} %bitcast.8, f32[6,64,256]{2,1,0:T(8,128)} %bitcast.10, f32[6,64]{1,0:T(8,128)} %refs_0_.1, f32[6,64]{1,0:T(8,128)} %refs_1_.1, f32[6,64]{1,0:T(8,128)} %refs_2_.1, f32[6,64]{1,0:T(8,128)} %refs_3_.1), custom_call_target="tpu_custom_call" | custom-call | bytes 786432 | tf_op jit(solution)/shard_map/pallas_call | solution.py:176
  1.8 3.0 %collective-permute-start.1 = (f32[136,768]{1,0:T(8,128)S(1)}, f32[136,768]{1,0:T(8,128)S(1)}, u32[]{:S(2)}, u32[]{:S(2)}) collective-permute-start(f32[136,768]{1,0:T(8,128)S(1)} %shard_map.169.refs_0_.refs_4_), channel_id=1, source_target_pairs={{0,2},{1,3},{2,0},{3,1},{4,6},{5,7},{6,4},{7,5},{8,10},{9,11},{10,... | collective-permute-start | bytes 1253384 | tf_op jit(solution)/shard_map/ppermute | solution.py:751
  4.8 1.3 %shard_map.170 = (f32[2,64,768]{2,1,0:T(8,128)S(1)}, f32[1,64,768]{2,1,0:T(8,128)S(1)}, f32[1,64,768]{2,1,0:T(8,128)S(1)}) custom-call(f32[6,64,512]{2,1,0:T(8,128)} %bitcast.9, f32[6,64,256]{2,1,0:T(8,128)} %bitcast.11, f32[136,768]{1,0:T(8,128)S(1)} %shard_map.169.refs_0_.refs_4_), custom_call_target="tpu_custom_call" | custom-call | bytes 786432 | tf_op jit(solution)/shard_map/pallas_call | solution.py:176
  6.2 4.7 %shard_map.171 = (bf16[1024,512]{1,0:T(8,128)(2,1)S(1)}, bf16[1024,512]{1,0:T(8,128)(2,1)S(1)}, f32[1024,128]{1,0:T(8,128)S(1)}, f32[1024,768]{1,0:T(8,128)S(1)}) custom-call(s32[8]{0:T(128)S(1)} %copy-done.1, f32[2048,512]{1,0:T(8,128)} %ev_ref.1, f32[2048,768]{1,0:T(8,128)} %cot_ref.1, f32[14,512]{1,0:T(8,128)} %bitcast.6, ...), custom_call_target="tpu_custom_call" | custom-call | flops 402653184 | bytes 4194304 | tf_op jit(solution)/shard_map/pallas_call | solution.py:125
  10.9 3.6 %collective-permute-done.1.refs_0_.refs_6_ = f32[136,768]{1,0:T(8,128)S(1)} collective-permute-done((f32[136,768]{1,0:T(8,128)S(1)}, f32[136,768]{1,0:T(8,128)S(1)}, u32[]{:S(2)}, u32[]{:S(2)}) %collective-permute-start.1) | collective-permute-done | bytes 417824 | tf_op jit(solution)/shard_map/ppermute | solution.py:751
  14.6 1.8 %collective-permute-start.4 = (f32[2,64,768]{2,1,0:T(8,128)S(1)}, f32[2,64,768]{2,1,0:T(8,128)S(1)}, u32[]{:S(2)}, u32[]{:S(2)}) collective-permute-start(f32[2,64,768]{2,1,0:T(8,128)S(1)} %get-tuple-element.126), channel_id=1, source_target_pairs={{0,2},{1,3},{2,0},{3,1},{4,6},{5,7},{6,4},{7,5},{8,10},{9,11},{10,... | collective-permute-start | bytes 1179656 | tf_op jit(solution)/shard_map/ppermute | solution.py:811
  16.4 7.2 %shard_map.173 = (f32[1024,768]{1,0:T(8,128)S(1)}, f32[1024,128]{1,0:T(8,128)S(1)}, bf16[1024,512]{1,0:T(8,128)(2,1)S(1)}, bf16[1024,512]{1,0:T(8,128)(2,1)S(1)}...) custom-call(bf16[1024,512]{1,0:T(8,128)(2,1)S(1)} %get-tuple-element, ...), custom_call_target="tpu_custom_call" | custom-call | flops 8858370048 | bytes 14336000 | tf_op jit(solution)/shard_map/pallas_call | solution.py:406
  24.3 2.1 %shard_map.175 = (f32[1024,512]{1,0:T(8,128)S(1)}, f32[8,128]{1,0:T(8,128)S(1)}) custom-call(bf16[1024,512]{1,0:T(8,128)(2,1)S(1)} %get-tuple-element.128.refs_0_, bf16[1024,512]{1,0:T(8,128)(2,1)S(1)} %get-tuple-element.129.refs_1_, bf16[512,512]{1,0:T(8,128)(2,1)S(1)} %get-tuple-element.130.refs_2_, bf16[512,512]{1,0:T(8,128)(2,1)S(1)} %get-tuple-element.131.refs_3_, ...), custom_call_target="tpu_custom_call" | custom-call | flops 1610612736 | bytes 4096000 | tf_op jit(solution)/shard_map/pallas_call | solution.py:471
  26.8 1.6 %collective-permute-start.5 = (f32[384,128]{1,0:T(8,128)S(1)}, f32[384,128]{1,0:T(8,128)S(1)}, u32[]{:S(2)}, u32[]{:S(2)}) collective-permute-start(f32[384,128]{1,0:T(8,128)S(1)} %get-tuple-element.135), channel_id=1, source_target_pairs={{0,4},{4,0},{8,12},{12,8},{16,20},{20,16},{24,28},{28,24},{1,5},{5... | collective-permute-start | bytes 589832 | tf_op jit(solution)/shard_map/ppermute | solution.py:670
  28.4 1.5 %collective-permute-start.8 = (f32[1,64,768]{2,1,0:T(8,128)S(1)}, f32[1,64,768]{2,1,0:T(8,128)S(1)}, u32[]{:S(2)}, u32[]{:S(2)}) collective-permute-start(f32[1,64,768]{2,1,0:T(8,128)S(1)} %get-tuple-element.141), channel_id=1, source_target_pairs={{0,2},{1,3},{2,0},{3,1},{4,6},{5,7},{6,4},{7,5},{8,10},{9,11},{10,... | collective-permute-start | bytes 589832 | tf_op jit(solution)/shard_map/ppermute | solution.py:811
  30.0 7.6 %shard_map.177 = (f32[1024,768]{1,0:T(8,128)S(1)}, f32[1024,128]{1,0:T(8,128)S(1)}, bf16[1024,512]{1,0:T(8,128)(2,1)S(1)}, bf16[1024,512]{1,0:T(8,128)(2,1)S(1)}...) custom-call(bf16[1024,512]{1,0:T(8,128)(2,1)S(1)} %get-tuple-element, ...), custom_call_target="tpu_custom_call", output_to_operand_aliasing={{0}: (9, {})} | custom-call | flops 8858370048 | bytes 14336000 | tf_op jit(solution)/shard_map/pallas_call | solution.py:406
  39.5 1.6 %collective-permute-start.9 = (f32[192,128]{1,0:T(8,128)S(1)}, f32[192,128]{1,0:T(8,128)S(1)}, u32[]{:S(2)}, u32[]{:S(2)}) collective-permute-start(f32[192,128]{1,0:T(8,128)S(1)} %get-tuple-element.145), channel_id=1, source_target_pairs={{0,8},{4,12},{8,0},{12,4},{16,24},{20,28},{24,16},{28,20},{1,9},{5... | collective-permute-start | bytes 294920 | tf_op jit(solution)/shard_map/ppermute | solution.py:670
  41.9 4.8 %shard_map.180 = (f32[1024,768]{1,0:T(8,128)S(1)}, f32[1024,128]{1,0:T(8,128)S(1)}, bf16[1024,256]{1,0:T(8,128)(2,1)S(1)}, bf16[1024,256]{1,0:T(8,128)(2,1)S(1)}...) custom-call(bf16[1024,512]{1,0:T(8,128)(2,1)S(1)} %get-tuple-element, ...), custom_call_target="tpu_custom_call", output_to_operand_aliasing={{0}: (9, {})} | custom-call | flops 4429185024 | bytes 14336000 | tf_op jit(solution)/shard_map/pallas_call | solution.py:406
  46.7 1.2 %collective-permute-done.11.refs_3_ = f32[384,128]{1,0:T(8,128)S(1)} collective-permute-done((f32[384,128]{1,0:T(8,128)S(1)}, f32[384,128]{1,0:T(8,128)S(1)}, u32[]{:S(2)}, u32[]{:S(2)}) %collective-permute-start.11) | collective-permute-done | bytes 196640 | tf_op jit(solution)/shard_map/ppermute | solution.py:670
  48.1 2.7 %collective-permute-start.15 = (f32[192,128]{1,0:T(8,128)S(1)}, f32[192,128]{1,0:T(8,128)S(1)}, u32[]{:S(2)}, u32[]{:S(2)}) collective-permute-start(f32[192,128]{1,0:T(8,128)S(1)} %get-tuple-element.157.refs_0_), channel_id=1, source_target_pairs={{0,16},{4,20},{8,24},{12,28},{16,0},{20,4},{24,8},{28,12},{1,17},{... | collective-permute-start | bytes 294920 | tf_op jit(solution)/shard_map/ppermute | solution.py:670
  51.2 5.0 %shard_map.182 = (f32[1024,768]{1,0:T(8,128)S(1)}, f32[1024,128]{1,0:T(8,128)S(1)}, bf16[1024,256]{1,0:T(8,128)(2,1)S(1)}, bf16[1024,256]{1,0:T(8,128)(2,1)S(1)}...) custom-call(bf16[1024,512]{1,0:T(8,128)(2,1)S(1)} %get-tuple-element, ...), custom_call_target="tpu_custom_call", output_to_operand_aliasing={{0}: (9, {})} | custom-call | flops 4429185024 | bytes 14336000 | tf_op jit(solution)/shard_map/pallas_call | solution.py:406
  56.3 1.3 %collective-permute-done.16.refs_3_ = f32[192,128]{1,0:T(8,128)S(1)} collective-permute-done((f32[192,128]{1,0:T(8,128)S(1)}, f32[192,128]{1,0:T(8,128)S(1)}, u32[]{:S(2)}, u32[]{:S(2)}) %collective-permute-start.16) | collective-permute-done | bytes 98336 | tf_op jit(solution)/shard_map/ppermute | solution.py:670
  58.7 1.4 %collective-permute-start.20 = (f32[192,128]{1,0:T(8,128)S(1)}, f32[192,128]{1,0:T(8,128)S(1)}, u32[]{:S(2)}, u32[]{:S(2)}) collective-permute-start(f32[192,128]{1,0:T(8,128)S(1)} %get-tuple-element.169.refs_2_), channel_id=1, source_target_pairs={{0,16},{4,20},{8,24},{12,28},{16,0},{20,4},{24,8},{28,12},{1,17},{... | collective-permute-start | bytes 294920 | tf_op jit(solution)/shard_map/ppermute | solution.py:670
  60.0 1.2 %shard_map.184 = (f32[1024,512]{1,0:T(8,128)S(1)}, f32[8,128]{1,0:T(8,128)S(1)}) custom-call(bf16[1024,256]{1,0:T(8,128)(2,1)S(1)} %get-tuple-element.175.refs_0_, bf16[1024,256]{1,0:T(8,128)(2,1)S(1)} %get-tuple-element.176.refs_1_, bf16[256,512]{1,0:T(8,128)(2,1)S(1)} %get-tuple-element.177.refs_2_, ...), custom_call_target="tpu_custom_call", output_to_operand_aliasing={{0}: (4, {})} | custom-call | flops 805306368 | bytes 4096000 | tf_op jit(solution)/shard_map/pallas_call | solution.py:471
  62.5 2.3 %collective-permute-start.26 = (f32[216,128]{1,0:T(8,128)S(1)}, f32[216,128]{1,0:T(8,128)S(1)}, u32[]{:S(2)}, u32[]{:S(2)}) collective-permute-start(f32[216,128]{1,0:T(8,128)S(1)} %get-tuple-element.185), channel_id=1, source_target_pairs={{0,12},{4,8},{8,4},{12,0},{16,28},{20,24},{24,20},{28,16},{1,13},{... | collective-permute-start | bytes 331784 | tf_op jit(solution)/shard_map/ppermute | solution.py:670
  64.8 3.6 %shard_map.186 = (f32[1024,512]{1,0:T(8,128)S(1)}, f32[8,128]{1,0:T(8,128)S(1)}) custom-call(bf16[1024,512]{1,0:T(8,128)(2,1)S(1)} %get-tuple-element.187.refs_0_, bf16[1024,256]{1,0:T(8,128)(2,1)S(1)} %get-tuple-element.188.refs_1_, bf16[1024,512]{1,0:T(8,128)(2,1)S(1)} %get-tuple-element.189.refs_2_, ...), custom_call_target="tpu_custom_call", output_to_operand_aliasing={{0}: (10, {})} | custom-call | flops 2415919104 | bytes 4096000 | tf_op jit(solution)/shard_map/pallas_call | solution.py:471
  68.8 1.7 %collective-permute-done.26.refs_7_ = f32[216,128]{1,0:T(8,128)S(1)} collective-permute-done((f32[216,128]{1,0:T(8,128)S(1)}, f32[216,128]{1,0:T(8,128)S(1)}, u32[]{:S(2)}, u32[]{:S(2)}) %collective-permute-start.26) | collective-permute-done | bytes 110624 | tf_op jit(solution)/shard_map/ppermute | solution.py:670
  73.0 1.1 %collective-permute-start.29 = (f32[192,128]{1,0:T(8,128)S(1)}, f32[192,128]{1,0:T(8,128)S(1)}, u32[]{:S(2)}, u32[]{:S(2)}) collective-permute-start(f32[192,128]{1,0:T(8,128)S(1)} %get-tuple-element.202.refs_2_), channel_id=1, source_target_pairs={{0,8},{4,12},{8,0},{12,4},{16,24},{20,28},{24,16},{28,20},{1,9},{5... | collective-permute-start | bytes 294920 | tf_op jit(solution)/shard_map/ppermute | solution.py:670
  74.1 4.4 %collective-permute-done.29.refs_3_ = f32[192,128]{1,0:T(8,128)S(1)} collective-permute-done((f32[192,128]{1,0:T(8,128)S(1)}, f32[192,128]{1,0:T(8,128)S(1)}, u32[]{:S(2)}, u32[]{:S(2)}) %collective-permute-start.29) | collective-permute-done | bytes 98336 | tf_op jit(solution)/shard_map/ppermute | solution.py:670
  78.5 1.5 %collective-permute-done.30.refs_5_ = f32[216,128]{1,0:T(8,128)S(1)} collective-permute-done((f32[216,128]{1,0:T(8,128)S(1)}, f32[216,128]{1,0:T(8,128)S(1)}, u32[]{:S(2)}, u32[]{:S(2)}) %collective-permute-start.30) | collective-permute-done | bytes 110624 | tf_op jit(solution)/shard_map/ppermute | solution.py:670
  80.1 1.0 %collective-permute-start.32 = (f32[384,128]{1,0:T(8,128)S(1)}, f32[384,128]{1,0:T(8,128)S(1)}, u32[]{:S(2)}, u32[]{:S(2)}) collective-permute-start(f32[384,128]{1,0:T(8,128)S(1)} %get-tuple-element.211.refs_1_), channel_id=1, source_target_pairs={{0,4},{4,0},{8,12},{12,8},{16,20},{20,16},{24,28},{28,24},{1,5},{5... | collective-permute-start | bytes 589832 | tf_op jit(solution)/shard_map/ppermute | solution.py:670
  81.1 1.1 %collective-permute-start.33 = (f32[216,128]{1,0:T(8,128)S(1)}, f32[216,128]{1,0:T(8,128)S(1)}, u32[]{:S(2)}, u32[]{:S(2)}) collective-permute-start(f32[216,128]{1,0:T(8,128)S(1)} %get-tuple-element.212.refs_3_), channel_id=1, source_target_pairs={{0,4},{4,0},{8,12},{12,8},{16,20},{20,16},{24,28},{28,24},{1,5},{5... | collective-permute-start | bytes 331784 | tf_op jit(solution)/shard_map/ppermute | solution.py:670
  82.2 2.4 %collective-permute-start.35 = (f32[216,128]{1,0:T(8,128)S(1)}, f32[216,128]{1,0:T(8,128)S(1)}, u32[]{:S(2)}, u32[]{:S(2)}) collective-permute-start(f32[216,128]{1,0:T(8,128)S(1)} %get-tuple-element.212.refs_3_), channel_id=1, source_target_pairs={{0,12},{4,8},{8,4},{12,0},{16,28},{20,24},{24,20},{28,16},{1,13},{... | collective-permute-start | bytes 331784 | tf_op jit(solution)/shard_map/ppermute | solution.py:670
  84.6 2.7 %shard_map.189 = (f32[2048,768]{1,0:T(8,128)}, f32[8,128]{1,0:T(8,128)S(1)}) custom-call(f32[1024,768]{1,0:T(8,128)S(1)} %get-tuple-element.200.own, f32[1024,768]{1,0:T(8,128)S(1)} %collective-permute-done.27.other, f32[8,128]{1,0:T(8,128)S(1)} %get-tuple-element.205.refs_0_), custom_call_target="tpu_custom_call" | custom-call | bytes 12582912 | tf_op jit(solution)/shard_map/pallas_call | solution.py:504
  87.4 2.0 %shard_map.190 = (f32[2048,512]{1,0:T(8,128)}, f32[8,128]{1,0:T(8,128)S(1)}) custom-call(f32[1024,512]{1,0:T(8,128)S(1)} %get-tuple-element.207.own, f32[1024,512]{1,0:T(8,128)S(1)} %collective-permute-done.31.other, f32[8,128]{1,0:T(8,128)S(1)} %get-tuple-element.208.refs_0_), custom_call_target="tpu_custom_call" | custom-call | bytes 8388608 | tf_op jit(solution)/shard_map/pallas_call | solution.py:504
  89.4 2.4 %collective-permute-done.33.refs_4_ = f32[216,128]{1,0:T(8,128)S(1)} collective-permute-done((f32[216,128]{1,0:T(8,128)S(1)}, f32[216,128]{1,0:T(8,128)S(1)}, u32[]{:S(2)}, u32[]{:S(2)}) %collective-permute-start.33) | collective-permute-done | bytes 110624 | tf_op jit(solution)/shard_map/ppermute | solution.py:670
  91.8 1.2 %shard_map.191 = (f32[6,64,512]{2,1,0:T(8,128)}, f32[6,64]{1,0:T(8,128)}, f32[6,64,256]{2,1,0:T(8,128)}, f32[6,64]{1,0:T(8,128)}, f32[6,64]{1,0:T(8,128)}, /*ind...) custom-call(f32[768,128]{1,0:T(8,128)S(1)} %get-tuple-element.210.refs_0_, ...), custom_call_target="tpu_custom_call" | custom-call | bytes 2457600 | tf_op jit(solution)/shard_map/pallas_call | solution.py:545
  (67 shorter events, 9.6 us)
Async XLA Ops:
  1.8 12.7 %collective-permute-start.1 = (f32[136,768]{1,0:T(8,128)S(1)}, f32[136,768]{1,0:T(8,128)S(1)}, u32[]{:S(2)}, u32[]{:S(2)}) collective-permute-start(f32[136,768]{1,0:T(8,128)S(1)} %shard_map.169.refs_0_.refs_4_), channel_id=1, source_target_pairs={{0,2},{1,3},{2,0},{3,1},{4,6},{5,7},{6,4},{7,5},{8,10},{9,11},{10,... | collective-permute-start | bytes 1253384 | tf_op jit(solution)/shard_map/ppermute | solution.py:751
  4.8 11.6 %collective-permute-start = (f32[136,768]{1,0:T(8,128)S(1)}, f32[136,768]{1,0:T(8,128)S(1)}, u32[]{:S(2)}, u32[]{:S(2)}) collective-permute-start(f32[136,768]{1,0:T(8,128)S(1)} %shard_map.169.refs_0_.refs_4_), channel_id=1, source_target_pairs={{0,1},{1,0},{2,3},{3,2},{4,5},{5,4},{6,7},{7,6},{8,9},{9,8},{10,11... | collective-permute-start | bytes 1253384 | tf_op jit(solution)/shard_map/ppermute | solution.py:752
  14.6 11.8 %collective-permute-start.4 = (f32[2,64,768]{2,1,0:T(8,128)S(1)}, f32[2,64,768]{2,1,0:T(8,128)S(1)}, u32[]{:S(2)}, u32[]{:S(2)}) collective-permute-start(f32[2,64,768]{2,1,0:T(8,128)S(1)} %get-tuple-element.126), channel_id=1, source_target_pairs={{0,2},{1,3},{2,0},{3,1},{4,6},{5,7},{6,4},{7,5},{8,10},{9,11},{10,... | collective-permute-start | bytes 1179656 | tf_op jit(solution)/shard_map/ppermute | solution.py:811
  23.9 6.0 %collective-permute-start.6 = (f32[2,64,768]{2,1,0:T(8,128)S(1)}, f32[2,64,768]{2,1,0:T(8,128)S(1)}, u32[]{:S(2)}, u32[]{:S(2)}) collective-permute-start(f32[2,64,768]{2,1,0:T(8,128)S(1)} %get-tuple-element.126), channel_id=1, source_target_pairs={{0,1},{1,0},{2,3},{3,2},{4,5},{5,4},{6,7},{7,6},{8,9},{9,8},{10,11... | collective-permute-start | bytes 1179656 | tf_op jit(solution)/shard_map/ppermute | solution.py:812
  26.6 3.4 %collective-permute-start.7 = (f32[2,64,768]{2,1,0:T(8,128)S(1)}, f32[2,64,768]{2,1,0:T(8,128)S(1)}, u32[]{:S(2)}, u32[]{:S(2)}) collective-permute-start(f32[2,64,768]{2,1,0:T(8,128)S(1)} %get-tuple-element.136), channel_id=1, source_target_pairs={{0,1},{1,0},{2,3},{3,2},{4,5},{5,4},{6,7},{7,6},{8,9},{9,8},{10,11... | collective-permute-start | bytes 1179656 | tf_op jit(solution)/shard_map/ppermute | solution.py:809
  26.8 10.8 %collective-permute-start.5 = (f32[384,128]{1,0:T(8,128)S(1)}, f32[384,128]{1,0:T(8,128)S(1)}, u32[]{:S(2)}, u32[]{:S(2)}) collective-permute-start(f32[384,128]{1,0:T(8,128)S(1)} %get-tuple-element.135), channel_id=1, source_target_pairs={{0,4},{4,0},{8,12},{12,8},{16,20},{20,16},{24,28},{28,24},{1,5},{5... | collective-permute-start | bytes 589832 | tf_op jit(solution)/shard_map/ppermute | solution.py:670
  28.4 9.2 %collective-permute-start.8 = (f32[1,64,768]{2,1,0:T(8,128)S(1)}, f32[1,64,768]{2,1,0:T(8,128)S(1)}, u32[]{:S(2)}, u32[]{:S(2)}) collective-permute-start(f32[1,64,768]{2,1,0:T(8,128)S(1)} %get-tuple-element.141), channel_id=1, source_target_pairs={{0,2},{1,3},{2,0},{3,1},{4,6},{5,7},{6,4},{7,5},{8,10},{9,11},{10,... | collective-permute-start | bytes 589832 | tf_op jit(solution)/shard_map/ppermute | solution.py:811
  37.8 3.4 %collective-permute-start.12 = (f32[1,64,768]{2,1,0:T(8,128)S(1)}, f32[1,64,768]{2,1,0:T(8,128)S(1)}, u32[]{:S(2)}, u32[]{:S(2)}) collective-permute-start(f32[1,64,768]{2,1,0:T(8,128)S(1)} %get-tuple-element.141), channel_id=1, source_target_pairs={{0,1},{1,0},{2,3},{3,2},{4,5},{5,4},{6,7},{7,6},{8,9},{9,8},{10,11... | collective-permute-start | bytes 589832 | tf_op jit(solution)/shard_map/ppermute | solution.py:812
  38.3 3.5 %collective-permute-start.13 = (f32[1,64,768]{2,1,0:T(8,128)S(1)}, f32[1,64,768]{2,1,0:T(8,128)S(1)}, u32[]{:S(2)}, u32[]{:S(2)}) collective-permute-start(f32[1,64,768]{2,1,0:T(8,128)S(1)} %get-tuple-element.151), channel_id=1, source_target_pairs={{0,1},{1,0},{2,3},{3,2},{4,5},{5,4},{6,7},{7,6},{8,9},{9,8},{10,11... | collective-permute-start | bytes 589832 | tf_op jit(solution)/shard_map/ppermute | solution.py:809
  38.4 8.3 %collective-permute-start.14 = (f32[1,64,768]{2,1,0:T(8,128)S(1)}, f32[1,64,768]{2,1,0:T(8,128)S(1)}, u32[]{:S(2)}, u32[]{:S(2)}) collective-permute-start(f32[1,64,768]{2,1,0:T(8,128)S(1)} %get-tuple-element.155), channel_id=1, source_target_pairs={{0,2},{1,3},{2,0},{3,1},{4,6},{5,7},{6,4},{7,5},{8,10},{9,11},{10,... | collective-permute-start | bytes 589832 | tf_op jit(solution)/shard_map/ppermute | solution.py:811
  38.9 12.3 %collective-permute-start.17 = (f32[1,64,768]{2,1,0:T(8,128)S(1)}, f32[1,64,768]{2,1,0:T(8,128)S(1)}, u32[]{:S(2)}, u32[]{:S(2)}) collective-permute-start(f32[1,64,768]{2,1,0:T(8,128)S(1)} %get-tuple-element.155), channel_id=1, source_target_pairs={{0,1},{1,0},{2,3},{3,2},{4,5},{5,4},{6,7},{7,6},{8,9},{9,8},{10,11... | collective-permute-start | bytes 589832 | tf_op jit(solution)/shard_map/ppermute | solution.py:812
  39.5 7.2 %collective-permute-start.9 = (f32[192,128]{1,0:T(8,128)S(1)}, f32[192,128]{1,0:T(8,128)S(1)}, u32[]{:S(2)}, u32[]{:S(2)}) collective-permute-start(f32[192,128]{1,0:T(8,128)S(1)} %get-tuple-element.145), channel_id=1, source_target_pairs={{0,8},{4,12},{8,0},{12,4},{16,24},{20,28},{24,16},{28,20},{1,9},{5... | collective-permute-start | bytes 294920 | tf_op jit(solution)/shard_map/ppermute | solution.py:670
  41.2 6.7 %collective-permute-start.11 = (f32[384,128]{1,0:T(8,128)S(1)}, f32[384,128]{1,0:T(8,128)S(1)}, u32[]{:S(2)}, u32[]{:S(2)}) collective-permute-start(f32[384,128]{1,0:T(8,128)S(1)} %get-tuple-element.150), channel_id=1, source_target_pairs={{0,4},{4,0},{8,12},{12,8},{16,20},{20,16},{24,28},{28,24},{1,5},{5... | collective-permute-start | bytes 589832 | tf_op jit(solution)/shard_map/ppermute | solution.py:670
  48.1 8.2 %collective-permute-start.15 = (f32[192,128]{1,0:T(8,128)S(1)}, f32[192,128]{1,0:T(8,128)S(1)}, u32[]{:S(2)}, u32[]{:S(2)}) collective-permute-start(f32[192,128]{1,0:T(8,128)S(1)} %get-tuple-element.157.refs_0_), channel_id=1, source_target_pairs={{0,16},{4,20},{8,24},{12,28},{16,0},{20,4},{24,8},{28,12},{1,17},{... | collective-permute-start | bytes 294920 | tf_op jit(solution)/shard_map/ppermute | solution.py:670
  50.7 6.9 %collective-permute-start.16 = (f32[192,128]{1,0:T(8,128)S(1)}, f32[192,128]{1,0:T(8,128)S(1)}, u32[]{:S(2)}, u32[]{:S(2)}) collective-permute-start(f32[192,128]{1,0:T(8,128)S(1)} %get-tuple-element.159), channel_id=1, source_target_pairs={{0,8},{4,12},{8,0},{12,4},{16,24},{20,28},{24,16},{28,20},{1,9},{5... | collective-permute-start | bytes 294920 | tf_op jit(solution)/shard_map/ppermute | solution.py:670
  51.2 10.0 %collective-permute-start.21 = (f32[384,128]{1,0:T(8,128)S(1)}, f32[384,128]{1,0:T(8,128)S(1)}, u32[]{:S(2)}, u32[]{:S(2)}) collective-permute-start(f32[384,128]{1,0:T(8,128)S(1)} %get-tuple-element.172), channel_id=1, source_target_pairs={{0,1},{1,0},{2,3},{3,2},{4,5},{5,4},{6,7},{7,6},{8,9},{9,8},{10,11... | collective-permute-start | bytes 589832 | tf_op jit(solution)/shard_map/ppermute | solution.py:814
  57.7 3.5 %collective-permute-start.22 = (f32[384,128]{1,0:T(8,128)S(1)}, f32[384,128]{1,0:T(8,128)S(1)}, u32[]{:S(2)}, u32[]{:S(2)}) collective-permute-start(f32[384,128]{1,0:T(8,128)S(1)} %get-tuple-element.173), channel_id=1, source_target_pairs={{0,1},{1,0},{2,3},{3,2},{4,5},{5,4},{6,7},{7,6},{8,9},{9,8},{10,11... | collective-permute-start | bytes 589832 | tf_op jit(solution)/shard_map/ppermute | solution.py:814
  57.7 3.5 %collective-permute-start.23 = (f32[96,128]{1,0:T(8,128)S(1)}, f32[96,128]{1,0:T(8,128)S(1)}, u32[]{:S(2)}, u32[]{:S(2)}) collective-permute-start(f32[96,128]{1,0:T(8,128)S(1)} %get-tuple-element.174), channel_id=1, source_target_pairs={{0,1},{1,0},{2,3},{3,2},{4,5},{5,4},{6,7},{7,6},{8,9},{9,8},{10,11... | collective-permute-start | bytes 147464 | tf_op jit(solution)/shard_map/ppermute | solution.py:814
  58.2 10.2 %collective-permute-start.19 = (f32[192,128]{1,0:T(8,128)S(1)}, f32[192,128]{1,0:T(8,128)S(1)}, u32[]{:S(2)}, u32[]{:S(2)}) collective-permute-start(f32[192,128]{1,0:T(8,128)S(1)} %get-tuple-element.168.refs_0_), channel_id=1, source_target_pairs={{0,8},{4,12},{8,0},{12,4},{16,24},{20,28},{24,16},{28,20},{1,9},{5... | collective-permute-start | bytes 294920 | tf_op jit(solution)/shard_map/ppermute | solution.py:670
  58.7 9.8 %collective-permute-start.20 = (f32[192,128]{1,0:T(8,128)S(1)}, f32[192,128]{1,0:T(8,128)S(1)}, u32[]{:S(2)}, u32[]{:S(2)}) collective-permute-start(f32[192,128]{1,0:T(8,128)S(1)} %get-tuple-element.169.refs_2_), channel_id=1, source_target_pairs={{0,16},{4,20},{8,24},{12,28},{16,0},{20,4},{24,8},{28,12},{1,17},{... | collective-permute-start | bytes 294920 | tf_op jit(solution)/shard_map/ppermute | solution.py:670
  61.3 7.2 %collective-permute-start.24 = (f32[216,128]{1,0:T(8,128)S(1)}, f32[216,128]{1,0:T(8,128)S(1)}, u32[]{:S(2)}, u32[]{:S(2)}) collective-permute-start(f32[216,128]{1,0:T(8,128)S(1)} %get-tuple-element.183), channel_id=1, source_target_pairs={{0,4},{4,0},{8,12},{12,8},{16,20},{20,16},{24,28},{28,24},{1,5},{5... | collective-permute-start | bytes 331784 | tf_op jit(solution)/shard_map/ppermute | solution.py:670
  62.2 6.6 %collective-permute-start.25 = (f32[216,128]{1,0:T(8,128)S(1)}, f32[216,128]{1,0:T(8,128)S(1)}, u32[]{:S(2)}, u32[]{:S(2)}) collective-permute-start(f32[216,128]{1,0:T(8,128)S(1)} %get-tuple-element.184), channel_id=1, source_target_pairs={{0,8},{4,12},{8,0},{12,4},{16,24},{20,28},{24,16},{28,20},{1,9},{5... | collective-permute-start | bytes 331784 | tf_op jit(solution)/shard_map/ppermute | solution.py:670
  62.5 8.1 %collective-permute-start.26 = (f32[216,128]{1,0:T(8,128)S(1)}, f32[216,128]{1,0:T(8,128)S(1)}, u32[]{:S(2)}, u32[]{:S(2)}) collective-permute-start(f32[216,128]{1,0:T(8,128)S(1)} %get-tuple-element.185), channel_id=1, source_target_pairs={{0,12},{4,8},{8,4},{12,0},{16,28},{20,24},{24,20},{28,16},{1,13},{... | collective-permute-start | bytes 331784 | tf_op jit(solution)/shard_map/ppermute | solution.py:670
  70.6 11.6 %collective-permute-start.27 = (f32[1024,768]{1,0:T(8,128)S(1)}, f32[1024,768]{1,0:T(8,128)S(1)}, u32[]{:S(2)}, u32[]{:S(2)}) collective-permute-start(f32[1024,768]{1,0:T(8,128)S(1)} %get-tuple-element.200.own), channel_id=1, source_target_pairs={{0,1},{1,0},{2,3},{3,2},{4,5},{5,4},{6,7},{7,6},{8,9},{9,8},{10,11... | collective-permute-start | bytes 9437192 | tf_op jit(solution)/shard_map/ppermute | solution.py:820
  70.7 16.6 %collective-permute-start.31 = (f32[1024,512]{1,0:T(8,128)S(1)}, f32[1024,512]{1,0:T(8,128)S(1)}, u32[]{:S(2)}, u32[]{:S(2)}) collective-permute-start(f32[1024,512]{1,0:T(8,128)S(1)} %get-tuple-element.207.own), channel_id=1, source_target_pairs={{0,1},{1,0},{2,3},{3,2},{4,5},{5,4},{6,7},{7,6},{8,9},{9,8},{10,11... | collective-permute-start | bytes 6291464 | tf_op jit(solution)/shard_map/ppermute | solution.py:820
  71.2 8.9 %collective-permute-start.28 = (f32[384,128]{1,0:T(8,128)S(1)}, f32[384,128]{1,0:T(8,128)S(1)}, u32[]{:S(2)}, u32[]{:S(2)}) collective-permute-start(f32[384,128]{1,0:T(8,128)S(1)} %get-tuple-element.201.refs_0_), channel_id=1, source_target_pairs={{0,4},{4,0},{8,12},{12,8},{16,20},{20,16},{24,28},{28,24},{1,5},{5... | collective-permute-start | bytes 589832 | tf_op jit(solution)/shard_map/ppermute | solution.py:670
  72.1 8.0 %collective-permute-start.30 = (f32[216,128]{1,0:T(8,128)S(1)}, f32[216,128]{1,0:T(8,128)S(1)}, u32[]{:S(2)}, u32[]{:S(2)}) collective-permute-start(f32[216,128]{1,0:T(8,128)S(1)} %get-tuple-element.203.refs_4_), channel_id=1, source_target_pairs={{0,16},{4,20},{8,24},{12,28},{16,0},{20,4},{24,8},{28,12},{1,17},{... | collective-permute-start | bytes 331784 | tf_op jit(solution)/shard_map/ppermute | solution.py:670
  73.0 5.5 %collective-permute-start.29 = (f32[192,128]{1,0:T(8,128)S(1)}, f32[192,128]{1,0:T(8,128)S(1)}, u32[]{:S(2)}, u32[]{:S(2)}) collective-permute-start(f32[192,128]{1,0:T(8,128)S(1)} %get-tuple-element.202.refs_2_), channel_id=1, source_target_pairs={{0,8},{4,12},{8,0},{12,4},{16,24},{20,28},{24,16},{28,20},{1,9},{5... | collective-permute-start | bytes 294920 | tf_op jit(solution)/shard_map/ppermute | solution.py:670
  80.1 11.6 %collective-permute-start.32 = (f32[384,128]{1,0:T(8,128)S(1)}, f32[384,128]{1,0:T(8,128)S(1)}, u32[]{:S(2)}, u32[]{:S(2)}) collective-permute-start(f32[384,128]{1,0:T(8,128)S(1)} %get-tuple-element.211.refs_1_), channel_id=1, source_target_pairs={{0,4},{4,0},{8,12},{12,8},{16,20},{20,16},{24,28},{28,24},{1,5},{5... | collective-permute-start | bytes 589832 | tf_op jit(solution)/shard_map/ppermute | solution.py:670
  81.1 10.6 %collective-permute-start.33 = (f32[216,128]{1,0:T(8,128)S(1)}, f32[216,128]{1,0:T(8,128)S(1)}, u32[]{:S(2)}, u32[]{:S(2)}) collective-permute-start(f32[216,128]{1,0:T(8,128)S(1)} %get-tuple-element.212.refs_3_), channel_id=1, source_target_pairs={{0,4},{4,0},{8,12},{12,8},{16,20},{20,16},{24,28},{28,24},{1,5},{5... | collective-permute-start | bytes 331784 | tf_op jit(solution)/shard_map/ppermute | solution.py:670
  82.2 9.5 %collective-permute-start.34 = (f32[216,128]{1,0:T(8,128)S(1)}, f32[216,128]{1,0:T(8,128)S(1)}, u32[]{:S(2)}, u32[]{:S(2)}) collective-permute-start(f32[216,128]{1,0:T(8,128)S(1)} %get-tuple-element.212.refs_3_), channel_id=1, source_target_pairs={{0,8},{4,12},{8,0},{12,4},{16,24},{20,28},{24,16},{28,20},{1,9},{5... | collective-permute-start | bytes 331784 | tf_op jit(solution)/shard_map/ppermute | solution.py:670
  82.2 9.5 %collective-permute-start.35 = (f32[216,128]{1,0:T(8,128)S(1)}, f32[216,128]{1,0:T(8,128)S(1)}, u32[]{:S(2)}, u32[]{:S(2)}) collective-permute-start(f32[216,128]{1,0:T(8,128)S(1)} %get-tuple-element.212.refs_3_), channel_id=1, source_target_pairs={{0,12},{4,8},{8,4},{12,0},{16,28},{20,24},{24,20},{28,16},{1,13},{... | collective-permute-start | bytes 331784 | tf_op jit(solution)/shard_map/ppermute | solution.py:670
  (6 other events, 23.8 us)

commit v9 on v8

--- a/solution.py
+++ b/solution.py
@@ -38,9 +38,8 @@
     ("small", "send fetch", (0, 1)),
     ("experts", 3, ()),
     ("small", "send", (0, 1)),
-    ("events", (2,), ()),
     ("small", "", (2,)),
-    ("events", (1, 3), ()),
+    ("events", (1, 2, 3), ()),
     ("small", "mix grad", (0, 1, 2)),
     ("small", "", (0, 1, 2)),
     ("place", None, ()),

time: 93.2 us -> 92.9 us (level)
    pallas_call x3 -> x2, Pallas kernels: 6.87 us -> 6.52 us  [event_grads(): pl.pallas_call(functools.partial(event_kernel, len(highs), bool(gating),...]
  transfers between devices with their start and end apart: 36 -> 36, of which waited for: 9 -> 10; matrix products, arithmetic and copies ran while one was open for 0% -> 0% of each run, Pallas kernels for 46% -> 45%
where the time goes in v9:
time: 92.9 us; the launch traced here: 92.7 us
  Pallas kernels  44.7 us (48%)
  starting transfers between devices  29.4 us (32%)
  waiting for transfers between devices  17.7 us (19%)
  between operations  0.95 us (1%)
    pallas_call x4, Pallas kernels, experts(): pl.pallas_call(functools.partial(expert_kernel, group, first, last, len(d...  24.4 us
    ppermute x17, starting transfers between devices, exchange(): lax.ppermute(whole if parts is None else parts[m - 1], 'dp', [(i, i ^ m <...  19.6 us
    ppermute x17, waiting for transfers between devices, exchange(): lax.ppermute(whole if parts is None else parts[m - 1], 'dp', [(i, i ^ m <...  13.5 us
    pallas_call x2, Pallas kernels, event_grads(): pl.pallas_call(functools.partial(event_kernel, len(highs), bool(gating),...  6.52 us
    pallas_call x2, Pallas kernels, place(): pl.pallas_call(place_kernel, in_specs=[anywhere] * (2 + len(deps)), out_s...  4.75 us
    pallas_call x1, Pallas kernels, gates(): pl.pallas_call(functools.partial(gate_kernel, len(deps)), in_specs=[pl.Bl...  4.67 us
    ppermute x3, starting transfers between devices, per_device(): far.append(lax.ppermute(outs[-1][1], 'tp', across))  3.83 us
    ppermute x1, waiting for transfers between devices, per_device(): far = [lax.ppermute(own[0], 'tp', across)]  3.62 us
  transfers between devices with their start and end apart: 36, of which 10 were waited for; matrix products, arithmetic and copies ran while one was open for 0% of the time, Pallas kernels for 45%

profile of v9, /device:TPU:0, one launch (start us, length us, event | category | flops | bytes accessed | tf_op | source)
XLA Modules:
  0.0 92.7 jit_solution(12497475956012317194)
XLA Ops:
  0.7 1.1 %shard_map.169.refs_0_.refs_4_ = f32[136,768]{1,0:T(8,128)S(1)} custom-call(f32[6,64,512]{2,1,0:T(8,128)} %bitcast.8, f32[6,64,256]{2,1,0:T(8,128)} %bitcast.10, f32[6,64]{1,0:T(8,128)} %refs_0_.1, f32[6,64]{1,0:T(8,128)} %refs_1_.1, f32[6,64]{1,0:T(8,128)} %refs_2_.1, f32[6,64]{1,0:T(8,128)} %refs_3_.1), custom_call_target="tpu_custom_call" | custom-call | bytes 786432 | tf_op jit(solution)/shard_map/pallas_call | solution.py:175
  1.8 3.0 %collective-permute-start.1 = (f32[136,768]{1,0:T(8,128)S(1)}, f32[136,768]{1,0:T(8,128)S(1)}, u32[]{:S(2)}, u32[]{:S(2)}) collective-permute-start(f32[136,768]{1,0:T(8,128)S(1)} %shard_map.169.refs_0_.refs_4_), channel_id=1, source_target_pairs={{0,2},{1,3},{2,0},{3,1},{4,6},{5,7},{6,4},{7,5},{8,10},{9,11},{10,... | collective-permute-start | bytes 1253384 | tf_op jit(solution)/shard_map/ppermute | solution.py:750
  4.8 1.3 %shard_map.170 = (f32[2,64,768]{2,1,0:T(8,128)S(1)}, f32[1,64,768]{2,1,0:T(8,128)S(1)}, f32[1,64,768]{2,1,0:T(8,128)S(1)}) custom-call(f32[6,64,512]{2,1,0:T(8,128)} %bitcast.9, f32[6,64,256]{2,1,0:T(8,128)} %bitcast.11, f32[136,768]{1,0:T(8,128)S(1)} %shard_map.169.refs_0_.refs_4_), custom_call_target="tpu_custom_call" | custom-call | bytes 786432 | tf_op jit(solution)/shard_map/pallas_call | solution.py:175
  6.2 4.7 %shard_map.171 = (bf16[1024,512]{1,0:T(8,128)(2,1)S(1)}, bf16[1024,512]{1,0:T(8,128)(2,1)S(1)}, f32[1024,128]{1,0:T(8,128)S(1)}, f32[1024,768]{1,0:T(8,128)S(1)}) custom-call(s32[8]{0:T(128)S(1)} %copy-done.1, f32[2048,512]{1,0:T(8,128)} %ev_ref.1, f32[2048,768]{1,0:T(8,128)} %cot_ref.1, f32[14,512]{1,0:T(8,128)} %bitcast.6, ...), custom_call_target="tpu_custom_call" | custom-call | flops 402653184 | bytes 4194304 | tf_op jit(solution)/shard_map/pallas_call | solution.py:124
  10.9 3.6 %collective-permute-done.1.refs_0_.refs_6_ = f32[136,768]{1,0:T(8,128)S(1)} collective-permute-done((f32[136,768]{1,0:T(8,128)S(1)}, f32[136,768]{1,0:T(8,128)S(1)}, u32[]{:S(2)}, u32[]{:S(2)}) %collective-permute-start.1) | collective-permute-done | bytes 417824 | tf_op jit(solution)/shard_map/ppermute | solution.py:750
  14.6 1.8 %collective-permute-start.4 = (f32[2,64,768]{2,1,0:T(8,128)S(1)}, f32[2,64,768]{2,1,0:T(8,128)S(1)}, u32[]{:S(2)}, u32[]{:S(2)}) collective-permute-start(f32[2,64,768]{2,1,0:T(8,128)S(1)} %get-tuple-element.124), channel_id=1, source_target_pairs={{0,2},{1,3},{2,0},{3,1},{4,6},{5,7},{6,4},{7,5},{8,10},{9,11},{10,... | collective-permute-start | bytes 1179656 | tf_op jit(solution)/shard_map/ppermute | solution.py:810
  16.4 7.1 %shard_map.173 = (f32[1024,768]{1,0:T(8,128)S(1)}, f32[1024,128]{1,0:T(8,128)S(1)}, bf16[1024,512]{1,0:T(8,128)(2,1)S(1)}, bf16[1024,512]{1,0:T(8,128)(2,1)S(1)}...) custom-call(bf16[1024,512]{1,0:T(8,128)(2,1)S(1)} %get-tuple-element, ...), custom_call_target="tpu_custom_call" | custom-call | flops 8858370048 | bytes 14336000 | tf_op jit(solution)/shard_map/pallas_call | solution.py:405
  24.2 2.1 %shard_map.175 = (f32[1024,512]{1,0:T(8,128)S(1)}, f32[8,128]{1,0:T(8,128)S(1)}) custom-call(bf16[1024,512]{1,0:T(8,128)(2,1)S(1)} %get-tuple-element.126.refs_0_, bf16[1024,512]{1,0:T(8,128)(2,1)S(1)} %get-tuple-element.127.refs_1_, bf16[512,512]{1,0:T(8,128)(2,1)S(1)} %get-tuple-element.128.refs_2_, bf16[512,512]{1,0:T(8,128)(2,1)S(1)} %get-tuple-element.129.refs_3_, ...), custom_call_target="tpu_custom_call" | custom-call | flops 1610612736 | bytes 4096000 | tf_op jit(solution)/shard_map/pallas_call | solution.py:470
  26.7 1.6 %collective-permute-start.5 = (f32[384,128]{1,0:T(8,128)S(1)}, f32[384,128]{1,0:T(8,128)S(1)}, u32[]{:S(2)}, u32[]{:S(2)}) collective-permute-start(f32[384,128]{1,0:T(8,128)S(1)} %get-tuple-element.133), channel_id=1, source_target_pairs={{0,4},{4,0},{8,12},{12,8},{16,20},{20,16},{24,28},{28,24},{1,5},{5... | collective-permute-start | bytes 589832 | tf_op jit(solution)/shard_map/ppermute | solution.py:669
  28.3 1.5 %collective-permute-start.8 = (f32[1,64,768]{2,1,0:T(8,128)S(1)}, f32[1,64,768]{2,1,0:T(8,128)S(1)}, u32[]{:S(2)}, u32[]{:S(2)}) collective-permute-start(f32[1,64,768]{2,1,0:T(8,128)S(1)} %get-tuple-element.139), channel_id=1, source_target_pairs={{0,2},{1,3},{2,0},{3,1},{4,6},{5,7},{6,4},{7,5},{8,10},{9,11},{10,... | collective-permute-start | bytes 589832 | tf_op jit(solution)/shard_map/ppermute | solution.py:810
  29.9 7.6 %shard_map.177 = (f32[1024,768]{1,0:T(8,128)S(1)}, f32[1024,128]{1,0:T(8,128)S(1)}, bf16[1024,512]{1,0:T(8,128)(2,1)S(1)}, bf16[1024,512]{1,0:T(8,128)(2,1)S(1)}...) custom-call(bf16[1024,512]{1,0:T(8,128)(2,1)S(1)} %get-tuple-element, ...), custom_call_target="tpu_custom_call", output_to_operand_aliasing={{0}: (9, {})} | custom-call | flops 8858370048 | bytes 14336000 | tf_op jit(solution)/shard_map/pallas_call | solution.py:405
  39.4 1.6 %collective-permute-start.9 = (f32[192,128]{1,0:T(8,128)S(1)}, f32[192,128]{1,0:T(8,128)S(1)}, u32[]{:S(2)}, u32[]{:S(2)}) collective-permute-start(f32[192,128]{1,0:T(8,128)S(1)} %get-tuple-element.143), channel_id=1, source_target_pairs={{0,8},{4,12},{8,0},{12,4},{16,24},{20,28},{24,16},{28,20},{1,9},{5... | collective-permute-start | bytes 294920 | tf_op jit(solution)/shard_map/ppermute | solution.py:669
  41.7 4.8 %shard_map.180 = (f32[1024,768]{1,0:T(8,128)S(1)}, f32[1024,128]{1,0:T(8,128)S(1)}, bf16[1024,256]{1,0:T(8,128)(2,1)S(1)}, bf16[1024,256]{1,0:T(8,128)(2,1)S(1)}...) custom-call(bf16[1024,512]{1,0:T(8,128)(2,1)S(1)} %get-tuple-element, ...), custom_call_target="tpu_custom_call", output_to_operand_aliasing={{0}: (9, {})} | custom-call | flops 4429185024 | bytes 14336000 | tf_op jit(solution)/shard_map/pallas_call | solution.py:405
  46.5 1.3 %collective-permute-done.11.refs_3_ = f32[384,128]{1,0:T(8,128)S(1)} collective-permute-done((f32[384,128]{1,0:T(8,128)S(1)}, f32[384,128]{1,0:T(8,128)S(1)}, u32[]{:S(2)}, u32[]{:S(2)}) %collective-permute-start.11) | collective-permute-done | bytes 196640 | tf_op jit(solution)/shard_map/ppermute | solution.py:669
  47.9 2.6 %collective-permute-start.15 = (f32[192,128]{1,0:T(8,128)S(1)}, f32[192,128]{1,0:T(8,128)S(1)}, u32[]{:S(2)}, u32[]{:S(2)}) collective-permute-start(f32[192,128]{1,0:T(8,128)S(1)} %get-tuple-element.155.refs_0_), channel_id=1, source_target_pairs={{0,16},{4,20},{8,24},{12,28},{16,0},{20,4},{24,8},{28,12},{1,17},{... | collective-permute-start | bytes 294920 | tf_op jit(solution)/shard_map/ppermute | solution.py:669
  51.1 4.9 %shard_map.182 = (f32[1024,768]{1,0:T(8,128)S(1)}, f32[1024,128]{1,0:T(8,128)S(1)}, bf16[1024,256]{1,0:T(8,128)(2,1)S(1)}, bf16[1024,256]{1,0:T(8,128)(2,1)S(1)}...) custom-call(bf16[1024,512]{1,0:T(8,128)(2,1)S(1)} %get-tuple-element, ...), custom_call_target="tpu_custom_call", output_to_operand_aliasing={{0}: (9, {})} | custom-call | flops 4429185024 | bytes 14336000 | tf_op jit(solution)/shard_map/pallas_call | solution.py:405
  56.1 1.3 %collective-permute-done.16.refs_3_ = f32[192,128]{1,0:T(8,128)S(1)} collective-permute-done((f32[192,128]{1,0:T(8,128)S(1)}, f32[192,128]{1,0:T(8,128)S(1)}, u32[]{:S(2)}, u32[]{:S(2)}) %collective-permute-start.16) | collective-permute-done | bytes 98336 | tf_op jit(solution)/shard_map/ppermute | solution.py:669
  58.5 1.4 %collective-permute-start.20 = (f32[192,128]{1,0:T(8,128)S(1)}, f32[192,128]{1,0:T(8,128)S(1)}, u32[]{:S(2)}, u32[]{:S(2)}) collective-permute-start(f32[192,128]{1,0:T(8,128)S(1)} %get-tuple-element.167.refs_2_), channel_id=1, source_target_pairs={{0,16},{4,20},{8,24},{12,28},{16,0},{20,4},{24,8},{28,12},{1,17},{... | collective-permute-start | bytes 294920 | tf_op jit(solution)/shard_map/ppermute | solution.py:669
  60.0 1.0 %collective-permute-start.24 = (f32[216,128]{1,0:T(8,128)S(1)}, f32[216,128]{1,0:T(8,128)S(1)}, u32[]{:S(2)}, u32[]{:S(2)}) collective-permute-start(f32[216,128]{1,0:T(8,128)S(1)} %get-tuple-element.175), channel_id=1, source_target_pairs={{0,4},{4,0},{8,12},{12,8},{16,20},{20,16},{24,28},{28,24},{1,5},{5... | collective-permute-start | bytes 331784 | tf_op jit(solution)/shard_map/ppermute | solution.py:669
  61.2 2.3 %collective-permute-start.26 = (f32[216,128]{1,0:T(8,128)S(1)}, f32[216,128]{1,0:T(8,128)S(1)}, u32[]{:S(2)}, u32[]{:S(2)}) collective-permute-start(f32[216,128]{1,0:T(8,128)S(1)} %get-tuple-element.177), channel_id=1, source_target_pairs={{0,12},{4,8},{8,4},{12,0},{16,28},{20,24},{24,20},{28,16},{1,13},{... | collective-permute-start | bytes 331784 | tf_op jit(solution)/shard_map/ppermute | solution.py:669
  63.5 4.4 %shard_map.185 = (f32[1024,512]{1,0:T(8,128)S(1)}, f32[8,128]{1,0:T(8,128)S(1)}) custom-call(bf16[1024,512]{1,0:T(8,128)(2,1)S(1)} %get-tuple-element.179.refs_0_, bf16[1024,256]{1,0:T(8,128)(2,1)S(1)} %get-tuple-element.180.refs_1_, bf16[1024,256]{1,0:T(8,128)(2,1)S(1)} %get-tuple-element.181.refs_2_, ...), custom_call_target="tpu_custom_call", output_to_operand_aliasing={{0}: (14, {})} | custom-call | flops 3221225472 | bytes 4096000 | tf_op jit(solution)/shard_map/pallas_call | solution.py:470
  68.2 1.8 %collective-permute-done.26.refs_7_ = f32[216,128]{1,0:T(8,128)S(1)} collective-permute-done((f32[216,128]{1,0:T(8,128)S(1)}, f32[216,128]{1,0:T(8,128)S(1)}, u32[]{:S(2)}, u32[]{:S(2)}) %collective-permute-start.26) | collective-permute-done | bytes 110624 | tf_op jit(solution)/shard_map/ppermute | solution.py:669
  70.7 1.1 %collective-permute-start.28 = (f32[384,128]{1,0:T(8,128)S(1)}, f32[384,128]{1,0:T(8,128)S(1)}, u32[]{:S(2)}, u32[]{:S(2)}) collective-permute-start(f32[384,128]{1,0:T(8,128)S(1)} %get-tuple-element.197.refs_0_), channel_id=1, source_target_pairs={{0,4},{4,0},{8,12},{12,8},{16,20},{20,16},{24,28},{28,24},{1,5},{5... | collective-permute-start | bytes 589832 | tf_op jit(solution)/shard_map/ppermute | solution.py:669
  72.4 1.2 %collective-permute-start.29 = (f32[192,128]{1,0:T(8,128)S(1)}, f32[192,128]{1,0:T(8,128)S(1)}, u32[]{:S(2)}, u32[]{:S(2)}) collective-permute-start(f32[192,128]{1,0:T(8,128)S(1)} %get-tuple-element.198.refs_2_), channel_id=1, source_target_pairs={{0,8},{4,12},{8,0},{12,4},{16,24},{20,28},{24,16},{28,20},{1,9},{5... | collective-permute-start | bytes 294920 | tf_op jit(solution)/shard_map/ppermute | solution.py:669
  73.6 4.0 %collective-permute-done.29.refs_3_ = f32[192,128]{1,0:T(8,128)S(1)} collective-permute-done((f32[192,128]{1,0:T(8,128)S(1)}, f32[192,128]{1,0:T(8,128)S(1)}, u32[]{:S(2)}, u32[]{:S(2)}) %collective-permute-start.29) | collective-permute-done | bytes 98336 | tf_op jit(solution)/shard_map/ppermute | solution.py:669
  77.6 2.2 %collective-permute-done.30.refs_5_ = f32[216,128]{1,0:T(8,128)S(1)} collective-permute-done((f32[216,128]{1,0:T(8,128)S(1)}, f32[216,128]{1,0:T(8,128)S(1)}, u32[]{:S(2)}, u32[]{:S(2)}) %collective-permute-start.30) | collective-permute-done | bytes 110624 | tf_op jit(solution)/shard_map/ppermute | solution.py:669
  80.8 1.1 %collective-permute-start.33 = (f32[216,128]{1,0:T(8,128)S(1)}, f32[216,128]{1,0:T(8,128)S(1)}, u32[]{:S(2)}, u32[]{:S(2)}) collective-permute-start(f32[216,128]{1,0:T(8,128)S(1)} %get-tuple-element.208.refs_3_), channel_id=1, source_target_pairs={{0,4},{4,0},{8,12},{12,8},{16,20},{20,16},{24,28},{28,24},{1,5},{5... | collective-permute-start | bytes 331784 | tf_op jit(solution)/shard_map/ppermute | solution.py:669
  81.9 2.3 %collective-permute-start.35 = (f32[216,128]{1,0:T(8,128)S(1)}, f32[216,128]{1,0:T(8,128)S(1)}, u32[]{:S(2)}, u32[]{:S(2)}) collective-permute-start(f32[216,128]{1,0:T(8,128)S(1)} %get-tuple-element.208.refs_3_), channel_id=1, source_target_pairs={{0,12},{4,8},{8,4},{12,0},{16,28},{20,24},{24,20},{28,16},{1,13},{... | collective-permute-start | bytes 331784 | tf_op jit(solution)/shard_map/ppermute | solution.py:669
  84.3 2.7 %shard_map.188 = (f32[2048,768]{1,0:T(8,128)}, f32[8,128]{1,0:T(8,128)S(1)}) custom-call(f32[1024,768]{1,0:T(8,128)S(1)} %get-tuple-element.196.own, f32[1024,768]{1,0:T(8,128)S(1)} %collective-permute-done.27.other, f32[8,128]{1,0:T(8,128)S(1)} %get-tuple-element.201.refs_0_), custom_call_target="tpu_custom_call" | custom-call | bytes 12582912 | tf_op jit(solution)/shard_map/pallas_call | solution.py:503
  87.0 2.0 %shard_map.189 = (f32[2048,512]{1,0:T(8,128)}, f32[8,128]{1,0:T(8,128)S(1)}) custom-call(f32[1024,512]{1,0:T(8,128)S(1)} %get-tuple-element.203.own, f32[1024,512]{1,0:T(8,128)S(1)} %collective-permute-done.31.other, f32[8,128]{1,0:T(8,128)S(1)} %get-tuple-element.204.refs_0_), custom_call_target="tpu_custom_call" | custom-call | bytes 8388608 | tf_op jit(solution)/shard_map/pallas_call | solution.py:503
  89.1 2.4 %collective-permute-done.33.refs_4_ = f32[216,128]{1,0:T(8,128)S(1)} collective-permute-done((f32[216,128]{1,0:T(8,128)S(1)}, f32[216,128]{1,0:T(8,128)S(1)}, u32[]{:S(2)}, u32[]{:S(2)}) %collective-permute-start.33) | collective-permute-done | bytes 110624 | tf_op jit(solution)/shard_map/ppermute | solution.py:669
  91.5 1.2 %shard_map.190 = (f32[6,64,512]{2,1,0:T(8,128)}, f32[6,64]{1,0:T(8,128)}, f32[6,64,256]{2,1,0:T(8,128)}, f32[6,64]{1,0:T(8,128)}, f32[6,64]{1,0:T(8,128)}, /*ind...) custom-call(f32[768,128]{1,0:T(8,128)S(1)} %get-tuple-element.206.refs_0_, ...), custom_call_target="tpu_custom_call" | custom-call | bytes 2457600 | tf_op jit(solution)/shard_map/pallas_call | solution.py:544
  (66 shorter events, 8.4 us)
Async XLA Ops:
  1.8 12.7 %collective-permute-start.1 = (f32[136,768]{1,0:T(8,128)S(1)}, f32[136,768]{1,0:T(8,128)S(1)}, u32[]{:S(2)}, u32[]{:S(2)}) collective-permute-start(f32[136,768]{1,0:T(8,128)S(1)} %shard_map.169.refs_0_.refs_4_), channel_id=1, source_target_pairs={{0,2},{1,3},{2,0},{3,1},{4,6},{5,7},{6,4},{7,5},{8,10},{9,11},{10,... | collective-permute-start | bytes 1253384 | tf_op jit(solution)/shard_map/ppermute | solution.py:750
  4.8 11.6 %collective-permute-start = (f32[136,768]{1,0:T(8,128)S(1)}, f32[136,768]{1,0:T(8,128)S(1)}, u32[]{:S(2)}, u32[]{:S(2)}) collective-permute-start(f32[136,768]{1,0:T(8,128)S(1)} %shard_map.169.refs_0_.refs_4_), channel_id=1, source_target_pairs={{0,1},{1,0},{2,3},{3,2},{4,5},{5,4},{6,7},{7,6},{8,9},{9,8},{10,11... | collective-permute-start | bytes 1253384 | tf_op jit(solution)/shard_map/ppermute | solution.py:751
  14.6 11.7 %collective-permute-start.4 = (f32[2,64,768]{2,1,0:T(8,128)S(1)}, f32[2,64,768]{2,1,0:T(8,128)S(1)}, u32[]{:S(2)}, u32[]{:S(2)}) collective-permute-start(f32[2,64,768]{2,1,0:T(8,128)S(1)} %get-tuple-element.124), channel_id=1, source_target_pairs={{0,2},{1,3},{2,0},{3,1},{4,6},{5,7},{6,4},{7,5},{8,10},{9,11},{10,... | collective-permute-start | bytes 1179656 | tf_op jit(solution)/shard_map/ppermute | solution.py:810
  23.6 2.7 %collective-permute-start.3 = (f32[768,128]{1,0:T(8,128)S(1)}, f32[768,128]{1,0:T(8,128)S(1)}, u32[]{:S(2)}, u32[]{:S(2)}) collective-permute-start(f32[768,128]{1,0:T(8,128)S(1)} %get-tuple-element.123), channel_id=1, source_target_pairs={{0,1},{1,0},{2,3},{3,2},{4,5},{5,4},{6,7},{7,6},{8,9},{9,8},{10,11... | collective-permute-start | bytes 1179656 | tf_op jit(solution)/shard_map/ppermute | solution.py:813
  23.8 6.0 %collective-permute-start.6 = (f32[2,64,768]{2,1,0:T(8,128)S(1)}, f32[2,64,768]{2,1,0:T(8,128)S(1)}, u32[]{:S(2)}, u32[]{:S(2)}) collective-permute-start(f32[2,64,768]{2,1,0:T(8,128)S(1)} %get-tuple-element.124), channel_id=1, source_target_pairs={{0,1},{1,0},{2,3},{3,2},{4,5},{5,4},{6,7},{7,6},{8,9},{9,8},{10,11... | collective-permute-start | bytes 1179656 | tf_op jit(solution)/shard_map/ppermute | solution.py:811
  26.5 3.4 %collective-permute-start.7 = (f32[2,64,768]{2,1,0:T(8,128)S(1)}, f32[2,64,768]{2,1,0:T(8,128)S(1)}, u32[]{:S(2)}, u32[]{:S(2)}) collective-permute-start(f32[2,64,768]{2,1,0:T(8,128)S(1)} %get-tuple-element.134), channel_id=1, source_target_pairs={{0,1},{1,0},{2,3},{3,2},{4,5},{5,4},{6,7},{7,6},{8,9},{9,8},{10,11... | collective-permute-start | bytes 1179656 | tf_op jit(solution)/shard_map/ppermute | solution.py:808
  26.7 10.8 %collective-permute-start.5 = (f32[384,128]{1,0:T(8,128)S(1)}, f32[384,128]{1,0:T(8,128)S(1)}, u32[]{:S(2)}, u32[]{:S(2)}) collective-permute-start(f32[384,128]{1,0:T(8,128)S(1)} %get-tuple-element.133), channel_id=1, source_target_pairs={{0,4},{4,0},{8,12},{12,8},{16,20},{20,16},{24,28},{28,24},{1,5},{5... | collective-permute-start | bytes 589832 | tf_op jit(solution)/shard_map/ppermute | solution.py:669
  28.3 9.2 %collective-permute-start.8 = (f32[1,64,768]{2,1,0:T(8,128)S(1)}, f32[1,64,768]{2,1,0:T(8,128)S(1)}, u32[]{:S(2)}, u32[]{:S(2)}) collective-permute-start(f32[1,64,768]{2,1,0:T(8,128)S(1)} %get-tuple-element.139), channel_id=1, source_target_pairs={{0,2},{1,3},{2,0},{3,1},{4,6},{5,7},{6,4},{7,5},{8,10},{9,11},{10,... | collective-permute-start | bytes 589832 | tf_op jit(solution)/shard_map/ppermute | solution.py:810
  37.7 3.4 %collective-permute-start.12 = (f32[1,64,768]{2,1,0:T(8,128)S(1)}, f32[1,64,768]{2,1,0:T(8,128)S(1)}, u32[]{:S(2)}, u32[]{:S(2)}) collective-permute-start(f32[1,64,768]{2,1,0:T(8,128)S(1)} %get-tuple-element.139), channel_id=1, source_target_pairs={{0,1},{1,0},{2,3},{3,2},{4,5},{5,4},{6,7},{7,6},{8,9},{9,8},{10,11... | collective-permute-start | bytes 589832 | tf_op jit(solution)/shard_map/ppermute | solution.py:811
  38.2 3.5 %collective-permute-start.13 = (f32[1,64,768]{2,1,0:T(8,128)S(1)}, f32[1,64,768]{2,1,0:T(8,128)S(1)}, u32[]{:S(2)}, u32[]{:S(2)}) collective-permute-start(f32[1,64,768]{2,1,0:T(8,128)S(1)} %get-tuple-element.149), channel_id=1, source_target_pairs={{0,1},{1,0},{2,3},{3,2},{4,5},{5,4},{6,7},{7,6},{8,9},{9,8},{10,11... | collective-permute-start | bytes 589832 | tf_op jit(solution)/shard_map/ppermute | solution.py:808
  38.3 8.2 %collective-permute-start.14 = (f32[1,64,768]{2,1,0:T(8,128)S(1)}, f32[1,64,768]{2,1,0:T(8,128)S(1)}, u32[]{:S(2)}, u32[]{:S(2)}) collective-permute-start(f32[1,64,768]{2,1,0:T(8,128)S(1)} %get-tuple-element.153), channel_id=1, source_target_pairs={{0,2},{1,3},{2,0},{3,1},{4,6},{5,7},{6,4},{7,5},{8,10},{9,11},{10,... | collective-permute-start | bytes 589832 | tf_op jit(solution)/shard_map/ppermute | solution.py:810
  38.8 12.3 %collective-permute-start.17 = (f32[1,64,768]{2,1,0:T(8,128)S(1)}, f32[1,64,768]{2,1,0:T(8,128)S(1)}, u32[]{:S(2)}, u32[]{:S(2)}) collective-permute-start(f32[1,64,768]{2,1,0:T(8,128)S(1)} %get-tuple-element.153), channel_id=1, source_target_pairs={{0,1},{1,0},{2,3},{3,2},{4,5},{5,4},{6,7},{7,6},{8,9},{9,8},{10,11... | collective-permute-start | bytes 589832 | tf_op jit(solution)/shard_map/ppermute | solution.py:811
  39.4 7.1 %collective-permute-start.9 = (f32[192,128]{1,0:T(8,128)S(1)}, f32[192,128]{1,0:T(8,128)S(1)}, u32[]{:S(2)}, u32[]{:S(2)}) collective-permute-start(f32[192,128]{1,0:T(8,128)S(1)} %get-tuple-element.143), channel_id=1, source_target_pairs={{0,8},{4,12},{8,0},{12,4},{16,24},{20,28},{24,16},{28,20},{1,9},{5... | collective-permute-start | bytes 294920 | tf_op jit(solution)/shard_map/ppermute | solution.py:669
  41.1 6.7 %collective-permute-start.11 = (f32[384,128]{1,0:T(8,128)S(1)}, f32[384,128]{1,0:T(8,128)S(1)}, u32[]{:S(2)}, u32[]{:S(2)}) collective-permute-start(f32[384,128]{1,0:T(8,128)S(1)} %get-tuple-element.148), channel_id=1, source_target_pairs={{0,4},{4,0},{8,12},{12,8},{16,20},{20,16},{24,28},{28,24},{1,5},{5... | collective-permute-start | bytes 589832 | tf_op jit(solution)/shard_map/ppermute | solution.py:669
  47.9 3.2 %collective-permute-start.18 = (f32[1,64,768]{2,1,0:T(8,128)S(1)}, f32[1,64,768]{2,1,0:T(8,128)S(1)}, u32[]{:S(2)}, u32[]{:S(2)}) collective-permute-start(f32[1,64,768]{2,1,0:T(8,128)S(1)} %get-tuple-element.158), channel_id=1, source_target_pairs={{0,1},{1,0},{2,3},{3,2},{4,5},{5,4},{6,7},{7,6},{8,9},{9,8},{10,11... | collective-permute-start | bytes 589832 | tf_op jit(solution)/shard_map/ppermute | solution.py:808
  47.9 8.2 %collective-permute-start.15 = (f32[192,128]{1,0:T(8,128)S(1)}, f32[192,128]{1,0:T(8,128)S(1)}, u32[]{:S(2)}, u32[]{:S(2)}) collective-permute-start(f32[192,128]{1,0:T(8,128)S(1)} %get-tuple-element.155.refs_0_), channel_id=1, source_target_pairs={{0,16},{4,20},{8,24},{12,28},{16,0},{20,4},{24,8},{28,12},{1,17},{... | collective-permute-start | bytes 294920 | tf_op jit(solution)/shard_map/ppermute | solution.py:669
  50.6 6.9 %collective-permute-start.16 = (f32[192,128]{1,0:T(8,128)S(1)}, f32[192,128]{1,0:T(8,128)S(1)}, u32[]{:S(2)}, u32[]{:S(2)}) collective-permute-start(f32[192,128]{1,0:T(8,128)S(1)} %get-tuple-element.157), channel_id=1, source_target_pairs={{0,8},{4,12},{8,0},{12,4},{16,24},{20,28},{24,16},{28,20},{1,9},{5... | collective-permute-start | bytes 294920 | tf_op jit(solution)/shard_map/ppermute | solution.py:669
  51.0 8.8 %collective-permute-start.21 = (f32[384,128]{1,0:T(8,128)S(1)}, f32[384,128]{1,0:T(8,128)S(1)}, u32[]{:S(2)}, u32[]{:S(2)}) collective-permute-start(f32[384,128]{1,0:T(8,128)S(1)} %get-tuple-element.170), channel_id=1, source_target_pairs={{0,1},{1,0},{2,3},{3,2},{4,5},{5,4},{6,7},{7,6},{8,9},{9,8},{10,11... | collective-permute-start | bytes 589832 | tf_op jit(solution)/shard_map/ppermute | solution.py:813
  58.1 9.8 %collective-permute-start.19 = (f32[192,128]{1,0:T(8,128)S(1)}, f32[192,128]{1,0:T(8,128)S(1)}, u32[]{:S(2)}, u32[]{:S(2)}) collective-permute-start(f32[192,128]{1,0:T(8,128)S(1)} %get-tuple-element.166.refs_0_), channel_id=1, source_target_pairs={{0,8},{4,12},{8,0},{12,4},{16,24},{20,28},{24,16},{28,20},{1,9},{5... | collective-permute-start | bytes 294920 | tf_op jit(solution)/shard_map/ppermute | solution.py:669
  58.5 9.4 %collective-permute-start.20 = (f32[192,128]{1,0:T(8,128)S(1)}, f32[192,128]{1,0:T(8,128)S(1)}, u32[]{:S(2)}, u32[]{:S(2)}) collective-permute-start(f32[192,128]{1,0:T(8,128)S(1)} %get-tuple-element.167.refs_2_), channel_id=1, source_target_pairs={{0,16},{4,20},{8,24},{12,28},{16,0},{20,4},{24,8},{28,12},{1,17},{... | collective-permute-start | bytes 294920 | tf_op jit(solution)/shard_map/ppermute | solution.py:669
  60.0 8.0 %collective-permute-start.24 = (f32[216,128]{1,0:T(8,128)S(1)}, f32[216,128]{1,0:T(8,128)S(1)}, u32[]{:S(2)}, u32[]{:S(2)}) collective-permute-start(f32[216,128]{1,0:T(8,128)S(1)} %get-tuple-element.175), channel_id=1, source_target_pairs={{0,4},{4,0},{8,12},{12,8},{16,20},{20,16},{24,28},{28,24},{1,5},{5... | collective-permute-start | bytes 331784 | tf_op jit(solution)/shard_map/ppermute | solution.py:669
  60.9 7.3 %collective-permute-start.25 = (f32[216,128]{1,0:T(8,128)S(1)}, f32[216,128]{1,0:T(8,128)S(1)}, u32[]{:S(2)}, u32[]{:S(2)}) collective-permute-start(f32[216,128]{1,0:T(8,128)S(1)} %get-tuple-element.176), channel_id=1, source_target_pairs={{0,8},{4,12},{8,0},{12,4},{16,24},{20,28},{24,16},{28,20},{1,9},{5... | collective-permute-start | bytes 331784 | tf_op jit(solution)/shard_map/ppermute | solution.py:669
  61.2 8.9 %collective-permute-start.26 = (f32[216,128]{1,0:T(8,128)S(1)}, f32[216,128]{1,0:T(8,128)S(1)}, u32[]{:S(2)}, u32[]{:S(2)}) collective-permute-start(f32[216,128]{1,0:T(8,128)S(1)} %get-tuple-element.177), channel_id=1, source_target_pairs={{0,12},{4,8},{8,4},{12,0},{16,28},{20,24},{24,20},{28,16},{1,13},{... | collective-permute-start | bytes 331784 | tf_op jit(solution)/shard_map/ppermute | solution.py:669
  70.1 11.9 %collective-permute-start.27 = (f32[1024,768]{1,0:T(8,128)S(1)}, f32[1024,768]{1,0:T(8,128)S(1)}, u32[]{:S(2)}, u32[]{:S(2)}) collective-permute-start(f32[1024,768]{1,0:T(8,128)S(1)} %get-tuple-element.196.own), channel_id=1, source_target_pairs={{0,1},{1,0},{2,3},{3,2},{4,5},{5,4},{6,7},{7,6},{8,9},{9,8},{10,11... | collective-permute-start | bytes 9437192 | tf_op jit(solution)/shard_map/ppermute | solution.py:819
  70.2 16.9 %collective-permute-start.31 = (f32[1024,512]{1,0:T(8,128)S(1)}, f32[1024,512]{1,0:T(8,128)S(1)}, u32[]{:S(2)}, u32[]{:S(2)}) collective-permute-start(f32[1024,512]{1,0:T(8,128)S(1)} %get-tuple-element.203.own), channel_id=1, source_target_pairs={{0,1},{1,0},{2,3},{3,2},{4,5},{5,4},{6,7},{7,6},{8,9},{9,8},{10,11... | collective-permute-start | bytes 6291464 | tf_op jit(solution)/shard_map/ppermute | solution.py:819
  70.7 9.1 %collective-permute-start.28 = (f32[384,128]{1,0:T(8,128)S(1)}, f32[384,128]{1,0:T(8,128)S(1)}, u32[]{:S(2)}, u32[]{:S(2)}) collective-permute-start(f32[384,128]{1,0:T(8,128)S(1)} %get-tuple-element.197.refs_0_), channel_id=1, source_target_pairs={{0,4},{4,0},{8,12},{12,8},{16,20},{20,16},{24,28},{28,24},{1,5},{5... | collective-permute-start | bytes 589832 | tf_op jit(solution)/shard_map/ppermute | solution.py:669
  71.8 8.0 %collective-permute-start.30 = (f32[216,128]{1,0:T(8,128)S(1)}, f32[216,128]{1,0:T(8,128)S(1)}, u32[]{:S(2)}, u32[]{:S(2)}) collective-permute-start(f32[216,128]{1,0:T(8,128)S(1)} %get-tuple-element.199.refs_4_), channel_id=1, source_target_pairs={{0,16},{4,20},{8,24},{12,28},{16,0},{20,4},{24,8},{28,12},{1,17},{... | collective-permute-start | bytes 331784 | tf_op jit(solution)/shard_map/ppermute | solution.py:669
  72.4 5.2 %collective-permute-start.29 = (f32[192,128]{1,0:T(8,128)S(1)}, f32[192,128]{1,0:T(8,128)S(1)}, u32[]{:S(2)}, u32[]{:S(2)}) collective-permute-start(f32[192,128]{1,0:T(8,128)S(1)} %get-tuple-element.198.refs_2_), channel_id=1, source_target_pairs={{0,8},{4,12},{8,0},{12,4},{16,24},{20,28},{24,16},{28,20},{1,9},{5... | collective-permute-start | bytes 294920 | tf_op jit(solution)/shard_map/ppermute | solution.py:669
  79.9 11.6 %collective-permute-start.32 = (f32[384,128]{1,0:T(8,128)S(1)}, f32[384,128]{1,0:T(8,128)S(1)}, u32[]{:S(2)}, u32[]{:S(2)}) collective-permute-start(f32[384,128]{1,0:T(8,128)S(1)} %get-tuple-element.207.refs_1_), channel_id=1, source_target_pairs={{0,4},{4,0},{8,12},{12,8},{16,20},{20,16},{24,28},{28,24},{1,5},{5... | collective-permute-start | bytes 589832 | tf_op jit(solution)/shard_map/ppermute | solution.py:669
  80.8 10.7 %collective-permute-start.33 = (f32[216,128]{1,0:T(8,128)S(1)}, f32[216,128]{1,0:T(8,128)S(1)}, u32[]{:S(2)}, u32[]{:S(2)}) collective-permute-start(f32[216,128]{1,0:T(8,128)S(1)} %get-tuple-element.208.refs_3_), channel_id=1, source_target_pairs={{0,4},{4,0},{8,12},{12,8},{16,20},{20,16},{24,28},{28,24},{1,5},{5... | collective-permute-start | bytes 331784 | tf_op jit(solution)/shard_map/ppermute | solution.py:669
  81.9 9.5 %collective-permute-start.34 = (f32[216,128]{1,0:T(8,128)S(1)}, f32[216,128]{1,0:T(8,128)S(1)}, u32[]{:S(2)}, u32[]{:S(2)}) collective-permute-start(f32[216,128]{1,0:T(8,128)S(1)} %get-tuple-element.208.refs_3_), channel_id=1, source_target_pairs={{0,8},{4,12},{8,0},{12,4},{16,24},{20,28},{24,16},{28,20},{1,9},{5... | collective-permute-start | bytes 331784 | tf_op jit(solution)/shard_map/ppermute | solution.py:669
  81.9 9.5 %collective-permute-start.35 = (f32[216,128]{1,0:T(8,128)S(1)}, f32[216,128]{1,0:T(8,128)S(1)}, u32[]{:S(2)}, u32[]{:S(2)}) collective-permute-start(f32[216,128]{1,0:T(8,128)S(1)} %get-tuple-element.208.refs_3_), channel_id=1, source_target_pairs={{0,12},{4,8},{8,4},{12,0},{16,28},{20,24},{24,20},{28,16},{1,13},{... | collective-permute-start | bytes 331784 | tf_op jit(solution)/shard_map/ppermute | solution.py:669
  (6 other events, 26.3 us)
